TPU v7x, 128 devices: a whole 4x4x4 slice. The times are simulated.
128 devices in a mesh: dp: 16 (over z, x_lo, core), ctx: 8 (over y, x_hi).
Axes of the slice: x: 4 (x_hi: 2, x_lo: 2; x = x_hi * 2 + x_lo), y: 4, z: 4, core: 2. Of those that a mesh axis runs over, the one named last changes fastest.
Arguments:
- layer_input: bfloat16 [4096, 8192], P('ctx'), may hold values from -6 to 6
- queries: bfloat16 [4096, 8192], P('ctx', 'dp'), may hold values from -13 to 13
- key_vectors: bfloat16 [4096, 1024], P('ctx'), may hold values from -6 to 6
- value_vectors: bfloat16 [4096, 1024], P('ctx'), may hold values from -6 to 6
- grad_output: bfloat16 [4096, 8192], P('ctx', 'dp'), may hold values from -1.5 to 1.5
- positions: int32 [4096], P('ctx'), may hold values from 0 to 4095, as said below
Outputs:
- grad_queries: bfloat16 [4096, 8192], P('ctx', 'dp')
- grad_keys: bfloat16 [4096, 1024], P('ctx', 'dp')
- grad_values: bfloat16 [4096, 1024], P('ctx', 'dp')
- grad_wq: float32 [8192, 8192], P('ctx', 'dp')
- grad_wk: float32 [8192, 1024], P('ctx', 'dp')
- grad_wv: float32 [8192, 1024], P('ctx', 'dp')
Inputs may be any that keep to these rules, and one draw needn't show every extreme that they name: The positions are 0 to 4095, each once, in aligned runs of 256 rows that hold consecutive ascending positions starting at a multiple of 256.
All inputs are finite; a program needn't handle non-finite values.
Results may differ from a plain program's by a relative error of at most 0.0061.
Values may be sent and summed in bfloat16 or wider, within the bound.
No kernel may reach another device: no remote copies, remote signals or barrier semaphores. Data moves between devices by JAX's collectives and lax.ppermute only.
A program may use at most 128 MiB of HBM per device.

v0:
```python
import math

import jax
import jax.numpy as jnp
from jax import lax
from jax.sharding import PartitionSpec as P

HD = 128
QH = 64
KVH = 8


LOW_VALUE = -1e30


def swapped(value, axis, distance):
    mask = 2**distance
    pairs = [(source, source ^ mask) for source in range(lax.axis_size(axis))]
    return lax.ppermute(value, axis, pairs)


def contract(left, right, left_dim, right_dim):
    return lax.dot_general(
        left, right, (((left_dim,), (right_dim,)), ((), ())), preferred_element_type=jnp.float32
    )


def over_blocks(step_fn, running, key_rows, value_rows, key_pos, block):
    count = key_rows.shape[0]
    number = count // block
    stacked = (
        key_rows.reshape(number, block, key_rows.shape[1]),
        value_rows.reshape(number, block, value_rows.shape[1]),
        key_pos.reshape(number, block),
    )

    def advance(state, items):
        return step_fn(state, items[0], items[1], items[2])

    return lax.scan(advance, running, stacked)


def make_stat_step(query_rows, grad_rows, query_pos, row_limit, factor):

    def stat_step(running, key_block, value_block, key_pos):

        def stat_compute(state):
            row_max, denom, weighted = state
            scores = contract(query_rows, key_block, 1, 1) * factor
            visible = key_pos[None, :] <= query_pos[:, None]
            scores = jnp.where(visible, scores, LOW_VALUE)
            grad_probs = contract(grad_rows, value_block, 1, 1)
            new_max = jnp.maximum(row_max, jnp.max(scores, axis=1))
            keep = jnp.exp(row_max - new_max)
            expo = jnp.where(visible, jnp.exp(scores - new_max[:, None]), 0.0)
            return (
                new_max,
                denom * keep + jnp.sum(expo, axis=1),
                weighted * keep + jnp.sum(expo * grad_probs, axis=1),
            )

        def stat_skipped(state):
            return state

        return (lax.cond(jnp.min(key_pos) <= row_limit, stat_compute, stat_skipped, running), None)

    return stat_step


def make_grad_step(query_rows, grad_rows, query_pos, row_limit, lse, row_dots, factor):

    def grad_step(running, key_block, value_block, key_pos):

        def grad_compute(dq_sum):
            scores = contract(query_rows, key_block, 1, 1) * factor
            visible = key_pos[None, :] <= query_pos[:, None]
            probs = jnp.where(visible, jnp.exp(scores - lse[:, None]), 0.0)
            grad_probs = contract(grad_rows, value_block, 1, 1)
            grad_scores = (probs * (grad_probs - row_dots[:, None])).astype(jnp.bfloat16)
            probs_low = probs.astype(jnp.bfloat16)
            return (
                dq_sum + contract(grad_scores, key_block, 1, 0),
                contract(grad_scores, query_rows, 0, 0),
                contract(probs_low, grad_rows, 0, 0),
            )

        def grad_skipped(dq_sum):
            empty = jnp.zeros((key_block.shape[0], query_rows.shape[1]), jnp.float32)
            return (dq_sum, empty, empty)

        new_dq, key_part, value_part = lax.cond(
            jnp.min(key_pos) <= row_limit, grad_compute, grad_skipped, running
        )
        return (new_dq, (key_part, value_part))

    return grad_step


def local(layer_input, queries, key_vectors, value_vectors, grad_output, positions):
    local_count = queries.shape[0]
    head_size = HD
    local_heads = queries.shape[1] // head_size
    group = QH // KVH
    kv_index = lax.axis_index("dp") * local_heads // group
    key_local = lax.dynamic_slice_in_dim(key_vectors, kv_index * head_size, head_size, 1)
    value_local = lax.dynamic_slice_in_dim(value_vectors, kv_index * head_size, head_size, 1)
    query_rows = (
        queries.reshape(local_count, local_heads, head_size)
        .transpose(1, 0, 2)
        .reshape(-1, head_size)
    )
    grad_rows = (
        grad_output.reshape(local_count, local_heads, head_size)
        .transpose(1, 0, 2)
        .reshape(-1, head_size)
    )
    query_pos = jnp.tile(positions, local_heads)
    stacked_count = query_rows.shape[0]
    block = local_count // 2
    factor = 1.0 / math.sqrt(head_size)
    row_limit = jnp.max(positions)
    empty_rows = jnp.zeros((stacked_count,), jnp.float32)
    start_stats = (jnp.full((stacked_count,), LOW_VALUE, jnp.float32), empty_rows, empty_rows)
    zeros_query = jnp.zeros((stacked_count, head_size), jnp.float32)
    stat_step = make_stat_step(query_rows, grad_rows, query_pos, row_limit, factor)
    key_all, value_all, pos_all = (
        lax.all_gather(key_local, "ctx", axis=0, tiled=True),
        lax.all_gather(value_local, "ctx", axis=0, tiled=True),
        lax.all_gather(positions, "ctx", axis=0, tiled=True),
    )
    (row_max, denom, weighted), _ = over_blocks(
        stat_step, start_stats, key_all, value_all, pos_all, block
    )
    lse = row_max + jnp.log(denom)
    row_dots = weighted / denom
    grad_step = make_grad_step(query_rows, grad_rows, query_pos, row_limit, lse, row_dots, factor)
    dq_sum, (key_parts, value_parts) = over_blocks(
        grad_step, zeros_query, key_all, value_all, pos_all, block
    )
    partials = jnp.concatenate(
        [key_parts.reshape(-1, head_size), value_parts.reshape(-1, head_size)], axis=1
    )
    summed = lax.psum_scatter(partials, "ctx", scatter_dimension=0, tiled=True)
    key_sum = summed[:, :head_size]
    value_sum = summed[:, head_size:]
    group_devices = lax.axis_size("dp") // KVH
    other_key, other_value = swapped((key_sum, value_sum), "dp", 0)
    key_sum = key_sum + other_key
    value_sum = value_sum + other_value
    share_width = head_size // group_devices
    member = lax.axis_index("dp") % group_devices
    key_share = lax.dynamic_slice_in_dim(key_sum, member * share_width, share_width, 1)
    value_share = lax.dynamic_slice_in_dim(value_sum, member * share_width, share_width, 1)
    grad_query = (dq_sum * factor).astype(jnp.bfloat16)
    grad_query = (
        grad_query.reshape(local_heads, local_count, head_size)
        .transpose(1, 0, 2)
        .reshape(local_count, local_heads * head_size)
    )
    grad_key = (key_share * factor).astype(jnp.bfloat16)
    grad_value = value_share.astype(jnp.bfloat16)
    grad_qkv = jnp.concatenate([grad_query, grad_key, grad_value], axis=1)
    ctx_count = lax.axis_size("ctx")
    norm_factor = 1.0 / math.sqrt(ctx_count * local_count)
    weights = lax.psum_scatter(
        contract(layer_input, grad_qkv, 0, 0) * norm_factor, "ctx", scatter_dimension=0, tiled=True
    )
    query_cols = grad_query.shape[1]
    key_cols = grad_key.shape[1]
    return (
        grad_query,
        grad_key,
        grad_value,
        weights[:, :query_cols],
        weights[:, query_cols : query_cols + key_cols],
        weights[:, query_cols + key_cols :],
    )


def solution(mesh):
    in_specs = (
        P("ctx", None),
        P("ctx", "dp"),
        P("ctx", None),
        P("ctx", None),
        P("ctx", "dp"),
        P("ctx"),
    )
    out_specs = (
        P("ctx", "dp"),
        P("ctx", "dp"),
        P("ctx", "dp"),
        P("ctx", "dp"),
        P("ctx", "dp"),
        P("ctx", "dp"),
    )
    return jax.shard_map(local, mesh=mesh, in_specs=in_specs, out_specs=out_specs, check_vma=False)
```

profile of v0, /device:TPU:1, one launch (start us, length us, event | category | flops | bytes accessed | tf_op | source)
XLA Modules:
  0.0 668.3 jit_solution(9316910174135121111)
XLA Ops:
  9.3 1.6 constant_dynamic-slice_fusion.2
  12.3 26.8 %all-gather = s32[8,1,512]{2,1,0:T(1,128)S(1)} all-gather(s32[1,1,512]{2,1,0:T(1,128)} %bitcast.97), channel_id=1, replica_groups=mesh['dp'=16,'ctx'=8] {'ctx'}, dimensions={0}, use_global_device_ids=true | all-gather | bytes 18432 | tf_op jit(solution)/shard_map/all_gather | solution.py:129
  40.4 18.7 %all-gather.4.cloned.1.call-done = bf16[4096,128]{1,0:T(8,128)(2,1)} async-done(((bf16[512,128]{1,0:T(8,128)(2,1)}), bf16[4096,128]{1,0:T(8,128)(2,1)}) %all-gather.4.cloned.1.call-update) | async-done | bytes 1048592 | tf_op jit(solution)/shard_map/all_gather | solution.py:127
  59.1 48.0 %all-gather.6.cloned.1.call-done = bf16[4096,128]{1,0:T(8,128)(2,1)} async-done(((bf16[512,128]{1,0:T(8,128)(2,1)}), bf16[4096,128]{1,0:T(8,128)(2,1)}) %all-gather.6.cloned.1.call-update) | async-done | bytes 1048592 | tf_op jit(solution)/shard_map/all_gather | solution.py:128
  107.1 68.3 %while.33 = (s32[]{:T(128)}, f32[2048]{0:T(1024)S(1)}, f32[2048]{0:T(1024)S(1)}, f32[2048]{0:T(1024)S(1)}, s32[16,256]{1,0:T(8,128)S(1)}, /*index=5*/s32[]{:T(12...) while((s32[]{:T(128)}, f32[2048]{0:T(1024)S(1)}, ...), condition=%wide.region_8.9_spmd.clone, body=%wide.region_1.8_spmd.clone.sunk | while | flops 275257600 | bytes 7676187 | solution.py:40
  109.1 3.4 conditional.6
  114.4 3.3 conditional.6
  119.7 3.3 conditional.6
  130.9 3.4 conditional.6
  138.2 3.3 conditional.6
  143.6 3.3 conditional.6
  148.9 3.3 conditional.6
  156.2 3.3 conditional.6
  161.5 3.3 conditional.6
  166.8 3.3 conditional.6
  172.1 3.3 conditional.6
  175.6 99.7 %while.34 = (s32[]{:T(128)}, f32[2048,128]{1,0:T(8,128)S(1)}, f32[16,256,128]{2,1,0:T(8,128)}, f32[16,256,128]{2,1,0:T(8,128)}, s32[16,256]{1,0:T(8,128)S(1)}, /...) while((s32[]{:T(128)}, f32[2048,128]{1,0:T(8,128)S(1)}, ...), condition=%wide.region_13.14_spmd.clone, body=%wide.region_9.13_spmd.clone.sunk | while | flops 675545344 | bytes 14671115 | solution.py:40
  177.5 5.2 conditional.7
  181.2 1.5 convolution_add_fusion
  185.3 5.2 conditional.7
  189.0 1.5 convolution_add_fusion
  193.2 5.2 conditional.7
  196.8 1.5 convolution_add_fusion
  209.2 5.2 conditional.7
  212.8 1.5 convolution_add_fusion
  219.7 5.2 conditional.7
  223.4 1.5 convolution_add_fusion
  227.5 5.2 conditional.7
  231.2 1.5 convolution_add_fusion
  235.4 5.2 conditional.7
  239.0 1.5 convolution_add_fusion
  245.9 5.2 conditional.7
  249.6 1.5 convolution_add_fusion
  253.7 5.2 conditional.7
  257.4 1.5 convolution_add_fusion
  261.5 5.2 conditional.7
  269.4 5.2 conditional.7
  273.0 1.5 convolution_add_fusion
  275.3 2.9 copy.29
  278.2 2.9 copy.28
  281.1 4.6 pad_maximum_fusion
  285.8 124.7 %reduce-scatter.3.cloned.1.call-done = f32[512,256]{0,1:T(8,128)} async-done(((f32[4096,256]{0,1:T(8,128)}), f32[512,256]{0,1:T(8,128)}) %reduce-scatter.3.cloned.1.call-update) | async-done | bytes 524304 | tf_op jit(solution)/shard_map/reduce_scatter | solution.py:143
  411.6 1.8 collective-permute-start.1
  416.1 12.3 %multiply_bitcast_fusion = f32[8192,640]{0,1:T(8,128)} fusion(bf16[512,8192]{1,0:T(8,128)(2,1)} %param.14, bf16[512,64]{1,0:T(8,128)(2,1)S(1)} %copy.26, bf16[512,64]{1,0:T(8,128)(2,1)S(1)} %copy.25, bf16[512,512]{1,0:T(8,128)(2,1)S(1)} %bitcast.92), kind=kOutput, calls=%fused_computation.47 | convolution fusion | flops 5375918080 | bytes 30015488 | tf_op jit(solution)/shard_map/dot_general | solution.py:23
  428.4 225.4 %reduce-scatter.5.cloned.1.call-done = f32[1024,640]{0,1:T(8,128)} async-done(((f32[8192,640]{0,1:T(8,128)}), f32[1024,640]{0,1:T(8,128)}) %reduce-scatter.5.cloned.1.call-update) | async-done | bytes 2621456 | tf_op jit(solution)/shard_map/reduce_scatter | solution.py:165
  653.9 3.2 slice.22
  657.0 2.9 copy.27
  659.9 1.9 fusion.44
  (267 shorter events, 118.2 us)
Async XLA Ops:
  7.2 1.4 copy-start
  7.2 99.9 %copy-start.3 = (s32[512]{0:T(512)S(1)}, s32[512]{0:T(512)}, u32[]{:S(2)}) copy-start(s32[512]{0:T(512)} %param.19) | copy-start | bytes 6148
  7.2 33.1 %copy-start.2 = (bf16[512,512]{1,0:T(8,128)(2,1)S(1)}, bf16[512,512]{1,0:T(8,128)(2,1)}, u32[]{:S(2)}) copy-start(bf16[512,512]{1,0:T(8,128)(2,1)} %param.18) | copy-start | bytes 1572868
  7.2 51.9 %all-gather.4.cloned.1.call-start = ((), (), s32[]{:S(2)}) async-start(), calls=%async_computation.2 | async-start | bytes 1179648 | tf_op jit(solution)/shard_map/all_gather | solution.py:127
  9.3 97.8 %all-gather.6.cloned.1.call-start = ((), (), s32[]{:S(2)}) async-start(), calls=%async_computation.3 | async-start | bytes 1179648 | tf_op jit(solution)/shard_map/all_gather | solution.py:128
  10.9 399.6 %reduce-scatter.3.cloned.1.call-start = ((), (), s32[]{:S(2)}) async-start(), calls=%async_computation.4 | async-start | bytes 4718592 | tf_op jit(solution)/shard_map/reduce_scatter | solution.py:143
  285.7 368.1 %reduce-scatter.5.cloned.1.call-start = ((), (), s32[]{:S(2)}) async-start(), calls=%async_computation.5 | async-start | bytes 23592960 | tf_op jit(solution)/shard_map/reduce_scatter | solution.py:165
  411.6 3.0 collective-permute-start.1
  413.4 1.7 collective-permute-start
  414.0 14.3 %copy-start.1 = (bf16[64,8,4,128]{3,1,2,0:T(8,128)(2,1)}, bf16[64,8,4,128]{3,1,2,0:T(8,128)(2,1)S(1)}, u32[]{:S(2)}) copy-start(bf16[64,8,4,128]{3,1,2,0:T(8,128)(2,1)S(1)} %copy.38) | copy-start | bytes 1572868
  414.5 13.8 %copy-start.4 = (bf16[512,64]{0,1:T(8,128)(2,1)}, bf16[512,64]{0,1:T(8,128)(2,1)S(1)}, u32[]{:S(2)}) copy-start(bf16[512,64]{0,1:T(8,128)(2,1)S(1)} %fusion.37) | copy-start | bytes 196612
  416.0 12.4 %copy-start.5 = (bf16[512,64]{0,1:T(8,128)(2,1)}, bf16[512,64]{0,1:T(8,128)(2,1)S(1)}, u32[]{:S(2)}) copy-start(bf16[512,64]{0,1:T(8,128)(2,1)S(1)} %fusion.39) | copy-start | bytes 196612
Sparse Core Ops, SparseCore 0:
  11.0 48.0 all-gather.3
  62.0 45.0 all-gather.5
  285.9 124.5 reduce-scatter.2
  428.5 225.2 reduce-scatter.4
where the time goes:
time: 673 us; the launch traced here: 668 us
  waiting for transfers between devices  418 us (62%)
  matrix products  98.9 us (15%)
  loops' own time  43.9 us (7%)
  other arithmetic  32.7 us (5%)
  local copies, waits for them, and re-layouts  32.3 us (5%)
  blocking collectives  26.8 us (4%)
  between operations  14 us (2%)
    reduce_scatter x1, waiting for transfers between devices, local(): lax.psum_scatter(contract(layer_input, grad_qkv, 0, 0) * norm_factor, 'ct...  225 us
    reduce_scatter x1, waiting for transfers between devices, local(): summed = lax.psum_scatter(partials, 'ctx', scatter_dimension=0, tiled=True)  125 us
    dot_general x78, matrix products, contract(): lax.dot_general(left, right, (((left_dim,), (right_dim,)), ((), ())), pre...  98.9 us
    all_gather x1, waiting for transfers between devices, local(): lax.all_gather(value_local, 'ctx', axis=0, tiled=True)  48 us
    another operation x2, loops' own time, over_blocks(): return lax.scan(advance, running, stacked)  42.2 us
    all_gather x1, blocking collectives, local(): lax.all_gather(positions, 'ctx', axis=0, tiled=True)  26.8 us
    all_gather x1, waiting for transfers between devices, local(): lax.all_gather(key_local, 'ctx', axis=0, tiled=True)  18.7 us
  transfers between devices with their start and end apart: 6, of which 6 were waited for; matrix products, arithmetic and copies ran while one was open for 1% of the time, Pallas kernels for 0%

commit v1 on v0

v1 whole, which is shorter than its diff:
```python
import functools
import math

import jax
import jax.numpy as jnp
from jax import lax
from jax.experimental import pallas as pl
from jax.experimental.pallas import tpu as pltpu
from jax.sharding import PartitionSpec as P

HD = 128
QH = 64
KVH = 8
RUN = 256
LOW = -1e30
LOG2E = 1.4426950408889634
VMEM_BYTES = 60 * 1024 * 1024


def contract(left, right, left_dim, right_dim):
    return lax.dot_general(
        left, right, (((left_dim,), (right_dim,)), ((), ())), preferred_element_type=jnp.float32
    )


def ctx_peer(index, dy, dx):
    return ((index // 2 + dy) % 4) * 2 + (index % 2 + dx) % 2


def to_peer(value, dy, dx):
    return lax.ppermute(value, "ctx", [(i, ctx_peer(i, dy, dx)) for i in range(8)])


def swap_cores(value):
    return lax.ppermute(value, "dp", [(i, i ^ 1) for i in range(16)])


SHIFTS = [(s // 2, s % 2) for s in range(8)]


def attention_kernel(
    heads, info_ref, q_ref, g_ref, a_ref, b_ref, dq_ref, keep_ref, give_ref,
    ks, vs, kt, scores, grads, dka, dva, qh, gh, dqt,
):
    slots, slot_rows, _ = a_ref.shape
    runs_per_slot = 2
    scale = 1.0 / math.sqrt(HD)
    core = info_ref[2 * slots]
    for b in range(slots * runs_per_slot):
        slot, part = b // runs_per_slot, b % runs_per_slot
        rows = slice(part * RUN, (part + 1) * RUN)
        at = pl.multiple_of(info_ref[b] * RUN, RUN)
        first, second = a_ref[slot, rows, :], b_ref[slot, rows, :]
        key_block = jnp.where(core == 0, first, second)
        ks[pl.ds(at, RUN), :] = key_block
        kt[:, pl.ds(at, RUN)] = key_block.T
        vs[pl.ds(at, RUN), :] = jnp.where(core == 0, second, first)
    dka[...] = jnp.zeros_like(dka)
    dva[...] = jnp.zeros_like(dva)
    for half in range(2):
        run = info_ref[half]
        rows = slice(half * RUN, (half + 1) * RUN)
        for h in range(heads):
            qh[h * RUN : (h + 1) * RUN, :] = q_ref[rows, h * HD : (h + 1) * HD]
            gh[h * RUN : (h + 1) * RUN, :] = g_ref[rows, h * HD : (h + 1) * HD]

        def stat_step(j, state, diagonal):
            at = pl.multiple_of(j * RUN, RUN)
            key_block = ks[pl.ds(at, RUN), :]
            value_block = vs[pl.ds(at, RUN), :]
            new_state = []
            for h in range(heads):
                row_max, denom, weighted = state[h]
                cols = slice(h * RUN, (h + 1) * RUN)
                s = contract(key_block, qh[cols, :], 1, 1) * (scale * LOG2E)
                if diagonal:
                    key_at = lax.broadcasted_iota(jnp.int32, (RUN, RUN), 0)
                    query_at = lax.broadcasted_iota(jnp.int32, (RUN, RUN), 1)
                    s = jnp.where(key_at <= query_at, s, LOW)
                scores[pl.ds(at, RUN), cols] = s
                dp = contract(value_block, gh[cols, :], 1, 1)
                grads[pl.ds(at, RUN), cols] = dp
                s3 = s.reshape(RUN // 8, 8, RUN)
                dp3 = dp.reshape(RUN // 8, 8, RUN)
                new_max = jnp.maximum(row_max, jnp.max(s3, axis=0))
                fade = jnp.exp2(row_max - new_max)
                expo = jnp.exp2(s3 - new_max[None])
                if diagonal:
                    expo = jnp.where(s3 > 0.5 * LOW, expo, 0.0)
                new_state.append(
                    (
                        new_max,
                        denom * fade + jnp.sum(expo, axis=0),
                        weighted * fade + jnp.sum(expo * dp3, axis=0),
                    )
                )
            return tuple(new_state)

        zeros = jnp.zeros((8, RUN), jnp.float32)
        state = tuple((jnp.full((8, RUN), LOW, jnp.float32), zeros, zeros) for _ in range(heads))
        state = lax.fori_loop(0, run, lambda j, st: stat_step(j, st, False), state)
        state = stat_step(run, state, True)
        lse, dots = [], []
        for h in range(heads):
            row_max, denom, weighted = state[h]
            top = jnp.max(row_max, axis=0, keepdims=True)
            fade = jnp.exp2(row_max - top)
            total = jnp.sum(denom * fade, axis=0, keepdims=True)
            lse.append(top + jnp.log2(total))
            dots.append(jnp.sum(weighted * fade, axis=0, keepdims=True) / total)
        dqt[...] = jnp.zeros_like(dqt)

        def grad_step(j, carry):
            at = pl.multiple_of(j * RUN, RUN)
            key_cols = kt[:, pl.ds(at, RUN)]
            dk, dv = 0.0, 0.0
            for h in range(heads):
                cols = slice(h * RUN, (h + 1) * RUN)
                p = jnp.exp2(scores[pl.ds(at, RUN), cols] - lse[h])
                ds = (p * (grads[pl.ds(at, RUN), cols] - dots[h])).astype(jnp.bfloat16)
                dv += contract(p.astype(jnp.bfloat16), gh[cols, :], 1, 0)
                dk += contract(ds, qh[cols, :], 1, 0)
                dqt[:, cols] += contract(key_cols, ds, 1, 0)
            dka[pl.ds(at, RUN), :] += dk
            dva[pl.ds(at, RUN), :] += dv
            return carry

        lax.fori_loop(0, run + 1, grad_step, 0)
        for h in range(heads):
            cols = slice(h * RUN, (h + 1) * RUN)
            dq_ref[rows, h * HD : (h + 1) * HD] = (dqt[:, cols] * scale).T.astype(jnp.bfloat16)
    half_head = HD // 2
    for b in range(slots * runs_per_slot):
        slot, part = b // runs_per_slot, b % runs_per_slot
        rows = slice(part * RUN, (part + 1) * RUN)
        at = pl.multiple_of(info_ref[b] * RUN, RUN)
        dk = dka[pl.ds(at, RUN), :] * scale
        dv = dva[pl.ds(at, RUN), :]
        low = jnp.concatenate([dk[:, :half_head], dv[:, :half_head]], axis=1)
        high = jnp.concatenate([dk[:, half_head:], dv[:, half_head:]], axis=1)
        keep_ref[slot, rows, :] = jnp.where(core == 0, low, high).astype(jnp.bfloat16)
        give_ref[slot, rows, :] = jnp.where(core == 0, high, low).astype(jnp.bfloat16)


def attention(info, queries, grad_output, mine, other):
    slots = mine.shape[0]
    count = slots * 2 * RUN
    heads = queries.shape[1] // HD
    wide = heads * RUN
    smem = pl.BlockSpec(memory_space=pltpu.SMEM)
    vmem = pl.BlockSpec(memory_space=pltpu.VMEM)
    shared = jax.ShapeDtypeStruct((slots, 2 * RUN, HD), jnp.bfloat16)
    pairs = heads * 2 * RUN * count // 2
    return pl.pallas_call(
        functools.partial(attention_kernel, heads),
        out_shape=(jax.ShapeDtypeStruct(queries.shape, jnp.bfloat16), shared, shared),
        in_specs=[smem, vmem, vmem, vmem, vmem],
        out_specs=(vmem, vmem, vmem),
        scratch_shapes=[
            pltpu.VMEM((count, HD), jnp.bfloat16),
            pltpu.VMEM((count, HD), jnp.bfloat16),
            pltpu.VMEM((HD, count), jnp.bfloat16),
            pltpu.VMEM((count, wide), jnp.float32),
            pltpu.VMEM((count, wide), jnp.float32),
            pltpu.VMEM((count, HD), jnp.float32),
            pltpu.VMEM((count, HD), jnp.float32),
            pltpu.VMEM((wide, HD), jnp.bfloat16),
            pltpu.VMEM((wide, HD), jnp.bfloat16),
            pltpu.VMEM((HD, wide), jnp.float32),
        ],
        compiler_params=pltpu.CompilerParams(vmem_limit_bytes=VMEM_BYTES),
        cost_estimate=pl.CostEstimate(
            flops=5 * 4 * pairs * HD, bytes_accessed=8 * 1024 * 1024, transcendentals=2 * pairs
        ),
    )(info, queries, grad_output, mine, other)


def local(layer_input, queries, key_vectors, value_vectors, grad_output, positions):
    member = lax.axis_index("dp") % 2
    here = lax.axis_index("ctx")
    head = lax.axis_index("dp") // 2
    count = queries.shape[0]
    width = layer_input.shape[1] // 8
    half = width // 2
    first = member == 0

    key_local = lax.dynamic_slice_in_dim(key_vectors, head * HD, HD, 1)
    value_local = lax.dynamic_slice_in_dim(value_vectors, head * HD, HD, 1)
    runs_here = (positions[::RUN] // RUN).astype(jnp.bfloat16)
    tail = jnp.broadcast_to(jnp.pad(runs_here, (0, HD - 2))[None], (16, HD))
    own = jnp.concatenate([jnp.where(first, key_local, value_local), tail], axis=0)
    got = [own] + [to_peer(own, dy, dx) for dy, dx in SHIFTS[1:]]
    mine = jnp.stack(got)
    other = swap_cores(mine)
    info = jnp.concatenate(
        [mine[:, count, :2].reshape(16).astype(jnp.int32), member.astype(jnp.int32)[None]]
    )

    base = layer_input
    blocks = []
    for dy, dx in SHIFTS:
        target = ((here // 2 + dy) % 4) * 2 + (here % 2 + dx) % 2
        part = lax.dynamic_slice(base, (0, target * width + member * half), (count, half))
        blocks.append(part if (dy, dx) == (0, 0) else to_peer(part, dy, dx))
    input_mine = jnp.concatenate(blocks, axis=0)
    input_other = swap_cores(input_mine)

    grad_query, keep, give = attention(info, queries, grad_output, mine, other)

    summed = (keep.astype(jnp.float32) + swap_cores(give).astype(jnp.float32)).astype(jnp.bfloat16)
    terms = [summed[0]] + [
        to_peer(summed[s], -dy, dx) for s, (dy, dx) in enumerate(SHIFTS) if s > 0
    ]
    total = sum(term.astype(jnp.float32) for term in terms).astype(jnp.bfloat16)

    queries_all = jnp.concatenate([grad_query] + [to_peer(grad_query, dy, dx) for dy, dx in SHIFTS[1:]])
    shared_all = jnp.concatenate([total] + [to_peer(total, dy, dx) for dy, dx in SHIFTS[1:]])
    norm = 1.0 / math.sqrt(count * 8)

    def in_order(a, b):
        return jnp.concatenate([jnp.where(first, a, b), jnp.where(first, b, a)], axis=0)

    grad_wq = in_order(
        contract(input_mine, queries_all, 0, 0), contract(input_other, queries_all, 0, 0)
    )
    grad_wkv = in_order(
        contract(input_mine, shared_all, 0, 0), contract(input_other, shared_all, 0, 0)
    )
    share = HD // 2
    return (
        grad_query,
        total[:, :share],
        total[:, share:],
        grad_wq * norm,
        grad_wkv[:, :share] * norm,
        grad_wkv[:, share:] * norm,
    )


def solution(mesh):
    in_specs = (
        P("ctx", None),
        P("ctx", "dp"),
        P("ctx", None),
        P("ctx", None),
        P("ctx", "dp"),
        P("ctx"),
    )
    out_specs = (P("ctx", "dp"),) * 6
    return jax.shard_map(local, mesh=mesh, in_specs=in_specs, out_specs=out_specs, check_vma=False)
```

time: 673 us -> 266 us (0.40)
  waiting for transfers between devices: 418 us -> 119 us
  matrix products: 98.9 us -> 15.3 us
  starting transfers between devices: 2.06 us -> 79.9 us
  loops' own time: 43.9 us -> 0 us
  other arithmetic: 32.7 us -> 5.19 us
  blocking collectives: 26.8 us -> 0 us
  Pallas kernels: 0 us -> 13.6 us
  between operations: 14 us -> 0.89 us
    reduce_scatter x2 -> x0, waiting for transfers between devices: 350 us -> none  [the longest x1 225 us: local(): lax.psum_scatter(contract(layer_input, grad_qkv, 0, 0) * norm_factor, 'ct...]
    ppermute x2 -> x38, waiting for transfers between devices: 0.81 us -> 119 us  [the longest x35 119 us: to_peer(): lax.ppermute(value, 'ctx', [(i, ctx_peer(i, dy, dx)) for i in range(8)])]
    dot_general x78 -> x4, matrix products: 98.9 us -> 15.3 us  [contract(): lax.dot_general(left, right, (((left_dim,), (right_dim,)), ((), ())), pre...]
    ppermute x2 -> x38, starting transfers between devices: 1.9 us -> 79.9 us  [the longest x35 73.8 us: to_peer(): lax.ppermute(value, 'ctx', [(i, ctx_peer(i, dy, dx)) for i in range(8)])]
    all_gather x2 -> x0, waiting for transfers between devices: 66.7 us -> none  [the longest x1 48 us: local(): lax.all_gather(value_local, 'ctx', axis=0, tiled=True)]
    another operation x34 -> x0, loops' own time: 43.9 us -> none  [the longest x2 42.2 us: over_blocks(): return lax.scan(advance, running, stacked)]
    all_gather x1 -> x0, blocking collectives: 26.8 us -> none  [local(): lax.all_gather(positions, 'ctx', axis=0, tiled=True)]
    reduce_min x32 -> x0, other arithmetic: 20.4 us -> none  [the longest x16 10.2 us: stat_step(): jnp.min(key_pos) <= row_limit]
  transfers between devices with their start and end apart: 6 -> 38, of which waited for: 6 -> 17; matrix products, arithmetic and copies ran while one was open for 1% -> 10% of each run, Pallas kernels for 0% -> 5%
where the time goes in v1:
time: 266 us; the launch traced here: 261 us
  waiting for transfers between devices  119 us (45%)
  starting transfers between devices  79.9 us (30%)
  local copies, waits for them, and re-layouts  26.7 us (10%)
  matrix products  15.3 us (6%)
  Pallas kernels  13.6 us (5%)
  other arithmetic  5.19 us (2%)
    ppermute x35, waiting for transfers between devices, to_peer(): lax.ppermute(value, 'ctx', [(i, ctx_peer(i, dy, dx)) for i in range(8)])  119 us
    ppermute x35, starting transfers between devices, to_peer(): lax.ppermute(value, 'ctx', [(i, ctx_peer(i, dy, dx)) for i in range(8)])  73.8 us
    unnamed x35, local copies, waits for them, and re-layouts  19.4 us
    dot_general x4, matrix products, contract(): lax.dot_general(left, right, (((left_dim,), (right_dim,)), ((), ())), pre...  15.3 us
    pallas_call x1, Pallas kernels, attention(): pl.pallas_call(functools.partial(attention_kernel, heads), out_shape=(jax...  13.6 us
    ppermute x3, starting transfers between devices, swap_cores(): return lax.ppermute(value, 'dp', [(i, i ^ 1) for i in range(16)])  6.05 us
  transfers between devices with their start and end apart: 38, of which 17 were waited for; matrix products, arithmetic and copies ran while one was open for 10% of the time, Pallas kernels for 5%

profile of v1, /device:TPU:1, one launch (start us, length us, event | category | flops | bytes accessed | tf_op | source)
XLA Modules:
  0.0 260.7 jit_solution(897352283594586536)
XLA Ops:
  1.5 1.0 dynamic-slice_select_fusion
  2.5 3.6 %collective-permute-start.5 = (bf16[528,128]{1,0:T(8,128)(2,1)S(1)}, bf16[528,128]{1,0:T(8,128)(2,1)S(1)}, u32[]{:S(2)}, u32[]{:S(2)}) collective-permute-start(bf16[528,128]{1,0:T(8,128)(2,1)S(1)} %pad_maximum_fusion.1), channel_id=1, source_target_pairs={{0,6},{1,7},{2,0},{3,1},{4,2},{5,3},{6,4},{7,5},{8,14},{9,15},{10,... | collective-permute-start | bytes 405512 | tf_op jit(solution)/shard_map/ppermute | solution.py:31
  6.1 2.8 %collective-permute-start.4 = (bf16[528,128]{1,0:T(8,128)(2,1)S(1)}, bf16[528,128]{1,0:T(8,128)(2,1)S(1)}, u32[]{:S(2)}, u32[]{:S(2)}) collective-permute-start(bf16[528,128]{1,0:T(8,128)(2,1)S(1)} %pad_maximum_fusion.1), channel_id=1, source_target_pairs={{0,5},{1,4},{2,7},{3,6},{4,1},{5,0},{6,3},{7,2},{8,13},{9,12},{10,... | collective-permute-start | bytes 405512 | tf_op jit(solution)/shard_map/ppermute | solution.py:31
  8.9 2.6 %collective-permute-start.3 = (bf16[528,128]{1,0:T(8,128)(2,1)S(1)}, bf16[528,128]{1,0:T(8,128)(2,1)S(1)}, u32[]{:S(2)}, u32[]{:S(2)}) collective-permute-start(bf16[528,128]{1,0:T(8,128)(2,1)S(1)} %pad_maximum_fusion.1), channel_id=1, source_target_pairs={{0,4},{1,5},{2,6},{3,7},{4,0},{5,1},{6,2},{7,3},{8,12},{9,13},{10,... | collective-permute-start | bytes 405512 | tf_op jit(solution)/shard_map/ppermute | solution.py:31
  11.6 1.4 collective-permute-start
  13.0 3.9 %constant_dynamic-slice_fusion = (bf16[512,512]{1,0:T(8,128)(2,1)S(1)}, bf16[512,512]{1,0:T(8,128)(2,1)}, bf16[512,512]{1,0:T(8,128)(2,1)}, bf16[512,512]{1,0:T(...) fusion(bf16[512,8192]{1,0:T(8,128)(2,1)} %param.6, ...), kind=kLoop, calls=%fused_computation.61 | loop fusion | bytes 8388640 | tf_op jit(solution)/shard_map/dynamic_slice | solution.py:203
  18.3 0.9 collective-permute-start.1
  19.9 4.1 %collective-permute-done.1 = bf16[528,128]{1,0:T(8,128)(2,1)S(1)} collective-permute-done((bf16[528,128]{1,0:T(8,128)(2,1)S(1)}, bf16[528,128]{1,0:T(8,128)(2,1)S(1)}, u32[]{:S(2)}, u32[]{:S(2)}) %collective-permute-start.1) | collective-permute-done | bytes 135200 | tf_op jit(solution)/shard_map/ppermute | solution.py:31
  24.0 2.6 %collective-permute-start.6 = (bf16[528,128]{1,0:T(8,128)(2,1)S(1)}, bf16[528,128]{1,0:T(8,128)(2,1)S(1)}, u32[]{:S(2)}, u32[]{:S(2)}) collective-permute-start(bf16[528,128]{1,0:T(8,128)(2,1)S(1)} %pad_maximum_fusion.1), channel_id=1, source_target_pairs={{0,7},{1,6},{2,1},{3,0},{4,3},{5,2},{6,5},{7,4},{8,15},{9,14},{10,... | collective-permute-start | bytes 405512 | tf_op jit(solution)/shard_map/ppermute | solution.py:31
  30.1 2.5 collective-permute-start.17
  33.2 1.5 collective-permute-start.16
  36.0 4.7 %collective-permute-start.7 = (bf16[8,528,128]{2,1,0:T(8,128)(2,1)}, bf16[8,528,128]{2,1,0:T(8,128)(2,1)}, u32[]{:S(2)}, u32[]{:S(2)}) collective-permute-start(bf16[8,528,128]{2,1,0:T(8,128)(2,1)} %bitcast_dynamic-update-slice_fusion.a_ref), channel_id=1, source_target_pairs={{0,8},{8,0},{16,24},{24,16},{32,40},{40,32},{48,56},{56,48},{64,72... | collective-permute-start | bytes 3244040 | tf_op jit(solution)/shard_map/ppermute | solution.py:35
  41.5 2.0 collective-permute-done.18
  43.5 2.6 collective-permute-start.20
  46.6 7.8 %collective-permute-done.16 = bf16[512,512]{1,0:T(8,128)(2,1)S(1)} collective-permute-done((bf16[512,512]{1,0:T(8,128)(2,1)}, bf16[512,512]{1,0:T(8,128)(2,1)S(1)}, u32[]{:S(2)}, u32[]{:S(2)}) %collective-permute-start.16) | collective-permute-done | bytes 524320 | tf_op jit(solution)/shard_map/ppermute | solution.py:31
  55.7 20.9 %collective-permute-done.17 = bf16[512,512]{1,0:T(8,128)(2,1)S(1)} collective-permute-done((bf16[512,512]{1,0:T(8,128)(2,1)}, bf16[512,512]{1,0:T(8,128)(2,1)S(1)}, u32[]{:S(2)}, u32[]{:S(2)}) %collective-permute-start.17) | collective-permute-done | bytes 524320 | tf_op jit(solution)/shard_map/ppermute | solution.py:31
  81.4 10.6 %collective-permute-done.22 = bf16[512,512]{1,0:T(8,128)(2,1)S(1)} collective-permute-done((bf16[512,512]{1,0:T(8,128)(2,1)S(1)}, bf16[512,512]{1,0:T(8,128)(2,1)S(1)}, u32[]{:S(2)}, u32[]{:S(2)}) %collective-permute-start.22) | collective-permute-done | bytes 524320 | tf_op jit(solution)/shard_map/ppermute | solution.py:31
  92.9 1.3 collective-permute-start.30
  94.2 13.6 %shard_map.109 = (bf16[512,512]{1,0:T(8,128)(2,1)}, bf16[8,512,128]{2,1,0:T(8,128)(2,1)}, bf16[8,512,128]{2,1,0:T(8,128)(2,1)}) custom-call(s32[17]{0:T(128)} %pad_add_fusion.info_ref, bf16[512,512]{1,0:T(8,128)(2,1)} %q_ref.1, bf16[512,512]{1,0:T(8,128)(2,1)} %g_ref.1, bf16[8,528,128]{2,1,0:T(8,128)(2,1)} %bitcast_dynamic-update-slice_fusion.a_ref, ...), custom_call_target="tpu_custom_call" | custom-call | flops 10737418240 | bytes 8388608 | tf_op jit(solution)/shard_map/pallas_call | solution.py:154
  107.9 22.1 %collective-permute-start.23 = (bf16[512,512]{1,0:T(8,128)(2,1)}, bf16[512,512]{1,0:T(8,128)(2,1)S(1)}, u32[]{:S(2)}, u32[]{:S(2)}) collective-permute-start(bf16[512,512]{1,0:T(8,128)(2,1)} %get-tuple-element.18), channel_id=1, source_target_pairs={{0,1},{1,0},{2,3},{3,2},{4,5},{5,4},{6,7},{7,6},{8,9},{9,8},{10,11... | collective-permute-start | bytes 1572872 | tf_op jit(solution)/shard_map/ppermute | solution.py:31
  130.0 2.0 constant_dynamic-update-slice_fusion.14
  132.0 10.3 %collective-permute-done.23 = bf16[512,512]{1,0:T(8,128)(2,1)S(1)} collective-permute-done((bf16[512,512]{1,0:T(8,128)(2,1)}, bf16[512,512]{1,0:T(8,128)(2,1)S(1)}, u32[]{:S(2)}, u32[]{:S(2)}) %collective-permute-start.23) | collective-permute-done | bytes 524320 | tf_op jit(solution)/shard_map/ppermute | solution.py:31
  143.2 12.4 %collective-permute-done.24 = bf16[512,512]{1,0:T(8,128)(2,1)S(1)} collective-permute-done((bf16[512,512]{1,0:T(8,128)(2,1)}, bf16[512,512]{1,0:T(8,128)(2,1)S(1)}, u32[]{:S(2)}, u32[]{:S(2)}) %collective-permute-start.24) | collective-permute-done | bytes 524320 | tf_op jit(solution)/shard_map/ppermute | solution.py:31
  157.3 3.2 %collective-permute-start.26 = (bf16[512,512]{1,0:T(8,128)(2,1)S(1)}, bf16[512,512]{1,0:T(8,128)(2,1)S(1)}, u32[]{:S(2)}, u32[]{:S(2)}) collective-permute-start(bf16[512,512]{1,0:T(8,128)(2,1)S(1)} %copy-done.2), channel_id=1, source_target_pairs={{0,4},{1,5},{2,6},{3,7},{4,0},{5,1},{6,2},{7,3},{8,12},{9,13},{10,... | collective-permute-start | bytes 1572872 | tf_op jit(solution)/shard_map/ppermute | solution.py:31
  160.8 6.9 %collective-permute-done.29 = bf16[512,512]{1,0:T(8,128)(2,1)S(1)} collective-permute-done((bf16[512,512]{1,0:T(8,128)(2,1)}, bf16[512,512]{1,0:T(8,128)(2,1)S(1)}, u32[]{:S(2)}, u32[]{:S(2)}) %collective-permute-start.29) | collective-permute-done | bytes 524320 | tf_op jit(solution)/shard_map/ppermute | solution.py:31
  167.7 12.5 %collective-permute-done.27 = bf16[512,512]{1,0:T(8,128)(2,1)S(1)} collective-permute-done((bf16[512,512]{1,0:T(8,128)(2,1)}, bf16[512,512]{1,0:T(8,128)(2,1)S(1)}, u32[]{:S(2)}, u32[]{:S(2)}) %collective-permute-start.27) | collective-permute-done | bytes 524320 | tf_op jit(solution)/shard_map/ppermute | solution.py:31
  180.2 4.6 %collective-permute-done.26 = bf16[512,512]{1,0:T(8,128)(2,1)S(1)} collective-permute-done((bf16[512,512]{1,0:T(8,128)(2,1)S(1)}, bf16[512,512]{1,0:T(8,128)(2,1)S(1)}, u32[]{:S(2)}, u32[]{:S(2)}) %collective-permute-start.26) | collective-permute-done | bytes 524320 | tf_op jit(solution)/shard_map/ppermute | solution.py:31
  184.7 8.5 %collective-permute-start.14 = (bf16[512,128]{1,0:T(8,128)(2,1)S(1)}, bf16[512,128]{1,0:T(8,128)(2,1)S(1)}, u32[]{:S(2)}, u32[]{:S(2)}) collective-permute-start(bf16[512,128]{1,0:T(8,128)(2,1)S(1)} %get-tuple-element.38), channel_id=1, source_target_pairs={{0,2},{1,3},{2,4},{3,5},{4,6},{5,7},{6,0},{7,1},{8,10},{9,11},{10,... | collective-permute-start | bytes 393224 | tf_op jit(solution)/shard_map/ppermute | solution.py:31
  194.9 3.0 %collective-permute-done.28 = bf16[512,512]{1,0:T(8,128)(2,1)S(1)} collective-permute-done((bf16[512,512]{1,0:T(8,128)(2,1)}, bf16[512,512]{1,0:T(8,128)(2,1)S(1)}, u32[]{:S(2)}, u32[]{:S(2)}) %collective-permute-start.28) | collective-permute-done | bytes 524320 | tf_op jit(solution)/shard_map/ppermute | solution.py:31
  197.9 2.3 collective-permute-start.13
  200.2 3.3 %collective-permute-start.12 = (bf16[512,128]{1,0:T(8,128)(2,1)S(1)}, bf16[512,128]{1,0:T(8,128)(2,1)S(1)}, u32[]{:S(2)}, u32[]{:S(2)}) collective-permute-start(bf16[512,128]{1,0:T(8,128)(2,1)S(1)} %get-tuple-element.40), channel_id=1, source_target_pairs={{0,4},{1,5},{2,6},{3,7},{4,0},{5,1},{6,2},{7,3},{8,12},{9,13},{10,... | collective-permute-start | bytes 393224 | tf_op jit(solution)/shard_map/ppermute | solution.py:31
  203.5 3.1 %collective-permute-start.11 = (bf16[512,128]{1,0:T(8,128)(2,1)S(1)}, bf16[512,128]{1,0:T(8,128)(2,1)S(1)}, u32[]{:S(2)}, u32[]{:S(2)}) collective-permute-start(bf16[512,128]{1,0:T(8,128)(2,1)S(1)} %get-tuple-element.41), channel_id=1, source_target_pairs={{0,7},{1,6},{2,1},{3,0},{4,3},{5,2},{6,5},{7,4},{8,15},{9,14},{10,... | collective-permute-start | bytes 393224 | tf_op jit(solution)/shard_map/ppermute | solution.py:31
  208.6 1.5 collective-permute-done.12
  210.0 8.1 %collective-permute-done.10 = bf16[512,128]{1,0:T(8,128)(2,1)S(1)} collective-permute-done((bf16[512,128]{1,0:T(8,128)(2,1)S(1)}, bf16[512,128]{1,0:T(8,128)(2,1)S(1)}, u32[]{:S(2)}, u32[]{:S(2)}) %collective-permute-start.10) | collective-permute-done | bytes 131104 | tf_op jit(solution)/shard_map/ppermute | solution.py:31
  218.7 1.6 collective-permute-start.32
  220.3 1.9 collective-permute-start.31
  223.8 3.9 %collective-permute-done.31 = bf16[512,128]{1,0:T(8,128)(2,1)S(1)} collective-permute-done((bf16[512,128]{1,0:T(8,128)(2,1)S(1)}, bf16[512,128]{1,0:T(8,128)(2,1)S(1)}, u32[]{:S(2)}, u32[]{:S(2)}) %collective-permute-start.31) | collective-permute-done | bytes 131104 | tf_op jit(solution)/shard_map/ppermute | solution.py:31
  227.6 1.1 collective-permute-start.33
  228.8 2.4 collective-permute-start.34
  231.2 4.4 %collective-permute-done.33 = bf16[512,128]{1,0:T(8,128)(2,1)S(1)} collective-permute-done((bf16[512,128]{1,0:T(8,128)(2,1)S(1)}, bf16[512,128]{1,0:T(8,128)(2,1)S(1)}, u32[]{:S(2)}, u32[]{:S(2)}) %collective-permute-start.33) | collective-permute-done | bytes 131104 | tf_op jit(solution)/shard_map/ppermute | solution.py:31
  236.3 5.5 %collective-permute-done.37 = bf16[512,128]{1,0:T(8,128)(2,1)S(1)} collective-permute-done((bf16[512,128]{1,0:T(8,128)(2,1)S(1)}, bf16[512,128]{1,0:T(8,128)(2,1)S(1)}, u32[]{:S(2)}, u32[]{:S(2)}) %collective-permute-start.37) | collective-permute-done | bytes 131104 | tf_op jit(solution)/shard_map/ppermute | solution.py:31
  241.9 5.9 %fusion.12 = f32[512,512]{1,0:T(8,128)S(1)} fusion(bf16[4096,512]{1,0:T(8,128)(2,1)} %collective-permute-done.30, bf16[4096,512]{1,0:T(8,128)(2,1)} %constant_dynamic-update-slice_fusion.7), kind=kOutput, calls=%fused_computation.75 | convolution fusion | flops 2147483648 | bytes 9437184 | tf_op jit(solution)/shard_map/dot_general | solution.py:21
  247.8 4.6 %broadcast_select_fusion.1 = (f32[512,512]{1,0:T(8,128)S(1)}, f32[512,512]{1,0:T(8,128)S(1)}) fusion(f32[512,512]{1,0:T(8,128)S(1)} %fusion.12, pred[]{:T(512)S(6)} %eq.29, bf16[4096,512]{1,0:T(8,128)(2,1)S(1)} %copy-done, bf16[4096,512]{1,0:T(8,128)(2,1)} %constant_dynamic-update-slice_fusion.7), kind=kOutput, calls=%fused_computation.7 | convolution fusion | flops 2148007936 | bytes 11534337 | tf_op jit(solution)/shard_map/dot_general | solution.py:21
  252.4 3.5 %fusion.13 = f32[512,128]{1,0:T(8,128)S(1)} fusion(bf16[4096,512]{1,0:T(8,128)(2,1)} %collective-permute-done.30, bf16[4096,128]{1,0:T(8,128)(2,1)S(1)} %constant_dynamic-update-slice_fusion.15), kind=kOutput, calls=%fused_computation.76 | convolution fusion | flops 536870912 | bytes 5505024 | tf_op jit(solution)/shard_map/dot_general | solution.py:21
  255.9 1.3 broadcast_select_fusion.3
  257.4 0.9 copy.19
  258.3 0.9 copy.18
  259.2 1.6 maximum_multiply_fusion
  (89 shorter events, 26.3 us)
Async XLA Ops:
  2.5 30.7 %collective-permute-start.5 = (bf16[528,128]{1,0:T(8,128)(2,1)S(1)}, bf16[528,128]{1,0:T(8,128)(2,1)S(1)}, u32[]{:S(2)}, u32[]{:S(2)}) collective-permute-start(bf16[528,128]{1,0:T(8,128)(2,1)S(1)} %pad_maximum_fusion.1), channel_id=1, source_target_pairs={{0,6},{1,7},{2,0},{3,1},{4,2},{5,3},{6,4},{7,5},{8,14},{9,15},{10,... | collective-permute-start | bytes 405512 | tf_op jit(solution)/shard_map/ppermute | solution.py:31
  6.1 23.9 %collective-permute-start.4 = (bf16[528,128]{1,0:T(8,128)(2,1)S(1)}, bf16[528,128]{1,0:T(8,128)(2,1)S(1)}, u32[]{:S(2)}, u32[]{:S(2)}) collective-permute-start(bf16[528,128]{1,0:T(8,128)(2,1)S(1)} %pad_maximum_fusion.1), channel_id=1, source_target_pairs={{0,5},{1,4},{2,7},{3,6},{4,1},{5,0},{6,3},{7,2},{8,13},{9,12},{10,... | collective-permute-start | bytes 405512 | tf_op jit(solution)/shard_map/ppermute | solution.py:31
  8.9 19.6 %collective-permute-start.3 = (bf16[528,128]{1,0:T(8,128)(2,1)S(1)}, bf16[528,128]{1,0:T(8,128)(2,1)S(1)}, u32[]{:S(2)}, u32[]{:S(2)}) collective-permute-start(bf16[528,128]{1,0:T(8,128)(2,1)S(1)} %pad_maximum_fusion.1), channel_id=1, source_target_pairs={{0,4},{1,5},{2,6},{3,7},{4,0},{5,1},{6,2},{7,3},{8,12},{9,13},{10,... | collective-permute-start | bytes 405512 | tf_op jit(solution)/shard_map/ppermute | solution.py:31
  11.6 15.8 %collective-permute-start.2 = (bf16[528,128]{1,0:T(8,128)(2,1)S(1)}, bf16[528,128]{1,0:T(8,128)(2,1)S(1)}, u32[]{:S(2)}, u32[]{:S(2)}) collective-permute-start(bf16[528,128]{1,0:T(8,128)(2,1)S(1)} %pad_maximum_fusion.1), channel_id=1, source_target_pairs={{0,3},{1,2},{2,5},{3,4},{4,7},{5,6},{6,1},{7,0},{8,11},{9,10},{10,... | collective-permute-start | bytes 405512 | tf_op jit(solution)/shard_map/ppermute | solution.py:31
  11.6 6.8 %collective-permute-start = (bf16[528,128]{1,0:T(8,128)(2,1)S(1)}, bf16[528,128]{1,0:T(8,128)(2,1)S(1)}, u32[]{:S(2)}, u32[]{:S(2)}) collective-permute-start(bf16[528,128]{1,0:T(8,128)(2,1)S(1)} %pad_maximum_fusion.1), channel_id=1, source_target_pairs={{0,1},{1,0},{2,3},{3,2},{4,5},{5,4},{6,7},{7,6},{8,9},{9,8},{10,11... | collective-permute-start | bytes 405512 | tf_op jit(solution)/shard_map/ppermute | solution.py:31
  18.3 5.7 %collective-permute-start.1 = (bf16[528,128]{1,0:T(8,128)(2,1)S(1)}, bf16[528,128]{1,0:T(8,128)(2,1)S(1)}, u32[]{:S(2)}, u32[]{:S(2)}) collective-permute-start(bf16[528,128]{1,0:T(8,128)(2,1)S(1)} %pad_maximum_fusion.1), channel_id=1, source_target_pairs={{0,2},{1,3},{2,4},{3,5},{4,6},{5,7},{6,0},{7,1},{8,10},{9,11},{10,... | collective-permute-start | bytes 405512 | tf_op jit(solution)/shard_map/ppermute | solution.py:31
  24.0 11.3 %collective-permute-start.6 = (bf16[528,128]{1,0:T(8,128)(2,1)S(1)}, bf16[528,128]{1,0:T(8,128)(2,1)S(1)}, u32[]{:S(2)}, u32[]{:S(2)}) collective-permute-start(bf16[528,128]{1,0:T(8,128)(2,1)S(1)} %pad_maximum_fusion.1), channel_id=1, source_target_pairs={{0,7},{1,6},{2,1},{3,0},{4,3},{5,2},{6,5},{7,4},{8,15},{9,14},{10,... | collective-permute-start | bytes 405512 | tf_op jit(solution)/shard_map/ppermute | solution.py:31
  27.3 51.5 %collective-permute-start.19 = (bf16[512,512]{1,0:T(8,128)(2,1)}, bf16[512,512]{1,0:T(8,128)(2,1)S(1)}, u32[]{:S(2)}, u32[]{:S(2)}) collective-permute-start(bf16[512,512]{1,0:T(8,128)(2,1)} %get-tuple-element.28), channel_id=1, source_target_pairs={{0,4},{1,5},{2,6},{3,7},{4,0},{5,1},{6,2},{7,3},{8,12},{9,13},{10,... | collective-permute-start | bytes 1572872 | tf_op jit(solution)/shard_map/ppermute | solution.py:31
  28.6 14.9 %collective-permute-start.18 = (bf16[512,512]{1,0:T(8,128)(2,1)}, bf16[512,512]{1,0:T(8,128)(2,1)S(1)}, u32[]{:S(2)}, u32[]{:S(2)}) collective-permute-start(bf16[512,512]{1,0:T(8,128)(2,1)} %get-tuple-element.29), channel_id=1, source_target_pairs={{0,3},{1,2},{2,5},{3,4},{4,7},{5,6},{6,1},{7,0},{8,11},{9,10},{10,... | collective-permute-start | bytes 1572872 | tf_op jit(solution)/shard_map/ppermute | solution.py:31
  30.1 46.5 %collective-permute-start.17 = (bf16[512,512]{1,0:T(8,128)(2,1)}, bf16[512,512]{1,0:T(8,128)(2,1)S(1)}, u32[]{:S(2)}, u32[]{:S(2)}) collective-permute-start(bf16[512,512]{1,0:T(8,128)(2,1)} %get-tuple-element.30), channel_id=1, source_target_pairs={{0,2},{1,3},{2,4},{3,5},{4,6},{5,7},{6,0},{7,1},{8,10},{9,11},{10,... | collective-permute-start | bytes 1572872 | tf_op jit(solution)/shard_map/ppermute | solution.py:31
  33.2 21.2 %collective-permute-start.16 = (bf16[512,512]{1,0:T(8,128)(2,1)}, bf16[512,512]{1,0:T(8,128)(2,1)S(1)}, u32[]{:S(2)}, u32[]{:S(2)}) collective-permute-start(bf16[512,512]{1,0:T(8,128)(2,1)} %get-tuple-element.31), channel_id=1, source_target_pairs={{0,1},{1,0},{2,3},{3,2},{4,5},{5,4},{6,7},{7,6},{8,9},{9,8},{10,11... | collective-permute-start | bytes 1572872 | tf_op jit(solution)/shard_map/ppermute | solution.py:31
  36.0 58.2 %collective-permute-start.7 = (bf16[8,528,128]{2,1,0:T(8,128)(2,1)}, bf16[8,528,128]{2,1,0:T(8,128)(2,1)}, u32[]{:S(2)}, u32[]{:S(2)}) collective-permute-start(bf16[8,528,128]{2,1,0:T(8,128)(2,1)} %bitcast_dynamic-update-slice_fusion.a_ref), channel_id=1, source_target_pairs={{0,8},{8,0},{16,24},{24,16},{32,40},{40,32},{48,56},{56,48},{64,72... | collective-permute-start | bytes 3244040 | tf_op jit(solution)/shard_map/ppermute | solution.py:35
  43.5 36.2 %collective-permute-start.20 = (bf16[512,512]{1,0:T(8,128)(2,1)}, bf16[512,512]{1,0:T(8,128)(2,1)S(1)}, u32[]{:S(2)}, u32[]{:S(2)}) collective-permute-start(bf16[512,512]{1,0:T(8,128)(2,1)} %get-tuple-element.27), channel_id=1, source_target_pairs={{0,5},{1,4},{2,7},{3,6},{4,1},{5,0},{6,3},{7,2},{8,13},{9,12},{10,... | collective-permute-start | bytes 1572872 | tf_op jit(solution)/shard_map/ppermute | solution.py:31
  54.5 26.1 %collective-permute-start.21 = (bf16[512,512]{1,0:T(8,128)(2,1)S(1)}, bf16[512,512]{1,0:T(8,128)(2,1)S(1)}, u32[]{:S(2)}, u32[]{:S(2)}) collective-permute-start(bf16[512,512]{1,0:T(8,128)(2,1)S(1)} %get-tuple-element.33), channel_id=1, source_target_pairs={{0,6},{1,7},{2,0},{3,1},{4,2},{5,3},{6,4},{7,5},{8,14},{9,15},{10,... | collective-permute-start | bytes 1572872 | tf_op jit(solution)/shard_map/ppermute | solution.py:31
  76.6 15.4 %collective-permute-start.22 = (bf16[512,512]{1,0:T(8,128)(2,1)S(1)}, bf16[512,512]{1,0:T(8,128)(2,1)S(1)}, u32[]{:S(2)}, u32[]{:S(2)}) collective-permute-start(bf16[512,512]{1,0:T(8,128)(2,1)S(1)} %get-tuple-element.26), channel_id=1, source_target_pairs={{0,7},{1,6},{2,1},{3,0},{4,3},{5,2},{6,5},{7,4},{8,15},{9,14},{10,... | collective-permute-start | bytes 1572872 | tf_op jit(solution)/shard_map/ppermute | solution.py:31
  92.9 149.0 %collective-permute-start.30 = (bf16[4096,512]{1,0:T(8,128)(2,1)}, bf16[4096,512]{1,0:T(8,128)(2,1)}, u32[]{:S(2)}, u32[]{:S(2)}) collective-permute-start(bf16[4096,512]{1,0:T(8,128)(2,1)} %constant_dynamic-update-slice_fusion), channel_id=1, source_target_pairs={{0,8},{8,0},{16,24},{24,16},{32,40},{40,32},{48,56},{56,48},{64,72... | collective-permute-start | bytes 12582920 | tf_op jit(solution)/shard_map/ppermute | solution.py:35
  107.8 49.4 %copy-start.2 = (bf16[512,512]{1,0:T(8,128)(2,1)S(1)}, bf16[512,512]{1,0:T(8,128)(2,1)}, u32[]{:S(2)}) copy-start(bf16[512,512]{1,0:T(8,128)(2,1)} %get-tuple-element.18) | copy-start | bytes 1572868
  107.8 52.6 %copy-start.1 = (bf16[8,512,128]{2,1,0:T(8,128)(2,1)S(1)}, bf16[8,512,128]{2,1,0:T(8,128)(2,1)}, u32[]{:S(2)}) copy-start(bf16[8,512,128]{2,1,0:T(8,128)(2,1)} %get-tuple-element.10) | copy-start | bytes 3145732
  107.8 49.4 %collective-permute-start.8 = (bf16[8,512,128]{2,1,0:T(8,128)(2,1)}, bf16[8,512,128]{2,1,0:T(8,128)(2,1)S(1)}, u32[]{:S(2)}, u32[]{:S(2)}) collective-permute-start(bf16[8,512,128]{2,1,0:T(8,128)(2,1)} %get-tuple-element.11), channel_id=1, source_target_pairs={{0,8},{8,0},{16,24},{24,16},{32,40},{40,32},{48,56},{56,48},{64,72... | collective-permute-start | bytes 3145736 | tf_op jit(solution)/shard_map/ppermute | solution.py:35
  107.9 34.5 %collective-permute-start.23 = (bf16[512,512]{1,0:T(8,128)(2,1)}, bf16[512,512]{1,0:T(8,128)(2,1)S(1)}, u32[]{:S(2)}, u32[]{:S(2)}) collective-permute-start(bf16[512,512]{1,0:T(8,128)(2,1)} %get-tuple-element.18), channel_id=1, source_target_pairs={{0,1},{1,0},{2,3},{3,2},{4,5},{5,4},{6,7},{7,6},{8,9},{9,8},{10,11... | collective-permute-start | bytes 1572872 | tf_op jit(solution)/shard_map/ppermute | solution.py:31
  130.0 25.6 %collective-permute-start.24 = (bf16[512,512]{1,0:T(8,128)(2,1)}, bf16[512,512]{1,0:T(8,128)(2,1)S(1)}, u32[]{:S(2)}, u32[]{:S(2)}) collective-permute-start(bf16[512,512]{1,0:T(8,128)(2,1)} %get-tuple-element.18), channel_id=1, source_target_pairs={{0,2},{1,3},{2,4},{3,5},{4,6},{5,7},{6,0},{7,1},{8,10},{9,11},{10,... | collective-permute-start | bytes 1572872 | tf_op jit(solution)/shard_map/ppermute | solution.py:31
  130.0 26.5 %collective-permute-start.25 = (bf16[512,512]{1,0:T(8,128)(2,1)}, bf16[512,512]{1,0:T(8,128)(2,1)S(1)}, u32[]{:S(2)}, u32[]{:S(2)}) collective-permute-start(bf16[512,512]{1,0:T(8,128)(2,1)} %get-tuple-element.18), channel_id=1, source_target_pairs={{0,3},{1,2},{2,5},{3,4},{4,7},{5,6},{6,1},{7,0},{8,11},{9,10},{10,... | collective-permute-start | bytes 1572872 | tf_op jit(solution)/shard_map/ppermute | solution.py:31
  142.3 25.4 %collective-permute-start.29 = (bf16[512,512]{1,0:T(8,128)(2,1)}, bf16[512,512]{1,0:T(8,128)(2,1)S(1)}, u32[]{:S(2)}, u32[]{:S(2)}) collective-permute-start(bf16[512,512]{1,0:T(8,128)(2,1)} %get-tuple-element.18), channel_id=1, source_target_pairs={{0,7},{1,6},{2,1},{3,0},{4,3},{5,2},{6,5},{7,4},{8,15},{9,14},{10,... | collective-permute-start | bytes 1572872 | tf_op jit(solution)/shard_map/ppermute | solution.py:31
  155.6 42.3 %collective-permute-start.28 = (bf16[512,512]{1,0:T(8,128)(2,1)}, bf16[512,512]{1,0:T(8,128)(2,1)S(1)}, u32[]{:S(2)}, u32[]{:S(2)}) collective-permute-start(bf16[512,512]{1,0:T(8,128)(2,1)} %get-tuple-element.18), channel_id=1, source_target_pairs={{0,6},{1,7},{2,0},{3,1},{4,2},{5,3},{6,4},{7,5},{8,14},{9,15},{10,... | collective-permute-start | bytes 1572872 | tf_op jit(solution)/shard_map/ppermute | solution.py:31
  156.4 23.7 %collective-permute-start.27 = (bf16[512,512]{1,0:T(8,128)(2,1)}, bf16[512,512]{1,0:T(8,128)(2,1)S(1)}, u32[]{:S(2)}, u32[]{:S(2)}) collective-permute-start(bf16[512,512]{1,0:T(8,128)(2,1)} %get-tuple-element.18), channel_id=1, source_target_pairs={{0,5},{1,4},{2,7},{3,6},{4,1},{5,0},{6,3},{7,2},{8,13},{9,12},{10,... | collective-permute-start | bytes 1572872 | tf_op jit(solution)/shard_map/ppermute | solution.py:31
  157.3 27.5 %collective-permute-start.26 = (bf16[512,512]{1,0:T(8,128)(2,1)S(1)}, bf16[512,512]{1,0:T(8,128)(2,1)S(1)}, u32[]{:S(2)}, u32[]{:S(2)}) collective-permute-start(bf16[512,512]{1,0:T(8,128)(2,1)S(1)} %copy-done.2), channel_id=1, source_target_pairs={{0,4},{1,5},{2,6},{3,7},{4,0},{5,1},{6,2},{7,3},{8,12},{9,13},{10,... | collective-permute-start | bytes 1572872 | tf_op jit(solution)/shard_map/ppermute | solution.py:31
  167.7 32.5 %collective-permute-start.9 = (bf16[512,128]{1,0:T(8,128)(2,1)S(1)}, bf16[512,128]{1,0:T(8,128)(2,1)S(1)}, u32[]{:S(2)}, u32[]{:S(2)}) collective-permute-start(bf16[512,128]{1,0:T(8,128)(2,1)S(1)} %get-tuple-element.36), channel_id=1, source_target_pairs={{0,1},{1,0},{2,3},{3,2},{4,5},{5,4},{6,7},{7,6},{8,9},{9,8},{10,11... | collective-permute-start | bytes 393224 | tf_op jit(solution)/shard_map/ppermute | solution.py:31
  180.2 23.3 %collective-permute-start.15 = (bf16[512,128]{1,0:T(8,128)(2,1)S(1)}, bf16[512,128]{1,0:T(8,128)(2,1)S(1)}, u32[]{:S(2)}, u32[]{:S(2)}) collective-permute-start(bf16[512,128]{1,0:T(8,128)(2,1)S(1)} %get-tuple-element.37), channel_id=1, source_target_pairs={{0,3},{1,2},{2,5},{3,4},{4,7},{5,6},{6,1},{7,0},{8,11},{9,10},{10,... | collective-permute-start | bytes 393224 | tf_op jit(solution)/shard_map/ppermute | solution.py:31
  184.7 21.8 %collective-permute-start.14 = (bf16[512,128]{1,0:T(8,128)(2,1)S(1)}, bf16[512,128]{1,0:T(8,128)(2,1)S(1)}, u32[]{:S(2)}, u32[]{:S(2)}) collective-permute-start(bf16[512,128]{1,0:T(8,128)(2,1)S(1)} %get-tuple-element.38), channel_id=1, source_target_pairs={{0,2},{1,3},{2,4},{3,5},{4,6},{5,7},{6,0},{7,1},{8,10},{9,11},{10,... | collective-permute-start | bytes 393224 | tf_op jit(solution)/shard_map/ppermute | solution.py:31
  197.9 10.7 %collective-permute-start.13 = (bf16[512,128]{1,0:T(8,128)(2,1)S(1)}, bf16[512,128]{1,0:T(8,128)(2,1)S(1)}, u32[]{:S(2)}, u32[]{:S(2)}) collective-permute-start(bf16[512,128]{1,0:T(8,128)(2,1)S(1)} %get-tuple-element.39), channel_id=1, source_target_pairs={{0,5},{1,4},{2,7},{3,6},{4,1},{5,0},{6,3},{7,2},{8,13},{9,12},{10,... | collective-permute-start | bytes 393224 | tf_op jit(solution)/shard_map/ppermute | solution.py:31
  200.2 9.9 %collective-permute-start.12 = (bf16[512,128]{1,0:T(8,128)(2,1)S(1)}, bf16[512,128]{1,0:T(8,128)(2,1)S(1)}, u32[]{:S(2)}, u32[]{:S(2)}) collective-permute-start(bf16[512,128]{1,0:T(8,128)(2,1)S(1)} %get-tuple-element.40), channel_id=1, source_target_pairs={{0,4},{1,5},{2,6},{3,7},{4,0},{5,1},{6,2},{7,3},{8,12},{9,13},{10,... | collective-permute-start | bytes 393224 | tf_op jit(solution)/shard_map/ppermute | solution.py:31
  203.5 6.5 %collective-permute-start.11 = (bf16[512,128]{1,0:T(8,128)(2,1)S(1)}, bf16[512,128]{1,0:T(8,128)(2,1)S(1)}, u32[]{:S(2)}, u32[]{:S(2)}) collective-permute-start(bf16[512,128]{1,0:T(8,128)(2,1)S(1)} %get-tuple-element.41), channel_id=1, source_target_pairs={{0,7},{1,6},{2,1},{3,0},{4,3},{5,2},{6,5},{7,4},{8,15},{9,14},{10,... | collective-permute-start | bytes 393224 | tf_op jit(solution)/shard_map/ppermute | solution.py:31
  206.6 11.5 %collective-permute-start.10 = (bf16[512,128]{1,0:T(8,128)(2,1)S(1)}, bf16[512,128]{1,0:T(8,128)(2,1)S(1)}, u32[]{:S(2)}, u32[]{:S(2)}) collective-permute-start(bf16[512,128]{1,0:T(8,128)(2,1)S(1)} %get-tuple-element.42), channel_id=1, source_target_pairs={{0,6},{1,7},{2,0},{3,1},{4,2},{5,3},{6,4},{7,5},{8,14},{9,15},{10,... | collective-permute-start | bytes 393224 | tf_op jit(solution)/shard_map/ppermute | solution.py:31
  218.2 18.1 %collective-permute-start.36 = (bf16[512,128]{1,0:T(8,128)(2,1)S(1)}, bf16[512,128]{1,0:T(8,128)(2,1)S(1)}, u32[]{:S(2)}, u32[]{:S(2)}) collective-permute-start(bf16[512,128]{1,0:T(8,128)(2,1)S(1)} %get-tuple-element.25), channel_id=1, source_target_pairs={{0,6},{1,7},{2,0},{3,1},{4,2},{5,3},{6,4},{7,5},{8,14},{9,15},{10,... | collective-permute-start | bytes 393224 | tf_op jit(solution)/shard_map/ppermute | solution.py:31
  218.3 17.9 %collective-permute-start.35 = (bf16[512,128]{1,0:T(8,128)(2,1)S(1)}, bf16[512,128]{1,0:T(8,128)(2,1)S(1)}, u32[]{:S(2)}, u32[]{:S(2)}) collective-permute-start(bf16[512,128]{1,0:T(8,128)(2,1)S(1)} %get-tuple-element.25), channel_id=1, source_target_pairs={{0,5},{1,4},{2,7},{3,6},{4,1},{5,0},{6,3},{7,2},{8,13},{9,12},{10,... | collective-permute-start | bytes 393224 | tf_op jit(solution)/shard_map/ppermute | solution.py:31
  218.7 10.1 %collective-permute-start.32 = (bf16[512,128]{1,0:T(8,128)(2,1)S(1)}, bf16[512,128]{1,0:T(8,128)(2,1)S(1)}, u32[]{:S(2)}, u32[]{:S(2)}) collective-permute-start(bf16[512,128]{1,0:T(8,128)(2,1)S(1)} %get-tuple-element.25), channel_id=1, source_target_pairs={{0,2},{1,3},{2,4},{3,5},{4,6},{5,7},{6,0},{7,1},{8,10},{9,11},{10,... | collective-permute-start | bytes 393224 | tf_op jit(solution)/shard_map/ppermute | solution.py:31
  220.3 7.3 %collective-permute-start.31 = (bf16[512,128]{1,0:T(8,128)(2,1)S(1)}, bf16[512,128]{1,0:T(8,128)(2,1)S(1)}, u32[]{:S(2)}, u32[]{:S(2)}) collective-permute-start(bf16[512,128]{1,0:T(8,128)(2,1)S(1)} %get-tuple-element.25), channel_id=1, source_target_pairs={{0,1},{1,0},{2,3},{3,2},{4,5},{5,4},{6,7},{7,6},{8,9},{9,8},{10,11... | collective-permute-start | bytes 393224 | tf_op jit(solution)/shard_map/ppermute | solution.py:31
  227.6 8.0 %collective-permute-start.33 = (bf16[512,128]{1,0:T(8,128)(2,1)S(1)}, bf16[512,128]{1,0:T(8,128)(2,1)S(1)}, u32[]{:S(2)}, u32[]{:S(2)}) collective-permute-start(bf16[512,128]{1,0:T(8,128)(2,1)S(1)} %get-tuple-element.25), channel_id=1, source_target_pairs={{0,3},{1,2},{2,5},{3,4},{4,7},{5,6},{6,1},{7,0},{8,11},{9,10},{10,... | collective-permute-start | bytes 393224 | tf_op jit(solution)/shard_map/ppermute | solution.py:31
  228.8 7.4 %collective-permute-start.34 = (bf16[512,128]{1,0:T(8,128)(2,1)S(1)}, bf16[512,128]{1,0:T(8,128)(2,1)S(1)}, u32[]{:S(2)}, u32[]{:S(2)}) collective-permute-start(bf16[512,128]{1,0:T(8,128)(2,1)S(1)} %get-tuple-element.25), channel_id=1, source_target_pairs={{0,4},{1,5},{2,6},{3,7},{4,0},{5,1},{6,2},{7,3},{8,12},{9,13},{10,... | collective-permute-start | bytes 393224 | tf_op jit(solution)/shard_map/ppermute | solution.py:31
  235.6 6.2 %collective-permute-start.37 = (bf16[512,128]{1,0:T(8,128)(2,1)S(1)}, bf16[512,128]{1,0:T(8,128)(2,1)S(1)}, u32[]{:S(2)}, u32[]{:S(2)}) collective-permute-start(bf16[512,128]{1,0:T(8,128)(2,1)S(1)} %get-tuple-element.25), channel_id=1, source_target_pairs={{0,7},{1,6},{2,1},{3,0},{4,3},{5,2},{6,5},{7,4},{8,15},{9,14},{10,... | collective-permute-start | bytes 393224 | tf_op jit(solution)/shard_map/ppermute | solution.py:31
  241.9 6.0 %copy-start = (bf16[4096,512]{1,0:T(8,128)(2,1)S(1)}, bf16[4096,512]{1,0:T(8,128)(2,1)}, u32[]{:S(2)}) copy-start(bf16[4096,512]{1,0:T(8,128)(2,1)} %constant_dynamic-update-slice_fusion) | copy-start | bytes 12582916

commit v2 on v1

--- a/solution.py
+++ b/solution.py
@@ -23,26 +23,36 @@
     )
 
 
-def ctx_peer(index, dy, dx):
-    return ((index // 2 + dy) % 4) * 2 + (index % 2 + dx) % 2
-
-
-def to_peer(value, dy, dx):
-    return lax.ppermute(value, "ctx", [(i, ctx_peer(i, dy, dx)) for i in range(8)])
+def along_y(value, step):
+    return lax.ppermute(value, "ctx", [(i, (i + 2 * step) % 8) for i in range(8)])
+
+
+def swap_x(value):
+    return lax.ppermute(value, "ctx", [(i, i ^ 1) for i in range(8)])
+
+
+def along_z(value, step):
+    return lax.ppermute(value, "dp", [(i, (i + 4 * step) % 16) for i in range(16)])
 
 
 def swap_cores(value):
     return lax.ppermute(value, "dp", [(i, i ^ 1) for i in range(16)])
 
 
-SHIFTS = [(s // 2, s % 2) for s in range(8)]
+def to_all_y(value):
+    return [along_y(value, step) for step in (1, 3, 2)]
+
+
+def by_source(one, three, two):
+    return [one, two, three]
 
 
 def attention_kernel(
-    heads, info_ref, q_ref, g_ref, a_ref, b_ref, dq_ref, keep_ref, give_ref,
+    heads, info_ref, q_ref, g_ref, mine_refs, other_refs, dq_ref, keep_ref, give_ref,
     ks, vs, kt, scores, grads, dka, dva, qh, gh, dqt,
 ):
-    slots, slot_rows, _ = a_ref.shape
+    per_ref = mine_refs[0].shape[0]
+    slots = per_ref * len(mine_refs)
     runs_per_slot = 2
     scale = 1.0 / math.sqrt(HD)
     core = info_ref[2 * slots]
@@ -50,7 +60,8 @@
         slot, part = b // runs_per_slot, b % runs_per_slot
         rows = slice(part * RUN, (part + 1) * RUN)
         at = pl.multiple_of(info_ref[b] * RUN, RUN)
-        first, second = a_ref[slot, rows, :], b_ref[slot, rows, :]
+        first = mine_refs[slot // per_ref][slot % per_ref, rows, :]
+        second = other_refs[slot // per_ref][slot % per_ref, rows, :]
         key_block = jnp.where(core == 0, first, second)
         ks[pl.ds(at, RUN), :] = key_block
         kt[:, pl.ds(at, RUN)] = key_block.T
@@ -143,7 +154,7 @@
 
 
 def attention(info, queries, grad_output, mine, other):
-    slots = mine.shape[0]
+    slots = mine[0].shape[0] * len(mine)
     count = slots * 2 * RUN
     heads = queries.shape[1] // HD
     wide = heads * RUN
@@ -154,7 +165,7 @@
     return pl.pallas_call(
         functools.partial(attention_kernel, heads),
         out_shape=(jax.ShapeDtypeStruct(queries.shape, jnp.bfloat16), shared, shared),
-        in_specs=[smem, vmem, vmem, vmem, vmem],
+        in_specs=[smem, vmem, vmem, [vmem] * len(mine), [vmem] * len(other)],
         out_specs=(vmem, vmem, vmem),
         scratch_shapes=[
             pltpu.VMEM((count, HD), jnp.bfloat16),
@@ -176,12 +187,13 @@
 
 
 def local(layer_input, queries, key_vectors, value_vectors, grad_output, positions):
-    member = lax.axis_index("dp") % 2
+    group = lax.axis_index("dp")
+    member, head, z = group % 2, group // 2, group // 4
     here = lax.axis_index("ctx")
-    head = lax.axis_index("dp") // 2
+    y, x_hi = here // 2, here % 2
     count = queries.shape[0]
     width = layer_input.shape[1] // 8
-    half = width // 2
+    slab = width // 8
     first = member == 0
 
     key_local = lax.dynamic_slice_in_dim(key_vectors, head * HD, HD, 1)
@@ -189,51 +201,73 @@
     runs_here = (positions[::RUN] // RUN).astype(jnp.bfloat16)
     tail = jnp.broadcast_to(jnp.pad(runs_here, (0, HD - 2))[None], (16, HD))
     own = jnp.concatenate([jnp.where(first, key_local, value_local), tail], axis=0)
-    got = [own] + [to_peer(own, dy, dx) for dy, dx in SHIFTS[1:]]
-    mine = jnp.stack(got)
-    other = swap_cores(mine)
+    column = jnp.stack([own] + by_source(*to_all_y(own)))
+    start = (2 * z + member) * slab
+
+    def block(dy, dx):
+        target = ((y + dy) % 4) * 2 + (x_hi + dx) % 2
+        return lax.dynamic_slice(layer_input, (0, target * width + start), (count, slab))
+
+    from_x = swap_x(jnp.stack([block(dy, 1) for dy in range(4)]))
+    partner_column = swap_x(column)
+    column_other = swap_cores(column)
+    pairs = [jnp.stack([block(dy, 0), from_x[dy]]) for dy in range(4)]
+    pairs = [pairs[0]] + [along_y(pairs[dy], dy) for dy in range(1, 4)]
+    slab_own = jnp.concatenate([p[dx] for dx in range(2) for p in pairs], axis=0)
+    partner_other = swap_cores(partner_column)
     info = jnp.concatenate(
-        [mine[:, count, :2].reshape(16).astype(jnp.int32), member.astype(jnp.int32)[None]]
-    )
-
-    base = layer_input
-    blocks = []
-    for dy, dx in SHIFTS:
-        target = ((here // 2 + dy) % 4) * 2 + (here % 2 + dx) % 2
-        part = lax.dynamic_slice(base, (0, target * width + member * half), (count, half))
-        blocks.append(part if (dy, dx) == (0, 0) else to_peer(part, dy, dx))
-    input_mine = jnp.concatenate(blocks, axis=0)
-    input_other = swap_cores(input_mine)
-
-    grad_query, keep, give = attention(info, queries, grad_output, mine, other)
+        [
+            column[:, count, :2].reshape(8).astype(jnp.int32),
+            partner_column[:, count, :2].reshape(8).astype(jnp.int32),
+            member.astype(jnp.int32)[None],
+        ]
+    )
+    slab_back, slab_ahead = along_z(slab_own, 1), along_z(slab_own, 3)
+
+    grad_query, keep, give = attention(
+        info, queries, grad_output, [column, partner_column], [column_other, partner_other]
+    )
+
+    cut = slab_own.shape[0] // 2
+    slab_far = jnp.concatenate([along_z(slab_back[:cut], 1), along_z(slab_ahead[cut:], 3)])
+    slabs = jnp.zeros((4, 2) + slab_own.shape, jnp.bfloat16)
+    for away, value in ((0, slab_own), (3, slab_back), (1, slab_ahead), (2, slab_far)):
+        other = swap_cores(value)
+        slabs = lax.dynamic_update_slice(slabs, value[None, None], ((z + away) % 4, member, 0, 0))
+        slabs = lax.dynamic_update_slice(slabs, other[None, None], ((z + away) % 4, 1 - member, 0, 0))
+    slabs = slabs.reshape((8,) + slab_own.shape)
 
     summed = (keep.astype(jnp.float32) + swap_cores(give).astype(jnp.float32)).astype(jnp.bfloat16)
-    terms = [summed[0]] + [
-        to_peer(summed[s], -dy, dx) for s, (dy, dx) in enumerate(SHIFTS) if s > 0
-    ]
-    total = sum(term.astype(jnp.float32) for term in terms).astype(jnp.bfloat16)
-
-    queries_all = jnp.concatenate([grad_query] + [to_peer(grad_query, dy, dx) for dy, dx in SHIFTS[1:]])
-    shared_all = jnp.concatenate([total] + [to_peer(total, dy, dx) for dy, dx in SHIFTS[1:]])
-    norm = 1.0 / math.sqrt(count * 8)
-
-    def in_order(a, b):
-        return jnp.concatenate([jnp.where(first, a, b), jnp.where(first, b, a)], axis=0)
-
-    grad_wq = in_order(
-        contract(input_mine, queries_all, 0, 0), contract(input_other, queries_all, 0, 0)
-    )
-    grad_wkv = in_order(
-        contract(input_mine, shared_all, 0, 0), contract(input_other, shared_all, 0, 0)
-    )
+    summed = summed.reshape(2, 4, count, HD)
+    rows_y = summed[:, 0].astype(jnp.float32)
+    for dy in (1, 3, 2):
+        rows_y = rows_y + along_y(summed[:, dy], -dy).astype(jnp.float32)
+    total = rows_y[0] + swap_x(rows_y[1].astype(jnp.bfloat16)).astype(jnp.float32)
+    total = total.astype(jnp.bfloat16)
+    both = jnp.stack([total, swap_x(total)])
+    shared = jnp.stack([both] + by_source(*to_all_y(both)), axis=1)
+    shared = shared.reshape(8 * count, HD)
+
+    mark = count * 3 // 4
+    part_a, part_b = grad_query[:mark], grad_query[mark:]
+    column_a = jnp.stack([part_a] + by_source(*to_all_y(part_a)))
+    all_a = jnp.concatenate([column_a, swap_x(column_a)])
+    both_b = jnp.stack([part_b, swap_x(part_b)])
+    all_b = jnp.stack([both_b] + by_source(*to_all_y(both_b)), axis=1)
+    all_b = all_b.reshape((8,) + part_b.shape)
+    queries_all = jnp.concatenate([all_a, all_b], axis=1).reshape(8 * count, -1)
+
+    norm = 1.0 / math.sqrt(8 * count)
+    grad_wq = contract(slabs, queries_all, 1, 0).reshape(width, -1) * norm
+    grad_wkv = contract(slabs, shared, 1, 0).reshape(width, -1) * norm
     share = HD // 2
     return (
         grad_query,
         total[:, :share],
         total[:, share:],
-        grad_wq * norm,
-        grad_wkv[:, :share] * norm,
-        grad_wkv[:, share:] * norm,
+        grad_wq,
+        grad_wkv[:, :share],
+        grad_wkv[:, share:],
     )
 
 

time: 266 us -> 218 us (0.82)
  waiting for transfers between devices: 119 us -> 52.3 us
  local copies, waits for them, and re-layouts: 26.7 us -> 40.4 us
  other arithmetic: 5.19 us -> 12.8 us
  Pallas kernels: 13.6 us -> 19 us
  starting transfers between devices: 79.9 us -> 76.4 us
  matrix products: 15.3 us -> 12.2 us
    ppermute x35 -> x28, waiting for transfers between devices: 119 us -> 52.3 us  [the longest x18 26.1 us: along_y(): lax.ppermute(value, 'ctx', [(i, (i + 2 * step) % 8) for i in range(8)])]
    ppermute x35 -> x28, starting transfers between devices: 73.8 us -> 59.6 us  [the longest x18 42.9 us: along_y(): lax.ppermute(value, 'ctx', [(i, (i + 2 * step) % 8) for i in range(8)])]
    broadcast_in_dim x0 -> x9, local copies, waits for them, and re-layouts: none -> 11 us  [the longest x4 4.97 us: local(): value[None, None]]
    ppermute x3 -> x7, starting transfers between devices: 6.05 us -> 16.8 us  [swap_cores(): return lax.ppermute(value, 'dp', [(i, i ^ 1) for i in range(16)])]
    unnamed x35 -> x33, local copies, waits for them, and re-layouts: 19.4 us -> 9.05 us
    dynamic_update_slice x0 -> x8, local copies, waits for them, and re-layouts: none -> 7.54 us  [the longest x4 4.22 us: local(): lax.dynamic_update_slice(slabs, other[None, None], ((z + away) % 4, 1 - m...]
    pallas_call x1, Pallas kernels: 13.6 us -> 19 us  [attention(): pl.pallas_call(functools.partial(attention_kernel, heads), out_shape=(jax...]
    another operation x0 -> x11, other arithmetic: none -> 4.63 us  [the longest x2 2.88 us: local(): shared = jnp.stack([both] + by_source(*to_all_y(both)), axis=1)]
  transfers between devices with their start and end apart: 38 -> 35, of which waited for: 17 -> 13; matrix products, arithmetic and copies ran while one was open for 10% -> 21% of each run, Pallas kernels for 5% -> 9%
where the time goes in v2:
time: 218 us; the launch traced here: 214 us
  starting transfers between devices  76.4 us (35%)
  waiting for transfers between devices  52.3 us (24%)
  local copies, waits for them, and re-layouts  40.4 us (19%)
  Pallas kernels  19 us (9%)
  other arithmetic  12.8 us (6%)
  matrix products  12.2 us (6%)
    ppermute x18, starting transfers between devices, along_y(): lax.ppermute(value, 'ctx', [(i, (i + 2 * step) % 8) for i in range(8)])  42.9 us
    ppermute x18, waiting for transfers between devices, along_y(): lax.ppermute(value, 'ctx', [(i, (i + 2 * step) % 8) for i in range(8)])  26.1 us
    ppermute x6, waiting for transfers between devices, swap_x(): return lax.ppermute(value, 'ctx', [(i, i ^ 1) for i in range(8)])  25.1 us
    pallas_call x1, Pallas kernels, attention(): pl.pallas_call(functools.partial(attention_kernel, heads), out_shape=(jax...  19 us
    ppermute x7, starting transfers between devices, swap_cores(): return lax.ppermute(value, 'dp', [(i, i ^ 1) for i in range(16)])  16.8 us
    dot_general x2, matrix products, contract(): lax.dot_general(left, right, (((left_dim,), (right_dim,)), ((), ())), pre...  12.2 us
    unnamed x33, local copies, waits for them, and re-layouts  9.05 us
    ppermute x6, starting transfers between devices, swap_x(): return lax.ppermute(value, 'ctx', [(i, i ^ 1) for i in range(8)])  8.58 us
  transfers between devices with their start and end apart: 35, of which 13 were waited for; matrix products, arithmetic and copies ran while one was open for 21% of the time, Pallas kernels for 9%

profile of v2, /device:TPU:1, one launch (start us, length us, event | category | flops | bytes accessed | tf_op | source)
XLA Modules:
  0.0 214.4 jit_solution(10828836032272612407)
XLA Ops:
  0.8 2.1 dynamic-slice_bitcast_fusion
  3.0 3.7 %collective-permute-start.11 = (bf16[4,512,128]{2,1,0:T(8,128)(2,1)S(1)}, bf16[4,512,128]{2,1,0:T(8,128)(2,1)S(1)}, u32[]{:S(2)}, u32[]{:S(2)}) collective-permute-start(bf16[4,512,128]{2,1,0:T(8,128)(2,1)S(1)} %pad_maximum_fusion.5), channel_id=1, source_target_pairs={{0,1},{1,0},{2,3},{3,2},{4,5},{5,4},{6,7},{7,6},{8,9},{9,8},{10,11... | collective-permute-start | bytes 1572872 | tf_op jit(solution)/shard_map/ppermute | solution.py:31
  9.8 2.6 %collective-permute-start.1 = (bf16[528,128]{1,0:T(8,128)(2,1)S(1)}, bf16[528,128]{1,0:T(8,128)(2,1)S(1)}, u32[]{:S(2)}, u32[]{:S(2)}) collective-permute-start(bf16[528,128]{1,0:T(8,128)(2,1)S(1)} %get-tuple-element.43), channel_id=1, source_target_pairs={{0,4},{1,5},{2,6},{3,7},{4,0},{5,1},{6,2},{7,3},{8,12},{9,13},{10,... | collective-permute-start | bytes 405512 | tf_op jit(solution)/shard_map/ppermute | solution.py:27
  14.0 4.0 %collective-permute-done.1 = bf16[528,128]{1,0:T(8,128)(2,1)S(1)} collective-permute-done((bf16[528,128]{1,0:T(8,128)(2,1)S(1)}, bf16[528,128]{1,0:T(8,128)(2,1)S(1)}, u32[]{:S(2)}, u32[]{:S(2)}) %collective-permute-start.1) | collective-permute-done | bytes 135200 | tf_op jit(solution)/shard_map/ppermute | solution.py:27
  18.3 2.3 %collective-permute-start.4 = (bf16[4,528,128]{2,1,0:T(8,128)(2,1)S(1)}, bf16[4,528,128]{2,1,0:T(8,128)(2,1)}, u32[]{:S(2)}, u32[]{:S(2)}) collective-permute-start(bf16[4,528,128]{2,1,0:T(8,128)(2,1)S(1)} %pad_maximum_fusion.4.mine_refs_0_), channel_id=1, source_target_pairs={{0,8},{8,0},{16,24},{24,16},{32,40},{40,32},{48,56},{56,48},{64,72... | collective-permute-start | bytes 1622024 | tf_op jit(solution)/shard_map/ppermute | solution.py:39
  20.7 2.0 collective-permute-start.14
  22.8 1.9 collective-permute-start.13
  24.8 6.8 %collective-permute-done.3.mine_refs_1_ = bf16[4,528,128]{2,1,0:T(8,128)(2,1)S(1)} collective-permute-done((bf16[4,528,128]{2,1,0:T(8,128)(2,1)S(1)}, bf16[4,528,128]{2,1,0:T(8,128)(2,1)S(1)}, u32[]{:S(2)}, u32[]{:S(2)}) %collective-permute-start.3) | collective-permute-done | bytes 540704 | tf_op jit(solution)/shard_map/ppermute | solution.py:31
  32.3 2.8 %collective-permute-start.5 = (bf16[4,528,128]{2,1,0:T(8,128)(2,1)S(1)}, bf16[4,528,128]{2,1,0:T(8,128)(2,1)}, u32[]{:S(2)}, u32[]{:S(2)}) collective-permute-start(bf16[4,528,128]{2,1,0:T(8,128)(2,1)S(1)} %collective-permute-done.3.mine_refs_1_), channel_id=1, source_target_pairs={{0,8},{8,0},{16,24},{24,16},{32,40},{40,32},{48,56},{56,48},{64,72... | collective-permute-start | bytes 1622024 | tf_op jit(solution)/shard_map/ppermute | solution.py:39
  40.5 2.5 %collective-permute-start.15 = (bf16[4096,128]{1,0:T(8,128)(2,1)}, bf16[4096,128]{1,0:T(8,128)(2,1)S(1)}, u32[]{:S(2)}, u32[]{:S(2)}) collective-permute-start(bf16[4096,128]{1,0:T(8,128)(2,1)} %fusion.5), channel_id=1, source_target_pairs={{0,8},{8,0},{16,24},{24,16},{32,40},{40,32},{48,56},{56,48},{64,72... | collective-permute-start | bytes 3145736 | tf_op jit(solution)/shard_map/ppermute | solution.py:39
  43.0 1.5 copy.20
  44.5 19.0 %shard_map.109 = (bf16[512,512]{1,0:T(8,128)(2,1)}, bf16[8,512,128]{2,1,0:T(8,128)(2,1)}, bf16[8,512,128]{2,1,0:T(8,128)(2,1)}) custom-call(s32[17]{0:T(128)} %pad_add_fusion.info_ref, bf16[512,512]{1,0:T(8,128)(2,1)} %q_ref.1, bf16[512,512]{1,0:T(8,128)(2,1)} %g_ref.1, bf16[4,528,128]{2,1,0:T(8,128)(2,1)} %copy-done.8, bf16[4,528,128]{2,1,0:T(8,128)(2,1)} %copy-done.9, ...), custom_call_target="tpu_custom_call" | custom-call | flops 10737418240 | bytes 8388608 | tf_op jit(solution)/shard_map/pallas_call | solution.py:165
  65.6 6.0 %collective-permute-start.23 = (bf16[384,512]{1,0:T(8,128)(2,1)S(1)}, bf16[384,512]{1,0:T(8,128)(2,1)S(1)}, u32[]{:S(2)}, u32[]{:S(2)}) collective-permute-start(bf16[384,512]{1,0:T(8,128)(2,1)S(1)} %get-tuple-element.32), channel_id=1, source_target_pairs={{0,2},{1,3},{2,4},{3,5},{4,6},{5,7},{6,0},{7,1},{8,10},{9,11},{10,... | collective-permute-start | bytes 1179656 | tf_op jit(solution)/shard_map/ppermute | solution.py:27
  71.6 7.4 %collective-permute-start.28 = (bf16[2,128,512]{2,1,0:T(8,128)(2,1)S(1)}, bf16[2,128,512]{2,1,0:T(8,128)(2,1)S(1)}, u32[]{:S(2)}, u32[]{:S(2)}) collective-permute-start(bf16[2,128,512]{2,1,0:T(8,128)(2,1)S(1)} %get-tuple-element.41), channel_id=1, source_target_pairs={{0,2},{1,3},{2,4},{3,5},{4,6},{5,7},{6,0},{7,1},{8,10},{9,11},{10,... | collective-permute-start | bytes 786440 | tf_op jit(solution)/shard_map/ppermute | solution.py:27
  79.0 5.9 %collective-permute-start.29 = (bf16[2,128,512]{2,1,0:T(8,128)(2,1)S(1)}, bf16[2,128,512]{2,1,0:T(8,128)(2,1)S(1)}, u32[]{:S(2)}, u32[]{:S(2)}) collective-permute-start(bf16[2,128,512]{2,1,0:T(8,128)(2,1)S(1)} %get-tuple-element.41), channel_id=1, source_target_pairs={{0,4},{1,5},{2,6},{3,7},{4,0},{5,1},{6,2},{7,3},{8,12},{9,13},{10,... | collective-permute-start | bytes 786440 | tf_op jit(solution)/shard_map/ppermute | solution.py:27
  84.9 2.0 collective-permute-start.30
  88.1 4.2 %collective-permute-done.28 = bf16[2,128,512]{2,1,0:T(8,128)(2,1)S(1)} collective-permute-done((bf16[2,128,512]{2,1,0:T(8,128)(2,1)S(1)}, bf16[2,128,512]{2,1,0:T(8,128)(2,1)S(1)}, u32[]{:S(2)}, u32[]{:S(2)}) %collective-permute-start.28) | collective-permute-done | bytes 262176 | tf_op jit(solution)/shard_map/ppermute | solution.py:27
  92.3 1.6 collective-permute-start.16
  93.9 6.0 %collective-permute-done.29 = bf16[2,128,512]{2,1,0:T(8,128)(2,1)S(1)} collective-permute-done((bf16[2,128,512]{2,1,0:T(8,128)(2,1)S(1)}, bf16[2,128,512]{2,1,0:T(8,128)(2,1)S(1)}, u32[]{:S(2)}, u32[]{:S(2)}) %collective-permute-start.29) | collective-permute-done | bytes 262176 | tf_op jit(solution)/shard_map/ppermute | solution.py:27
  99.9 3.0 %collective-permute-start.24 = (bf16[384,512]{1,0:T(8,128)(2,1)S(1)}, bf16[384,512]{1,0:T(8,128)(2,1)S(1)}, u32[]{:S(2)}, u32[]{:S(2)}) collective-permute-start(bf16[384,512]{1,0:T(8,128)(2,1)S(1)} %get-tuple-element.32), channel_id=1, source_target_pairs={{0,4},{1,5},{2,6},{3,7},{4,0},{5,1},{6,2},{7,3},{8,12},{9,13},{10,... | collective-permute-start | bytes 1179656 | tf_op jit(solution)/shard_map/ppermute | solution.py:27
  104.1 2.1 collective-permute-start.18
  106.3 5.0 %collective-permute-done.24 = bf16[384,512]{1,0:T(8,128)(2,1)S(1)} collective-permute-done((bf16[384,512]{1,0:T(8,128)(2,1)S(1)}, bf16[384,512]{1,0:T(8,128)(2,1)S(1)}, u32[]{:S(2)}, u32[]{:S(2)}) %collective-permute-start.24) | collective-permute-done | bytes 393248 | tf_op jit(solution)/shard_map/ppermute | solution.py:27
  111.3 1.7 collective-permute-start.6
  113.0 4.4 %collective-permute-done.25 = bf16[384,512]{1,0:T(8,128)(2,1)S(1)} collective-permute-done((bf16[384,512]{1,0:T(8,128)(2,1)S(1)}, bf16[384,512]{1,0:T(8,128)(2,1)S(1)}, u32[]{:S(2)}, u32[]{:S(2)}) %collective-permute-start.25) | collective-permute-done | bytes 393248 | tf_op jit(solution)/shard_map/ppermute | solution.py:27
  118.8 1.6 copy-done.4
  122.3 1.7 collective-permute-start.20
  125.0 1.8 add_convert_fusion
  127.8 3.4 %collective-permute-start.7 = (bf16[2,512,128]{2,1,0:T(8,128)(2,1)}, bf16[2,512,128]{2,1,0:T(8,128)(2,1)S(1)}, u32[]{:S(2)}, u32[]{:S(2)}) collective-permute-start(bf16[2,512,128]{2,1,0:T(8,128)(2,1)} %get-tuple-element.26), channel_id=1, source_target_pairs={{0,6},{1,7},{2,0},{3,1},{4,2},{5,3},{6,4},{7,5},{8,14},{9,15},{10,... | collective-permute-start | bytes 786440 | tf_op jit(solution)/shard_map/ppermute | solution.py:27
  131.2 3.4 %collective-permute-start.9 = (bf16[2,512,128]{2,1,0:T(8,128)(2,1)}, bf16[2,512,128]{2,1,0:T(8,128)(2,1)}, u32[]{:S(2)}, u32[]{:S(2)}) collective-permute-start(bf16[2,512,128]{2,1,0:T(8,128)(2,1)} %get-tuple-element.28), channel_id=1, source_target_pairs={{0,4},{1,5},{2,6},{3,7},{4,0},{5,1},{6,2},{7,3},{8,12},{9,13},{10,... | collective-permute-start | bytes 786440 | tf_op jit(solution)/shard_map/ppermute | solution.py:27
  135.7 2.3 %collective-permute-start.26 = (bf16[4,384,512]{2,1,0:T(8,128)(2,1)}, bf16[4,384,512]{2,1,0:T(8,128)(2,1)}, u32[]{:S(2)}, u32[]{:S(2)}) collective-permute-start(bf16[4,384,512]{2,1,0:T(8,128)(2,1)} %pad_maximum_fusion.1), channel_id=1, source_target_pairs={{0,1},{1,0},{2,3},{3,2},{4,5},{5,4},{6,7},{7,6},{8,9},{9,8},{10,11... | collective-permute-start | bytes 4718600 | tf_op jit(solution)/shard_map/ppermute | solution.py:31
  138.0 1.5 copy.24
  140.6 2.7 %collective-permute-start.21 = (bf16[2048,128]{1,0:T(8,128)(2,1)S(1)}, bf16[2048,128]{1,0:T(8,128)(2,1)S(1)}, u32[]{:S(2)}, u32[]{:S(2)}) collective-permute-start(bf16[2048,128]{1,0:T(8,128)(2,1)S(1)} %slice.130), channel_id=1, source_target_pairs={{0,96},{8,104},{16,112},{24,120},{32,0},{40,8},{48,16},{56,24},{64... | collective-permute-start | bytes 1572872 | tf_op jit(solution)/shard_map/ppermute | solution.py:35
  143.3 1.9 constant_dynamic-update-slice_fusion.1
  145.1 3.5 %collective-permute-start.17 = (bf16[4096,128]{1,0:T(8,128)(2,1)S(1)}, bf16[4096,128]{1,0:T(8,128)(2,1)}, u32[]{:S(2)}, u32[]{:S(2)}) collective-permute-start(bf16[4096,128]{1,0:T(8,128)(2,1)S(1)} %collective-permute-done.16), channel_id=1, source_target_pairs={{0,8},{8,0},{16,24},{24,16},{32,40},{40,32},{48,56},{56,48},{64,72... | collective-permute-start | bytes 3145736 | tf_op jit(solution)/shard_map/ppermute | solution.py:39
  152.2 4.0 %collective-permute-start.22 = (bf16[4096,128]{1,0:T(8,128)(2,1)}, bf16[4096,128]{1,0:T(8,128)(2,1)}, u32[]{:S(2)}, u32[]{:S(2)}) collective-permute-start(bf16[4096,128]{1,0:T(8,128)(2,1)} %constant_dynamic-update-slice_fusion), channel_id=1, source_target_pairs={{0,8},{8,0},{16,24},{24,16},{32,40},{40,32},{48,56},{56,48},{64,72... | collective-permute-start | bytes 3145736 | tf_op jit(solution)/shard_map/ppermute | solution.py:39
  156.2 1.5 copy.26
  157.7 16.4 %collective-permute-done.10 = bf16[512,128]{1,0:T(8,128)(2,1)S(1)} collective-permute-done((bf16[512,128]{1,0:T(8,128)(2,1)S(1)}, bf16[512,128]{1,0:T(8,128)(2,1)S(1)}, u32[]{:S(2)}, u32[]{:S(2)}) %collective-permute-start.10) | collective-permute-done | bytes 131104 | tf_op jit(solution)/shard_map/ppermute | solution.py:31
  175.1 2.0 collective-permute-start.31
  178.6 1.9 collective-permute-done.31
  180.6 1.6 fusion.16
  182.6 1.7 collective-permute-start.33
  184.3 1.5 copy.23
  187.6 1.5 copy.25
  194.6 1.5 constant_dynamic-update-slice_fusion.2
  196.2 2.5 %pad_maximum_fusion = bf16[8,512,512]{2,1,0:T(8,128)(2,1)} fusion(bf16[8,128,512]{2,1,0:T(8,128)(2,1)S(1)} %bitcast.132, bf16[8,384,512]{2,1,0:T(8,128)(2,1)S(1)} %constant_dynamic-update-slice_fusion.2), kind=kLoop, calls=%fused_computation | loop fusion | flops 8388608 | bytes 8388608 | tf_op jit(solution)/shard_map/concatenate | solution.py:258
  198.7 1.5 copy.27
  201.3 6.4 %convolution_multiply_fusion.1 = f32[1024,128]{0,1:T(8,128)S(1)} fusion(bf16[1024,4096]{1,0:T(8,128)(2,1)} %bitcast.126, bf16[4096,128]{1,0:T(8,128)(2,1)S(1)} %bitcast.130), kind=kOutput, calls=%fused_computation.4 | convolution fusion | flops 1073872896 | bytes 9961472 | tf_op jit(solution)/shard_map/dot_general | solution.py:21
  208.5 5.8 %convolution_multiply_fusion = f32[1024,512]{1,0:T(8,128)} fusion(bf16[1024,4096]{1,0:T(8,128)(2,1)S(1)} %bitcast.127, bf16[4096,512]{1,0:T(8,128)(2,1)S(1)} %bitcast.131), kind=kOutput, calls=%fused_computation.2 | convolution fusion | flops 4295491584 | bytes 14680064 | tf_op jit(solution)/shard_map/dot_general | solution.py:21
  (114 shorter events, 39.1 us)
Async XLA Ops:
  3.0 17.7 %collective-permute-start.11 = (bf16[4,512,128]{2,1,0:T(8,128)(2,1)S(1)}, bf16[4,512,128]{2,1,0:T(8,128)(2,1)S(1)}, u32[]{:S(2)}, u32[]{:S(2)}) collective-permute-start(bf16[4,512,128]{2,1,0:T(8,128)(2,1)S(1)} %pad_maximum_fusion.5), channel_id=1, source_target_pairs={{0,1},{1,0},{2,3},{3,2},{4,5},{5,4},{6,7},{7,6},{8,9},{9,8},{10,11... | collective-permute-start | bytes 1572872 | tf_op jit(solution)/shard_map/ppermute | solution.py:31
  8.5 5.5 %collective-permute-start = (bf16[528,128]{1,0:T(8,128)(2,1)S(1)}, bf16[528,128]{1,0:T(8,128)(2,1)S(1)}, u32[]{:S(2)}, u32[]{:S(2)}) collective-permute-start(bf16[528,128]{1,0:T(8,128)(2,1)S(1)} %get-tuple-element.43), channel_id=1, source_target_pairs={{0,2},{1,3},{2,4},{3,5},{4,6},{5,7},{6,0},{7,1},{8,10},{9,11},{10,... | collective-permute-start | bytes 405512 | tf_op jit(solution)/shard_map/ppermute | solution.py:27
  9.8 8.2 %collective-permute-start.1 = (bf16[528,128]{1,0:T(8,128)(2,1)S(1)}, bf16[528,128]{1,0:T(8,128)(2,1)S(1)}, u32[]{:S(2)}, u32[]{:S(2)}) collective-permute-start(bf16[528,128]{1,0:T(8,128)(2,1)S(1)} %get-tuple-element.43), channel_id=1, source_target_pairs={{0,4},{1,5},{2,6},{3,7},{4,0},{5,1},{6,2},{7,3},{8,12},{9,13},{10,... | collective-permute-start | bytes 405512 | tf_op jit(solution)/shard_map/ppermute | solution.py:27
  12.4 5.6 %collective-permute-start.2 = (bf16[528,128]{1,0:T(8,128)(2,1)S(1)}, bf16[528,128]{1,0:T(8,128)(2,1)S(1)}, u32[]{:S(2)}, u32[]{:S(2)}) collective-permute-start(bf16[528,128]{1,0:T(8,128)(2,1)S(1)} %get-tuple-element.43), channel_id=1, source_target_pairs={{0,6},{1,7},{2,0},{3,1},{4,2},{5,3},{6,4},{7,5},{8,14},{9,15},{10,... | collective-permute-start | bytes 405512 | tf_op jit(solution)/shard_map/ppermute | solution.py:27
  18.1 26.4 %copy-start.8 = (bf16[4,528,128]{2,1,0:T(8,128)(2,1)}, bf16[4,528,128]{2,1,0:T(8,128)(2,1)S(1)}, u32[]{:S(2)}) copy-start(bf16[4,528,128]{2,1,0:T(8,128)(2,1)S(1)} %pad_maximum_fusion.4.mine_refs_0_) | copy-start | bytes 1622020
  18.1 13.5 %collective-permute-start.3 = (bf16[4,528,128]{2,1,0:T(8,128)(2,1)S(1)}, bf16[4,528,128]{2,1,0:T(8,128)(2,1)S(1)}, u32[]{:S(2)}, u32[]{:S(2)}) collective-permute-start(bf16[4,528,128]{2,1,0:T(8,128)(2,1)S(1)} %pad_maximum_fusion.4.mine_refs_0_), channel_id=1, source_target_pairs={{0,1},{1,0},{2,3},{3,2},{4,5},{5,4},{6,7},{7,6},{8,9},{9,8},{10,11... | collective-permute-start | bytes 1622024 | tf_op jit(solution)/shard_map/ppermute | solution.py:31
  18.3 26.2 %collective-permute-start.4 = (bf16[4,528,128]{2,1,0:T(8,128)(2,1)S(1)}, bf16[4,528,128]{2,1,0:T(8,128)(2,1)}, u32[]{:S(2)}, u32[]{:S(2)}) collective-permute-start(bf16[4,528,128]{2,1,0:T(8,128)(2,1)S(1)} %pad_maximum_fusion.4.mine_refs_0_), channel_id=1, source_target_pairs={{0,8},{8,0},{16,24},{24,16},{32,40},{40,32},{48,56},{56,48},{64,72... | collective-permute-start | bytes 1622024 | tf_op jit(solution)/shard_map/ppermute | solution.py:39
  20.7 16.4 %collective-permute-start.14 = (bf16[2,512,128]{2,1,0:T(8,128)(2,1)S(1)}, bf16[2,512,128]{2,1,0:T(8,128)(2,1)S(1)}, u32[]{:S(2)}, u32[]{:S(2)}) collective-permute-start(bf16[2,512,128]{2,1,0:T(8,128)(2,1)S(1)} %pad_maximum_fusion.8), channel_id=1, source_target_pairs={{0,6},{1,7},{2,0},{3,1},{4,2},{5,3},{6,4},{7,5},{8,14},{9,15},{10,... | collective-permute-start | bytes 786440 | tf_op jit(solution)/shard_map/ppermute | solution.py:27
  22.7 12.4 %collective-permute-start.12 = (bf16[2,512,128]{2,1,0:T(8,128)(2,1)S(1)}, bf16[2,512,128]{2,1,0:T(8,128)(2,1)S(1)}, u32[]{:S(2)}, u32[]{:S(2)}) collective-permute-start(bf16[2,512,128]{2,1,0:T(8,128)(2,1)S(1)} %pad_maximum_fusion.6), channel_id=1, source_target_pairs={{0,2},{1,3},{2,4},{3,5},{4,6},{5,7},{6,0},{7,1},{8,10},{9,11},{10,... | collective-permute-start | bytes 786440 | tf_op jit(solution)/shard_map/ppermute | solution.py:27
  22.8 13.6 %collective-permute-start.13 = (bf16[2,512,128]{2,1,0:T(8,128)(2,1)S(1)}, bf16[2,512,128]{2,1,0:T(8,128)(2,1)S(1)}, u32[]{:S(2)}, u32[]{:S(2)}) collective-permute-start(bf16[2,512,128]{2,1,0:T(8,128)(2,1)S(1)} %pad_maximum_fusion.7), channel_id=1, source_target_pairs={{0,4},{1,5},{2,6},{3,7},{4,0},{5,1},{6,2},{7,3},{8,12},{9,13},{10,... | collective-permute-start | bytes 786440 | tf_op jit(solution)/shard_map/ppermute | solution.py:27
  31.6 12.9 %copy-start.9 = (bf16[4,528,128]{2,1,0:T(8,128)(2,1)}, bf16[4,528,128]{2,1,0:T(8,128)(2,1)S(1)}, u32[]{:S(2)}) copy-start(bf16[4,528,128]{2,1,0:T(8,128)(2,1)S(1)} %collective-permute-done.3.mine_refs_1_) | copy-start | bytes 1622020
  32.3 12.2 %collective-permute-start.5 = (bf16[4,528,128]{2,1,0:T(8,128)(2,1)S(1)}, bf16[4,528,128]{2,1,0:T(8,128)(2,1)}, u32[]{:S(2)}, u32[]{:S(2)}) collective-permute-start(bf16[4,528,128]{2,1,0:T(8,128)(2,1)S(1)} %collective-permute-done.3.mine_refs_1_), channel_id=1, source_target_pairs={{0,8},{8,0},{16,24},{24,16},{32,40},{40,32},{48,56},{56,48},{64,72... | collective-permute-start | bytes 1622024 | tf_op jit(solution)/shard_map/ppermute | solution.py:39
  40.5 78.3 %collective-permute-start.15 = (bf16[4096,128]{1,0:T(8,128)(2,1)}, bf16[4096,128]{1,0:T(8,128)(2,1)S(1)}, u32[]{:S(2)}, u32[]{:S(2)}) collective-permute-start(bf16[4096,128]{1,0:T(8,128)(2,1)} %fusion.5), channel_id=1, source_target_pairs={{0,8},{8,0},{16,24},{24,16},{32,40},{40,32},{48,56},{56,48},{64,72... | collective-permute-start | bytes 3145736 | tf_op jit(solution)/shard_map/ppermute | solution.py:39
  64.4 7.1 %collective-permute-start.27 = (bf16[128,512]{1,0:T(8,128)(2,1)S(1)}, bf16[128,512]{1,0:T(8,128)(2,1)S(1)}, u32[]{:S(2)}, u32[]{:S(2)}) collective-permute-start(bf16[128,512]{1,0:T(8,128)(2,1)S(1)} %get-tuple-element.34), channel_id=1, source_target_pairs={{0,1},{1,0},{2,3},{3,2},{4,5},{5,4},{6,7},{7,6},{8,9},{9,8},{10,11... | collective-permute-start | bytes 393224 | tf_op jit(solution)/shard_map/ppermute | solution.py:31
  65.6 38.6 %collective-permute-start.23 = (bf16[384,512]{1,0:T(8,128)(2,1)S(1)}, bf16[384,512]{1,0:T(8,128)(2,1)S(1)}, u32[]{:S(2)}, u32[]{:S(2)}) collective-permute-start(bf16[384,512]{1,0:T(8,128)(2,1)S(1)} %get-tuple-element.32), channel_id=1, source_target_pairs={{0,2},{1,3},{2,4},{3,5},{4,6},{5,7},{6,0},{7,1},{8,10},{9,11},{10,... | collective-permute-start | bytes 1179656 | tf_op jit(solution)/shard_map/ppermute | solution.py:27
  71.6 31.3 %copy-start.7 = (bf16[512,512]{1,0:T(8,128)(2,1)S(1)}, bf16[512,512]{1,0:T(8,128)(2,1)}, u32[]{:S(2)}) copy-start(bf16[512,512]{1,0:T(8,128)(2,1)} %get-tuple-element.12) | copy-start | bytes 1572868
  71.6 20.7 %collective-permute-start.28 = (bf16[2,128,512]{2,1,0:T(8,128)(2,1)S(1)}, bf16[2,128,512]{2,1,0:T(8,128)(2,1)S(1)}, u32[]{:S(2)}, u32[]{:S(2)}) collective-permute-start(bf16[2,128,512]{2,1,0:T(8,128)(2,1)S(1)} %get-tuple-element.41), channel_id=1, source_target_pairs={{0,2},{1,3},{2,4},{3,5},{4,6},{5,7},{6,0},{7,1},{8,10},{9,11},{10,... | collective-permute-start | bytes 786440 | tf_op jit(solution)/shard_map/ppermute | solution.py:27
  79.0 20.9 %collective-permute-start.29 = (bf16[2,128,512]{2,1,0:T(8,128)(2,1)S(1)}, bf16[2,128,512]{2,1,0:T(8,128)(2,1)S(1)}, u32[]{:S(2)}, u32[]{:S(2)}) collective-permute-start(bf16[2,128,512]{2,1,0:T(8,128)(2,1)S(1)} %get-tuple-element.41), channel_id=1, source_target_pairs={{0,4},{1,5},{2,6},{3,7},{4,0},{5,1},{6,2},{7,3},{8,12},{9,13},{10,... | collective-permute-start | bytes 786440 | tf_op jit(solution)/shard_map/ppermute | solution.py:27
  84.9 18.0 %collective-permute-start.30 = (bf16[2,128,512]{2,1,0:T(8,128)(2,1)S(1)}, bf16[2,128,512]{2,1,0:T(8,128)(2,1)S(1)}, u32[]{:S(2)}, u32[]{:S(2)}) collective-permute-start(bf16[2,128,512]{2,1,0:T(8,128)(2,1)S(1)} %get-tuple-element.41), channel_id=1, source_target_pairs={{0,6},{1,7},{2,0},{3,1},{4,2},{5,3},{6,4},{7,5},{8,14},{9,15},{10,... | collective-permute-start | bytes 786440 | tf_op jit(solution)/shard_map/ppermute | solution.py:27
  88.1 30.6 %copy-start = (bf16[4,2,4096,128]{2,3,1,0:T(8,128)(2,1)}, bf16[4,2,4096,128]{2,3,1,0:T(8,128)(2,1)S(1)}, u32[]{:S(2)}) copy-start(bf16[4,2,4096,128]{2,3,1,0:T(8,128)(2,1)S(1)} %constant_dynamic-update-slice_fusion.14) | copy-start | bytes 25165828
  92.3 28.6 %collective-permute-start.16 = (bf16[4096,128]{1,0:T(8,128)(2,1)}, bf16[4096,128]{1,0:T(8,128)(2,1)S(1)}, u32[]{:S(2)}, u32[]{:S(2)}) collective-permute-start(bf16[4096,128]{1,0:T(8,128)(2,1)} %fusion.5), channel_id=1, source_target_pairs={{0,32},{8,40},{16,48},{24,56},{32,64},{40,72},{48,80},{56,88},{64,... | collective-permute-start | bytes 3145736 | tf_op jit(solution)/shard_map/ppermute | solution.py:35
  99.9 11.4 %collective-permute-start.24 = (bf16[384,512]{1,0:T(8,128)(2,1)S(1)}, bf16[384,512]{1,0:T(8,128)(2,1)S(1)}, u32[]{:S(2)}, u32[]{:S(2)}) collective-permute-start(bf16[384,512]{1,0:T(8,128)(2,1)S(1)} %get-tuple-element.32), channel_id=1, source_target_pairs={{0,4},{1,5},{2,6},{3,7},{4,0},{5,1},{6,2},{7,3},{8,12},{9,13},{10,... | collective-permute-start | bytes 1179656 | tf_op jit(solution)/shard_map/ppermute | solution.py:27
  102.9 14.5 %collective-permute-start.25 = (bf16[384,512]{1,0:T(8,128)(2,1)S(1)}, bf16[384,512]{1,0:T(8,128)(2,1)S(1)}, u32[]{:S(2)}, u32[]{:S(2)}) collective-permute-start(bf16[384,512]{1,0:T(8,128)(2,1)S(1)} %get-tuple-element.32), channel_id=1, source_target_pairs={{0,6},{1,7},{2,0},{3,1},{4,2},{5,3},{6,4},{7,5},{8,14},{9,15},{10,... | collective-permute-start | bytes 1179656 | tf_op jit(solution)/shard_map/ppermute | solution.py:27
  104.1 31.6 %collective-permute-start.18 = (bf16[4096,128]{1,0:T(8,128)(2,1)}, bf16[4096,128]{1,0:T(8,128)(2,1)}, u32[]{:S(2)}, u32[]{:S(2)}) collective-permute-start(bf16[4096,128]{1,0:T(8,128)(2,1)} %fusion.5), channel_id=1, source_target_pairs={{0,96},{8,104},{16,112},{24,120},{32,0},{40,8},{48,16},{56,24},{64... | collective-permute-start | bytes 3145736 | tf_op jit(solution)/shard_map/ppermute | solution.py:35
  111.3 13.7 %collective-permute-start.6 = (bf16[8,512,128]{2,1,0:T(8,128)(2,1)}, bf16[8,512,128]{2,1,0:T(8,128)(2,1)}, u32[]{:S(2)}, u32[]{:S(2)}) collective-permute-start(bf16[8,512,128]{2,1,0:T(8,128)(2,1)} %get-tuple-element.11), channel_id=1, source_target_pairs={{0,8},{8,0},{16,24},{24,16},{32,40},{40,32},{48,56},{56,48},{64,72... | collective-permute-start | bytes 3145736 | tf_op jit(solution)/shard_map/ppermute | solution.py:39
  118.8 1.6 copy-start.4
  122.3 18.2 %collective-permute-start.20 = (bf16[2048,128]{1,0:T(8,128)(2,1)}, bf16[2048,128]{1,0:T(8,128)(2,1)}, u32[]{:S(2)}, u32[]{:S(2)}) collective-permute-start(bf16[2048,128]{1,0:T(8,128)(2,1)} %slice.129), channel_id=1, source_target_pairs={{0,32},{8,40},{16,48},{24,56},{32,64},{40,72},{48,80},{56,88},{64,... | collective-permute-start | bytes 1572872 | tf_op jit(solution)/shard_map/ppermute | solution.py:35
  127.8 17.4 %collective-permute-start.7 = (bf16[2,512,128]{2,1,0:T(8,128)(2,1)}, bf16[2,512,128]{2,1,0:T(8,128)(2,1)S(1)}, u32[]{:S(2)}, u32[]{:S(2)}) collective-permute-start(bf16[2,512,128]{2,1,0:T(8,128)(2,1)} %get-tuple-element.26), channel_id=1, source_target_pairs={{0,6},{1,7},{2,0},{3,1},{4,2},{5,3},{6,4},{7,5},{8,14},{9,15},{10,... | collective-permute-start | bytes 786440 | tf_op jit(solution)/shard_map/ppermute | solution.py:27
  131.2 17.4 %collective-permute-start.8 = (bf16[2,512,128]{2,1,0:T(8,128)(2,1)}, bf16[2,512,128]{2,1,0:T(8,128)(2,1)}, u32[]{:S(2)}, u32[]{:S(2)}) collective-permute-start(bf16[2,512,128]{2,1,0:T(8,128)(2,1)} %get-tuple-element.27), channel_id=1, source_target_pairs={{0,2},{1,3},{2,4},{3,5},{4,6},{5,7},{6,0},{7,1},{8,10},{9,11},{10,... | collective-permute-start | bytes 786440 | tf_op jit(solution)/shard_map/ppermute | solution.py:27
  131.2 17.5 %collective-permute-start.9 = (bf16[2,512,128]{2,1,0:T(8,128)(2,1)}, bf16[2,512,128]{2,1,0:T(8,128)(2,1)}, u32[]{:S(2)}, u32[]{:S(2)}) collective-permute-start(bf16[2,512,128]{2,1,0:T(8,128)(2,1)} %get-tuple-element.28), channel_id=1, source_target_pairs={{0,4},{1,5},{2,6},{3,7},{4,0},{5,1},{6,2},{7,3},{8,12},{9,13},{10,... | collective-permute-start | bytes 786440 | tf_op jit(solution)/shard_map/ppermute | solution.py:27
  135.7 58.9 %collective-permute-start.26 = (bf16[4,384,512]{2,1,0:T(8,128)(2,1)}, bf16[4,384,512]{2,1,0:T(8,128)(2,1)}, u32[]{:S(2)}, u32[]{:S(2)}) collective-permute-start(bf16[4,384,512]{2,1,0:T(8,128)(2,1)} %pad_maximum_fusion.1), channel_id=1, source_target_pairs={{0,1},{1,0},{2,3},{3,2},{4,5},{5,4},{6,7},{7,6},{8,9},{9,8},{10,11... | collective-permute-start | bytes 4718600 | tf_op jit(solution)/shard_map/ppermute | solution.py:31
  140.6 10.8 %collective-permute-start.21 = (bf16[2048,128]{1,0:T(8,128)(2,1)S(1)}, bf16[2048,128]{1,0:T(8,128)(2,1)S(1)}, u32[]{:S(2)}, u32[]{:S(2)}) collective-permute-start(bf16[2048,128]{1,0:T(8,128)(2,1)S(1)} %slice.130), channel_id=1, source_target_pairs={{0,96},{8,104},{16,112},{24,120},{32,0},{40,8},{48,16},{56,24},{64... | collective-permute-start | bytes 1572872 | tf_op jit(solution)/shard_map/ppermute | solution.py:35
  145.1 37.5 %collective-permute-start.17 = (bf16[4096,128]{1,0:T(8,128)(2,1)S(1)}, bf16[4096,128]{1,0:T(8,128)(2,1)}, u32[]{:S(2)}, u32[]{:S(2)}) collective-permute-start(bf16[4096,128]{1,0:T(8,128)(2,1)S(1)} %collective-permute-done.16), channel_id=1, source_target_pairs={{0,8},{8,0},{16,24},{24,16},{32,40},{40,32},{48,56},{56,48},{64,72... | collective-permute-start | bytes 3145736 | tf_op jit(solution)/shard_map/ppermute | solution.py:39
  148.6 38.2 %collective-permute-start.19 = (bf16[4096,128]{1,0:T(8,128)(2,1)}, bf16[4096,128]{1,0:T(8,128)(2,1)}, u32[]{:S(2)}, u32[]{:S(2)}) collective-permute-start(bf16[4096,128]{1,0:T(8,128)(2,1)} %collective-permute-done.18), channel_id=1, source_target_pairs={{0,8},{8,0},{16,24},{24,16},{32,40},{40,32},{48,56},{56,48},{64,72... | collective-permute-start | bytes 3145736 | tf_op jit(solution)/shard_map/ppermute | solution.py:39
  149.8 6.4 %copy-start.6 = (f32[2,512,128]{2,1,0:T(8,128)}, f32[2,512,128]{2,1,0:T(8,128)S(1)}, u32[]{:S(2)}) copy-start(f32[2,512,128]{2,1,0:T(8,128)S(1)} %fusion.1) | copy-start | bytes 1572868
  149.9 24.2 %collective-permute-start.10 = (bf16[512,128]{1,0:T(8,128)(2,1)S(1)}, bf16[512,128]{1,0:T(8,128)(2,1)S(1)}, u32[]{:S(2)}, u32[]{:S(2)}) collective-permute-start(bf16[512,128]{1,0:T(8,128)(2,1)S(1)} %fusion.4), channel_id=1, source_target_pairs={{0,1},{1,0},{2,3},{3,2},{4,5},{5,4},{6,7},{7,6},{8,9},{9,8},{10,11... | collective-permute-start | bytes 393224 | tf_op jit(solution)/shard_map/ppermute | solution.py:31
  152.2 46.5 %collective-permute-start.22 = (bf16[4096,128]{1,0:T(8,128)(2,1)}, bf16[4096,128]{1,0:T(8,128)(2,1)}, u32[]{:S(2)}, u32[]{:S(2)}) collective-permute-start(bf16[4096,128]{1,0:T(8,128)(2,1)} %constant_dynamic-update-slice_fusion), channel_id=1, source_target_pairs={{0,8},{8,0},{16,24},{24,16},{32,40},{40,32},{48,56},{56,48},{64,72... | collective-permute-start | bytes 3145736 | tf_op jit(solution)/shard_map/ppermute | solution.py:39
  175.1 5.5 %collective-permute-start.31 = (bf16[512,128]{1,0:T(8,128)(2,1)S(1)}, bf16[512,128]{1,0:T(8,128)(2,1)}, u32[]{:S(2)}, u32[]{:S(2)}) collective-permute-start(bf16[512,128]{1,0:T(8,128)(2,1)S(1)} %fusion.3), channel_id=1, source_target_pairs={{0,1},{1,0},{2,3},{3,2},{4,5},{5,4},{6,7},{7,6},{8,9},{9,8},{10,11... | collective-permute-start | bytes 393224 | tf_op jit(solution)/shard_map/ppermute | solution.py:31
  182.2 10.0 %collective-permute-start.32 = (bf16[2,512,128]{2,1,0:T(8,128)(2,1)}, bf16[2,512,128]{2,1,0:T(8,128)(2,1)}, u32[]{:S(2)}, u32[]{:S(2)}) collective-permute-start(bf16[2,512,128]{2,1,0:T(8,128)(2,1)} %get-tuple-element.39), channel_id=1, source_target_pairs={{0,2},{1,3},{2,4},{3,5},{4,6},{5,7},{6,0},{7,1},{8,10},{9,11},{10,... | collective-permute-start | bytes 786440 | tf_op jit(solution)/shard_map/ppermute | solution.py:27
  182.6 9.9 %collective-permute-start.33 = (bf16[2,512,128]{2,1,0:T(8,128)(2,1)}, bf16[2,512,128]{2,1,0:T(8,128)(2,1)}, u32[]{:S(2)}, u32[]{:S(2)}) collective-permute-start(bf16[2,512,128]{2,1,0:T(8,128)(2,1)} %get-tuple-element.39), channel_id=1, source_target_pairs={{0,4},{1,5},{2,6},{3,7},{4,0},{5,1},{6,2},{7,3},{8,12},{9,13},{10,... | collective-permute-start | bytes 786440 | tf_op jit(solution)/shard_map/ppermute | solution.py:27
  186.8 6.5 %collective-permute-start.34 = (bf16[2,512,128]{2,1,0:T(8,128)(2,1)}, bf16[2,512,128]{2,1,0:T(8,128)(2,1)}, u32[]{:S(2)}, u32[]{:S(2)}) collective-permute-start(bf16[2,512,128]{2,1,0:T(8,128)(2,1)} %get-tuple-element.39), channel_id=1, source_target_pairs={{0,6},{1,7},{2,0},{3,1},{4,2},{5,3},{6,4},{7,5},{8,14},{9,15},{10,... | collective-permute-start | bytes 786440 | tf_op jit(solution)/shard_map/ppermute | solution.py:27
  189.0 5.6 %copy-start.5 = (bf16[8,384,512]{2,1,0:T(8,128)(2,1)S(1)}, bf16[8,384,512]{2,1,0:T(8,128)(2,1)}, u32[]{:S(2)}) copy-start(bf16[8,384,512]{2,1,0:T(8,128)(2,1)} %copy-done.4) | copy-start | bytes 9437188
  191.1 5.0 %copy-start.3 = (bf16[2,4,128,512]{3,2,1,0:T(8,128)(2,1)S(1)}, bf16[2,4,128,512]{3,2,1,0:T(8,128)(2,1)}, u32[]{:S(2)}) copy-start(bf16[2,4,128,512]{3,2,1,0:T(8,128)(2,1)} %copy.28) | copy-start | bytes 3145732
  201.3 7.3 %copy-start.1 = (bf16[4,2,4096,128]{2,3,1,0:T(8,128)(2,1)S(1)}, bf16[4,2,4096,128]{2,3,1,0:T(8,128)(2,1)}, u32[]{:S(2)}) copy-start(bf16[4,2,4096,128]{2,3,1,0:T(8,128)(2,1)} %constant_dynamic-update-slice_fusion.7) | copy-start | bytes 25165828
  201.3 7.3 %copy-start.2 = (bf16[8,512,512]{2,1,0:T(8,128)(2,1)S(1)}, bf16[8,512,512]{2,1,0:T(8,128)(2,1)}, u32[]{:S(2)}) copy-start(bf16[8,512,512]{2,1,0:T(8,128)(2,1)} %pad_maximum_fusion) | copy-start | bytes 12582916

commit v3 on v2

--- a/solution.py
+++ b/solution.py
@@ -48,7 +48,7 @@
 
 
 def attention_kernel(
-    heads, info_ref, q_ref, g_ref, mine_refs, other_refs, dq_ref, keep_ref, give_ref,
+    heads, info_ref, q_ref, g_ref, mine_refs, other_refs, dq_ref, dqt_ref, keep_ref, give_ref,
     ks, vs, kt, scores, grads, dka, dva, qh, gh, dqt,
 ):
     per_ref = mine_refs[0].shape[0]
@@ -139,7 +139,9 @@
         lax.fori_loop(0, run + 1, grad_step, 0)
         for h in range(heads):
             cols = slice(h * RUN, (h + 1) * RUN)
-            dq_ref[rows, h * HD : (h + 1) * HD] = (dqt[:, cols] * scale).T.astype(jnp.bfloat16)
+            dq = dqt[:, cols] * scale
+            dq_ref[rows, h * HD : (h + 1) * HD] = dq.T.astype(jnp.bfloat16)
+            dqt_ref[h * HD : (h + 1) * HD, rows] = dq.astype(jnp.bfloat16)
     half_head = HD // 2
     for b in range(slots * runs_per_slot):
         slot, part = b // runs_per_slot, b % runs_per_slot
@@ -164,9 +166,14 @@
     pairs = heads * 2 * RUN * count // 2
     return pl.pallas_call(
         functools.partial(attention_kernel, heads),
-        out_shape=(jax.ShapeDtypeStruct(queries.shape, jnp.bfloat16), shared, shared),
+        out_shape=(
+            jax.ShapeDtypeStruct(queries.shape, jnp.bfloat16),
+            jax.ShapeDtypeStruct(queries.shape[::-1], jnp.bfloat16),
+            shared,
+            shared,
+        ),
         in_specs=[smem, vmem, vmem, [vmem] * len(mine), [vmem] * len(other)],
-        out_specs=(vmem, vmem, vmem),
+        out_specs=(vmem, vmem, vmem, vmem),
         scratch_shapes=[
             pltpu.VMEM((count, HD), jnp.bfloat16),
             pltpu.VMEM((count, HD), jnp.bfloat16),
@@ -186,6 +193,111 @@
     )(info, queries, grad_output, mine, other)
 
 
+def join_kernel(in_refs, out_ref, sems):
+    copies, at = [], 0
+    for i, ref in enumerate(in_refs):
+        copies.append(pltpu.make_async_copy(ref, out_ref.at[pl.ds(at, ref.shape[0])], sems.at[i]))
+        copies[-1].start()
+        at += ref.shape[0]
+    for copy in copies:
+        copy.wait()
+
+
+def join(pieces):
+    hbm = pl.BlockSpec(memory_space=pl.ANY)
+    total = sum(p.shape[0] for p in pieces)
+    return pl.pallas_call(
+        join_kernel,
+        out_shape=jax.ShapeDtypeStruct((total,) + pieces[0].shape[1:], pieces[0].dtype),
+        in_specs=[[hbm] * len(pieces)],
+        out_specs=hbm,
+        scratch_shapes=[pltpu.SemaphoreType.DMA((len(pieces),))],
+        cost_estimate=pl.CostEstimate(flops=0, bytes_accessed=2 * 1024 * 1024, transcendentals=0),
+    )(list(pieces))
+
+
+def weight_kernel(dx, last, place_ref, own_refs, other_refs, grad_refs, *rest):
+    if last:
+        sum_ref, shared_refs, wq_ref, wk_ref, wv_ref, inputs, sems = rest
+        sides = (dx, 1 - dx)
+    else:
+        sum_ref, inputs, sems = rest
+        sides = (dx,)
+    core, z = place_ref[0], place_ref[1]
+    lanes = own_refs[0].shape[-1]
+    mine_at = pl.multiple_of(core * lanes, lanes)
+    other_at = pl.multiple_of((1 - core) * lanes, lanes)
+    copies = {}
+    for away in range(4):
+        for n, side in enumerate(sides):
+            for which, (ref, at) in enumerate(((own_refs[away], mine_at), (other_refs[away], other_at))):
+                copies[away, n, which] = pltpu.make_async_copy(
+                    ref.at[:, side], inputs.at[away, n, :, :, pl.ds(at, lanes)], sems.at[away, n, which]
+                )
+                copies[away, n, which].start()
+    for away in range(4):
+        for which in range(2):
+            copies[away, 0, which].wait()
+        total = sum_ref[away] if last else 0.0
+        for dy in range(4):
+            total += contract(grad_refs[dy][...], inputs[away, 0, dy], 1, 0)
+        if not last:
+            sum_ref[away] = total
+            continue
+        norm = 1.0 / math.sqrt(8 * inputs.shape[3])
+        at = pl.multiple_of(lax.rem(z + away, 4) * 2 * lanes, 2 * lanes)
+        wq_ref[pl.ds(at, 2 * lanes), :] = (total * norm).T
+    if not last:
+        return
+    shared = [[shared_refs[dy][side].T for dy in range(4)] for side in sides]
+    for away in range(4):
+        for which in range(2):
+            copies[away, 1, which].wait()
+        total = 0.0
+        for n in range(2):
+            for dy in range(4):
+                total += contract(shared[n][dy], inputs[away, n, dy], 1, 0)
+        at = pl.multiple_of(lax.rem(z + away, 4) * 2 * lanes, 2 * lanes)
+        total = (total * norm).T
+        half = lanes // 2
+        wk_ref[pl.ds(at, 2 * lanes), :] = total[:, :half]
+        wv_ref[pl.ds(at, 2 * lanes), :] = total[:, half:]
+
+
+def weights(dx, place, own, other, grads, total=None, shared=None):
+    last = total is not None
+    smem = pl.BlockSpec(memory_space=pltpu.SMEM)
+    vmem = pl.BlockSpec(memory_space=pltpu.VMEM)
+    hbm = pl.BlockSpec(memory_space=pl.ANY)
+    lanes, count, cols = own[0].shape[-1], own[0].shape[2], grads[0].shape[0]
+    sides = 2 if last else 1
+    f32 = jnp.float32
+    if last:
+        out_shape = (
+            jax.ShapeDtypeStruct((8 * lanes, cols), f32),
+            jax.ShapeDtypeStruct((8 * lanes, lanes // 2), f32),
+            jax.ShapeDtypeStruct((8 * lanes, lanes // 2), f32),
+        )
+        more, more_specs, out_specs = (total, shared), [vmem, [vmem] * 4], (vmem,) * 3
+    else:
+        out_shape = jax.ShapeDtypeStruct((4, cols, 2 * lanes), f32)
+        more, more_specs, out_specs = (), [], vmem
+    return pl.pallas_call(
+        functools.partial(weight_kernel, dx, last),
+        out_shape=out_shape,
+        in_specs=[smem, [hbm] * 4, [hbm] * 4, [vmem] * 4] + more_specs,
+        out_specs=out_specs,
+        scratch_shapes=[
+            pltpu.VMEM((4, sides, 4, count, 2 * lanes), jnp.bfloat16),
+            pltpu.SemaphoreType.DMA((4, sides, 2)),
+        ],
+        compiler_params=pltpu.CompilerParams(vmem_limit_bytes=VMEM_BYTES),
+        cost_estimate=pl.CostEstimate(
+            flops=2 * 4 * count * cols * 8 * lanes, bytes_accessed=10 * 1024 * 1024, transcendentals=0
+        ),
+    )(place, list(own), list(other), list(grads), *more)
+
+
 def local(layer_input, queries, key_vectors, value_vectors, grad_output, positions):
     group = lax.axis_index("dp")
     member, head, z = group % 2, group // 2, group // 4
@@ -195,6 +307,7 @@
     width = layer_input.shape[1] // 8
     slab = width // 8
     first = member == 0
+    place = jnp.stack([member, z]).astype(jnp.int32)
 
     key_local = lax.dynamic_slice_in_dim(key_vectors, head * HD, HD, 1)
     value_local = lax.dynamic_slice_in_dim(value_vectors, head * HD, HD, 1)
@@ -213,7 +326,6 @@
     column_other = swap_cores(column)
     pairs = [jnp.stack([block(dy, 0), from_x[dy]]) for dy in range(4)]
     pairs = [pairs[0]] + [along_y(pairs[dy], dy) for dy in range(1, 4)]
-    slab_own = jnp.concatenate([p[dx] for dx in range(2) for p in pairs], axis=0)
     partner_other = swap_cores(partner_column)
     info = jnp.concatenate(
         [
@@ -222,53 +334,39 @@
             member.astype(jnp.int32)[None],
         ]
     )
+    slab_own = join(pairs).reshape(4, 2, count, slab)
     slab_back, slab_ahead = along_z(slab_own, 1), along_z(slab_own, 3)
 
-    grad_query, keep, give = attention(
+    grad_query, grad_query_t, keep, give = attention(
         info, queries, grad_output, [column, partner_column], [column_other, partner_other]
     )
-
-    cut = slab_own.shape[0] // 2
-    slab_far = jnp.concatenate([along_z(slab_back[:cut], 1), along_z(slab_ahead[cut:], 3)])
-    slabs = jnp.zeros((4, 2) + slab_own.shape, jnp.bfloat16)
-    for away, value in ((0, slab_own), (3, slab_back), (1, slab_ahead), (2, slab_far)):
-        other = swap_cores(value)
-        slabs = lax.dynamic_update_slice(slabs, value[None, None], ((z + away) % 4, member, 0, 0))
-        slabs = lax.dynamic_update_slice(slabs, other[None, None], ((z + away) % 4, 1 - member, 0, 0))
-    slabs = slabs.reshape((8,) + slab_own.shape)
+    grad_query_t, give, slab_back, slab_ahead = lax.optimization_barrier(
+        (grad_query_t, give, slab_back, slab_ahead)
+    )
 
     summed = (keep.astype(jnp.float32) + swap_cores(give).astype(jnp.float32)).astype(jnp.bfloat16)
     summed = summed.reshape(2, 4, count, HD)
+    queries_x = [swap_x(grad_query_t)]
+    queries_y = {1: along_y(grad_query_t, 1), 3: along_y(grad_query_t, 3)}
     rows_y = summed[:, 0].astype(jnp.float32)
     for dy in (1, 3, 2):
         rows_y = rows_y + along_y(summed[:, dy], -dy).astype(jnp.float32)
-    total = rows_y[0] + swap_x(rows_y[1].astype(jnp.bfloat16)).astype(jnp.float32)
-    total = total.astype(jnp.bfloat16)
-    both = jnp.stack([total, swap_x(total)])
-    shared = jnp.stack([both] + by_source(*to_all_y(both)), axis=1)
-    shared = shared.reshape(8 * count, HD)
-
-    mark = count * 3 // 4
-    part_a, part_b = grad_query[:mark], grad_query[mark:]
-    column_a = jnp.stack([part_a] + by_source(*to_all_y(part_a)))
-    all_a = jnp.concatenate([column_a, swap_x(column_a)])
-    both_b = jnp.stack([part_b, swap_x(part_b)])
-    all_b = jnp.stack([both_b] + by_source(*to_all_y(both_b)), axis=1)
-    all_b = all_b.reshape((8,) + part_b.shape)
-    queries_all = jnp.concatenate([all_a, all_b], axis=1).reshape(8 * count, -1)
-
-    norm = 1.0 / math.sqrt(8 * count)
-    grad_wq = contract(slabs, queries_all, 1, 0).reshape(width, -1) * norm
-    grad_wkv = contract(slabs, shared, 1, 0).reshape(width, -1) * norm
+    rows_y = rows_y.astype(jnp.bfloat16)
+    both = (rows_y.astype(jnp.float32) + swap_x(rows_y).astype(jnp.float32)[::-1]).astype(jnp.bfloat16)
+    total = both[0]
+    queries_y[2] = along_y(grad_query_t, 2)
+    queries_x += [swap_x(queries_y[dy]) for dy in (1, 2, 3)]
+    shared = [both] + by_source(*to_all_y(both))
+
+    slab_far = along_z(slab_own, 2)
+    slabs = [slab_own, slab_ahead, slab_far, slab_back]
+    slabs_other = [swap_cores(value) for value in slabs]
+    partial = weights(
+        0, place, slabs, slabs_other, [grad_query_t] + [queries_y[dy] for dy in (1, 2, 3)]
+    )
+    grad_wq, grad_wk, grad_wv = weights(1, place, slabs, slabs_other, queries_x, partial, shared)
     share = HD // 2
-    return (
-        grad_query,
-        total[:, :share],
-        total[:, share:],
-        grad_wq,
-        grad_wkv[:, :share],
-        grad_wkv[:, share:],
-    )
+    return grad_query, total[:, :share], total[:, share:], grad_wq, grad_wk, grad_wv
 
 
 def solution(mesh):

time: 218 us -> 238 us (1.092)
  Pallas kernels: 19 us -> 71.2 us
  waiting for transfers between devices: 52.3 us -> 92 us
  local copies, waits for them, and re-layouts: 40.4 us -> 10.2 us
  starting transfers between devices: 76.4 us -> 56.2 us
  matrix products: 12.2 us -> 0 us
  other arithmetic: 12.8 us -> 5.87 us
    pallas_call x0 -> x3, Pallas kernels: none -> 55.3 us  [the longest x1 32.9 us: join(): pl.pallas_call(join_kernel, out_shape=jax.ShapeDtypeStruct((total,) + pie...]
    ppermute x4 -> x3, waiting for transfers between devices: 1.08 us -> 19.2 us  [along_z(): lax.ppermute(value, 'dp', [(i, (i + 4 * step) % 16) for i in range(16)])]
    ppermute x18 -> x15, waiting for transfers between devices: 26.1 us -> 39.3 us  [along_y(): lax.ppermute(value, 'ctx', [(i, (i + 2 * step) % 8) for i in range(8)])]
    ppermute x18 -> x15, starting transfers between devices: 42.9 us -> 30 us  [along_y(): lax.ppermute(value, 'ctx', [(i, (i + 2 * step) % 8) for i in range(8)])]
    dot_general x2 -> x0, matrix products: 12.2 us -> none  [contract(): lax.dot_general(left, right, (((left_dim,), (right_dim,)), ((), ())), pre...]
    broadcast_in_dim x9 -> x0, local copies, waits for them, and re-layouts: 11 us -> none  [the longest x4 4.97 us: local(): value[None, None]]
    ppermute x6 -> x7, waiting for transfers between devices: 25.1 us -> 33.6 us  [swap_x(): return lax.ppermute(value, 'ctx', [(i, i ^ 1) for i in range(8)])]
    ppermute x7, starting transfers between devices: 16.8 us -> 8.48 us  [swap_cores(): return lax.ppermute(value, 'dp', [(i, i ^ 1) for i in range(16)])]
  transfers between devices with their start and end apart: 35 -> 32, of which waited for: 13 -> 13; matrix products, arithmetic and copies ran while one was open for 21% -> 4% of each run, Pallas kernels for 9% -> 24%
where the time goes in v3:
time: 238 us; the launch traced here: 237 us
  waiting for transfers between devices  92 us (39%)
  Pallas kernels  71.2 us (30%)
  starting transfers between devices  56.2 us (24%)
  local copies, waits for them, and re-layouts  10.2 us (4%)
  other arithmetic  5.87 us (2%)
    ppermute x15, waiting for transfers between devices, along_y(): lax.ppermute(value, 'ctx', [(i, (i + 2 * step) % 8) for i in range(8)])  39.3 us
    ppermute x7, waiting for transfers between devices, swap_x(): return lax.ppermute(value, 'ctx', [(i, i ^ 1) for i in range(8)])  33.6 us
    pallas_call x1, Pallas kernels, join(): pl.pallas_call(join_kernel, out_shape=jax.ShapeDtypeStruct((total,) + pie...  32.9 us
    ppermute x15, starting transfers between devices, along_y(): lax.ppermute(value, 'ctx', [(i, (i + 2 * step) % 8) for i in range(8)])  30 us
    pallas_call x2, Pallas kernels, weights(): pl.pallas_call(functools.partial(weight_kernel, dx, last), out_shape=out_...  22.4 us
    ppermute x3, waiting for transfers between devices, along_z(): lax.ppermute(value, 'dp', [(i, (i + 4 * step) % 16) for i in range(16)])  19.2 us
    pallas_call x1, Pallas kernels, attention(): pl.pallas_call(functools.partial(attention_kernel, heads), out_shape=(jax...  16 us
    ppermute x7, starting transfers between devices, swap_x(): return lax.ppermute(value, 'ctx', [(i, i ^ 1) for i in range(8)])  11.3 us
  transfers between devices with their start and end apart: 32, of which 13 were waited for; matrix products, arithmetic and copies ran while one was open for 4% of the time, Pallas kernels for 24%

profile of v3, /device:TPU:1, one launch (start us, length us, event | category | flops | bytes accessed | tf_op | source)
XLA Modules:
  0.0 236.6 jit_solution(13851380479855037022)
XLA Ops:
  0.8 1.4 dynamic-slice_bitcast_fusion
  2.3 3.7 %collective-permute-start.6 = (bf16[4,512,128]{2,1,0:T(8,128)(2,1)S(1)}, bf16[4,512,128]{2,1,0:T(8,128)(2,1)S(1)}, u32[]{:S(2)}, u32[]{:S(2)}) collective-permute-start(bf16[4,512,128]{2,1,0:T(8,128)(2,1)S(1)} %pad_maximum_fusion.1), channel_id=1, source_target_pairs={{0,1},{1,0},{2,3},{3,2},{4,5},{5,4},{6,7},{7,6},{8,9},{9,8},{10,11... | collective-permute-start | bytes 1572872 | tf_op jit(solution)/shard_map/ppermute | solution.py:31
  5.9 0.8 slice.42
  6.7 1.0 dynamic-slice_select_fusion
  7.8 1.4 collective-permute-start
  9.2 2.6 %collective-permute-start.1 = (bf16[528,128]{1,0:T(8,128)(2,1)S(1)}, bf16[528,128]{1,0:T(8,128)(2,1)S(1)}, u32[]{:S(2)}, u32[]{:S(2)}) collective-permute-start(bf16[528,128]{1,0:T(8,128)(2,1)S(1)} %get-tuple-element.56), channel_id=1, source_target_pairs={{0,4},{1,5},{2,6},{3,7},{4,0},{5,1},{6,2},{7,3},{8,12},{9,13},{10,... | collective-permute-start | bytes 405512 | tf_op jit(solution)/shard_map/ppermute | solution.py:27
  11.8 1.1 collective-permute-start.2
  13.3 4.0 %collective-permute-done.1 = bf16[528,128]{1,0:T(8,128)(2,1)S(1)} collective-permute-done((bf16[528,128]{1,0:T(8,128)(2,1)S(1)}, bf16[528,128]{1,0:T(8,128)(2,1)S(1)}, u32[]{:S(2)}, u32[]{:S(2)}) %collective-permute-start.1) | collective-permute-done | bytes 135200 | tf_op jit(solution)/shard_map/ppermute | solution.py:27
  17.6 2.3 collective-permute-start.4
  20.0 2.0 collective-permute-start.9
  22.0 0.9 collective-permute-start.8
  22.9 8.1 %collective-permute-done.3.mine_refs_1_ = bf16[4,528,128]{2,1,0:T(8,128)(2,1)} collective-permute-done((bf16[4,528,128]{2,1,0:T(8,128)(2,1)S(1)}, bf16[4,528,128]{2,1,0:T(8,128)(2,1)}, u32[]{:S(2)}, u32[]{:S(2)}) %collective-permute-start.3) | collective-permute-done | bytes 540704 | tf_op jit(solution)/shard_map/ppermute | solution.py:31
  31.0 2.8 %collective-permute-start.5 = (bf16[4,528,128]{2,1,0:T(8,128)(2,1)}, bf16[4,528,128]{2,1,0:T(8,128)(2,1)}, u32[]{:S(2)}, u32[]{:S(2)}) collective-permute-start(bf16[4,528,128]{2,1,0:T(8,128)(2,1)} %collective-permute-done.3.mine_refs_1_), channel_id=1, source_target_pairs={{0,8},{8,0},{16,24},{24,16},{32,40},{40,32},{48,56},{56,48},{64,72... | collective-permute-start | bytes 1622024 | tf_op jit(solution)/shard_map/ppermute | solution.py:39
  33.9 1.2 collective-permute-start.7
  36.7 6.4 %collective-permute-done.7.in_refs_1_ = bf16[2,512,128]{2,1,0:T(8,128)(2,1)S(1)} collective-permute-done((bf16[2,512,128]{2,1,0:T(8,128)(2,1)S(1)}, bf16[2,512,128]{2,1,0:T(8,128)(2,1)S(1)}, u32[]{:S(2)}, u32[]{:S(2)}) %collective-permute-start.7) | collective-permute-done | bytes 262176 | tf_op jit(solution)/shard_map/ppermute | solution.py:27
  43.8 32.9 %shard_map.110 = bf16[8,512,128]{2,1,0:T(8,128)(2,1)} custom-call(bf16[2,512,128]{2,1,0:T(8,128)(2,1)} %pad_maximum_fusion.2.in_refs_0_, bf16[2,512,128]{2,1,0:T(8,128)(2,1)} %copy-done.17, bf16[2,512,128]{2,1,0:T(8,128)(2,1)} %copy-done.16, bf16[2,512,128]{2,1,0:T(8,128)(2,1)} %copy-done.15), custom_call_target="tpu_custom_call" | custom-call | bytes 2097152 | tf_op jit(solution)/shard_map/pallas_call | solution.py:209
  76.7 1.7 collective-permute-start.10
  78.4 2.2 collective-permute-start.11
  81.2 16.0 %shard_map.109 = (bf16[512,512]{1,0:T(8,128)(2,1)}, bf16[512,512]{1,0:T(8,128)(2,1)}, bf16[8,512,128]{2,1,0:T(8,128)(2,1)}, bf16[8,512,128]{2,1,0:T(8,128)(2,1)}) custom-call(s32[17]{0:T(128)} %pad_add_fusion.info_ref, bf16[512,512]{1,0:T(8,128)(2,1)} %q_ref.1, bf16[512,512]{1,0:T(8,128)(2,1)} %g_ref.1, bf16[4,528,128]{2,1,0:T(8,128)(2,1)} %copy-done.9, ...), custom_call_target="tpu_custom_call" | custom-call | flops 10737418240 | bytes 8388608 | tf_op jit(solution)/shard_map/pallas_call | solution.py:167
  97.2 6.3 %collective-permute-done.10.own_refs_3_ = bf16[4,2,512,128]{3,2,1,0:T(8,128)(2,1)S(1)} collective-permute-done((bf16[4,2,512,128]{3,2,1,0:T(8,128)(2,1)}, bf16[4,2,512,128]{3,2,1,0:T(8,128)(2,1)S(1)}, u32[]{:S(2)}, u32[]{:S(2)}) %collective-permute-start.10) | collective-permute-done | bytes 1048608 | tf_op jit(solution)/shard_map/ppermute | solution.py:35
  103.5 1.4 collective-permute-start.12
  104.9 2.6 %collective-permute-start.17 = (bf16[4,2,512,128]{3,2,1,0:T(8,128)(2,1)S(1)}, bf16[4,2,512,128]{3,2,1,0:T(8,128)(2,1)S(1)}, u32[]{:S(2)}, u32[]{:S(2)}) collective-permute-start(bf16[4,2,512,128]{3,2,1,0:T(8,128)(2,1)S(1)} %bitcast.50), channel_id=1, source_target_pairs={{0,64},{8,72},{16,80},{24,88},{32,96},{40,104},{48,112},{56,120},{... | collective-permute-start | bytes 3145736 | tf_op jit(solution)/shard_map/ppermute | solution.py:35
  107.9 5.1 %collective-permute-start.23 = (bf16[512,512]{1,0:T(8,128)(2,1)}, bf16[512,512]{1,0:T(8,128)(2,1)}, u32[]{:S(2)}, u32[]{:S(2)}) collective-permute-start(bf16[512,512]{1,0:T(8,128)(2,1)} %get-tuple-element.24.grad_refs_0_), channel_id=1, source_target_pairs={{0,2},{1,3},{2,4},{3,5},{4,6},{5,7},{6,0},{7,1},{8,10},{9,11},{10,... | collective-permute-start | bytes 1572872 | tf_op jit(solution)/shard_map/ppermute | solution.py:27
  113.0 1.6 add_convert_fusion
  114.6 3.0 %collective-permute-start.13 = (bf16[2,512,128]{2,1,0:T(8,128)(2,1)S(1)}, bf16[2,512,128]{2,1,0:T(8,128)(2,1)S(1)}, u32[]{:S(2)}, u32[]{:S(2)}) collective-permute-start(bf16[2,512,128]{2,1,0:T(8,128)(2,1)S(1)} %get-tuple-element.48), channel_id=1, source_target_pairs={{0,6},{1,7},{2,0},{3,1},{4,2},{5,3},{6,4},{7,5},{8,14},{9,15},{10,... | collective-permute-start | bytes 786440 | tf_op jit(solution)/shard_map/ppermute | solution.py:27
  118.3 12.8 %collective-permute-done.17.own_refs_2_ = bf16[4,2,512,128]{3,2,1,0:T(8,128)(2,1)S(1)} collective-permute-done((bf16[4,2,512,128]{3,2,1,0:T(8,128)(2,1)S(1)}, bf16[4,2,512,128]{3,2,1,0:T(8,128)(2,1)S(1)}, u32[]{:S(2)}, u32[]{:S(2)}) %collective-permute-start.17) | collective-permute-done | bytes 1048608 | tf_op jit(solution)/shard_map/ppermute | solution.py:35
  131.2 0.9 collective-permute-start.21
  132.1 6.2 %collective-permute-start.14 = (bf16[2,512,128]{2,1,0:T(8,128)(2,1)S(1)}, bf16[2,512,128]{2,1,0:T(8,128)(2,1)S(1)}, u32[]{:S(2)}, u32[]{:S(2)}) collective-permute-start(bf16[2,512,128]{2,1,0:T(8,128)(2,1)S(1)} %get-tuple-element.49), channel_id=1, source_target_pairs={{0,2},{1,3},{2,4},{3,5},{4,6},{5,7},{6,0},{7,1},{8,10},{9,11},{10,... | collective-permute-start | bytes 786440 | tf_op jit(solution)/shard_map/ppermute | solution.py:27
  138.3 3.5 %collective-permute-start.15 = (bf16[2,512,128]{2,1,0:T(8,128)(2,1)S(1)}, bf16[2,512,128]{2,1,0:T(8,128)(2,1)S(1)}, u32[]{:S(2)}, u32[]{:S(2)}) collective-permute-start(bf16[2,512,128]{2,1,0:T(8,128)(2,1)S(1)} %get-tuple-element.50), channel_id=1, source_target_pairs={{0,4},{1,5},{2,6},{3,7},{4,0},{5,1},{6,2},{7,3},{8,12},{9,13},{10,... | collective-permute-start | bytes 786440 | tf_op jit(solution)/shard_map/ppermute | solution.py:27
  141.9 5.1 %collective-permute-done.14 = bf16[2,512,128]{2,1,0:T(8,128)(2,1)S(1)} collective-permute-done((bf16[2,512,128]{2,1,0:T(8,128)(2,1)S(1)}, bf16[2,512,128]{2,1,0:T(8,128)(2,1)S(1)}, u32[]{:S(2)}, u32[]{:S(2)}) %collective-permute-start.14) | collective-permute-done | bytes 262176 | tf_op jit(solution)/shard_map/ppermute | solution.py:27
  147.1 6.3 %collective-permute-done.15 = bf16[2,512,128]{2,1,0:T(8,128)(2,1)S(1)} collective-permute-done((bf16[2,512,128]{2,1,0:T(8,128)(2,1)S(1)}, bf16[2,512,128]{2,1,0:T(8,128)(2,1)S(1)}, u32[]{:S(2)}, u32[]{:S(2)}) %collective-permute-start.15) | collective-permute-done | bytes 262176 | tf_op jit(solution)/shard_map/ppermute | solution.py:27
  153.6 11.2 %collective-permute-done.25.grad_refs_2_ = bf16[512,512]{1,0:T(8,128)(2,1)} collective-permute-done((bf16[512,512]{1,0:T(8,128)(2,1)S(1)}, bf16[512,512]{1,0:T(8,128)(2,1)}, u32[]{:S(2)}, u32[]{:S(2)}) %collective-permute-start.25) | collective-permute-done | bytes 524320 | tf_op jit(solution)/shard_map/ppermute | solution.py:27
  164.8 0.8 collective-permute-start.22
  165.6 5.7 %collective-permute-done.27.grad_refs_3_ = bf16[512,512]{1,0:T(8,128)(2,1)} collective-permute-done((bf16[512,512]{1,0:T(8,128)(2,1)S(1)}, bf16[512,512]{1,0:T(8,128)(2,1)}, u32[]{:S(2)}, u32[]{:S(2)}) %collective-permute-start.27) | collective-permute-done | bytes 524320 | tf_op jit(solution)/shard_map/ppermute | solution.py:27
  171.3 2.9 %collective-permute-start.24 = (bf16[512,512]{1,0:T(8,128)(2,1)}, bf16[512,512]{1,0:T(8,128)(2,1)}, u32[]{:S(2)}, u32[]{:S(2)}) collective-permute-start(bf16[512,512]{1,0:T(8,128)(2,1)} %collective-permute-done.23.grad_refs_1_), channel_id=1, source_target_pairs={{0,1},{1,0},{2,3},{3,2},{4,5},{5,4},{6,7},{7,6},{8,9},{9,8},{10,11... | collective-permute-start | bytes 1572872 | tf_op jit(solution)/shard_map/ppermute | solution.py:31
  174.3 0.8 pad_add_fusion.1.place_ref
  175.1 2.8 %collective-permute-start.26 = (bf16[512,512]{1,0:T(8,128)(2,1)}, bf16[512,512]{1,0:T(8,128)(2,1)S(1)}, u32[]{:S(2)}, u32[]{:S(2)}) collective-permute-start(bf16[512,512]{1,0:T(8,128)(2,1)} %collective-permute-done.25.grad_refs_2_), channel_id=1, source_target_pairs={{0,1},{1,0},{2,3},{3,2},{4,5},{5,4},{6,7},{7,6},{8,9},{9,8},{10,11... | collective-permute-start | bytes 1572872 | tf_op jit(solution)/shard_map/ppermute | solution.py:31
  178.0 0.9 collective-permute-start.28
  178.9 9.1 %shard_map.111.rest_0_ = f32[4,512,256]{2,1,0:T(8,128)} custom-call(s32[2]{0:T(128)} %pad_add_fusion.1.place_ref, bf16[4,2,512,128]{3,2,1,0:T(8,128)(2,1)} %bitcast.48, bf16[4,2,512,128]{3,2,1,0:T(8,128)(2,1)} %copy-done.2, bf16[4,2,512,128]{3,2,1,0:T(8,128)(2,1)} %copy-done.3, bf16[4,2,512,128]{3,2,1,0:T(8,128)(2,1)} %copy-done.1, ...), custom_call_target="tpu_custom_call" | custom-call | flops 2147483648 | bytes 10485760 | tf_op jit(solution)/shard_map/pallas_call | solution.py:285
  188.0 7.4 %collective-permute-done.16 = bf16[2,512,128]{2,1,0:T(8,128)(2,1)S(1)} collective-permute-done((bf16[2,512,128]{2,1,0:T(8,128)(2,1)S(1)}, bf16[2,512,128]{2,1,0:T(8,128)(2,1)S(1)}, u32[]{:S(2)}, u32[]{:S(2)}) %collective-permute-start.16) | collective-permute-done | bytes 262176 | tf_op jit(solution)/shard_map/ppermute | solution.py:31
  195.6 1.0 collective-permute-start.30
  196.6 1.7 collective-permute-start.31
  198.4 0.7 copy.20
  199.9 6.7 %collective-permute-done.26.grad_refs_2_ = bf16[512,512]{1,0:T(8,128)(2,1)S(1)} collective-permute-done((bf16[512,512]{1,0:T(8,128)(2,1)}, bf16[512,512]{1,0:T(8,128)(2,1)S(1)}, u32[]{:S(2)}, u32[]{:S(2)}) %collective-permute-start.26) | collective-permute-done | bytes 524320 | tf_op jit(solution)/shard_map/ppermute | solution.py:31
  206.6 11.3 %collective-permute-done.28.grad_refs_3_ = bf16[512,512]{1,0:T(8,128)(2,1)} collective-permute-done((bf16[512,512]{1,0:T(8,128)(2,1)}, bf16[512,512]{1,0:T(8,128)(2,1)}, u32[]{:S(2)}, u32[]{:S(2)}) %collective-permute-start.28) | collective-permute-done | bytes 524320 | tf_op jit(solution)/shard_map/ppermute | solution.py:31
  219.4 13.3 %shard_map.112 = (f32[1024,512]{1,0:T(8,128)}, f32[1024,64]{1,0:T(8,128)}, f32[1024,64]{1,0:T(8,128)}) custom-call(s32[2]{0:T(128)} %pad_add_fusion.1.place_ref, bf16[4,2,512,128]{3,2,1,0:T(8,128)(2,1)} %bitcast.49, bf16[4,2,512,128]{3,2,1,0:T(8,128)(2,1)} %copy-done.2, bf16[4,2,512,128]{3,2,1,0:T(8,128)(2,1)} %copy-done.3, ...), custom_call_target="tpu_custom_call" | custom-call | flops 2147483648 | bytes 10485760 | tf_op jit(solution)/shard_map/pallas_call | solution.py:285
  232.7 1.9 copy.22
  234.7 1.9 copy.23
  (87 shorter events, 8.0 us)
Async XLA Ops:
  2.3 17.6 %collective-permute-start.6 = (bf16[4,512,128]{2,1,0:T(8,128)(2,1)S(1)}, bf16[4,512,128]{2,1,0:T(8,128)(2,1)S(1)}, u32[]{:S(2)}, u32[]{:S(2)}) collective-permute-start(bf16[4,512,128]{2,1,0:T(8,128)(2,1)S(1)} %pad_maximum_fusion.1), channel_id=1, source_target_pairs={{0,1},{1,0},{2,3},{3,2},{4,5},{5,4},{6,7},{7,6},{8,9},{9,8},{10,11... | collective-permute-start | bytes 1572872 | tf_op jit(solution)/shard_map/ppermute | solution.py:31
  7.8 5.5 %collective-permute-start = (bf16[528,128]{1,0:T(8,128)(2,1)S(1)}, bf16[528,128]{1,0:T(8,128)(2,1)S(1)}, u32[]{:S(2)}, u32[]{:S(2)}) collective-permute-start(bf16[528,128]{1,0:T(8,128)(2,1)S(1)} %get-tuple-element.56), channel_id=1, source_target_pairs={{0,2},{1,3},{2,4},{3,5},{4,6},{5,7},{6,0},{7,1},{8,10},{9,11},{10,... | collective-permute-start | bytes 405512 | tf_op jit(solution)/shard_map/ppermute | solution.py:27
  9.2 8.2 %collective-permute-start.1 = (bf16[528,128]{1,0:T(8,128)(2,1)S(1)}, bf16[528,128]{1,0:T(8,128)(2,1)S(1)}, u32[]{:S(2)}, u32[]{:S(2)}) collective-permute-start(bf16[528,128]{1,0:T(8,128)(2,1)S(1)} %get-tuple-element.56), channel_id=1, source_target_pairs={{0,4},{1,5},{2,6},{3,7},{4,0},{5,1},{6,2},{7,3},{8,12},{9,13},{10,... | collective-permute-start | bytes 405512 | tf_op jit(solution)/shard_map/ppermute | solution.py:27
  11.8 5.6 %collective-permute-start.2 = (bf16[528,128]{1,0:T(8,128)(2,1)S(1)}, bf16[528,128]{1,0:T(8,128)(2,1)S(1)}, u32[]{:S(2)}, u32[]{:S(2)}) collective-permute-start(bf16[528,128]{1,0:T(8,128)(2,1)S(1)} %get-tuple-element.56), channel_id=1, source_target_pairs={{0,6},{1,7},{2,0},{3,1},{4,2},{5,3},{6,4},{7,5},{8,14},{9,15},{10,... | collective-permute-start | bytes 405512 | tf_op jit(solution)/shard_map/ppermute | solution.py:27
  17.4 59.3 %copy-start.9 = (bf16[4,528,128]{2,1,0:T(8,128)(2,1)}, bf16[4,528,128]{2,1,0:T(8,128)(2,1)S(1)}, u32[]{:S(2)}) copy-start(bf16[4,528,128]{2,1,0:T(8,128)(2,1)S(1)} %pad_maximum_fusion.mine_refs_0_) | copy-start | bytes 1622020
  17.4 13.6 %collective-permute-start.3 = (bf16[4,528,128]{2,1,0:T(8,128)(2,1)S(1)}, bf16[4,528,128]{2,1,0:T(8,128)(2,1)}, u32[]{:S(2)}, u32[]{:S(2)}) collective-permute-start(bf16[4,528,128]{2,1,0:T(8,128)(2,1)S(1)} %pad_maximum_fusion.mine_refs_0_), channel_id=1, source_target_pairs={{0,1},{1,0},{2,3},{3,2},{4,5},{5,4},{6,7},{7,6},{8,9},{9,8},{10,11... | collective-permute-start | bytes 1622024 | tf_op jit(solution)/shard_map/ppermute | solution.py:31
  17.6 63.6 %collective-permute-start.4 = (bf16[4,528,128]{2,1,0:T(8,128)(2,1)S(1)}, bf16[4,528,128]{2,1,0:T(8,128)(2,1)}, u32[]{:S(2)}, u32[]{:S(2)}) collective-permute-start(bf16[4,528,128]{2,1,0:T(8,128)(2,1)S(1)} %pad_maximum_fusion.mine_refs_0_), channel_id=1, source_target_pairs={{0,8},{8,0},{16,24},{24,16},{32,40},{40,32},{48,56},{56,48},{64,72... | collective-permute-start | bytes 1622024 | tf_op jit(solution)/shard_map/ppermute | solution.py:39
  20.0 16.7 %collective-permute-start.9 = (bf16[2,512,128]{2,1,0:T(8,128)(2,1)S(1)}, bf16[2,512,128]{2,1,0:T(8,128)(2,1)S(1)}, u32[]{:S(2)}, u32[]{:S(2)}) collective-permute-start(bf16[2,512,128]{2,1,0:T(8,128)(2,1)S(1)} %pad_maximum_fusion.5), channel_id=1, source_target_pairs={{0,6},{1,7},{2,0},{3,1},{4,2},{5,3},{6,4},{7,5},{8,14},{9,15},{10,... | collective-permute-start | bytes 786440 | tf_op jit(solution)/shard_map/ppermute | solution.py:27
  22.0 14.7 %collective-permute-start.8 = (bf16[2,512,128]{2,1,0:T(8,128)(2,1)S(1)}, bf16[2,512,128]{2,1,0:T(8,128)(2,1)S(1)}, u32[]{:S(2)}, u32[]{:S(2)}) collective-permute-start(bf16[2,512,128]{2,1,0:T(8,128)(2,1)S(1)} %pad_maximum_fusion.4), channel_id=1, source_target_pairs={{0,4},{1,5},{2,6},{3,7},{4,0},{5,1},{6,2},{7,3},{8,12},{9,13},{10,... | collective-permute-start | bytes 786440 | tf_op jit(solution)/shard_map/ppermute | solution.py:27
  31.0 50.2 %collective-permute-start.5 = (bf16[4,528,128]{2,1,0:T(8,128)(2,1)}, bf16[4,528,128]{2,1,0:T(8,128)(2,1)}, u32[]{:S(2)}, u32[]{:S(2)}) collective-permute-start(bf16[4,528,128]{2,1,0:T(8,128)(2,1)} %collective-permute-done.3.mine_refs_1_), channel_id=1, source_target_pairs={{0,8},{8,0},{16,24},{24,16},{32,40},{40,32},{48,56},{56,48},{64,72... | collective-permute-start | bytes 1622024 | tf_op jit(solution)/shard_map/ppermute | solution.py:39
  33.9 9.2 %collective-permute-start.7 = (bf16[2,512,128]{2,1,0:T(8,128)(2,1)S(1)}, bf16[2,512,128]{2,1,0:T(8,128)(2,1)S(1)}, u32[]{:S(2)}, u32[]{:S(2)}) collective-permute-start(bf16[2,512,128]{2,1,0:T(8,128)(2,1)S(1)} %pad_maximum_fusion.3), channel_id=1, source_target_pairs={{0,2},{1,3},{2,4},{3,5},{4,6},{5,7},{6,0},{7,1},{8,10},{9,11},{10,... | collective-permute-start | bytes 786440 | tf_op jit(solution)/shard_map/ppermute | solution.py:27
  36.7 6.4 %copy-start.15 = (bf16[2,512,128]{2,1,0:T(8,128)(2,1)}, bf16[2,512,128]{2,1,0:T(8,128)(2,1)S(1)}, u32[]{:S(2)}) copy-start(bf16[2,512,128]{2,1,0:T(8,128)(2,1)S(1)} %collective-permute-done.9.in_refs_3_) | copy-start | bytes 786436
  36.7 6.4 %copy-start.16 = (bf16[2,512,128]{2,1,0:T(8,128)(2,1)}, bf16[2,512,128]{2,1,0:T(8,128)(2,1)S(1)}, u32[]{:S(2)}) copy-start(bf16[2,512,128]{2,1,0:T(8,128)(2,1)S(1)} %collective-permute-done.8.in_refs_2_) | copy-start | bytes 786436
  76.7 26.8 %collective-permute-start.10 = (bf16[4,2,512,128]{3,2,1,0:T(8,128)(2,1)}, bf16[4,2,512,128]{3,2,1,0:T(8,128)(2,1)S(1)}, u32[]{:S(2)}, u32[]{:S(2)}) collective-permute-start(bf16[4,2,512,128]{3,2,1,0:T(8,128)(2,1)} %bitcast.46), channel_id=1, source_target_pairs={{0,32},{8,40},{16,48},{24,56},{32,64},{40,72},{48,80},{56,88},{64,... | collective-permute-start | bytes 3145736 | tf_op jit(solution)/shard_map/ppermute | solution.py:35
  78.4 25.1 %collective-permute-start.11 = (bf16[4,2,512,128]{3,2,1,0:T(8,128)(2,1)}, bf16[4,2,512,128]{3,2,1,0:T(8,128)(2,1)S(1)}, u32[]{:S(2)}, u32[]{:S(2)}) collective-permute-start(bf16[4,2,512,128]{3,2,1,0:T(8,128)(2,1)} %bitcast.47), channel_id=1, source_target_pairs={{0,96},{8,104},{16,112},{24,120},{32,0},{40,8},{48,16},{56,24},{64... | collective-permute-start | bytes 3145736 | tf_op jit(solution)/shard_map/ppermute | solution.py:35
  81.2 23.7 %copy-start = (bf16[8,512,128]{2,1,0:T(8,128)(2,1)S(1)}, bf16[8,512,128]{2,1,0:T(8,128)(2,1)}, u32[]{:S(2)}) copy-start(bf16[8,512,128]{2,1,0:T(8,128)(2,1)} %shard_map.110) | copy-start | bytes 3145732
  103.5 27.7 %copy-start.1 = (bf16[4,2,512,128]{3,2,1,0:T(8,128)(2,1)}, bf16[4,2,512,128]{3,2,1,0:T(8,128)(2,1)S(1)}, u32[]{:S(2)}) copy-start(bf16[4,2,512,128]{3,2,1,0:T(8,128)(2,1)S(1)} %collective-permute-done.10.own_refs_3_) | copy-start | bytes 3145732
  103.5 14.2 %copy-start.2 = (bf16[4,2,512,128]{3,2,1,0:T(8,128)(2,1)}, bf16[4,2,512,128]{3,2,1,0:T(8,128)(2,1)S(1)}, u32[]{:S(2)}) copy-start(bf16[4,2,512,128]{3,2,1,0:T(8,128)(2,1)S(1)} %collective-permute-done.11.own_refs_1_) | copy-start | bytes 3145732
  103.5 9.5 %collective-permute-start.12 = (bf16[8,512,128]{2,1,0:T(8,128)(2,1)}, bf16[8,512,128]{2,1,0:T(8,128)(2,1)S(1)}, u32[]{:S(2)}, u32[]{:S(2)}) collective-permute-start(bf16[8,512,128]{2,1,0:T(8,128)(2,1)} %get-tuple-element.21), channel_id=1, source_target_pairs={{0,8},{8,0},{16,24},{24,16},{32,40},{40,32},{48,56},{56,48},{64,72... | collective-permute-start | bytes 3145736 | tf_op jit(solution)/shard_map/ppermute | solution.py:39
  104.9 26.2 %collective-permute-start.17 = (bf16[4,2,512,128]{3,2,1,0:T(8,128)(2,1)S(1)}, bf16[4,2,512,128]{3,2,1,0:T(8,128)(2,1)S(1)}, u32[]{:S(2)}, u32[]{:S(2)}) collective-permute-start(bf16[4,2,512,128]{3,2,1,0:T(8,128)(2,1)S(1)} %bitcast.50), channel_id=1, source_target_pairs={{0,64},{8,72},{16,80},{24,88},{32,96},{40,104},{48,112},{56,120},{... | collective-permute-start | bytes 3145736 | tf_op jit(solution)/shard_map/ppermute | solution.py:35
  107.5 24.5 %collective-permute-start.18 = (bf16[4,2,512,128]{3,2,1,0:T(8,128)(2,1)S(1)}, bf16[4,2,512,128]{3,2,1,0:T(8,128)(2,1)S(1)}, u32[]{:S(2)}, u32[]{:S(2)}) collective-permute-start(bf16[4,2,512,128]{3,2,1,0:T(8,128)(2,1)S(1)} %bitcast.51), channel_id=1, source_target_pairs={{0,8},{8,0},{16,24},{24,16},{32,40},{40,32},{48,56},{56,48},{64,72... | collective-permute-start | bytes 3145736 | tf_op jit(solution)/shard_map/ppermute | solution.py:39
  107.9 24.3 %collective-permute-start.23 = (bf16[512,512]{1,0:T(8,128)(2,1)}, bf16[512,512]{1,0:T(8,128)(2,1)}, u32[]{:S(2)}, u32[]{:S(2)}) collective-permute-start(bf16[512,512]{1,0:T(8,128)(2,1)} %get-tuple-element.24.grad_refs_0_), channel_id=1, source_target_pairs={{0,2},{1,3},{2,4},{3,5},{4,6},{5,7},{6,0},{7,1},{8,10},{9,11},{10,... | collective-permute-start | bytes 1572872 | tf_op jit(solution)/shard_map/ppermute | solution.py:27
  113.0 34.0 %copy-start.10 = (bf16[512,512]{1,0:T(8,128)(2,1)S(1)}, bf16[512,512]{1,0:T(8,128)(2,1)}, u32[]{:S(2)}) copy-start(bf16[512,512]{1,0:T(8,128)(2,1)} %get-tuple-element.24.grad_refs_0_) | copy-start | bytes 1572868
  114.6 23.7 %collective-permute-start.13 = (bf16[2,512,128]{2,1,0:T(8,128)(2,1)S(1)}, bf16[2,512,128]{2,1,0:T(8,128)(2,1)S(1)}, u32[]{:S(2)}, u32[]{:S(2)}) collective-permute-start(bf16[2,512,128]{2,1,0:T(8,128)(2,1)S(1)} %get-tuple-element.48), channel_id=1, source_target_pairs={{0,6},{1,7},{2,0},{3,1},{4,2},{5,3},{6,4},{7,5},{8,14},{9,15},{10,... | collective-permute-start | bytes 786440 | tf_op jit(solution)/shard_map/ppermute | solution.py:27
  117.7 56.6 %collective-permute-start.19 = (bf16[4,2,512,128]{3,2,1,0:T(8,128)(2,1)S(1)}, bf16[4,2,512,128]{3,2,1,0:T(8,128)(2,1)S(1)}, u32[]{:S(2)}, u32[]{:S(2)}) collective-permute-start(bf16[4,2,512,128]{3,2,1,0:T(8,128)(2,1)S(1)} %collective-permute-done.11.own_refs_1_), channel_id=1, source_target_pairs={{0,8},{8,0},{16,24},{24,16},{32,40},{40,32},{48,56},{56,48},{64,72... | collective-permute-start | bytes 3145736 | tf_op jit(solution)/shard_map/ppermute | solution.py:39
  131.2 43.9 %copy-start.3 = (bf16[4,2,512,128]{3,2,1,0:T(8,128)(2,1)}, bf16[4,2,512,128]{3,2,1,0:T(8,128)(2,1)S(1)}, u32[]{:S(2)}) copy-start(bf16[4,2,512,128]{3,2,1,0:T(8,128)(2,1)S(1)} %collective-permute-done.17.own_refs_2_) | copy-start | bytes 3145732
  131.2 43.9 %collective-permute-start.21 = (bf16[4,2,512,128]{3,2,1,0:T(8,128)(2,1)S(1)}, bf16[4,2,512,128]{3,2,1,0:T(8,128)(2,1)S(1)}, u32[]{:S(2)}, u32[]{:S(2)}) collective-permute-start(bf16[4,2,512,128]{3,2,1,0:T(8,128)(2,1)S(1)} %collective-permute-done.10.own_refs_3_), channel_id=1, source_target_pairs={{0,8},{8,0},{16,24},{24,16},{32,40},{40,32},{48,56},{56,48},{64,72... | collective-permute-start | bytes 3145736 | tf_op jit(solution)/shard_map/ppermute | solution.py:39
  132.0 45.9 %copy-start.4 = (bf16[4,2,512,128]{3,2,1,0:T(8,128)(2,1)}, bf16[4,2,512,128]{3,2,1,0:T(8,128)(2,1)S(1)}, u32[]{:S(2)}) copy-start(bf16[4,2,512,128]{3,2,1,0:T(8,128)(2,1)S(1)} %collective-permute-done.18.other_refs_0_) | copy-start | bytes 3145732
  132.0 45.9 %collective-permute-start.20 = (bf16[4,2,512,128]{3,2,1,0:T(8,128)(2,1)S(1)}, bf16[4,2,512,128]{3,2,1,0:T(8,128)(2,1)S(1)}, u32[]{:S(2)}, u32[]{:S(2)}) collective-permute-start(bf16[4,2,512,128]{3,2,1,0:T(8,128)(2,1)S(1)} %collective-permute-done.17.own_refs_2_), channel_id=1, source_target_pairs={{0,8},{8,0},{16,24},{24,16},{32,40},{40,32},{48,56},{56,48},{64,72... | collective-permute-start | bytes 3145736 | tf_op jit(solution)/shard_map/ppermute | solution.py:39
  132.1 14.9 %collective-permute-start.14 = (bf16[2,512,128]{2,1,0:T(8,128)(2,1)S(1)}, bf16[2,512,128]{2,1,0:T(8,128)(2,1)S(1)}, u32[]{:S(2)}, u32[]{:S(2)}) collective-permute-start(bf16[2,512,128]{2,1,0:T(8,128)(2,1)S(1)} %get-tuple-element.49), channel_id=1, source_target_pairs={{0,2},{1,3},{2,4},{3,5},{4,6},{5,7},{6,0},{7,1},{8,10},{9,11},{10,... | collective-permute-start | bytes 786440 | tf_op jit(solution)/shard_map/ppermute | solution.py:27
  138.3 15.2 %collective-permute-start.15 = (bf16[2,512,128]{2,1,0:T(8,128)(2,1)S(1)}, bf16[2,512,128]{2,1,0:T(8,128)(2,1)S(1)}, u32[]{:S(2)}, u32[]{:S(2)}) collective-permute-start(bf16[2,512,128]{2,1,0:T(8,128)(2,1)S(1)} %get-tuple-element.50), channel_id=1, source_target_pairs={{0,4},{1,5},{2,6},{3,7},{4,0},{5,1},{6,2},{7,3},{8,12},{9,13},{10,... | collective-permute-start | bytes 786440 | tf_op jit(solution)/shard_map/ppermute | solution.py:27
  147.0 17.8 %collective-permute-start.25 = (bf16[512,512]{1,0:T(8,128)(2,1)S(1)}, bf16[512,512]{1,0:T(8,128)(2,1)}, u32[]{:S(2)}, u32[]{:S(2)}) collective-permute-start(bf16[512,512]{1,0:T(8,128)(2,1)S(1)} %copy-done.10), channel_id=1, source_target_pairs={{0,4},{1,5},{2,6},{3,7},{4,0},{5,1},{6,2},{7,3},{8,12},{9,13},{10,... | collective-permute-start | bytes 1572872 | tf_op jit(solution)/shard_map/ppermute | solution.py:27
  153.5 17.8 %collective-permute-start.27 = (bf16[512,512]{1,0:T(8,128)(2,1)S(1)}, bf16[512,512]{1,0:T(8,128)(2,1)}, u32[]{:S(2)}, u32[]{:S(2)}) collective-permute-start(bf16[512,512]{1,0:T(8,128)(2,1)S(1)} %copy-done.10), channel_id=1, source_target_pairs={{0,6},{1,7},{2,0},{3,1},{4,2},{5,3},{6,4},{7,5},{8,14},{9,15},{10,... | collective-permute-start | bytes 1572872 | tf_op jit(solution)/shard_map/ppermute | solution.py:27
  164.8 30.7 %collective-permute-start.22 = (bf16[512,512]{1,0:T(8,128)(2,1)S(1)}, bf16[512,512]{1,0:T(8,128)(2,1)}, u32[]{:S(2)}, u32[]{:S(2)}) collective-permute-start(bf16[512,512]{1,0:T(8,128)(2,1)S(1)} %copy-done.10), channel_id=1, source_target_pairs={{0,1},{1,0},{2,3},{3,2},{4,5},{5,4},{6,7},{7,6},{8,9},{9,8},{10,11... | collective-permute-start | bytes 1572872 | tf_op jit(solution)/shard_map/ppermute | solution.py:31
  171.3 25.2 %collective-permute-start.24 = (bf16[512,512]{1,0:T(8,128)(2,1)}, bf16[512,512]{1,0:T(8,128)(2,1)}, u32[]{:S(2)}, u32[]{:S(2)}) collective-permute-start(bf16[512,512]{1,0:T(8,128)(2,1)} %collective-permute-done.23.grad_refs_1_), channel_id=1, source_target_pairs={{0,1},{1,0},{2,3},{3,2},{4,5},{5,4},{6,7},{7,6},{8,9},{9,8},{10,11... | collective-permute-start | bytes 1572872 | tf_op jit(solution)/shard_map/ppermute | solution.py:31
  174.3 3.7 %copy-start.5 = (bf16[4,2,512,128]{3,2,1,0:T(8,128)(2,1)}, bf16[4,2,512,128]{3,2,1,0:T(8,128)(2,1)S(1)}, u32[]{:S(2)}) copy-start(bf16[4,2,512,128]{3,2,1,0:T(8,128)(2,1)S(1)} %collective-permute-done.19.other_refs_1_) | copy-start | bytes 3145732
  174.3 21.1 %collective-permute-start.16 = (bf16[2,512,128]{2,1,0:T(8,128)(2,1)S(1)}, bf16[2,512,128]{2,1,0:T(8,128)(2,1)S(1)}, u32[]{:S(2)}, u32[]{:S(2)}) collective-permute-start(bf16[2,512,128]{2,1,0:T(8,128)(2,1)S(1)} %fusion.2), channel_id=1, source_target_pairs={{0,1},{1,0},{2,3},{3,2},{4,5},{5,4},{6,7},{7,6},{8,9},{9,8},{10,11... | collective-permute-start | bytes 786440 | tf_op jit(solution)/shard_map/ppermute | solution.py:31
  175.1 2.9 %copy-start.6 = (bf16[4,2,512,128]{3,2,1,0:T(8,128)(2,1)}, bf16[4,2,512,128]{3,2,1,0:T(8,128)(2,1)S(1)}, u32[]{:S(2)}) copy-start(bf16[4,2,512,128]{3,2,1,0:T(8,128)(2,1)S(1)} %collective-permute-done.21.other_refs_3_) | copy-start | bytes 3145732
  175.1 31.5 %collective-permute-start.26 = (bf16[512,512]{1,0:T(8,128)(2,1)}, bf16[512,512]{1,0:T(8,128)(2,1)S(1)}, u32[]{:S(2)}, u32[]{:S(2)}) collective-permute-start(bf16[512,512]{1,0:T(8,128)(2,1)} %collective-permute-done.25.grad_refs_2_), channel_id=1, source_target_pairs={{0,1},{1,0},{2,3},{3,2},{4,5},{5,4},{6,7},{7,6},{8,9},{9,8},{10,11... | collective-permute-start | bytes 1572872 | tf_op jit(solution)/shard_map/ppermute | solution.py:31
  178.0 1.0 copy-start.7
  178.0 40.0 %collective-permute-start.28 = (bf16[512,512]{1,0:T(8,128)(2,1)}, bf16[512,512]{1,0:T(8,128)(2,1)}, u32[]{:S(2)}, u32[]{:S(2)}) collective-permute-start(bf16[512,512]{1,0:T(8,128)(2,1)} %collective-permute-done.27.grad_refs_3_), channel_id=1, source_target_pairs={{0,1},{1,0},{2,3},{3,2},{4,5},{5,4},{6,7},{7,6},{8,9},{9,8},{10,11... | collective-permute-start | bytes 1572872 | tf_op jit(solution)/shard_map/ppermute | solution.py:31
  195.5 22.5 %copy-start.8 = (bf16[2,512,128]{2,1,0:T(8,128)(2,1)}, bf16[2,512,128]{2,1,0:T(8,128)(2,1)S(1)}, u32[]{:S(2)}) copy-start(bf16[2,512,128]{2,1,0:T(8,128)(2,1)S(1)} %add_convert_fusion.1.rest_1__0_) | copy-start | bytes 786436
  195.5 22.5 %collective-permute-start.29 = (bf16[2,512,128]{2,1,0:T(8,128)(2,1)S(1)}, bf16[2,512,128]{2,1,0:T(8,128)(2,1)S(1)}, u32[]{:S(2)}, u32[]{:S(2)}) collective-permute-start(bf16[2,512,128]{2,1,0:T(8,128)(2,1)S(1)} %add_convert_fusion.1.rest_1__0_), channel_id=1, source_target_pairs={{0,2},{1,3},{2,4},{3,5},{4,6},{5,7},{6,0},{7,1},{8,10},{9,11},{10,... | collective-permute-start | bytes 786440 | tf_op jit(solution)/shard_map/ppermute | solution.py:27
  195.6 22.4 %collective-permute-start.30 = (bf16[2,512,128]{2,1,0:T(8,128)(2,1)S(1)}, bf16[2,512,128]{2,1,0:T(8,128)(2,1)S(1)}, u32[]{:S(2)}, u32[]{:S(2)}) collective-permute-start(bf16[2,512,128]{2,1,0:T(8,128)(2,1)S(1)} %add_convert_fusion.1.rest_1__0_), channel_id=1, source_target_pairs={{0,4},{1,5},{2,6},{3,7},{4,0},{5,1},{6,2},{7,3},{8,12},{9,13},{10,... | collective-permute-start | bytes 786440 | tf_op jit(solution)/shard_map/ppermute | solution.py:27
  196.6 21.4 %collective-permute-start.31 = (bf16[2,512,128]{2,1,0:T(8,128)(2,1)S(1)}, bf16[2,512,128]{2,1,0:T(8,128)(2,1)S(1)}, u32[]{:S(2)}, u32[]{:S(2)}) collective-permute-start(bf16[2,512,128]{2,1,0:T(8,128)(2,1)S(1)} %add_convert_fusion.1.rest_1__0_), channel_id=1, source_target_pairs={{0,6},{1,7},{2,0},{3,1},{4,2},{5,3},{6,4},{7,5},{8,14},{9,15},{10,... | collective-permute-start | bytes 786440 | tf_op jit(solution)/shard_map/ppermute | solution.py:27
  206.6 11.4 %copy-start.11 = (bf16[512,512]{1,0:T(8,128)(2,1)}, bf16[512,512]{1,0:T(8,128)(2,1)S(1)}, u32[]{:S(2)}) copy-start(bf16[512,512]{1,0:T(8,128)(2,1)S(1)} %collective-permute-done.26.grad_refs_2_) | copy-start | bytes 1572868
  217.9 0.8 copy-start.13
  218.7 0.7 copy-start.14
  (2 other events, 1.4 us)

commit v4 on v2

--- a/solution.py
+++ b/solution.py
@@ -164,7 +164,11 @@
     pairs = heads * 2 * RUN * count // 2
     return pl.pallas_call(
         functools.partial(attention_kernel, heads),
-        out_shape=(jax.ShapeDtypeStruct(queries.shape, jnp.bfloat16), shared, shared),
+        out_shape=(
+            jax.ShapeDtypeStruct(queries.shape, jnp.bfloat16),
+            shared,
+            shared,
+        ),
         in_specs=[smem, vmem, vmem, [vmem] * len(mine), [vmem] * len(other)],
         out_specs=(vmem, vmem, vmem),
         scratch_shapes=[
@@ -186,6 +190,151 @@
     )(info, queries, grad_output, mine, other)
 
 
+def turn_kernel(in_refs, out_ref):
+    for dy, ref in enumerate(in_refs):
+        for dx in range(2):
+            tokens = ref.shape[1]
+            at = (dx * len(in_refs) + dy) * tokens
+            out_ref[:, at : at + tokens] = ref[dx].T
+
+
+def turn(pieces):
+    vmem = pl.BlockSpec(memory_space=pltpu.VMEM)
+    sides, tokens, lanes = pieces[0].shape
+    return pl.pallas_call(
+        turn_kernel,
+        out_shape=jax.ShapeDtypeStruct((lanes, len(pieces) * sides * tokens), jnp.bfloat16),
+        in_specs=[[vmem] * len(pieces)],
+        out_specs=vmem,
+        compiler_params=pltpu.CompilerParams(vmem_limit_bytes=VMEM_BYTES),
+        cost_estimate=pl.CostEstimate(flops=0, bytes_accessed=2 * 1024 * 1024, transcendentals=0),
+    )(list(pieces))
+
+
+def weight_kernel(last, place_ref, own_refs, other_refs, grad_refs, *rest):
+    if last:
+        (sum_ref, shared_refs, wq_ref, wk_ref, wv_ref, k_ref, v_ref,
+         inputs, grads, sums, shared, in_sems, grad_sems, sum_sems, shared_sems, out_sems) = rest
+    else:
+        wq_ref, inputs, grads, sums, in_sems, grad_sems, out_sems = rest
+    core, z = place_ref[0], place_ref[1]
+    tall, across = own_refs[0].shape
+    tokens = grad_refs[0].shape[0]
+    side = across // 2
+    sides = (1, 0) if last else (0,)
+    grad_copies = [
+        pltpu.make_async_copy(ref, grads.at[pl.ds(dy * tokens, tokens)], grad_sems.at[dy])
+        for dy, ref in enumerate(grad_refs)
+    ]
+    for copy in grad_copies:
+        copy.start()
+    row, in_copies, sum_copies = [], {}, []
+    for away in range(4):
+        row.append(pl.multiple_of(lax.rem(z + away, 4) * 2 * tall, 2 * tall))
+    if last:
+        shared_copies = [
+            pltpu.make_async_copy(
+                shared_refs[dy].at[dx],
+                shared.at[pl.ds((dx * 4 + dy) * tokens, tokens)],
+                shared_sems.at[dx, dy],
+            )
+            for dx in range(2)
+            for dy in range(4)
+        ]
+    for away in range(4):
+        for n, dx in enumerate(sides):
+            for which, ref in enumerate((own_refs[away], other_refs[away])):
+                at = pl.multiple_of((core if which == 0 else 1 - core) * tall, tall)
+                in_copies[away, n, which] = pltpu.make_async_copy(
+                    ref.at[:, pl.ds(dx * side, side)],
+                    inputs.at[away, n, pl.ds(at, tall)],
+                    in_sems.at[away, n, which],
+                )
+                in_copies[away, n, which].start()
+        if last:
+            sum_copies.append(
+                pltpu.make_async_copy(
+                    sum_ref.at[pl.ds(row[away], 2 * tall)], sums.at[away], sum_sems.at[away]
+                )
+            )
+            sum_copies[away].start()
+            if away == 0:
+                for copy in shared_copies:
+                    copy.start()
+    for copy in grad_copies:
+        copy.wait()
+    norm = 1.0 / math.sqrt(8 * tokens)
+    out_copies = []
+    for away in range(4):
+        for which in range(2):
+            in_copies[away, 0, which].wait()
+        total = contract(inputs[away, 0], grads[...], 1, 0)
+        if last:
+            sum_copies[away].wait()
+            total = (total + sums[away]) * norm
+        sums[away] = total
+        out_copies.append(
+            pltpu.make_async_copy(
+                sums.at[away], wq_ref.at[pl.ds(row[away], 2 * tall)], out_sems.at[away]
+            )
+        )
+        out_copies[away].start()
+        if last:
+            if away == 0:
+                for copy in shared_copies:
+                    copy.wait()
+            for which in range(2):
+                in_copies[away, 1, which].wait()
+            part = contract(inputs[away, 0], shared[side:], 1, 0)
+            part += contract(inputs[away, 1], shared[:side], 1, 0)
+            part = (part * norm).T
+            half = part.shape[0] // 2
+            wk_ref[:, pl.ds(row[away], 2 * tall)] = part[:half]
+            wv_ref[:, pl.ds(row[away], 2 * tall)] = part[half:]
+    if last:
+        here = shared[:tokens].T
+        k_ref[...] = here[: here.shape[0] // 2]
+        v_ref[...] = here[here.shape[0] // 2 :]
+    for copy in out_copies:
+        copy.wait()
+
+
+def weights(place, own, other, grads, total=None, shared=None):
+    last = total is not None
+    smem = pl.BlockSpec(memory_space=pltpu.SMEM)
+    vmem = pl.BlockSpec(memory_space=pltpu.VMEM)
+    hbm = pl.BlockSpec(memory_space=pl.ANY)
+    tall, across = own[0].shape
+    tokens, cols = grads[0].shape
+    f32, bf16, sem = jnp.float32, jnp.bfloat16, pltpu.SemaphoreType.DMA
+    wq = jax.ShapeDtypeStruct((8 * tall, cols), f32)
+    narrow = jax.ShapeDtypeStruct((tall // 2, 8 * tall), f32)
+    narrow_in = jax.ShapeDtypeStruct((tall // 2, tokens), bf16)
+    sides = 2 if last else 1
+    scratch = [
+        pltpu.VMEM((4, sides, 2 * tall, across // 2), bf16),
+        pltpu.VMEM((4 * tokens, cols), bf16),
+        pltpu.VMEM((4, 2 * tall, cols), f32),
+    ]
+    if last:
+        scratch += [pltpu.VMEM((across, tall), bf16)]
+    scratch += [sem((4, sides, 2)), sem((4,))]
+    if last:
+        scratch += [sem((4,)), sem((2, 4))]
+    scratch += [sem((4,))]
+    return pl.pallas_call(
+        functools.partial(weight_kernel, last),
+        out_shape=(wq, narrow, narrow, narrow_in, narrow_in) if last else wq,
+        in_specs=[smem, [hbm] * 4, [hbm] * 4, [hbm] * 4] + ([hbm, [hbm] * 4] if last else []),
+        out_specs=(hbm, vmem, vmem, vmem, vmem) if last else hbm,
+        scratch_shapes=scratch,
+        compiler_params=pltpu.CompilerParams(vmem_limit_bytes=VMEM_BYTES),
+        cost_estimate=pl.CostEstimate(
+            flops=8 * tokens * cols * 8 * tall, bytes_accessed=10 * 1024 * 1024, transcendentals=0
+        ),
+    )(place, list(own), list(other), list(grads), *((total, list(shared)) if last else ()))
+
+
 def local(layer_input, queries, key_vectors, value_vectors, grad_output, positions):
     group = lax.axis_index("dp")
     member, head, z = group % 2, group // 2, group // 4
@@ -195,6 +344,7 @@
     width = layer_input.shape[1] // 8
     slab = width // 8
     first = member == 0
+    place = jnp.stack([member, z]).astype(jnp.int32)
 
     key_local = lax.dynamic_slice_in_dim(key_vectors, head * HD, HD, 1)
     value_local = lax.dynamic_slice_in_dim(value_vectors, head * HD, HD, 1)
@@ -213,7 +363,6 @@
     column_other = swap_cores(column)
     pairs = [jnp.stack([block(dy, 0), from_x[dy]]) for dy in range(4)]
     pairs = [pairs[0]] + [along_y(pairs[dy], dy) for dy in range(1, 4)]
-    slab_own = jnp.concatenate([p[dx] for dx in range(2) for p in pairs], axis=0)
     partner_other = swap_cores(partner_column)
     info = jnp.concatenate(
         [
@@ -222,53 +371,45 @@
             member.astype(jnp.int32)[None],
         ]
     )
+    slab_own = turn(pairs)
     slab_back, slab_ahead = along_z(slab_own, 1), along_z(slab_own, 3)
+    slab_far = along_z(slab_own, 2)
+    own_other = swap_cores(slab_own)
 
     grad_query, keep, give = attention(
         info, queries, grad_output, [column, partner_column], [column_other, partner_other]
     )
-
-    cut = slab_own.shape[0] // 2
-    slab_far = jnp.concatenate([along_z(slab_back[:cut], 1), along_z(slab_ahead[cut:], 3)])
-    slabs = jnp.zeros((4, 2) + slab_own.shape, jnp.bfloat16)
-    for away, value in ((0, slab_own), (3, slab_back), (1, slab_ahead), (2, slab_far)):
-        other = swap_cores(value)
-        slabs = lax.dynamic_update_slice(slabs, value[None, None], ((z + away) % 4, member, 0, 0))
-        slabs = lax.dynamic_update_slice(slabs, other[None, None], ((z + away) % 4, 1 - member, 0, 0))
-    slabs = slabs.reshape((8,) + slab_own.shape)
-
-    summed = (keep.astype(jnp.float32) + swap_cores(give).astype(jnp.float32)).astype(jnp.bfloat16)
+    grad_query, keep, give, slab_back, slab_ahead, own_other = lax.optimization_barrier(
+        (grad_query, keep, give, slab_back, slab_ahead, own_other)
+    )
+
+    give = swap_cores(give)
+    back_other, ahead_other = swap_cores(slab_back), swap_cores(slab_ahead)
+    summed = (keep.astype(jnp.float32) + give.astype(jnp.float32)).astype(jnp.bfloat16)
     summed = summed.reshape(2, 4, count, HD)
+    from_partner = swap_x(grad_query)
+    from_1, from_3 = along_y(grad_query, 1), along_y(grad_query, 3)
     rows_y = summed[:, 0].astype(jnp.float32)
     for dy in (1, 3, 2):
         rows_y = rows_y + along_y(summed[:, dy], -dy).astype(jnp.float32)
-    total = rows_y[0] + swap_x(rows_y[1].astype(jnp.bfloat16)).astype(jnp.float32)
-    total = total.astype(jnp.bfloat16)
-    both = jnp.stack([total, swap_x(total)])
-    shared = jnp.stack([both] + by_source(*to_all_y(both)), axis=1)
-    shared = shared.reshape(8 * count, HD)
-
-    mark = count * 3 // 4
-    part_a, part_b = grad_query[:mark], grad_query[mark:]
-    column_a = jnp.stack([part_a] + by_source(*to_all_y(part_a)))
-    all_a = jnp.concatenate([column_a, swap_x(column_a)])
-    both_b = jnp.stack([part_b, swap_x(part_b)])
-    all_b = jnp.stack([both_b] + by_source(*to_all_y(both_b)), axis=1)
-    all_b = all_b.reshape((8,) + part_b.shape)
-    queries_all = jnp.concatenate([all_a, all_b], axis=1).reshape(8 * count, -1)
-
-    norm = 1.0 / math.sqrt(8 * count)
-    grad_wq = contract(slabs, queries_all, 1, 0).reshape(width, -1) * norm
-    grad_wkv = contract(slabs, shared, 1, 0).reshape(width, -1) * norm
-    share = HD // 2
-    return (
-        grad_query,
-        total[:, :share],
-        total[:, share:],
-        grad_wq,
-        grad_wkv[:, :share],
-        grad_wkv[:, share:],
-    )
+    rows_y = rows_y.astype(jnp.bfloat16)
+    rows_y, from_partner, from_1, from_3, slab_far, back_other, ahead_other = lax.optimization_barrier(
+        (rows_y, from_partner, from_1, from_3, slab_far, back_other, ahead_other)
+    )
+    both = (rows_y.astype(jnp.float32) + swap_x(rows_y).astype(jnp.float32)[::-1]).astype(jnp.bfloat16)
+    far_other = swap_cores(slab_far)
+    from_2 = along_y(grad_query, 2)
+    other_1, other_3 = swap_x(from_1), swap_x(from_3)
+    other_2 = along_y(from_partner, 2)
+    shared = [both] + by_source(*to_all_y(both))
+
+    slabs = [slab_own, slab_ahead, slab_far, slab_back]
+    slabs_other = [own_other, ahead_other, far_other, back_other]
+    partial = weights(place, slabs, slabs_other, [grad_query, from_1, from_2, from_3])
+    grad_wq, grad_wk, grad_wv, grad_key, grad_value = weights(
+        place, slabs, slabs_other, [from_partner, other_1, other_2, other_3], partial, shared
+    )
+    return grad_query, grad_key.T, grad_value.T, grad_wq, grad_wk.T, grad_wv.T
 
 
 def solution(mesh):

time: 218 us -> 188 us (0.86); the launches traced: 214 us -> 191 us
  local copies, waits for them, and re-layouts: 40.4 us -> 4.1 us
  waiting for transfers between devices: 52.3 us -> 77.1 us
  Pallas kernels: 19 us -> 41.8 us
  starting transfers between devices: 76.4 us -> 61.1 us
  matrix products: 12.2 us -> 0 us
  other arithmetic: 12.8 us -> 5.86 us
    ppermute x4 -> x3, waiting for transfers between devices: 1.08 us -> 24.8 us  [along_z(): lax.ppermute(value, 'dp', [(i, (i + 4 * step) % 16) for i in range(16)])]
    pallas_call x0 -> x3, Pallas kernels: none -> 22.8 us  [the longest x2 20.3 us: weights(): pl.pallas_call(functools.partial(weight_kernel, last), out_shape=(wq, nar...]
    dot_general x2 -> x0, matrix products: 12.2 us -> none  [contract(): lax.dot_general(left, right, (((left_dim,), (right_dim,)), ((), ())), pre...]
    broadcast_in_dim x9 -> x0, local copies, waits for them, and re-layouts: 11 us -> none  [the longest x4 4.97 us: local(): value[None, None]]
    ppermute x6, waiting for transfers between devices: 25.1 us -> 14.3 us  [swap_x(): return lax.ppermute(value, 'ctx', [(i, i ^ 1) for i in range(8)])]
    ppermute x18 -> x16, waiting for transfers between devices: 26.1 us -> 36.1 us  [along_y(): lax.ppermute(value, 'ctx', [(i, (i + 2 * step) % 8) for i in range(8)])]
    dynamic_update_slice x8 -> x0, local copies, waits for them, and re-layouts: 7.54 us -> none  [the longest x4 4.22 us: local(): lax.dynamic_update_slice(slabs, other[None, None], ((z + away) % 4, 1 - m...]
    unnamed x33 -> x38, local copies, waits for them, and re-layouts: 9.05 us -> 1.67 us
  transfers between devices with their start and end apart: 35 -> 32, of which waited for: 13 -> 15; matrix products, arithmetic and copies ran while one was open for 21% -> 4% of each run, Pallas kernels for 9% -> 15%
where the time goes in v4:
time: 188 us; the launch traced here: 191 us
  waiting for transfers between devices  77.1 us (41%)
  starting transfers between devices  61.1 us (32%)
  Pallas kernels  41.8 us (22%)
  other arithmetic  5.86 us (3%)
  local copies, waits for them, and re-layouts  4.1 us (2%)
    ppermute x16, starting transfers between devices, along_y(): lax.ppermute(value, 'ctx', [(i, (i + 2 * step) % 8) for i in range(8)])  40.3 us
    ppermute x16, waiting for transfers between devices, along_y(): lax.ppermute(value, 'ctx', [(i, (i + 2 * step) % 8) for i in range(8)])  36.1 us
    ppermute x3, waiting for transfers between devices, along_z(): lax.ppermute(value, 'dp', [(i, (i + 4 * step) % 16) for i in range(16)])  24.8 us
    pallas_call x2, Pallas kernels, weights(): pl.pallas_call(functools.partial(weight_kernel, last), out_shape=(wq, nar...  20.3 us
    pallas_call x1, Pallas kernels, attention(): pl.pallas_call(functools.partial(attention_kernel, heads), out_shape=(jax...  19.1 us
    ppermute x6, waiting for transfers between devices, swap_x(): return lax.ppermute(value, 'ctx', [(i, i ^ 1) for i in range(8)])  14.3 us
    ppermute x7, starting transfers between devices, swap_cores(): return lax.ppermute(value, 'dp', [(i, i ^ 1) for i in range(16)])  10.2 us
    ppermute x6, starting transfers between devices, swap_x(): return lax.ppermute(value, 'ctx', [(i, i ^ 1) for i in range(8)])  6.83 us
  transfers between devices with their start and end apart: 32, of which 15 were waited for; matrix products, arithmetic and copies ran while one was open for 4% of the time, Pallas kernels for 15%

profile of v4, /device:TPU:1, one launch (start us, length us, event | category | flops | bytes accessed | tf_op | source)
XLA Modules:
  0.0 191.3 jit_solution(7892822132626334853)
XLA Ops:
  0.8 1.4 dynamic-slice_bitcast_fusion
  2.3 3.7 %collective-permute-start.6 = (bf16[4,512,128]{2,1,0:T(8,128)(2,1)S(1)}, bf16[4,512,128]{2,1,0:T(8,128)(2,1)S(1)}, u32[]{:S(2)}, u32[]{:S(2)}) collective-permute-start(bf16[4,512,128]{2,1,0:T(8,128)(2,1)S(1)} %pad_maximum_fusion.1), channel_id=1, source_target_pairs={{0,1},{1,0},{2,3},{3,2},{4,5},{5,4},{6,7},{7,6},{8,9},{9,8},{10,11... | collective-permute-start | bytes 1572872 | tf_op jit(solution)/shard_map/ppermute | solution.py:31
  5.9 0.8 slice.33
  6.7 1.0 dynamic-slice_select_fusion
  7.8 3.0 %collective-permute-start.1 = (bf16[528,128]{1,0:T(8,128)(2,1)S(1)}, bf16[528,128]{1,0:T(8,128)(2,1)S(1)}, u32[]{:S(2)}, u32[]{:S(2)}) collective-permute-start(bf16[528,128]{1,0:T(8,128)(2,1)S(1)} %get-tuple-element.64), channel_id=1, source_target_pairs={{0,4},{1,5},{2,6},{3,7},{4,0},{5,1},{6,2},{7,3},{8,12},{9,13},{10,... | collective-permute-start | bytes 405512 | tf_op jit(solution)/shard_map/ppermute | solution.py:27
  10.8 0.4 collective-permute-start
  11.2 2.3 %collective-permute-start.2 = (bf16[528,128]{1,0:T(8,128)(2,1)S(1)}, bf16[528,128]{1,0:T(8,128)(2,1)S(1)}, u32[]{:S(2)}, u32[]{:S(2)}) collective-permute-start(bf16[528,128]{1,0:T(8,128)(2,1)S(1)} %get-tuple-element.64), channel_id=1, source_target_pairs={{0,6},{1,7},{2,0},{3,1},{4,2},{5,3},{6,4},{7,5},{8,14},{9,15},{10,... | collective-permute-start | bytes 405512 | tf_op jit(solution)/shard_map/ppermute | solution.py:27
  13.5 3.7 %collective-permute-done = bf16[528,128]{1,0:T(8,128)(2,1)S(1)} collective-permute-done((bf16[528,128]{1,0:T(8,128)(2,1)S(1)}, bf16[528,128]{1,0:T(8,128)(2,1)S(1)}, u32[]{:S(2)}, u32[]{:S(2)}) %collective-permute-start) | collective-permute-done | bytes 135200 | tf_op jit(solution)/shard_map/ppermute | solution.py:27
  17.5 1.8 collective-permute-start.4
  19.4 1.2 collective-permute-start.7
  20.6 3.1 %collective-permute-start.8 = (bf16[2,512,128]{2,1,0:T(8,128)(2,1)S(1)}, bf16[2,512,128]{2,1,0:T(8,128)(2,1)S(1)}, u32[]{:S(2)}, u32[]{:S(2)}) collective-permute-start(bf16[2,512,128]{2,1,0:T(8,128)(2,1)S(1)} %pad_maximum_fusion.4), channel_id=1, source_target_pairs={{0,4},{1,5},{2,6},{3,7},{4,0},{5,1},{6,2},{7,3},{8,12},{9,13},{10,... | collective-permute-start | bytes 786440 | tf_op jit(solution)/shard_map/ppermute | solution.py:27
  23.7 7.6 %collective-permute-done.3.mine_refs_1_ = bf16[4,528,128]{2,1,0:T(8,128)(2,1)} collective-permute-done((bf16[4,528,128]{2,1,0:T(8,128)(2,1)S(1)}, bf16[4,528,128]{2,1,0:T(8,128)(2,1)}, u32[]{:S(2)}, u32[]{:S(2)}) %collective-permute-start.3) | collective-permute-done | bytes 540704 | tf_op jit(solution)/shard_map/ppermute | solution.py:31
  31.3 2.4 %collective-permute-start.5 = (bf16[4,528,128]{2,1,0:T(8,128)(2,1)}, bf16[4,528,128]{2,1,0:T(8,128)(2,1)}, u32[]{:S(2)}, u32[]{:S(2)}) collective-permute-start(bf16[4,528,128]{2,1,0:T(8,128)(2,1)} %collective-permute-done.3.mine_refs_1_), channel_id=1, source_target_pairs={{0,8},{8,0},{16,24},{24,16},{32,40},{40,32},{48,56},{56,48},{64,72... | collective-permute-start | bytes 1622024 | tf_op jit(solution)/shard_map/ppermute | solution.py:39
  33.7 2.9 %collective-permute-start.9 = (bf16[2,512,128]{2,1,0:T(8,128)(2,1)S(1)}, bf16[2,512,128]{2,1,0:T(8,128)(2,1)S(1)}, u32[]{:S(2)}, u32[]{:S(2)}) collective-permute-start(bf16[2,512,128]{2,1,0:T(8,128)(2,1)S(1)} %pad_maximum_fusion.5), channel_id=1, source_target_pairs={{0,6},{1,7},{2,0},{3,1},{4,2},{5,3},{6,4},{7,5},{8,14},{9,15},{10,... | collective-permute-start | bytes 786440 | tf_op jit(solution)/shard_map/ppermute | solution.py:27
  36.7 0.7 pad_maximum_fusion.2.in_refs_0_
  37.4 0.7 fusion.3
  38.2 4.1 %collective-permute-done.9.in_refs_3_ = bf16[2,512,128]{2,1,0:T(8,128)(2,1)S(1)} collective-permute-done((bf16[2,512,128]{2,1,0:T(8,128)(2,1)S(1)}, bf16[2,512,128]{2,1,0:T(8,128)(2,1)S(1)}, u32[]{:S(2)}, u32[]{:S(2)}) %collective-permute-start.9) | collective-permute-done | bytes 262176 | tf_op jit(solution)/shard_map/ppermute | solution.py:27
  42.3 0.7 copy-done.18
  43.0 2.5 %shard_map.110.own_refs_0_ = bf16[128,4096]{1,0:T(8,128)(2,1)} custom-call(bf16[2,512,128]{2,1,0:T(8,128)(2,1)} %pad_maximum_fusion.2.in_refs_0_, bf16[2,512,128]{2,1,0:T(8,128)(2,1)} %copy-done.16, bf16[2,512,128]{2,1,0:T(8,128)(2,1)} %copy-done.17, bf16[2,512,128]{2,1,0:T(8,128)(2,1)} %copy-done.18), custom_call_target="tpu_custom_call" | custom-call | bytes 2097152 | tf_op jit(solution)/shard_map/pallas_call | solution.py:204
  45.5 0.8 collective-permute-start.12
  46.3 3.8 %collective-permute-start.11 = (bf16[128,4096]{1,0:T(8,128)(2,1)}, bf16[128,4096]{1,0:T(8,128)(2,1)S(1)}, u32[]{:S(2)}, u32[]{:S(2)}) collective-permute-start(bf16[128,4096]{1,0:T(8,128)(2,1)} %shard_map.110.own_refs_0_), channel_id=1, source_target_pairs={{0,96},{8,104},{16,112},{24,120},{32,0},{40,8},{48,16},{56,24},{64... | collective-permute-start | bytes 3145736 | tf_op jit(solution)/shard_map/ppermute | solution.py:35
  50.0 0.6 pad_add_fusion.info_ref
  50.6 19.1 %shard_map.109 = (bf16[512,512]{1,0:T(8,128)(2,1)}, bf16[8,512,128]{2,1,0:T(8,128)(2,1)}, bf16[8,512,128]{2,1,0:T(8,128)(2,1)}) custom-call(s32[17]{0:T(128)} %pad_add_fusion.info_ref, bf16[512,512]{1,0:T(8,128)(2,1)} %q_ref.1, bf16[512,512]{1,0:T(8,128)(2,1)} %g_ref.1, bf16[4,528,128]{2,1,0:T(8,128)(2,1)} %copy-done.8, ...), custom_call_target="tpu_custom_call" | custom-call | flops 10737418240 | bytes 8388608 | tf_op jit(solution)/shard_map/pallas_call | solution.py:165
  69.7 3.2 %collective-permute-done.11.own_refs_1_ = bf16[128,4096]{1,0:T(8,128)(2,1)S(1)} collective-permute-done((bf16[128,4096]{1,0:T(8,128)(2,1)}, bf16[128,4096]{1,0:T(8,128)(2,1)S(1)}, u32[]{:S(2)}, u32[]{:S(2)}) %collective-permute-start.11) | collective-permute-done | bytes 1048608 | tf_op jit(solution)/shard_map/ppermute | solution.py:35
  72.9 3.1 %collective-permute-done.10.own_refs_3_ = bf16[128,4096]{1,0:T(8,128)(2,1)} collective-permute-done((bf16[128,4096]{1,0:T(8,128)(2,1)}, bf16[128,4096]{1,0:T(8,128)(2,1)}, u32[]{:S(2)}, u32[]{:S(2)}) %collective-permute-start.10) | collective-permute-done | bytes 1048608 | tf_op jit(solution)/shard_map/ppermute | solution.py:35
  76.0 1.1 collective-permute-start.13
  77.6 2.0 %collective-permute-done.13 = bf16[8,512,128]{2,1,0:T(8,128)(2,1)S(1)} collective-permute-done((bf16[8,512,128]{2,1,0:T(8,128)(2,1)}, bf16[8,512,128]{2,1,0:T(8,128)(2,1)S(1)}, u32[]{:S(2)}, u32[]{:S(2)}) %collective-permute-start.13) | collective-permute-done | bytes 1048608 | tf_op jit(solution)/shard_map/ppermute | solution.py:39
  79.6 1.5 add_convert_fusion
  81.2 3.7 %collective-permute-start.14 = (bf16[2,512,128]{2,1,0:T(8,128)(2,1)S(1)}, bf16[2,512,128]{2,1,0:T(8,128)(2,1)S(1)}, u32[]{:S(2)}, u32[]{:S(2)}) collective-permute-start(bf16[2,512,128]{2,1,0:T(8,128)(2,1)S(1)} %get-tuple-element.56), channel_id=1, source_target_pairs={{0,6},{1,7},{2,0},{3,1},{4,2},{5,3},{6,4},{7,5},{8,14},{9,15},{10,... | collective-permute-start | bytes 786440 | tf_op jit(solution)/shard_map/ppermute | solution.py:27
  84.9 18.5 %collective-permute-done.20.own_refs_2_ = bf16[128,4096]{1,0:T(8,128)(2,1)S(1)} collective-permute-done((bf16[128,4096]{1,0:T(8,128)(2,1)S(1)}, bf16[128,4096]{1,0:T(8,128)(2,1)S(1)}, u32[]{:S(2)}, u32[]{:S(2)}) %collective-permute-start.20) | collective-permute-done | bytes 1048608 | tf_op jit(solution)/shard_map/ppermute | solution.py:35
  103.4 14.0 %collective-permute-start.16 = (bf16[2,512,128]{2,1,0:T(8,128)(2,1)S(1)}, bf16[2,512,128]{2,1,0:T(8,128)(2,1)S(1)}, u32[]{:S(2)}, u32[]{:S(2)}) collective-permute-start(bf16[2,512,128]{2,1,0:T(8,128)(2,1)S(1)} %get-tuple-element.58), channel_id=1, source_target_pairs={{0,4},{1,5},{2,6},{3,7},{4,0},{5,1},{6,2},{7,3},{8,12},{9,13},{10,... | collective-permute-start | bytes 786440 | tf_op jit(solution)/shard_map/ppermute | solution.py:27
  117.4 1.5 collective-permute-start.18
  118.9 4.2 %collective-permute-done.16 = bf16[2,512,128]{2,1,0:T(8,128)(2,1)S(1)} collective-permute-done((bf16[2,512,128]{2,1,0:T(8,128)(2,1)S(1)}, bf16[2,512,128]{2,1,0:T(8,128)(2,1)S(1)}, u32[]{:S(2)}, u32[]{:S(2)}) %collective-permute-start.16) | collective-permute-done | bytes 262176 | tf_op jit(solution)/shard_map/ppermute | solution.py:27
  123.2 6.3 %collective-permute-done.19.grad_refs_3_ = bf16[512,512]{1,0:T(8,128)(2,1)S(1)} collective-permute-done((bf16[512,512]{1,0:T(8,128)(2,1)S(1)}, bf16[512,512]{1,0:T(8,128)(2,1)S(1)}, u32[]{:S(2)}, u32[]{:S(2)}) %collective-permute-start.19) | collective-permute-done | bytes 524320 | tf_op jit(solution)/shard_map/ppermute | solution.py:27
  129.5 6.0 %collective-permute-done.18.grad_refs_1_ = bf16[512,512]{1,0:T(8,128)(2,1)S(1)} collective-permute-done((bf16[512,512]{1,0:T(8,128)(2,1)S(1)}, bf16[512,512]{1,0:T(8,128)(2,1)S(1)}, u32[]{:S(2)}, u32[]{:S(2)}) %collective-permute-start.18) | collective-permute-done | bytes 524320 | tf_op jit(solution)/shard_map/ppermute | solution.py:27
  135.5 3.5 %collective-permute-start.23 = (bf16[128,4096]{1,0:T(8,128)(2,1)S(1)}, bf16[128,4096]{1,0:T(8,128)(2,1)S(1)}, u32[]{:S(2)}, u32[]{:S(2)}) collective-permute-start(bf16[128,4096]{1,0:T(8,128)(2,1)S(1)} %collective-permute-done.20.own_refs_2_), channel_id=1, source_target_pairs={{0,8},{8,0},{16,24},{24,16},{32,40},{40,32},{48,56},{56,48},{64,72... | collective-permute-start | bytes 3145736 | tf_op jit(solution)/shard_map/ppermute | solution.py:39
  139.1 2.7 %collective-permute-start.27 = (bf16[512,512]{1,0:T(8,128)(2,1)S(1)}, bf16[512,512]{1,0:T(8,128)(2,1)S(1)}, u32[]{:S(2)}, u32[]{:S(2)}) collective-permute-start(bf16[512,512]{1,0:T(8,128)(2,1)S(1)} %copy-done.9), channel_id=1, source_target_pairs={{0,4},{1,5},{2,6},{3,7},{4,0},{5,1},{6,2},{7,3},{8,12},{9,13},{10,... | collective-permute-start | bytes 1572872 | tf_op jit(solution)/shard_map/ppermute | solution.py:27
  141.8 6.7 %collective-permute-done.28 = bf16[2,512,128]{2,1,0:T(8,128)(2,1)S(1)} collective-permute-done((bf16[2,512,128]{2,1,0:T(8,128)(2,1)S(1)}, bf16[2,512,128]{2,1,0:T(8,128)(2,1)S(1)}, u32[]{:S(2)}, u32[]{:S(2)}) %collective-permute-start.28) | collective-permute-done | bytes 262176 | tf_op jit(solution)/shard_map/ppermute | solution.py:31
  148.6 2.8 %collective-permute-start.25 = (bf16[512,512]{1,0:T(8,128)(2,1)}, bf16[512,512]{1,0:T(8,128)(2,1)}, u32[]{:S(2)}, u32[]{:S(2)}) collective-permute-start(bf16[512,512]{1,0:T(8,128)(2,1)} %collective-permute-done.17.grad_refs_0_), channel_id=1, source_target_pairs={{0,4},{1,5},{2,6},{3,7},{4,0},{5,1},{6,2},{7,3},{8,12},{9,13},{10,... | collective-permute-start | bytes 1572872 | tf_op jit(solution)/shard_map/ppermute | solution.py:27
  151.4 2.3 %collective-permute-done.27.grad_refs_2_ = bf16[512,512]{1,0:T(8,128)(2,1)S(1)} collective-permute-done((bf16[512,512]{1,0:T(8,128)(2,1)S(1)}, bf16[512,512]{1,0:T(8,128)(2,1)S(1)}, u32[]{:S(2)}, u32[]{:S(2)}) %collective-permute-start.27) | collective-permute-done | bytes 524320 | tf_op jit(solution)/shard_map/ppermute | solution.py:27
  153.8 3.0 %collective-permute-start.26 = (bf16[512,512]{1,0:T(8,128)(2,1)S(1)}, bf16[512,512]{1,0:T(8,128)(2,1)S(1)}, u32[]{:S(2)}, u32[]{:S(2)}) collective-permute-start(bf16[512,512]{1,0:T(8,128)(2,1)S(1)} %collective-permute-done.19.grad_refs_3_), channel_id=1, source_target_pairs={{0,1},{1,0},{2,3},{3,2},{4,5},{5,4},{6,7},{7,6},{8,9},{9,8},{10,11... | collective-permute-start | bytes 1572872 | tf_op jit(solution)/shard_map/ppermute | solution.py:31
  156.7 2.8 %collective-permute-start.30 = (bf16[2,512,128]{2,1,0:T(8,128)(2,1)S(1)}, bf16[2,512,128]{2,1,0:T(8,128)(2,1)S(1)}, u32[]{:S(2)}, u32[]{:S(2)}) collective-permute-start(bf16[2,512,128]{2,1,0:T(8,128)(2,1)S(1)} %add_convert_fusion.1.rest_1__0_), channel_id=1, source_target_pairs={{0,4},{1,5},{2,6},{3,7},{4,0},{5,1},{6,2},{7,3},{8,12},{9,13},{10,... | collective-permute-start | bytes 786440 | tf_op jit(solution)/shard_map/ppermute | solution.py:27
  159.6 0.8 pad_add_fusion.1.place_ref
  160.5 7.1 %shard_map.111.rest_0_ = f32[1024,512]{1,0:T(8,128)} custom-call(s32[2]{0:T(128)} %pad_add_fusion.1.place_ref, bf16[128,4096]{1,0:T(8,128)(2,1)} %shard_map.110.own_refs_0_, bf16[128,4096]{1,0:T(8,128)(2,1)} %copy-done.2, bf16[128,4096]{1,0:T(8,128)(2,1)} %copy-done.3, bf16[128,4096]{1,0:T(8,128)(2,1)} %collective-permute-done.10.own_refs_3_, ...), custom_call_target="tpu_custom_call" | custom-call | flops 2147483648 | bytes 10485760 | tf_op jit(solution)/shard_map/pallas_call | solution.py:325
  167.6 3.1 %collective-permute-done.30.rest_1__2_ = bf16[2,512,128]{2,1,0:T(8,128)(2,1)S(1)} collective-permute-done((bf16[2,512,128]{2,1,0:T(8,128)(2,1)S(1)}, bf16[2,512,128]{2,1,0:T(8,128)(2,1)S(1)}, u32[]{:S(2)}, u32[]{:S(2)}) %collective-permute-start.30) | collective-permute-done | bytes 262176 | tf_op jit(solution)/shard_map/ppermute | solution.py:27
  170.7 6.4 %collective-permute-done.29.rest_1__1_ = bf16[2,512,128]{2,1,0:T(8,128)(2,1)} collective-permute-done((bf16[2,512,128]{2,1,0:T(8,128)(2,1)S(1)}, bf16[2,512,128]{2,1,0:T(8,128)(2,1)}, u32[]{:S(2)}, u32[]{:S(2)}) %collective-permute-start.29) | collective-permute-done | bytes 262176 | tf_op jit(solution)/shard_map/ppermute | solution.py:27
  177.1 0.8 copy-done.13
  177.9 13.2 %shard_map.112 = (f32[1024,512]{1,0:T(8,128)}, f32[64,1024]{1,0:T(8,128)}, f32[64,1024]{1,0:T(8,128)}, bf16[64,512]{1,0:T(8,128)(2,1)}, bf16[64,512]{1,0:T(8,128)(2,1)}) custom-call(s32[2]{0:T(128)} %pad_add_fusion.1.place_ref, bf16[128,4096]{1,0:T(8,128)(2,1)} %shard_map.110.own_refs_0_, bf16[128,4096]{1,0:T(8,128)(2,1)} %copy-done.2, ...), custom_call_target="tpu_custom_call" | custom-call | flops 2147483648 | bytes 10485760 | tf_op jit(solution)/shard_map/pallas_call | solution.py:325
  (83 shorter events, 1.9 us)
Async XLA Ops:
  2.3 17.0 %collective-permute-start.6 = (bf16[4,512,128]{2,1,0:T(8,128)(2,1)S(1)}, bf16[4,512,128]{2,1,0:T(8,128)(2,1)S(1)}, u32[]{:S(2)}, u32[]{:S(2)}) collective-permute-start(bf16[4,512,128]{2,1,0:T(8,128)(2,1)S(1)} %pad_maximum_fusion.1), channel_id=1, source_target_pairs={{0,1},{1,0},{2,3},{3,2},{4,5},{5,4},{6,7},{7,6},{8,9},{9,8},{10,11... | collective-permute-start | bytes 1572872 | tf_op jit(solution)/shard_map/ppermute | solution.py:31
  7.8 5.7 %collective-permute-start.1 = (bf16[528,128]{1,0:T(8,128)(2,1)S(1)}, bf16[528,128]{1,0:T(8,128)(2,1)S(1)}, u32[]{:S(2)}, u32[]{:S(2)}) collective-permute-start(bf16[528,128]{1,0:T(8,128)(2,1)S(1)} %get-tuple-element.64), channel_id=1, source_target_pairs={{0,4},{1,5},{2,6},{3,7},{4,0},{5,1},{6,2},{7,3},{8,12},{9,13},{10,... | collective-permute-start | bytes 405512 | tf_op jit(solution)/shard_map/ppermute | solution.py:27
  10.8 6.4 %collective-permute-start = (bf16[528,128]{1,0:T(8,128)(2,1)S(1)}, bf16[528,128]{1,0:T(8,128)(2,1)S(1)}, u32[]{:S(2)}, u32[]{:S(2)}) collective-permute-start(bf16[528,128]{1,0:T(8,128)(2,1)S(1)} %get-tuple-element.64), channel_id=1, source_target_pairs={{0,2},{1,3},{2,4},{3,5},{4,6},{5,7},{6,0},{7,1},{8,10},{9,11},{10,... | collective-permute-start | bytes 405512 | tf_op jit(solution)/shard_map/ppermute | solution.py:27
  11.2 6.0 %collective-permute-start.2 = (bf16[528,128]{1,0:T(8,128)(2,1)S(1)}, bf16[528,128]{1,0:T(8,128)(2,1)S(1)}, u32[]{:S(2)}, u32[]{:S(2)}) collective-permute-start(bf16[528,128]{1,0:T(8,128)(2,1)S(1)} %get-tuple-element.64), channel_id=1, source_target_pairs={{0,6},{1,7},{2,0},{3,1},{4,2},{5,3},{6,4},{7,5},{8,14},{9,15},{10,... | collective-permute-start | bytes 405512 | tf_op jit(solution)/shard_map/ppermute | solution.py:27
  17.3 28.2 %copy-start.8 = (bf16[4,528,128]{2,1,0:T(8,128)(2,1)}, bf16[4,528,128]{2,1,0:T(8,128)(2,1)S(1)}, u32[]{:S(2)}) copy-start(bf16[4,528,128]{2,1,0:T(8,128)(2,1)S(1)} %pad_maximum_fusion.mine_refs_0_) | copy-start | bytes 1622020
  17.3 14.0 %collective-permute-start.3 = (bf16[4,528,128]{2,1,0:T(8,128)(2,1)S(1)}, bf16[4,528,128]{2,1,0:T(8,128)(2,1)}, u32[]{:S(2)}, u32[]{:S(2)}) collective-permute-start(bf16[4,528,128]{2,1,0:T(8,128)(2,1)S(1)} %pad_maximum_fusion.mine_refs_0_), channel_id=1, source_target_pairs={{0,1},{1,0},{2,3},{3,2},{4,5},{5,4},{6,7},{7,6},{8,9},{9,8},{10,11... | collective-permute-start | bytes 1622024 | tf_op jit(solution)/shard_map/ppermute | solution.py:31
  17.5 33.1 %collective-permute-start.4 = (bf16[4,528,128]{2,1,0:T(8,128)(2,1)S(1)}, bf16[4,528,128]{2,1,0:T(8,128)(2,1)}, u32[]{:S(2)}, u32[]{:S(2)}) collective-permute-start(bf16[4,528,128]{2,1,0:T(8,128)(2,1)S(1)} %pad_maximum_fusion.mine_refs_0_), channel_id=1, source_target_pairs={{0,8},{8,0},{16,24},{24,16},{32,40},{40,32},{48,56},{56,48},{64,72... | collective-permute-start | bytes 1622024 | tf_op jit(solution)/shard_map/ppermute | solution.py:39
  19.4 18.8 %collective-permute-start.7 = (bf16[2,512,128]{2,1,0:T(8,128)(2,1)S(1)}, bf16[2,512,128]{2,1,0:T(8,128)(2,1)S(1)}, u32[]{:S(2)}, u32[]{:S(2)}) collective-permute-start(bf16[2,512,128]{2,1,0:T(8,128)(2,1)S(1)} %pad_maximum_fusion.3), channel_id=1, source_target_pairs={{0,2},{1,3},{2,4},{3,5},{4,6},{5,7},{6,0},{7,1},{8,10},{9,11},{10,... | collective-permute-start | bytes 786440 | tf_op jit(solution)/shard_map/ppermute | solution.py:27
  20.6 17.6 %collective-permute-start.8 = (bf16[2,512,128]{2,1,0:T(8,128)(2,1)S(1)}, bf16[2,512,128]{2,1,0:T(8,128)(2,1)S(1)}, u32[]{:S(2)}, u32[]{:S(2)}) collective-permute-start(bf16[2,512,128]{2,1,0:T(8,128)(2,1)S(1)} %pad_maximum_fusion.4), channel_id=1, source_target_pairs={{0,4},{1,5},{2,6},{3,7},{4,0},{5,1},{6,2},{7,3},{8,12},{9,13},{10,... | collective-permute-start | bytes 786440 | tf_op jit(solution)/shard_map/ppermute | solution.py:27
  31.3 19.4 %collective-permute-start.5 = (bf16[4,528,128]{2,1,0:T(8,128)(2,1)}, bf16[4,528,128]{2,1,0:T(8,128)(2,1)}, u32[]{:S(2)}, u32[]{:S(2)}) collective-permute-start(bf16[4,528,128]{2,1,0:T(8,128)(2,1)} %collective-permute-done.3.mine_refs_1_), channel_id=1, source_target_pairs={{0,8},{8,0},{16,24},{24,16},{32,40},{40,32},{48,56},{56,48},{64,72... | collective-permute-start | bytes 1622024 | tf_op jit(solution)/shard_map/ppermute | solution.py:39
  33.7 8.6 %collective-permute-start.9 = (bf16[2,512,128]{2,1,0:T(8,128)(2,1)S(1)}, bf16[2,512,128]{2,1,0:T(8,128)(2,1)S(1)}, u32[]{:S(2)}, u32[]{:S(2)}) collective-permute-start(bf16[2,512,128]{2,1,0:T(8,128)(2,1)S(1)} %pad_maximum_fusion.5), channel_id=1, source_target_pairs={{0,6},{1,7},{2,0},{3,1},{4,2},{5,3},{6,4},{7,5},{8,14},{9,15},{10,... | collective-permute-start | bytes 786440 | tf_op jit(solution)/shard_map/ppermute | solution.py:27
  38.2 4.1 %copy-start.16 = (bf16[2,512,128]{2,1,0:T(8,128)(2,1)}, bf16[2,512,128]{2,1,0:T(8,128)(2,1)S(1)}, u32[]{:S(2)}) copy-start(bf16[2,512,128]{2,1,0:T(8,128)(2,1)S(1)} %collective-permute-done.7.in_refs_1_) | copy-start | bytes 786436
  38.2 4.1 %copy-start.17 = (bf16[2,512,128]{2,1,0:T(8,128)(2,1)}, bf16[2,512,128]{2,1,0:T(8,128)(2,1)S(1)}, u32[]{:S(2)}) copy-start(bf16[2,512,128]{2,1,0:T(8,128)(2,1)S(1)} %collective-permute-done.8.in_refs_2_) | copy-start | bytes 786436
  45.5 24.2 %collective-permute-start.12 = (bf16[128,4096]{1,0:T(8,128)(2,1)}, bf16[128,4096]{1,0:T(8,128)(2,1)S(1)}, u32[]{:S(2)}, u32[]{:S(2)}) collective-permute-start(bf16[128,4096]{1,0:T(8,128)(2,1)} %shard_map.110.own_refs_0_), channel_id=1, source_target_pairs={{0,8},{8,0},{16,24},{24,16},{32,40},{40,32},{48,56},{56,48},{64,72... | collective-permute-start | bytes 3145736 | tf_op jit(solution)/shard_map/ppermute | solution.py:39
  46.3 26.7 %collective-permute-start.11 = (bf16[128,4096]{1,0:T(8,128)(2,1)}, bf16[128,4096]{1,0:T(8,128)(2,1)S(1)}, u32[]{:S(2)}, u32[]{:S(2)}) collective-permute-start(bf16[128,4096]{1,0:T(8,128)(2,1)} %shard_map.110.own_refs_0_), channel_id=1, source_target_pairs={{0,96},{8,104},{16,112},{24,120},{32,0},{40,8},{48,16},{56,24},{64... | collective-permute-start | bytes 3145736 | tf_op jit(solution)/shard_map/ppermute | solution.py:35
  50.0 26.0 %collective-permute-start.10 = (bf16[128,4096]{1,0:T(8,128)(2,1)}, bf16[128,4096]{1,0:T(8,128)(2,1)}, u32[]{:S(2)}, u32[]{:S(2)}) collective-permute-start(bf16[128,4096]{1,0:T(8,128)(2,1)} %shard_map.110.own_refs_0_), channel_id=1, source_target_pairs={{0,32},{8,40},{16,48},{24,56},{32,64},{40,72},{48,80},{56,88},{64,... | collective-permute-start | bytes 3145736 | tf_op jit(solution)/shard_map/ppermute | solution.py:35
  50.6 26.5 %copy-start = (bf16[128,4096]{1,0:T(8,128)(2,1)S(1)}, bf16[128,4096]{1,0:T(8,128)(2,1)}, u32[]{:S(2)}) copy-start(bf16[128,4096]{1,0:T(8,128)(2,1)} %shard_map.110.own_refs_0_) | copy-start | bytes 3145732
  69.7 11.5 %copy-start.1 = (bf16[128,4096]{1,0:T(8,128)(2,1)}, bf16[128,4096]{1,0:T(8,128)(2,1)S(1)}, u32[]{:S(2)}) copy-start(bf16[128,4096]{1,0:T(8,128)(2,1)S(1)} %collective-permute-done.12.other_refs_0_) | copy-start | bytes 3145732
  72.9 8.3 %copy-start.2 = (bf16[128,4096]{1,0:T(8,128)(2,1)}, bf16[128,4096]{1,0:T(8,128)(2,1)S(1)}, u32[]{:S(2)}) copy-start(bf16[128,4096]{1,0:T(8,128)(2,1)S(1)} %collective-permute-done.11.own_refs_1_) | copy-start | bytes 3145732
  76.0 41.4 %copy-start.9 = (bf16[512,512]{1,0:T(8,128)(2,1)S(1)}, bf16[512,512]{1,0:T(8,128)(2,1)}, u32[]{:S(2)}) copy-start(bf16[512,512]{1,0:T(8,128)(2,1)} %get-tuple-element.21.grad_refs_0_) | copy-start | bytes 1572868
  76.0 3.6 %collective-permute-start.13 = (bf16[8,512,128]{2,1,0:T(8,128)(2,1)}, bf16[8,512,128]{2,1,0:T(8,128)(2,1)S(1)}, u32[]{:S(2)}, u32[]{:S(2)}) collective-permute-start(bf16[8,512,128]{2,1,0:T(8,128)(2,1)} %get-tuple-element.33), channel_id=1, source_target_pairs={{0,8},{8,0},{16,24},{24,16},{32,40},{40,32},{48,56},{56,48},{64,72... | collective-permute-start | bytes 3145736 | tf_op jit(solution)/shard_map/ppermute | solution.py:39
  77.1 26.2 %collective-permute-start.20 = (bf16[128,4096]{1,0:T(8,128)(2,1)S(1)}, bf16[128,4096]{1,0:T(8,128)(2,1)S(1)}, u32[]{:S(2)}, u32[]{:S(2)}) collective-permute-start(bf16[128,4096]{1,0:T(8,128)(2,1)S(1)} %copy-done), channel_id=1, source_target_pairs={{0,64},{8,72},{16,80},{24,88},{32,96},{40,104},{48,112},{56,120},{... | collective-permute-start | bytes 3145736 | tf_op jit(solution)/shard_map/ppermute | solution.py:35
  77.1 58.4 %collective-permute-start.22 = (bf16[128,4096]{1,0:T(8,128)(2,1)S(1)}, bf16[128,4096]{1,0:T(8,128)(2,1)S(1)}, u32[]{:S(2)}, u32[]{:S(2)}) collective-permute-start(bf16[128,4096]{1,0:T(8,128)(2,1)S(1)} %collective-permute-done.11.own_refs_1_), channel_id=1, source_target_pairs={{0,8},{8,0},{16,24},{24,16},{32,40},{40,32},{48,56},{56,48},{64,72... | collective-permute-start | bytes 3145736 | tf_op jit(solution)/shard_map/ppermute | solution.py:39
  77.3 58.2 %collective-permute-start.21 = (bf16[128,4096]{1,0:T(8,128)(2,1)}, bf16[128,4096]{1,0:T(8,128)(2,1)S(1)}, u32[]{:S(2)}, u32[]{:S(2)}) collective-permute-start(bf16[128,4096]{1,0:T(8,128)(2,1)} %collective-permute-done.10.own_refs_3_), channel_id=1, source_target_pairs={{0,8},{8,0},{16,24},{24,16},{32,40},{40,32},{48,56},{56,48},{64,72... | collective-permute-start | bytes 3145736 | tf_op jit(solution)/shard_map/ppermute | solution.py:39
  81.2 36.2 %collective-permute-start.14 = (bf16[2,512,128]{2,1,0:T(8,128)(2,1)S(1)}, bf16[2,512,128]{2,1,0:T(8,128)(2,1)S(1)}, u32[]{:S(2)}, u32[]{:S(2)}) collective-permute-start(bf16[2,512,128]{2,1,0:T(8,128)(2,1)S(1)} %get-tuple-element.56), channel_id=1, source_target_pairs={{0,6},{1,7},{2,0},{3,1},{4,2},{5,3},{6,4},{7,5},{8,14},{9,15},{10,... | collective-permute-start | bytes 786440 | tf_op jit(solution)/shard_map/ppermute | solution.py:27
  84.9 32.5 %collective-permute-start.15 = (bf16[2,512,128]{2,1,0:T(8,128)(2,1)S(1)}, bf16[2,512,128]{2,1,0:T(8,128)(2,1)S(1)}, u32[]{:S(2)}, u32[]{:S(2)}) collective-permute-start(bf16[2,512,128]{2,1,0:T(8,128)(2,1)S(1)} %get-tuple-element.57), channel_id=1, source_target_pairs={{0,2},{1,3},{2,4},{3,5},{4,6},{5,7},{6,0},{7,1},{8,10},{9,11},{10,... | collective-permute-start | bytes 786440 | tf_op jit(solution)/shard_map/ppermute | solution.py:27
  103.4 32.2 %copy-start.3 = (bf16[128,4096]{1,0:T(8,128)(2,1)}, bf16[128,4096]{1,0:T(8,128)(2,1)S(1)}, u32[]{:S(2)}) copy-start(bf16[128,4096]{1,0:T(8,128)(2,1)S(1)} %collective-permute-done.20.own_refs_2_) | copy-start | bytes 3145732
  103.4 19.7 %collective-permute-start.16 = (bf16[2,512,128]{2,1,0:T(8,128)(2,1)S(1)}, bf16[2,512,128]{2,1,0:T(8,128)(2,1)S(1)}, u32[]{:S(2)}, u32[]{:S(2)}) collective-permute-start(bf16[2,512,128]{2,1,0:T(8,128)(2,1)S(1)} %get-tuple-element.58), channel_id=1, source_target_pairs={{0,4},{1,5},{2,6},{3,7},{4,0},{5,1},{6,2},{7,3},{8,12},{9,13},{10,... | collective-permute-start | bytes 786440 | tf_op jit(solution)/shard_map/ppermute | solution.py:27
  117.4 12.1 %collective-permute-start.19 = (bf16[512,512]{1,0:T(8,128)(2,1)S(1)}, bf16[512,512]{1,0:T(8,128)(2,1)S(1)}, u32[]{:S(2)}, u32[]{:S(2)}) collective-permute-start(bf16[512,512]{1,0:T(8,128)(2,1)S(1)} %copy-done.9), channel_id=1, source_target_pairs={{0,6},{1,7},{2,0},{3,1},{4,2},{5,3},{6,4},{7,5},{8,14},{9,15},{10,... | collective-permute-start | bytes 1572872 | tf_op jit(solution)/shard_map/ppermute | solution.py:27
  117.4 18.1 %collective-permute-start.18 = (bf16[512,512]{1,0:T(8,128)(2,1)S(1)}, bf16[512,512]{1,0:T(8,128)(2,1)S(1)}, u32[]{:S(2)}, u32[]{:S(2)}) collective-permute-start(bf16[512,512]{1,0:T(8,128)(2,1)S(1)} %copy-done.9), channel_id=1, source_target_pairs={{0,2},{1,3},{2,4},{3,5},{4,6},{5,7},{6,0},{7,1},{8,10},{9,11},{10,... | collective-permute-start | bytes 1572872 | tf_op jit(solution)/shard_map/ppermute | solution.py:27
  123.0 12.5 %collective-permute-start.17 = (bf16[512,512]{1,0:T(8,128)(2,1)S(1)}, bf16[512,512]{1,0:T(8,128)(2,1)}, u32[]{:S(2)}, u32[]{:S(2)}) collective-permute-start(bf16[512,512]{1,0:T(8,128)(2,1)S(1)} %copy-done.9), channel_id=1, source_target_pairs={{0,1},{1,0},{2,3},{3,2},{4,5},{5,4},{6,7},{7,6},{8,9},{9,8},{10,11... | collective-permute-start | bytes 1572872 | tf_op jit(solution)/shard_map/ppermute | solution.py:31
  129.5 30.9 %copy-start.10 = (bf16[512,512]{1,0:T(8,128)(2,1)}, bf16[512,512]{1,0:T(8,128)(2,1)S(1)}, u32[]{:S(2)}) copy-start(bf16[512,512]{1,0:T(8,128)(2,1)S(1)} %collective-permute-done.19.grad_refs_3_) | copy-start | bytes 1572868
  135.5 24.9 %copy-start.11 = (bf16[512,512]{1,0:T(8,128)(2,1)}, bf16[512,512]{1,0:T(8,128)(2,1)S(1)}, u32[]{:S(2)}) copy-start(bf16[512,512]{1,0:T(8,128)(2,1)S(1)} %collective-permute-done.18.grad_refs_1_) | copy-start | bytes 1572868
  135.5 24.0 %copy-start.4 = (bf16[128,4096]{1,0:T(8,128)(2,1)}, bf16[128,4096]{1,0:T(8,128)(2,1)S(1)}, u32[]{:S(2)}) copy-start(bf16[128,4096]{1,0:T(8,128)(2,1)S(1)} %collective-permute-done.22.other_refs_1_) | copy-start | bytes 3145732
  135.5 24.1 %copy-start.5 = (bf16[128,4096]{1,0:T(8,128)(2,1)}, bf16[128,4096]{1,0:T(8,128)(2,1)S(1)}, u32[]{:S(2)}) copy-start(bf16[128,4096]{1,0:T(8,128)(2,1)S(1)} %collective-permute-done.21.other_refs_3_) | copy-start | bytes 3145732
  135.5 24.0 %collective-permute-start.23 = (bf16[128,4096]{1,0:T(8,128)(2,1)S(1)}, bf16[128,4096]{1,0:T(8,128)(2,1)S(1)}, u32[]{:S(2)}, u32[]{:S(2)}) collective-permute-start(bf16[128,4096]{1,0:T(8,128)(2,1)S(1)} %collective-permute-done.20.own_refs_2_), channel_id=1, source_target_pairs={{0,8},{8,0},{16,24},{24,16},{32,40},{40,32},{48,56},{56,48},{64,72... | collective-permute-start | bytes 3145736 | tf_op jit(solution)/shard_map/ppermute | solution.py:39
  139.1 9.4 %collective-permute-start.28 = (bf16[2,512,128]{2,1,0:T(8,128)(2,1)S(1)}, bf16[2,512,128]{2,1,0:T(8,128)(2,1)S(1)}, u32[]{:S(2)}, u32[]{:S(2)}) collective-permute-start(bf16[2,512,128]{2,1,0:T(8,128)(2,1)S(1)} %fusion.2), channel_id=1, source_target_pairs={{0,1},{1,0},{2,3},{3,2},{4,5},{5,4},{6,7},{7,6},{8,9},{9,8},{10,11... | collective-permute-start | bytes 786440 | tf_op jit(solution)/shard_map/ppermute | solution.py:31
  139.1 14.7 %collective-permute-start.27 = (bf16[512,512]{1,0:T(8,128)(2,1)S(1)}, bf16[512,512]{1,0:T(8,128)(2,1)S(1)}, u32[]{:S(2)}, u32[]{:S(2)}) collective-permute-start(bf16[512,512]{1,0:T(8,128)(2,1)S(1)} %copy-done.9), channel_id=1, source_target_pairs={{0,4},{1,5},{2,6},{3,7},{4,0},{5,1},{6,2},{7,3},{8,12},{9,13},{10,... | collective-permute-start | bytes 1572872 | tf_op jit(solution)/shard_map/ppermute | solution.py:27
  148.6 19.0 %copy-start.7 = (bf16[2,512,128]{2,1,0:T(8,128)(2,1)}, bf16[2,512,128]{2,1,0:T(8,128)(2,1)S(1)}, u32[]{:S(2)}) copy-start(bf16[2,512,128]{2,1,0:T(8,128)(2,1)S(1)} %add_convert_fusion.1.rest_1__0_) | copy-start | bytes 786436
  148.6 8.2 %collective-permute-start.31 = (bf16[2,512,128]{2,1,0:T(8,128)(2,1)S(1)}, bf16[2,512,128]{2,1,0:T(8,128)(2,1)S(1)}, u32[]{:S(2)}, u32[]{:S(2)}) collective-permute-start(bf16[2,512,128]{2,1,0:T(8,128)(2,1)S(1)} %add_convert_fusion.1.rest_1__0_), channel_id=1, source_target_pairs={{0,6},{1,7},{2,0},{3,1},{4,2},{5,3},{6,4},{7,5},{8,14},{9,15},{10,... | collective-permute-start | bytes 786440 | tf_op jit(solution)/shard_map/ppermute | solution.py:27
  148.6 28.4 %collective-permute-start.25 = (bf16[512,512]{1,0:T(8,128)(2,1)}, bf16[512,512]{1,0:T(8,128)(2,1)}, u32[]{:S(2)}, u32[]{:S(2)}) collective-permute-start(bf16[512,512]{1,0:T(8,128)(2,1)} %collective-permute-done.17.grad_refs_0_), channel_id=1, source_target_pairs={{0,4},{1,5},{2,6},{3,7},{4,0},{5,1},{6,2},{7,3},{8,12},{9,13},{10,... | collective-permute-start | bytes 1572872 | tf_op jit(solution)/shard_map/ppermute | solution.py:27
  151.4 25.6 %collective-permute-start.24 = (bf16[512,512]{1,0:T(8,128)(2,1)S(1)}, bf16[512,512]{1,0:T(8,128)(2,1)}, u32[]{:S(2)}, u32[]{:S(2)}) collective-permute-start(bf16[512,512]{1,0:T(8,128)(2,1)S(1)} %collective-permute-done.18.grad_refs_1_), channel_id=1, source_target_pairs={{0,1},{1,0},{2,3},{3,2},{4,5},{5,4},{6,7},{7,6},{8,9},{9,8},{10,11... | collective-permute-start | bytes 1572872 | tf_op jit(solution)/shard_map/ppermute | solution.py:31
  153.8 6.7 %copy-start.12 = (bf16[512,512]{1,0:T(8,128)(2,1)}, bf16[512,512]{1,0:T(8,128)(2,1)S(1)}, u32[]{:S(2)}) copy-start(bf16[512,512]{1,0:T(8,128)(2,1)S(1)} %collective-permute-done.27.grad_refs_2_) | copy-start | bytes 1572868
  153.8 23.3 %collective-permute-start.26 = (bf16[512,512]{1,0:T(8,128)(2,1)S(1)}, bf16[512,512]{1,0:T(8,128)(2,1)S(1)}, u32[]{:S(2)}, u32[]{:S(2)}) collective-permute-start(bf16[512,512]{1,0:T(8,128)(2,1)S(1)} %collective-permute-done.19.grad_refs_3_), channel_id=1, source_target_pairs={{0,1},{1,0},{2,3},{3,2},{4,5},{5,4},{6,7},{7,6},{8,9},{9,8},{10,11... | collective-permute-start | bytes 1572872 | tf_op jit(solution)/shard_map/ppermute | solution.py:31
  156.7 10.8 %copy-start.14 = (bf16[2,512,128]{2,1,0:T(8,128)(2,1)}, bf16[2,512,128]{2,1,0:T(8,128)(2,1)S(1)}, u32[]{:S(2)}) copy-start(bf16[2,512,128]{2,1,0:T(8,128)(2,1)S(1)} %collective-permute-done.31.rest_1__3_) | copy-start | bytes 786436
  156.7 13.9 %collective-permute-start.30 = (bf16[2,512,128]{2,1,0:T(8,128)(2,1)S(1)}, bf16[2,512,128]{2,1,0:T(8,128)(2,1)S(1)}, u32[]{:S(2)}, u32[]{:S(2)}) collective-permute-start(bf16[2,512,128]{2,1,0:T(8,128)(2,1)S(1)} %add_convert_fusion.1.rest_1__0_), channel_id=1, source_target_pairs={{0,4},{1,5},{2,6},{3,7},{4,0},{5,1},{6,2},{7,3},{8,12},{9,13},{10,... | collective-permute-start | bytes 786440 | tf_op jit(solution)/shard_map/ppermute | solution.py:27
  159.5 17.5 %collective-permute-start.29 = (bf16[2,512,128]{2,1,0:T(8,128)(2,1)S(1)}, bf16[2,512,128]{2,1,0:T(8,128)(2,1)}, u32[]{:S(2)}, u32[]{:S(2)}) collective-permute-start(bf16[2,512,128]{2,1,0:T(8,128)(2,1)S(1)} %add_convert_fusion.1.rest_1__0_), channel_id=1, source_target_pairs={{0,2},{1,3},{2,4},{3,5},{4,6},{5,7},{6,0},{7,1},{8,10},{9,11},{10,... | collective-permute-start | bytes 786440 | tf_op jit(solution)/shard_map/ppermute | solution.py:27
  170.7 6.4 %copy-start.15 = (bf16[2,512,128]{2,1,0:T(8,128)(2,1)}, bf16[2,512,128]{2,1,0:T(8,128)(2,1)S(1)}, u32[]{:S(2)}) copy-start(bf16[2,512,128]{2,1,0:T(8,128)(2,1)S(1)} %collective-permute-done.30.rest_1__2_) | copy-start | bytes 786436
  (3 other events, 2.5 us)

commit v5 on v4

--- a/solution.py
+++ b/solution.py
@@ -48,7 +48,7 @@
 
 
 def attention_kernel(
-    heads, info_ref, q_ref, g_ref, mine_refs, other_refs, dq_ref, keep_ref, give_ref,
+    heads, info_ref, q_ref, g_ref, mine_refs, other_refs, dq_ref, dqh_ref, keep_ref, give_ref,
     ks, vs, kt, scores, grads, dka, dva, qh, gh, dqt,
 ):
     per_ref = mine_refs[0].shape[0]
@@ -139,7 +139,9 @@
         lax.fori_loop(0, run + 1, grad_step, 0)
         for h in range(heads):
             cols = slice(h * RUN, (h + 1) * RUN)
-            dq_ref[rows, h * HD : (h + 1) * HD] = (dqt[:, cols] * scale).T.astype(jnp.bfloat16)
+            dq = (dqt[:, cols] * scale).T.astype(jnp.bfloat16)
+            dq_ref[rows, h * HD : (h + 1) * HD] = dq
+            dqh_ref[h, rows, :] = dq
     half_head = HD // 2
     for b in range(slots * runs_per_slot):
         slot, part = b // runs_per_slot, b % runs_per_slot
@@ -166,11 +168,12 @@
         functools.partial(attention_kernel, heads),
         out_shape=(
             jax.ShapeDtypeStruct(queries.shape, jnp.bfloat16),
+            jax.ShapeDtypeStruct((heads, 2 * RUN, HD), jnp.bfloat16),
             shared,
             shared,
         ),
         in_specs=[smem, vmem, vmem, [vmem] * len(mine), [vmem] * len(other)],
-        out_specs=(vmem, vmem, vmem),
+        out_specs=(vmem, vmem, vmem, vmem),
         scratch_shapes=[
             pltpu.VMEM((count, HD), jnp.bfloat16),
             pltpu.VMEM((count, HD), jnp.bfloat16),
@@ -211,43 +214,63 @@
     )(list(pieces))
 
 
-def weight_kernel(last, place_ref, own_refs, other_refs, grad_refs, *rest):
+EARLY = (0, 1, 3, 4)
+LATE = (2, 5, 6, 7)
+
+
+def consecutive(slots):
+    spans = []
+    for at, slot in enumerate(slots):
+        if spans and spans[-1][1] + spans[-1][2] == slot:
+            spans[-1][2] += 1
+        else:
+            spans.append([at, slot, 1])
+    return spans
+
+
+def weight_kernel(last, starts, place_ref, own_refs, other_refs, grad_refs, *rest):
     if last:
         (sum_ref, shared_refs, wq_ref, wk_ref, wv_ref, k_ref, v_ref,
          inputs, grads, sums, shared, in_sems, grad_sems, sum_sems, shared_sems, out_sems) = rest
     else:
         wq_ref, inputs, grads, sums, in_sems, grad_sems, out_sems = rest
     core, z = place_ref[0], place_ref[1]
-    tall, across = own_refs[0].shape
-    tokens = grad_refs[0].shape[0]
-    side = across // 2
-    sides = (1, 0) if last else (0,)
+    tall = own_refs[0].shape[0]
+    tokens, wide = grad_refs[0].shape[1:]
+    heads = grads.shape[1] // wide
+    half = len(EARLY) * tokens
+    order = LATE + EARLY if last else EARLY
+    spans = consecutive(order)
+    first_spans = sum(1 for at, _, _ in spans if at < len(EARLY))
     grad_copies = [
-        pltpu.make_async_copy(ref, grads.at[pl.ds(dy * tokens, tokens)], grad_sems.at[dy])
-        for dy, ref in enumerate(grad_refs)
+        pltpu.make_async_copy(
+            ref.at[start + h],
+            grads.at[pl.ds(i * tokens, tokens), pl.ds(h * wide, wide)],
+            grad_sems.at[i, h],
+        )
+        for i, (ref, start) in enumerate(zip(grad_refs, starts))
+        for h in range(heads)
     ]
     for copy in grad_copies:
         copy.start()
-    row, in_copies, sum_copies = [], {}, []
-    for away in range(4):
-        row.append(pl.multiple_of(lax.rem(z + away, 4) * 2 * tall, 2 * tall))
+    row = [pl.multiple_of(lax.rem(z + away, 4) * 2 * tall, 2 * tall) for away in range(4)]
+    in_copies, sum_copies, shared_copies, out_copies = {}, [], [], []
     if last:
         shared_copies = [
             pltpu.make_async_copy(
-                shared_refs[dy].at[dx],
-                shared.at[pl.ds((dx * 4 + dy) * tokens, tokens)],
-                shared_sems.at[dx, dy],
+                shared_refs[slot % 4].at[slot // 4],
+                shared.at[pl.ds(i * tokens, tokens)],
+                shared_sems.at[i],
             )
-            for dx in range(2)
-            for dy in range(4)
+            for i, slot in enumerate(order)
         ]
     for away in range(4):
-        for n, dx in enumerate(sides):
+        for n, (at, slot, many) in enumerate(spans):
             for which, ref in enumerate((own_refs[away], other_refs[away])):
-                at = pl.multiple_of((core if which == 0 else 1 - core) * tall, tall)
+                down = pl.multiple_of((core if which == 0 else 1 - core) * tall, tall)
                 in_copies[away, n, which] = pltpu.make_async_copy(
-                    ref.at[:, pl.ds(dx * side, side)],
-                    inputs.at[away, n, pl.ds(at, tall)],
+                    ref.at[:, pl.ds(slot * tokens, many * tokens)],
+                    inputs.at[away, pl.ds(down, tall), pl.ds(at * tokens, many * tokens)],
                     in_sems.at[away, n, which],
                 )
                 in_copies[away, n, which].start()
@@ -264,11 +287,11 @@
     for copy in grad_copies:
         copy.wait()
     norm = 1.0 / math.sqrt(8 * tokens)
-    out_copies = []
     for away in range(4):
-        for which in range(2):
-            in_copies[away, 0, which].wait()
-        total = contract(inputs[away, 0], grads[...], 1, 0)
+        for n in range(first_spans):
+            for which in range(2):
+                in_copies[away, n, which].wait()
+        total = contract(inputs[away, :, :half], grads[...], 1, 0)
         if last:
             sum_copies[away].wait()
             total = (total + sums[away]) * norm
@@ -283,47 +306,47 @@
             if away == 0:
                 for copy in shared_copies:
                     copy.wait()
-            for which in range(2):
-                in_copies[away, 1, which].wait()
-            part = contract(inputs[away, 0], shared[side:], 1, 0)
-            part += contract(inputs[away, 1], shared[:side], 1, 0)
-            part = (part * norm).T
-            half = part.shape[0] // 2
-            wk_ref[:, pl.ds(row[away], 2 * tall)] = part[:half]
-            wv_ref[:, pl.ds(row[away], 2 * tall)] = part[half:]
+            for n in range(first_spans, len(spans)):
+                for which in range(2):
+                    in_copies[away, n, which].wait()
+            part = (contract(inputs[away], shared[...], 1, 0) * norm).T
+            wk_ref[:, pl.ds(row[away], 2 * tall)] = part[: tall // 2]
+            wv_ref[:, pl.ds(row[away], 2 * tall)] = part[tall // 2 :]
     if last:
-        here = shared[:tokens].T
+        at = order.index(0) * tokens
+        here = shared[at : at + tokens].T
         k_ref[...] = here[: here.shape[0] // 2]
         v_ref[...] = here[here.shape[0] // 2 :]
     for copy in out_copies:
         copy.wait()
 
 
-def weights(place, own, other, grads, total=None, shared=None):
+def weights(place, own, other, grads, heads, total=None, shared=None):
     last = total is not None
     smem = pl.BlockSpec(memory_space=pltpu.SMEM)
     vmem = pl.BlockSpec(memory_space=pltpu.VMEM)
     hbm = pl.BlockSpec(memory_space=pl.ANY)
     tall, across = own[0].shape
-    tokens, cols = grads[0].shape
+    tokens, wide = grads[0][0].shape[1:]
+    cols = heads * wide
     f32, bf16, sem = jnp.float32, jnp.bfloat16, pltpu.SemaphoreType.DMA
     wq = jax.ShapeDtypeStruct((8 * tall, cols), f32)
     narrow = jax.ShapeDtypeStruct((tall // 2, 8 * tall), f32)
     narrow_in = jax.ShapeDtypeStruct((tall // 2, tokens), bf16)
-    sides = 2 if last else 1
+    order = LATE + EARLY if last else EARLY
     scratch = [
-        pltpu.VMEM((4, sides, 2 * tall, across // 2), bf16),
-        pltpu.VMEM((4 * tokens, cols), bf16),
+        pltpu.VMEM((4, 2 * tall, len(order) * tokens), bf16),
+        pltpu.VMEM((len(grads) * tokens, cols), bf16),
         pltpu.VMEM((4, 2 * tall, cols), f32),
     ]
     if last:
         scratch += [pltpu.VMEM((across, tall), bf16)]
-    scratch += [sem((4, sides, 2)), sem((4,))]
+    scratch += [sem((4, len(consecutive(order)), 2)), sem((len(grads), heads))]
     if last:
-        scratch += [sem((4,)), sem((2, 4))]
+        scratch += [sem((4,)), sem((len(order),))]
     scratch += [sem((4,))]
     return pl.pallas_call(
-        functools.partial(weight_kernel, last),
+        functools.partial(weight_kernel, last, tuple(start for _, start in grads)),
         out_shape=(wq, narrow, narrow, narrow_in, narrow_in) if last else wq,
         in_specs=[smem, [hbm] * 4, [hbm] * 4, [hbm] * 4] + ([hbm, [hbm] * 4] if last else []),
         out_specs=(hbm, vmem, vmem, vmem, vmem) if last else hbm,
@@ -332,7 +355,13 @@
         cost_estimate=pl.CostEstimate(
             flops=8 * tokens * cols * 8 * tall, bytes_accessed=10 * 1024 * 1024, transcendentals=0
         ),
-    )(place, list(own), list(other), list(grads), *((total, list(shared)) if last else ()))
+    )(
+        place,
+        list(own),
+        list(other),
+        [array for array, _ in grads],
+        *((total, list(shared)) if last else ()),
+    )
 
 
 def local(layer_input, queries, key_vectors, value_vectors, grad_output, positions):
@@ -362,7 +391,9 @@
     partner_column = swap_x(column)
     column_other = swap_cores(column)
     pairs = [jnp.stack([block(dy, 0), from_x[dy]]) for dy in range(4)]
-    pairs = [pairs[0]] + [along_y(pairs[dy], dy) for dy in range(1, 4)]
+    moved = [along_y(pairs[dy], dy) for dy in range(1, 4)]
+    partner_column, *moved = lax.optimization_barrier((partner_column, *moved))
+    pairs = [pairs[0]] + moved
     partner_other = swap_cores(partner_column)
     info = jnp.concatenate(
         [
@@ -373,41 +404,46 @@
     )
     slab_own = turn(pairs)
     slab_back, slab_ahead = along_z(slab_own, 1), along_z(slab_own, 3)
-    slab_far = along_z(slab_own, 2)
     own_other = swap_cores(slab_own)
 
-    grad_query, keep, give = attention(
+    grad_query, grad_heads, keep, give = attention(
         info, queries, grad_output, [column, partner_column], [column_other, partner_other]
     )
-    grad_query, keep, give, slab_back, slab_ahead, own_other = lax.optimization_barrier(
-        (grad_query, keep, give, slab_back, slab_ahead, own_other)
-    )
-
-    give = swap_cores(give)
-    back_other, ahead_other = swap_cores(slab_back), swap_cores(slab_ahead)
+    heads = grad_heads.shape[0]
+    grad_heads, keep, give, slab_own, slab_back, slab_ahead, own_other = lax.optimization_barrier(
+        (grad_heads, keep, give, slab_own, slab_back, slab_ahead, own_other)
+    )
+
+    give, back_other = lax.optimization_barrier((swap_cores(give), swap_cores(slab_back)))
     summed = (keep.astype(jnp.float32) + give.astype(jnp.float32)).astype(jnp.bfloat16)
     summed = summed.reshape(2, 4, count, HD)
-    from_partner = swap_x(grad_query)
-    from_1, from_3 = along_y(grad_query, 1), along_y(grad_query, 3)
+    from_1 = along_y(jnp.concatenate([grad_heads, summed[:, 3]]), 1)
+    from_3 = along_y(jnp.concatenate([grad_heads, summed[:, 1]]), 3)
+    rows_2 = along_y(summed[:, 2], 2)
+    from_x = swap_x(grad_heads)
+    slab_far = along_z(slab_own, 2)
+    from_1, from_3, rows_2, from_x, slab_far = lax.optimization_barrier(
+        (from_1, from_3, rows_2, from_x, slab_far)
+    )
     rows_y = summed[:, 0].astype(jnp.float32)
-    for dy in (1, 3, 2):
-        rows_y = rows_y + along_y(summed[:, dy], -dy).astype(jnp.float32)
+    for term in (from_1[heads:], from_3[heads:], rows_2):
+        rows_y = rows_y + term.astype(jnp.float32)
     rows_y = rows_y.astype(jnp.bfloat16)
-    rows_y, from_partner, from_1, from_3, slab_far, back_other, ahead_other = lax.optimization_barrier(
-        (rows_y, from_partner, from_1, from_3, slab_far, back_other, ahead_other)
-    )
-    both = (rows_y.astype(jnp.float32) + swap_x(rows_y).astype(jnp.float32)[::-1]).astype(jnp.bfloat16)
-    far_other = swap_cores(slab_far)
-    from_2 = along_y(grad_query, 2)
-    other_1, other_3 = swap_x(from_1), swap_x(from_3)
-    other_2 = along_y(from_partner, 2)
+    rows_x = swap_x(rows_y)
+    from_x13 = swap_x(jnp.concatenate([from_1[:heads], from_3[:heads]]))
+    from_2 = along_y(jnp.concatenate([grad_heads, from_x]), 2)
+    far_other, ahead_other = swap_cores(slab_far), swap_cores(slab_ahead)
+    rows_x, far_other, ahead_other = lax.optimization_barrier((rows_x, far_other, ahead_other))
+    both = (rows_y.astype(jnp.float32) + rows_x.astype(jnp.float32)[::-1]).astype(jnp.bfloat16)
     shared = [both] + by_source(*to_all_y(both))
 
     slabs = [slab_own, slab_ahead, slab_far, slab_back]
     slabs_other = [own_other, ahead_other, far_other, back_other]
-    partial = weights(place, slabs, slabs_other, [grad_query, from_1, from_2, from_3])
+    early = [(grad_heads, 0), (from_1, 0), (from_3, 0), (from_x, 0)]
+    late = [(from_2, 0), (from_x13, 0), (from_2, heads), (from_x13, heads)]
+    partial = weights(place, slabs, slabs_other, early, heads)
     grad_wq, grad_wk, grad_wv, grad_key, grad_value = weights(
-        place, slabs, slabs_other, [from_partner, other_1, other_2, other_3], partial, shared
+        place, slabs, slabs_other, late, heads, partial, shared
     )
     return grad_query, grad_key.T, grad_value.T, grad_wq, grad_wk.T, grad_wv.T
 

time: 188 us -> 181 us (0.963); the launches traced: 191 us -> 182 us
  Pallas kernels: 41.8 us -> 34 us
  other arithmetic: 5.86 us -> 9.41 us
  waiting for transfers between devices: 77.1 us -> 74.6 us
  starting transfers between devices: 61.1 us -> 59.2 us
    ppermute x6 -> x5, waiting for transfers between devices: 14.3 us -> 45.6 us  [swap_x(): return lax.ppermute(value, 'ctx', [(i, i ^ 1) for i in range(8)])]
    ppermute x16 -> x13, waiting for transfers between devices: 36.1 us -> 11.4 us  [along_y(): lax.ppermute(value, 'ctx', [(i, (i + 2 * step) % 8) for i in range(8)])]
    ppermute x16 -> x13, starting transfers between devices: 40.3 us -> 20.2 us  [along_y(): lax.ppermute(value, 'ctx', [(i, (i + 2 * step) % 8) for i in range(8)])]
    ppermute x6 -> x5, starting transfers between devices: 6.83 us -> 26.3 us  [swap_x(): return lax.ppermute(value, 'ctx', [(i, i ^ 1) for i in range(8)])]
    ppermute x3, waiting for transfers between devices: 24.8 us -> 13.5 us  [along_z(): lax.ppermute(value, 'dp', [(i, (i + 4 * step) % 16) for i in range(16)])]
    pallas_call x1, Pallas kernels: 19.1 us -> 10.6 us  [attention(): pl.pallas_call(functools.partial(attention_kernel, heads), out_shape=(jax...]
    concatenate x0 -> x3, other arithmetic: none -> 2.24 us  [the longest x1 1.07 us: local(): from_x13 = swap_x(jnp.concatenate([from_1[:heads], from_3[:heads]]))]
    ppermute x7, waiting for transfers between devices: 2 us -> 4.13 us  [swap_cores(): return lax.ppermute(value, 'dp', [(i, i ^ 1) for i in range(16)])]
  transfers between devices with their start and end apart: 32 -> 28, of which waited for: 15 -> 14; matrix products, arithmetic and copies ran while one was open for 4% -> 6% of each run, Pallas kernels for 15% -> 11%
where the time goes in v5:
time: 181 us; the launch traced here: 182 us
  waiting for transfers between devices  74.6 us (41%)
  starting transfers between devices  59.2 us (33%)
  Pallas kernels  34 us (19%)
  other arithmetic  9.41 us (5%)
  local copies, waits for them, and re-layouts  3.29 us (2%)
    ppermute x5, waiting for transfers between devices, swap_x(): return lax.ppermute(value, 'ctx', [(i, i ^ 1) for i in range(8)])  45.6 us
    ppermute x5, starting transfers between devices, swap_x(): return lax.ppermute(value, 'ctx', [(i, i ^ 1) for i in range(8)])  26.3 us
    pallas_call x2, Pallas kernels, weights(): pl.pallas_call(functools.partial(weight_kernel, last, tuple((start for _,...  20.9 us
    ppermute x13, starting transfers between devices, along_y(): lax.ppermute(value, 'ctx', [(i, (i + 2 * step) % 8) for i in range(8)])  20.2 us
    ppermute x3, waiting for transfers between devices, along_z(): lax.ppermute(value, 'dp', [(i, (i + 4 * step) % 16) for i in range(16)])  13.5 us
    ppermute x13, waiting for transfers between devices, along_y(): lax.ppermute(value, 'ctx', [(i, (i + 2 * step) % 8) for i in range(8)])  11.4 us
    pallas_call x1, Pallas kernels, attention(): pl.pallas_call(functools.partial(attention_kernel, heads), out_shape=(jax...  10.6 us
    ppermute x7, starting transfers between devices, swap_cores(): return lax.ppermute(value, 'dp', [(i, i ^ 1) for i in range(16)])  8.94 us
  transfers between devices with their start and end apart: 28, of which 14 were waited for; matrix products, arithmetic and copies ran while one was open for 6% of the time, Pallas kernels for 11%

profile of v5, /device:TPU:1, one launch (start us, length us, event | category | flops | bytes accessed | tf_op | source)
XLA Modules:
  0.0 181.8 jit_solution(7256156942643625527)
XLA Ops:
  0.8 1.4 dynamic-slice_bitcast_fusion
  2.3 3.7 %collective-permute-start.4 = (bf16[4,512,128]{2,1,0:T(8,128)(2,1)S(1)}, bf16[4,512,128]{2,1,0:T(8,128)(2,1)S(1)}, u32[]{:S(2)}, u32[]{:S(2)}) collective-permute-start(bf16[4,512,128]{2,1,0:T(8,128)(2,1)S(1)} %pad_maximum_fusion.5), channel_id=1, source_target_pairs={{0,1},{1,0},{2,3},{3,2},{4,5},{5,4},{6,7},{7,6},{8,9},{9,8},{10,11... | collective-permute-start | bytes 1572872 | tf_op jit(solution)/shard_map/ppermute | solution.py:31
  5.9 0.8 slice.45
  6.8 1.0 dynamic-slice_select_fusion
  7.8 3.0 %collective-permute-start.1 = (bf16[528,128]{1,0:T(8,128)(2,1)S(1)}, bf16[528,128]{1,0:T(8,128)(2,1)S(1)}, u32[]{:S(2)}, u32[]{:S(2)}) collective-permute-start(bf16[528,128]{1,0:T(8,128)(2,1)S(1)} %get-tuple-element.84), channel_id=1, source_target_pairs={{0,4},{1,5},{2,6},{3,7},{4,0},{5,1},{6,2},{7,3},{8,12},{9,13},{10,... | collective-permute-start | bytes 405512 | tf_op jit(solution)/shard_map/ppermute | solution.py:27
  10.8 0.4 collective-permute-start
  11.2 2.3 %collective-permute-start.2 = (bf16[528,128]{1,0:T(8,128)(2,1)S(1)}, bf16[528,128]{1,0:T(8,128)(2,1)S(1)}, u32[]{:S(2)}, u32[]{:S(2)}) collective-permute-start(bf16[528,128]{1,0:T(8,128)(2,1)S(1)} %get-tuple-element.84), channel_id=1, source_target_pairs={{0,6},{1,7},{2,0},{3,1},{4,2},{5,3},{6,4},{7,5},{8,14},{9,15},{10,... | collective-permute-start | bytes 405512 | tf_op jit(solution)/shard_map/ppermute | solution.py:27
  13.6 3.7 %collective-permute-done = bf16[528,128]{1,0:T(8,128)(2,1)S(1)} collective-permute-done((bf16[528,128]{1,0:T(8,128)(2,1)S(1)}, bf16[528,128]{1,0:T(8,128)(2,1)S(1)}, u32[]{:S(2)}, u32[]{:S(2)}) %collective-permute-start) | collective-permute-done | bytes 135200 | tf_op jit(solution)/shard_map/ppermute | solution.py:27
  17.2 0.9 pad_maximum_fusion.4.mine_refs_0_
  18.3 2.0 %collective-permute-start.5 = (bf16[2,512,128]{2,1,0:T(8,128)(2,1)S(1)}, bf16[2,512,128]{2,1,0:T(8,128)(2,1)S(1)}, u32[]{:S(2)}, u32[]{:S(2)}) collective-permute-start(bf16[2,512,128]{2,1,0:T(8,128)(2,1)S(1)} %pad_maximum_fusion.6), channel_id=1, source_target_pairs={{0,2},{1,3},{2,4},{3,5},{4,6},{5,7},{6,0},{7,1},{8,10},{9,11},{10,... | collective-permute-start | bytes 786440 | tf_op jit(solution)/shard_map/ppermute | solution.py:27
  20.3 2.3 %collective-permute-start.6 = (bf16[2,512,128]{2,1,0:T(8,128)(2,1)S(1)}, bf16[2,512,128]{2,1,0:T(8,128)(2,1)S(1)}, u32[]{:S(2)}, u32[]{:S(2)}) collective-permute-start(bf16[2,512,128]{2,1,0:T(8,128)(2,1)S(1)} %pad_maximum_fusion.7), channel_id=1, source_target_pairs={{0,4},{1,5},{2,6},{3,7},{4,0},{5,1},{6,2},{7,3},{8,12},{9,13},{10,... | collective-permute-start | bytes 786440 | tf_op jit(solution)/shard_map/ppermute | solution.py:27
  22.9 2.3 %collective-permute-start.8 = (bf16[4,528,128]{2,1,0:T(8,128)(2,1)}, bf16[4,528,128]{2,1,0:T(8,128)(2,1)}, u32[]{:S(2)}, u32[]{:S(2)}) collective-permute-start(bf16[4,528,128]{2,1,0:T(8,128)(2,1)} %pad_maximum_fusion.4.mine_refs_0_), channel_id=1, source_target_pairs={{0,8},{8,0},{16,24},{24,16},{32,40},{40,32},{48,56},{56,48},{64,72... | collective-permute-start | bytes 1622024 | tf_op jit(solution)/shard_map/ppermute | solution.py:39
  25.2 7.0 %collective-permute-done.3.mine_refs_1_ = bf16[4,528,128]{2,1,0:T(8,128)(2,1)} collective-permute-done((bf16[4,528,128]{2,1,0:T(8,128)(2,1)}, bf16[4,528,128]{2,1,0:T(8,128)(2,1)}, u32[]{:S(2)}, u32[]{:S(2)}) %collective-permute-start.3) | collective-permute-done | bytes 540704 | tf_op jit(solution)/shard_map/ppermute | solution.py:31
  32.2 0.5 collective-permute-done.6.in_refs_2_
  32.7 0.5 collective-permute-done.7.in_refs_3_
  33.2 2.2 %collective-permute-start.9 = (bf16[4,528,128]{2,1,0:T(8,128)(2,1)}, bf16[4,528,128]{2,1,0:T(8,128)(2,1)}, u32[]{:S(2)}, u32[]{:S(2)}) collective-permute-start(bf16[4,528,128]{2,1,0:T(8,128)(2,1)} %collective-permute-done.3.mine_refs_1_), channel_id=1, source_target_pairs={{0,8},{8,0},{16,24},{24,16},{32,40},{40,32},{48,56},{56,48},{64,72... | collective-permute-start | bytes 1622024 | tf_op jit(solution)/shard_map/ppermute | solution.py:39
  35.4 0.7 fusion.3
  36.2 0.7 pad_maximum_fusion.9.in_refs_0_
  37.0 2.5 %shard_map.110.own_refs_0_ = bf16[128,4096]{1,0:T(8,128)(2,1)} custom-call(bf16[2,512,128]{2,1,0:T(8,128)(2,1)} %pad_maximum_fusion.9.in_refs_0_, bf16[2,512,128]{2,1,0:T(8,128)(2,1)} %copy-done.14, bf16[2,512,128]{2,1,0:T(8,128)(2,1)} %copy-done.15, bf16[2,512,128]{2,1,0:T(8,128)(2,1)} %copy-done.16), custom_call_target="tpu_custom_call" | custom-call | bytes 2097152 | tf_op jit(solution)/shard_map/pallas_call | solution.py:207
  39.5 3.8 %collective-permute-start.11 = (bf16[128,4096]{1,0:T(8,128)(2,1)}, bf16[128,4096]{1,0:T(8,128)(2,1)S(1)}, u32[]{:S(2)}, u32[]{:S(2)}) collective-permute-start(bf16[128,4096]{1,0:T(8,128)(2,1)} %shard_map.110.own_refs_0_), channel_id=1, source_target_pairs={{0,96},{8,104},{16,112},{24,120},{32,0},{40,8},{48,16},{56,24},{64... | collective-permute-start | bytes 3145736 | tf_op jit(solution)/shard_map/ppermute | solution.py:35
  43.3 0.7 convert_reduce_fusion
  44.1 0.6 pad_add_fusion.info_ref
  44.7 10.6 %shard_map.109 = (bf16[512,512]{1,0:T(8,128)(2,1)}, bf16[4,512,128]{2,1,0:T(8,128)(2,1)}, bf16[8,512,128]{2,1,0:T(8,128)(2,1)}, bf16[8,512,128]{2,1,0:T(8,128)(2,1)}) custom-call(s32[17]{0:T(128)} %pad_add_fusion.info_ref, bf16[512,512]{1,0:T(8,128)(2,1)} %q_ref.1, bf16[512,512]{1,0:T(8,128)(2,1)} %g_ref.1, ...), custom_call_target="tpu_custom_call" | custom-call | flops 10737418240 | bytes 8388608 | tf_op jit(solution)/shard_map/pallas_call | solution.py:167
  55.3 10.4 %collective-permute-done.11.own_refs_1_ = bf16[128,4096]{1,0:T(8,128)(2,1)S(1)} collective-permute-done((bf16[128,4096]{1,0:T(8,128)(2,1)}, bf16[128,4096]{1,0:T(8,128)(2,1)S(1)}, u32[]{:S(2)}, u32[]{:S(2)}) %collective-permute-start.11) | collective-permute-done | bytes 1048608 | tf_op jit(solution)/shard_map/ppermute | solution.py:35
  65.6 3.1 %collective-permute-done.10.own_refs_3_ = bf16[128,4096]{1,0:T(8,128)(2,1)} collective-permute-done((bf16[128,4096]{1,0:T(8,128)(2,1)}, bf16[128,4096]{1,0:T(8,128)(2,1)}, u32[]{:S(2)}, u32[]{:S(2)}) %collective-permute-start.10) | collective-permute-done | bytes 1048608 | tf_op jit(solution)/shard_map/ppermute | solution.py:35
  68.7 1.6 collective-permute-start.13
  70.4 3.9 %collective-permute-done.13 = bf16[8,512,128]{2,1,0:T(8,128)(2,1)S(1)} collective-permute-done((bf16[8,512,128]{2,1,0:T(8,128)(2,1)}, bf16[8,512,128]{2,1,0:T(8,128)(2,1)S(1)}, u32[]{:S(2)}, u32[]{:S(2)}) %collective-permute-start.13) | collective-permute-done | bytes 1048608 | tf_op jit(solution)/shard_map/ppermute | solution.py:39
  74.5 1.5 add_convert_fusion
  76.2 5.3 %collective-permute-start.16 = (bf16[6,512,128]{2,1,0:T(8,128)(2,1)S(1)}, bf16[6,512,128]{2,1,0:T(8,128)(2,1)S(1)}, u32[]{:S(2)}, u32[]{:S(2)}) collective-permute-start(bf16[6,512,128]{2,1,0:T(8,128)(2,1)S(1)} %get-tuple-element.77), channel_id=1, source_target_pairs={{0,6},{1,7},{2,0},{3,1},{4,2},{5,3},{6,4},{7,5},{8,14},{9,15},{10,... | collective-permute-start | bytes 2359304 | tf_op jit(solution)/shard_map/ppermute | solution.py:27
  81.5 11.2 %collective-permute-start.18 = (bf16[4,512,128]{2,1,0:T(8,128)(2,1)S(1)}, bf16[4,512,128]{2,1,0:T(8,128)(2,1)S(1)}, u32[]{:S(2)}, u32[]{:S(2)}) collective-permute-start(bf16[4,512,128]{2,1,0:T(8,128)(2,1)S(1)} %copy-done.1), channel_id=1, source_target_pairs={{0,1},{1,0},{2,3},{3,2},{4,5},{5,4},{6,7},{7,6},{8,9},{9,8},{10,11... | collective-permute-start | bytes 1572872 | tf_op jit(solution)/shard_map/ppermute | solution.py:31
  92.7 1.7 collective-permute-start.17
  94.4 10.0 %collective-permute-done.18.grad_refs_3_ = bf16[4,512,128]{2,1,0:T(8,128)(2,1)S(1)} collective-permute-done((bf16[4,512,128]{2,1,0:T(8,128)(2,1)S(1)}, bf16[4,512,128]{2,1,0:T(8,128)(2,1)S(1)}, u32[]{:S(2)}, u32[]{:S(2)}) %collective-permute-start.18) | collective-permute-done | bytes 524320 | tf_op jit(solution)/shard_map/ppermute | solution.py:31
  104.4 1.2 collective-permute-start.22
  105.7 1.0 collective-permute-done.15.grad_refs_1_
  106.8 1.5 collective-permute-start.21
  108.4 1.1 pad_maximum_fusion
  109.4 0.4 collective-permute-start.23
  109.8 1.1 pad_maximum_fusion.1
  110.9 11.3 %collective-permute-start.24 = (bf16[8,512,128]{2,1,0:T(8,128)(2,1)}, bf16[8,512,128]{2,1,0:T(8,128)(2,1)}, u32[]{:S(2)}, u32[]{:S(2)}) collective-permute-start(bf16[8,512,128]{2,1,0:T(8,128)(2,1)} %pad_maximum_fusion.1), channel_id=1, source_target_pairs={{0,1},{1,0},{2,3},{3,2},{4,5},{5,4},{6,7},{7,6},{8,9},{9,8},{10,11... | collective-permute-start | bytes 3145736 | tf_op jit(solution)/shard_map/ppermute | solution.py:31
  122.5 28.6 %collective-permute-done.20 = bf16[2,512,128]{2,1,0:T(8,128)(2,1)S(1)} collective-permute-done((bf16[2,512,128]{2,1,0:T(8,128)(2,1)S(1)}, bf16[2,512,128]{2,1,0:T(8,128)(2,1)S(1)}, u32[]{:S(2)}, u32[]{:S(2)}) %collective-permute-start.20) | collective-permute-done | bytes 262176 | tf_op jit(solution)/shard_map/ppermute | solution.py:31
  151.2 0.8 collective-permute-start.27
  152.0 1.0 collective-permute-start.26
  153.0 0.8 collective-permute-start.25
  153.7 0.6 pad_add_fusion.1.place_ref
  154.4 7.4 %shard_map.111.rest_0_ = f32[1024,512]{1,0:T(8,128)} custom-call(s32[2]{0:T(128)} %pad_add_fusion.1.place_ref, bf16[128,4096]{1,0:T(8,128)(2,1)} %shard_map.110.own_refs_0_, bf16[128,4096]{1,0:T(8,128)(2,1)} %copy-done.3, bf16[128,4096]{1,0:T(8,128)(2,1)} %copy-done.4, bf16[128,4096]{1,0:T(8,128)(2,1)} %collective-permute-done.10.own_refs_3_, ...), custom_call_target="tpu_custom_call" | custom-call | flops 2147483648 | bytes 10485760 | tf_op jit(solution)/shard_map/pallas_call | solution.py:348
  161.8 5.5 %collective-permute-done.25.rest_1__1_ = bf16[2,512,128]{2,1,0:T(8,128)(2,1)S(1)} collective-permute-done((bf16[2,512,128]{2,1,0:T(8,128)(2,1)S(1)}, bf16[2,512,128]{2,1,0:T(8,128)(2,1)S(1)}, u32[]{:S(2)}, u32[]{:S(2)}) %collective-permute-start.25) | collective-permute-done | bytes 262176 | tf_op jit(solution)/shard_map/ppermute | solution.py:27
  167.3 0.7 copy-done.13
  168.1 13.6 %shard_map.112 = (f32[1024,512]{1,0:T(8,128)}, f32[64,1024]{1,0:T(8,128)}, f32[64,1024]{1,0:T(8,128)}, bf16[64,512]{1,0:T(8,128)(2,1)}, bf16[64,512]{1,0:T(8,128)(2,1)}) custom-call(s32[2]{0:T(128)} %pad_add_fusion.1.place_ref, bf16[128,4096]{1,0:T(8,128)(2,1)} %shard_map.110.own_refs_0_, bf16[128,4096]{1,0:T(8,128)(2,1)} %copy-done.3, ...), custom_call_target="tpu_custom_call" | custom-call | flops 2147483648 | bytes 10485760 | tf_op jit(solution)/shard_map/pallas_call | solution.py:348
  (76 shorter events, 1.9 us)
Async XLA Ops:
  2.3 15.9 %collective-permute-start.4 = (bf16[4,512,128]{2,1,0:T(8,128)(2,1)S(1)}, bf16[4,512,128]{2,1,0:T(8,128)(2,1)S(1)}, u32[]{:S(2)}, u32[]{:S(2)}) collective-permute-start(bf16[4,512,128]{2,1,0:T(8,128)(2,1)S(1)} %pad_maximum_fusion.5), channel_id=1, source_target_pairs={{0,1},{1,0},{2,3},{3,2},{4,5},{5,4},{6,7},{7,6},{8,9},{9,8},{10,11... | collective-permute-start | bytes 1572872 | tf_op jit(solution)/shard_map/ppermute | solution.py:31
  7.8 5.7 %collective-permute-start.1 = (bf16[528,128]{1,0:T(8,128)(2,1)S(1)}, bf16[528,128]{1,0:T(8,128)(2,1)S(1)}, u32[]{:S(2)}, u32[]{:S(2)}) collective-permute-start(bf16[528,128]{1,0:T(8,128)(2,1)S(1)} %get-tuple-element.84), channel_id=1, source_target_pairs={{0,4},{1,5},{2,6},{3,7},{4,0},{5,1},{6,2},{7,3},{8,12},{9,13},{10,... | collective-permute-start | bytes 405512 | tf_op jit(solution)/shard_map/ppermute | solution.py:27
  10.8 6.4 %collective-permute-start = (bf16[528,128]{1,0:T(8,128)(2,1)S(1)}, bf16[528,128]{1,0:T(8,128)(2,1)S(1)}, u32[]{:S(2)}, u32[]{:S(2)}) collective-permute-start(bf16[528,128]{1,0:T(8,128)(2,1)S(1)} %get-tuple-element.84), channel_id=1, source_target_pairs={{0,2},{1,3},{2,4},{3,5},{4,6},{5,7},{6,0},{7,1},{8,10},{9,11},{10,... | collective-permute-start | bytes 405512 | tf_op jit(solution)/shard_map/ppermute | solution.py:27
  11.2 6.0 %collective-permute-start.2 = (bf16[528,128]{1,0:T(8,128)(2,1)S(1)}, bf16[528,128]{1,0:T(8,128)(2,1)S(1)}, u32[]{:S(2)}, u32[]{:S(2)}) collective-permute-start(bf16[528,128]{1,0:T(8,128)(2,1)S(1)} %get-tuple-element.84), channel_id=1, source_target_pairs={{0,6},{1,7},{2,0},{3,1},{4,2},{5,3},{6,4},{7,5},{8,14},{9,15},{10,... | collective-permute-start | bytes 405512 | tf_op jit(solution)/shard_map/ppermute | solution.py:27
  18.1 14.1 %collective-permute-start.3 = (bf16[4,528,128]{2,1,0:T(8,128)(2,1)}, bf16[4,528,128]{2,1,0:T(8,128)(2,1)}, u32[]{:S(2)}, u32[]{:S(2)}) collective-permute-start(bf16[4,528,128]{2,1,0:T(8,128)(2,1)} %pad_maximum_fusion.4.mine_refs_0_), channel_id=1, source_target_pairs={{0,1},{1,0},{2,3},{3,2},{4,5},{5,4},{6,7},{7,6},{8,9},{9,8},{10,11... | collective-permute-start | bytes 1622024 | tf_op jit(solution)/shard_map/ppermute | solution.py:31
  18.3 13.9 %collective-permute-start.5 = (bf16[2,512,128]{2,1,0:T(8,128)(2,1)S(1)}, bf16[2,512,128]{2,1,0:T(8,128)(2,1)S(1)}, u32[]{:S(2)}, u32[]{:S(2)}) collective-permute-start(bf16[2,512,128]{2,1,0:T(8,128)(2,1)S(1)} %pad_maximum_fusion.6), channel_id=1, source_target_pairs={{0,2},{1,3},{2,4},{3,5},{4,6},{5,7},{6,0},{7,1},{8,10},{9,11},{10,... | collective-permute-start | bytes 786440 | tf_op jit(solution)/shard_map/ppermute | solution.py:27
  20.3 12.4 %collective-permute-start.6 = (bf16[2,512,128]{2,1,0:T(8,128)(2,1)S(1)}, bf16[2,512,128]{2,1,0:T(8,128)(2,1)S(1)}, u32[]{:S(2)}, u32[]{:S(2)}) collective-permute-start(bf16[2,512,128]{2,1,0:T(8,128)(2,1)S(1)} %pad_maximum_fusion.7), channel_id=1, source_target_pairs={{0,4},{1,5},{2,6},{3,7},{4,0},{5,1},{6,2},{7,3},{8,12},{9,13},{10,... | collective-permute-start | bytes 786440 | tf_op jit(solution)/shard_map/ppermute | solution.py:27
  22.6 10.6 %collective-permute-start.7 = (bf16[2,512,128]{2,1,0:T(8,128)(2,1)S(1)}, bf16[2,512,128]{2,1,0:T(8,128)(2,1)S(1)}, u32[]{:S(2)}, u32[]{:S(2)}) collective-permute-start(bf16[2,512,128]{2,1,0:T(8,128)(2,1)S(1)} %pad_maximum_fusion.8), channel_id=1, source_target_pairs={{0,6},{1,7},{2,0},{3,1},{4,2},{5,3},{6,4},{7,5},{8,14},{9,15},{10,... | collective-permute-start | bytes 786440 | tf_op jit(solution)/shard_map/ppermute | solution.py:27
  22.9 21.8 %collective-permute-start.8 = (bf16[4,528,128]{2,1,0:T(8,128)(2,1)}, bf16[4,528,128]{2,1,0:T(8,128)(2,1)}, u32[]{:S(2)}, u32[]{:S(2)}) collective-permute-start(bf16[4,528,128]{2,1,0:T(8,128)(2,1)} %pad_maximum_fusion.4.mine_refs_0_), channel_id=1, source_target_pairs={{0,8},{8,0},{16,24},{24,16},{32,40},{40,32},{48,56},{56,48},{64,72... | collective-permute-start | bytes 1622024 | tf_op jit(solution)/shard_map/ppermute | solution.py:39
  32.2 4.7 %copy-start.14 = (bf16[2,512,128]{2,1,0:T(8,128)(2,1)}, bf16[2,512,128]{2,1,0:T(8,128)(2,1)S(1)}, u32[]{:S(2)}) copy-start(bf16[2,512,128]{2,1,0:T(8,128)(2,1)S(1)} %collective-permute-done.5.in_refs_1_) | copy-start | bytes 786436
  32.7 4.3 %copy-start.15 = (bf16[2,512,128]{2,1,0:T(8,128)(2,1)}, bf16[2,512,128]{2,1,0:T(8,128)(2,1)S(1)}, u32[]{:S(2)}) copy-start(bf16[2,512,128]{2,1,0:T(8,128)(2,1)S(1)} %collective-permute-done.6.in_refs_2_) | copy-start | bytes 786436
  33.2 3.8 %copy-start.16 = (bf16[2,512,128]{2,1,0:T(8,128)(2,1)}, bf16[2,512,128]{2,1,0:T(8,128)(2,1)S(1)}, u32[]{:S(2)}) copy-start(bf16[2,512,128]{2,1,0:T(8,128)(2,1)S(1)} %collective-permute-done.7.in_refs_3_) | copy-start | bytes 786436
  33.2 11.4 %collective-permute-start.9 = (bf16[4,528,128]{2,1,0:T(8,128)(2,1)}, bf16[4,528,128]{2,1,0:T(8,128)(2,1)}, u32[]{:S(2)}, u32[]{:S(2)}) collective-permute-start(bf16[4,528,128]{2,1,0:T(8,128)(2,1)} %collective-permute-done.3.mine_refs_1_), channel_id=1, source_target_pairs={{0,8},{8,0},{16,24},{24,16},{32,40},{40,32},{48,56},{56,48},{64,72... | collective-permute-start | bytes 1622024 | tf_op jit(solution)/shard_map/ppermute | solution.py:39
  39.4 15.8 %collective-permute-start.12 = (bf16[128,4096]{1,0:T(8,128)(2,1)}, bf16[128,4096]{1,0:T(8,128)(2,1)S(1)}, u32[]{:S(2)}, u32[]{:S(2)}) collective-permute-start(bf16[128,4096]{1,0:T(8,128)(2,1)} %shard_map.110.own_refs_0_), channel_id=1, source_target_pairs={{0,8},{8,0},{16,24},{24,16},{32,40},{40,32},{48,56},{56,48},{64,72... | collective-permute-start | bytes 3145736 | tf_op jit(solution)/shard_map/ppermute | solution.py:39
  39.5 26.1 %collective-permute-start.11 = (bf16[128,4096]{1,0:T(8,128)(2,1)}, bf16[128,4096]{1,0:T(8,128)(2,1)S(1)}, u32[]{:S(2)}, u32[]{:S(2)}) collective-permute-start(bf16[128,4096]{1,0:T(8,128)(2,1)} %shard_map.110.own_refs_0_), channel_id=1, source_target_pairs={{0,96},{8,104},{16,112},{24,120},{32,0},{40,8},{48,16},{56,24},{64... | collective-permute-start | bytes 3145736 | tf_op jit(solution)/shard_map/ppermute | solution.py:35
  43.3 25.5 %collective-permute-start.10 = (bf16[128,4096]{1,0:T(8,128)(2,1)}, bf16[128,4096]{1,0:T(8,128)(2,1)}, u32[]{:S(2)}, u32[]{:S(2)}) collective-permute-start(bf16[128,4096]{1,0:T(8,128)(2,1)} %shard_map.110.own_refs_0_), channel_id=1, source_target_pairs={{0,32},{8,40},{16,48},{24,56},{32,64},{40,72},{48,80},{56,88},{64,... | collective-permute-start | bytes 3145736 | tf_op jit(solution)/shard_map/ppermute | solution.py:35
  44.6 25.7 %copy-start = (bf16[128,4096]{1,0:T(8,128)(2,1)S(1)}, bf16[128,4096]{1,0:T(8,128)(2,1)}, u32[]{:S(2)}) copy-start(bf16[128,4096]{1,0:T(8,128)(2,1)} %shard_map.110.own_refs_0_) | copy-start | bytes 3145732
  55.3 20.8 %copy-start.2 = (bf16[128,4096]{1,0:T(8,128)(2,1)}, bf16[128,4096]{1,0:T(8,128)(2,1)S(1)}, u32[]{:S(2)}) copy-start(bf16[128,4096]{1,0:T(8,128)(2,1)S(1)} %collective-permute-done.12.other_refs_0_) | copy-start | bytes 3145732
  65.6 38.7 %copy-start.3 = (bf16[128,4096]{1,0:T(8,128)(2,1)}, bf16[128,4096]{1,0:T(8,128)(2,1)S(1)}, u32[]{:S(2)}) copy-start(bf16[128,4096]{1,0:T(8,128)(2,1)S(1)} %collective-permute-done.11.own_refs_1_) | copy-start | bytes 3145732
  68.7 7.3 %copy-start.1 = (bf16[4,512,128]{2,1,0:T(8,128)(2,1)S(1)}, bf16[4,512,128]{2,1,0:T(8,128)(2,1)}, u32[]{:S(2)}) copy-start(bf16[4,512,128]{2,1,0:T(8,128)(2,1)} %get-tuple-element.46.grad_refs_0_) | copy-start | bytes 1572868
  68.7 5.6 %collective-permute-start.13 = (bf16[8,512,128]{2,1,0:T(8,128)(2,1)}, bf16[8,512,128]{2,1,0:T(8,128)(2,1)S(1)}, u32[]{:S(2)}, u32[]{:S(2)}) collective-permute-start(bf16[8,512,128]{2,1,0:T(8,128)(2,1)} %get-tuple-element.48), channel_id=1, source_target_pairs={{0,8},{8,0},{16,24},{24,16},{32,40},{40,32},{48,56},{56,48},{64,72... | collective-permute-start | bytes 3145736 | tf_op jit(solution)/shard_map/ppermute | solution.py:39
  70.4 4.1 %collective-permute-start.14 = (bf16[128,4096]{1,0:T(8,128)(2,1)}, bf16[128,4096]{1,0:T(8,128)(2,1)}, u32[]{:S(2)}, u32[]{:S(2)}) collective-permute-start(bf16[128,4096]{1,0:T(8,128)(2,1)} %collective-permute-done.10.own_refs_3_), channel_id=1, source_target_pairs={{0,8},{8,0},{16,24},{24,16},{32,40},{40,32},{48,56},{56,48},{64,72... | collective-permute-start | bytes 3145736 | tf_op jit(solution)/shard_map/ppermute | solution.py:39
  70.4 35.2 %collective-permute-start.19 = (bf16[128,4096]{1,0:T(8,128)(2,1)S(1)}, bf16[128,4096]{1,0:T(8,128)(2,1)S(1)}, u32[]{:S(2)}, u32[]{:S(2)}) collective-permute-start(bf16[128,4096]{1,0:T(8,128)(2,1)S(1)} %copy-done), channel_id=1, source_target_pairs={{0,64},{8,72},{16,80},{24,88},{32,96},{40,104},{48,112},{56,120},{... | collective-permute-start | bytes 3145736 | tf_op jit(solution)/shard_map/ppermute | solution.py:35
  76.2 29.5 %collective-permute-start.16 = (bf16[6,512,128]{2,1,0:T(8,128)(2,1)S(1)}, bf16[6,512,128]{2,1,0:T(8,128)(2,1)S(1)}, u32[]{:S(2)}, u32[]{:S(2)}) collective-permute-start(bf16[6,512,128]{2,1,0:T(8,128)(2,1)S(1)} %get-tuple-element.77), channel_id=1, source_target_pairs={{0,6},{1,7},{2,0},{3,1},{4,2},{5,3},{6,4},{7,5},{8,14},{9,15},{10,... | collective-permute-start | bytes 2359304 | tf_op jit(solution)/shard_map/ppermute | solution.py:27
  81.5 25.3 %collective-permute-start.15 = (bf16[6,512,128]{2,1,0:T(8,128)(2,1)S(1)}, bf16[6,512,128]{2,1,0:T(8,128)(2,1)S(1)}, u32[]{:S(2)}, u32[]{:S(2)}) collective-permute-start(bf16[6,512,128]{2,1,0:T(8,128)(2,1)S(1)} %get-tuple-element.78), channel_id=1, source_target_pairs={{0,2},{1,3},{2,4},{3,5},{4,6},{5,7},{6,0},{7,1},{8,10},{9,11},{10,... | collective-permute-start | bytes 2359304 | tf_op jit(solution)/shard_map/ppermute | solution.py:27
  81.5 22.9 %collective-permute-start.18 = (bf16[4,512,128]{2,1,0:T(8,128)(2,1)S(1)}, bf16[4,512,128]{2,1,0:T(8,128)(2,1)S(1)}, u32[]{:S(2)}, u32[]{:S(2)}) collective-permute-start(bf16[4,512,128]{2,1,0:T(8,128)(2,1)S(1)} %copy-done.1), channel_id=1, source_target_pairs={{0,1},{1,0},{2,3},{3,2},{4,5},{5,4},{6,7},{7,6},{8,9},{9,8},{10,11... | collective-permute-start | bytes 1572872 | tf_op jit(solution)/shard_map/ppermute | solution.py:31
  92.7 13.0 %collective-permute-start.17 = (bf16[2,512,128]{2,1,0:T(8,128)(2,1)S(1)}, bf16[2,512,128]{2,1,0:T(8,128)(2,1)S(1)}, u32[]{:S(2)}, u32[]{:S(2)}) collective-permute-start(bf16[2,512,128]{2,1,0:T(8,128)(2,1)S(1)} %get-tuple-element.74), channel_id=1, source_target_pairs={{0,4},{1,5},{2,6},{3,7},{4,0},{5,1},{6,2},{7,3},{8,12},{9,13},{10,... | collective-permute-start | bytes 786440 | tf_op jit(solution)/shard_map/ppermute | solution.py:27
  104.4 5.1 %copy-start.9 = (bf16[4,512,128]{2,1,0:T(8,128)(2,1)}, bf16[4,512,128]{2,1,0:T(8,128)(2,1)S(1)}, u32[]{:S(2)}) copy-start(bf16[4,512,128]{2,1,0:T(8,128)(2,1)S(1)} %collective-permute-done.18.grad_refs_3_) | copy-start | bytes 1572868
  104.4 18.1 %collective-permute-start.22 = (bf16[128,4096]{1,0:T(8,128)(2,1)S(1)}, bf16[128,4096]{1,0:T(8,128)(2,1)S(1)}, u32[]{:S(2)}, u32[]{:S(2)}) collective-permute-start(bf16[128,4096]{1,0:T(8,128)(2,1)S(1)} %collective-permute-done.11.own_refs_1_), channel_id=1, source_target_pairs={{0,8},{8,0},{16,24},{24,16},{32,40},{40,32},{48,56},{56,48},{64,72... | collective-permute-start | bytes 3145736 | tf_op jit(solution)/shard_map/ppermute | solution.py:39
  105.6 3.9 %copy-start.4 = (bf16[128,4096]{1,0:T(8,128)(2,1)}, bf16[128,4096]{1,0:T(8,128)(2,1)S(1)}, u32[]{:S(2)}) copy-start(bf16[128,4096]{1,0:T(8,128)(2,1)S(1)} %collective-permute-done.19.own_refs_2_) | copy-start | bytes 3145732
  105.7 16.5 %copy-start.7 = (bf16[6,512,128]{2,1,0:T(8,128)(2,1)}, bf16[6,512,128]{2,1,0:T(8,128)(2,1)S(1)}, u32[]{:S(2)}) copy-start(bf16[6,512,128]{2,1,0:T(8,128)(2,1)S(1)} %collective-permute-done.16.grad_refs_2_) | copy-start | bytes 2359300
  106.8 15.4 %copy-start.8 = (bf16[6,512,128]{2,1,0:T(8,128)(2,1)}, bf16[6,512,128]{2,1,0:T(8,128)(2,1)S(1)}, u32[]{:S(2)}) copy-start(bf16[6,512,128]{2,1,0:T(8,128)(2,1)S(1)} %collective-permute-done.15.grad_refs_1_) | copy-start | bytes 2359300
  106.8 44.3 %collective-permute-start.21 = (bf16[128,4096]{1,0:T(8,128)(2,1)S(1)}, bf16[128,4096]{1,0:T(8,128)(2,1)S(1)}, u32[]{:S(2)}, u32[]{:S(2)}) collective-permute-start(bf16[128,4096]{1,0:T(8,128)(2,1)S(1)} %collective-permute-done.19.own_refs_2_), channel_id=1, source_target_pairs={{0,8},{8,0},{16,24},{24,16},{32,40},{40,32},{48,56},{56,48},{64,72... | collective-permute-start | bytes 3145736 | tf_op jit(solution)/shard_map/ppermute | solution.py:39
  109.4 52.3 %collective-permute-start.23 = (bf16[8,512,128]{2,1,0:T(8,128)(2,1)}, bf16[8,512,128]{2,1,0:T(8,128)(2,1)}, u32[]{:S(2)}, u32[]{:S(2)}) collective-permute-start(bf16[8,512,128]{2,1,0:T(8,128)(2,1)} %pad_maximum_fusion), channel_id=1, source_target_pairs={{0,4},{1,5},{2,6},{3,7},{4,0},{5,1},{6,2},{7,3},{8,12},{9,13},{10,... | collective-permute-start | bytes 3145736 | tf_op jit(solution)/shard_map/ppermute | solution.py:27
  110.9 50.9 %collective-permute-start.24 = (bf16[8,512,128]{2,1,0:T(8,128)(2,1)}, bf16[8,512,128]{2,1,0:T(8,128)(2,1)}, u32[]{:S(2)}, u32[]{:S(2)}) collective-permute-start(bf16[8,512,128]{2,1,0:T(8,128)(2,1)} %pad_maximum_fusion.1), channel_id=1, source_target_pairs={{0,1},{1,0},{2,3},{3,2},{4,5},{5,4},{6,7},{7,6},{8,9},{9,8},{10,11... | collective-permute-start | bytes 3145736 | tf_op jit(solution)/shard_map/ppermute | solution.py:31
  122.3 28.7 %collective-permute-start.20 = (bf16[2,512,128]{2,1,0:T(8,128)(2,1)S(1)}, bf16[2,512,128]{2,1,0:T(8,128)(2,1)S(1)}, u32[]{:S(2)}, u32[]{:S(2)}) collective-permute-start(bf16[2,512,128]{2,1,0:T(8,128)(2,1)S(1)} %fusion.2), channel_id=1, source_target_pairs={{0,1},{1,0},{2,3},{3,2},{4,5},{5,4},{6,7},{7,6},{8,9},{9,8},{10,11... | collective-permute-start | bytes 786440 | tf_op jit(solution)/shard_map/ppermute | solution.py:31
  122.5 31.9 %copy-start.5 = (bf16[128,4096]{1,0:T(8,128)(2,1)}, bf16[128,4096]{1,0:T(8,128)(2,1)S(1)}, u32[]{:S(2)}) copy-start(bf16[128,4096]{1,0:T(8,128)(2,1)S(1)} %collective-permute-done.22.other_refs_1_) | copy-start | bytes 3145732
  151.1 3.3 %copy-start.6 = (bf16[128,4096]{1,0:T(8,128)(2,1)}, bf16[128,4096]{1,0:T(8,128)(2,1)S(1)}, u32[]{:S(2)}) copy-start(bf16[128,4096]{1,0:T(8,128)(2,1)S(1)} %collective-permute-done.21.other_refs_2_) | copy-start | bytes 3145732
  151.2 10.5 %copy-start.10 = (bf16[2,512,128]{2,1,0:T(8,128)(2,1)}, bf16[2,512,128]{2,1,0:T(8,128)(2,1)S(1)}, u32[]{:S(2)}) copy-start(bf16[2,512,128]{2,1,0:T(8,128)(2,1)S(1)} %add_convert_fusion.1.rest_1__0_) | copy-start | bytes 786436
  151.2 10.6 %collective-permute-start.27 = (bf16[2,512,128]{2,1,0:T(8,128)(2,1)S(1)}, bf16[2,512,128]{2,1,0:T(8,128)(2,1)S(1)}, u32[]{:S(2)}, u32[]{:S(2)}) collective-permute-start(bf16[2,512,128]{2,1,0:T(8,128)(2,1)S(1)} %add_convert_fusion.1.rest_1__0_), channel_id=1, source_target_pairs={{0,6},{1,7},{2,0},{3,1},{4,2},{5,3},{6,4},{7,5},{8,14},{9,15},{10,... | collective-permute-start | bytes 786440 | tf_op jit(solution)/shard_map/ppermute | solution.py:27
  152.0 9.8 %collective-permute-start.26 = (bf16[2,512,128]{2,1,0:T(8,128)(2,1)S(1)}, bf16[2,512,128]{2,1,0:T(8,128)(2,1)S(1)}, u32[]{:S(2)}, u32[]{:S(2)}) collective-permute-start(bf16[2,512,128]{2,1,0:T(8,128)(2,1)S(1)} %add_convert_fusion.1.rest_1__0_), channel_id=1, source_target_pairs={{0,4},{1,5},{2,6},{3,7},{4,0},{5,1},{6,2},{7,3},{8,12},{9,13},{10,... | collective-permute-start | bytes 786440 | tf_op jit(solution)/shard_map/ppermute | solution.py:27
  153.0 14.4 %collective-permute-start.25 = (bf16[2,512,128]{2,1,0:T(8,128)(2,1)S(1)}, bf16[2,512,128]{2,1,0:T(8,128)(2,1)S(1)}, u32[]{:S(2)}, u32[]{:S(2)}) collective-permute-start(bf16[2,512,128]{2,1,0:T(8,128)(2,1)S(1)} %add_convert_fusion.1.rest_1__0_), channel_id=1, source_target_pairs={{0,2},{1,3},{2,4},{3,5},{4,6},{5,7},{6,0},{7,1},{8,10},{9,11},{10,... | collective-permute-start | bytes 786440 | tf_op jit(solution)/shard_map/ppermute | solution.py:27
  161.8 5.6 %copy-start.11 = (bf16[2,512,128]{2,1,0:T(8,128)(2,1)}, bf16[2,512,128]{2,1,0:T(8,128)(2,1)S(1)}, u32[]{:S(2)}) copy-start(bf16[2,512,128]{2,1,0:T(8,128)(2,1)S(1)} %collective-permute-done.27.rest_1__3_) | copy-start | bytes 786436
  161.8 5.5 %copy-start.12 = (bf16[2,512,128]{2,1,0:T(8,128)(2,1)}, bf16[2,512,128]{2,1,0:T(8,128)(2,1)S(1)}, u32[]{:S(2)}) copy-start(bf16[2,512,128]{2,1,0:T(8,128)(2,1)S(1)} %collective-permute-done.26.rest_1__2_) | copy-start | bytes 786436
  167.3 0.7 copy-start.13

commit v6 on v5

--- a/solution.py
+++ b/solution.py
@@ -392,16 +392,14 @@
     column_other = swap_cores(column)
     pairs = [jnp.stack([block(dy, 0), from_x[dy]]) for dy in range(4)]
     moved = [along_y(pairs[dy], dy) for dy in range(1, 4)]
-    partner_column, *moved = lax.optimization_barrier((partner_column, *moved))
-    pairs = [pairs[0]] + moved
+    info = column[:, count, :2].reshape(8).astype(jnp.int32)
+    partner_column, info, place, kept, *moved = lax.optimization_barrier(
+        (partner_column, info, place, pairs[0], *moved)
+    )
+    pairs = [kept] + moved
     partner_other = swap_cores(partner_column)
-    info = jnp.concatenate(
-        [
-            column[:, count, :2].reshape(8).astype(jnp.int32),
-            partner_column[:, count, :2].reshape(8).astype(jnp.int32),
-            member.astype(jnp.int32)[None],
-        ]
-    )
+    partner_info = partner_column[:, count, :2].reshape(8).astype(jnp.int32)
+    info = jnp.concatenate([info, partner_info, place[:1]])
     slab_own = turn(pairs)
     slab_back, slab_ahead = along_z(slab_own, 1), along_z(slab_own, 3)
     own_other = swap_cores(slab_own)
@@ -430,10 +428,13 @@
         rows_y = rows_y + term.astype(jnp.float32)
     rows_y = rows_y.astype(jnp.bfloat16)
     rows_x = swap_x(rows_y)
-    from_x13 = swap_x(jnp.concatenate([from_1[:heads], from_3[:heads]]))
     from_2 = along_y(jnp.concatenate([grad_heads, from_x]), 2)
     far_other, ahead_other = swap_cores(slab_far), swap_cores(slab_ahead)
-    rows_x, far_other, ahead_other = lax.optimization_barrier((rows_x, far_other, ahead_other))
+    to_x = jnp.concatenate([from_1[:heads], from_3[:heads]])
+    rows_x, far_other, ahead_other, to_x = lax.optimization_barrier(
+        (rows_x, far_other, ahead_other, to_x)
+    )
+    from_x13 = swap_x(to_x)
     both = (rows_y.astype(jnp.float32) + rows_x.astype(jnp.float32)[::-1]).astype(jnp.bfloat16)
     shared = [both] + by_source(*to_all_y(both))
 

time: 181 us -> 169 us (0.934)
  waiting for transfers between devices: 74.6 us -> 46.7 us
  Pallas kernels: 34 us -> 51.2 us
    ppermute x5, waiting for transfers between devices: 45.6 us -> 19 us  [swap_x(): return lax.ppermute(value, 'ctx', [(i, i ^ 1) for i in range(8)])]
    pallas_call x1, Pallas kernels: 10.6 us -> 27.8 us  [attention(): pl.pallas_call(functools.partial(attention_kernel, heads), out_shape=(jax...]
    ppermute x13, waiting for transfers between devices: 11.4 us -> 25.1 us  [along_y(): lax.ppermute(value, 'ctx', [(i, (i + 2 * step) % 8) for i in range(8)])]
    ppermute x3, waiting for transfers between devices: 13.5 us -> 0.01 us  [along_z(): lax.ppermute(value, 'dp', [(i, (i + 4 * step) % 16) for i in range(16)])]
    ppermute x13, starting transfers between devices: 20.2 us -> 16.2 us  [along_y(): lax.ppermute(value, 'ctx', [(i, (i + 2 * step) % 8) for i in range(8)])]
    ppermute x5, starting transfers between devices: 26.3 us -> 29.3 us  [swap_x(): return lax.ppermute(value, 'ctx', [(i, i ^ 1) for i in range(8)])]
  transfers between devices with their start and end apart: 28 -> 28, of which waited for: 14 -> 13; matrix products, arithmetic and copies ran while one was open for 6% -> 6% of each run, Pallas kernels for 11% -> 22%
where the time goes in v6:
time: 169 us; the launch traced here: 171 us
  starting transfers between devices  59 us (35%)
  Pallas kernels  51.2 us (30%)
  waiting for transfers between devices  46.7 us (28%)
  other arithmetic  8.97 us (5%)
  local copies, waits for them, and re-layouts  3.59 us (2%)
    ppermute x5, starting transfers between devices, swap_x(): return lax.ppermute(value, 'ctx', [(i, i ^ 1) for i in range(8)])  29.3 us
    pallas_call x1, Pallas kernels, attention(): pl.pallas_call(functools.partial(attention_kernel, heads), out_shape=(jax...  27.8 us
    ppermute x13, waiting for transfers between devices, along_y(): lax.ppermute(value, 'ctx', [(i, (i + 2 * step) % 8) for i in range(8)])  25.1 us
    pallas_call x2, Pallas kernels, weights(): pl.pallas_call(functools.partial(weight_kernel, last, tuple((start for _,...  21 us
    ppermute x5, waiting for transfers between devices, swap_x(): return lax.ppermute(value, 'ctx', [(i, i ^ 1) for i in range(8)])  19 us
    ppermute x13, starting transfers between devices, along_y(): lax.ppermute(value, 'ctx', [(i, (i + 2 * step) % 8) for i in range(8)])  16.2 us
    ppermute x7, starting transfers between devices, swap_cores(): return lax.ppermute(value, 'dp', [(i, i ^ 1) for i in range(16)])  8.34 us
    ppermute x3, starting transfers between devices, along_z(): lax.ppermute(value, 'dp', [(i, (i + 4 * step) % 16) for i in range(16)])  5.21 us
  transfers between devices with their start and end apart: 28, of which 13 were waited for; matrix products, arithmetic and copies ran while one was open for 6% of the time, Pallas kernels for 22%

profile of v6, /device:TPU:1, one launch (start us, length us, event | category | flops | bytes accessed | tf_op | source)
XLA Modules:
  0.0 170.7 jit_solution(3511830450113373824)
XLA Ops:
  0.8 1.4 dynamic-slice_bitcast_fusion
  2.3 3.7 %collective-permute-start.4 = (bf16[4,512,128]{2,1,0:T(8,128)(2,1)S(1)}, bf16[4,512,128]{2,1,0:T(8,128)(2,1)S(1)}, u32[]{:S(2)}, u32[]{:S(2)}) collective-permute-start(bf16[4,512,128]{2,1,0:T(8,128)(2,1)S(1)} %pad_maximum_fusion.5), channel_id=1, source_target_pairs={{0,1},{1,0},{2,3},{3,2},{4,5},{5,4},{6,7},{7,6},{8,9},{9,8},{10,11... | collective-permute-start | bytes 1572872 | tf_op jit(solution)/shard_map/ppermute | solution.py:31
  5.9 0.8 slice.48
  6.8 1.0 dynamic-slice_select_fusion
  7.8 3.0 %collective-permute-start.1 = (bf16[528,128]{1,0:T(8,128)(2,1)S(1)}, bf16[528,128]{1,0:T(8,128)(2,1)S(1)}, u32[]{:S(2)}, u32[]{:S(2)}) collective-permute-start(bf16[528,128]{1,0:T(8,128)(2,1)S(1)} %get-tuple-element.92), channel_id=1, source_target_pairs={{0,4},{1,5},{2,6},{3,7},{4,0},{5,1},{6,2},{7,3},{8,12},{9,13},{10,... | collective-permute-start | bytes 405512 | tf_op jit(solution)/shard_map/ppermute | solution.py:27
  10.8 0.4 collective-permute-start
  11.2 2.3 %collective-permute-start.2 = (bf16[528,128]{1,0:T(8,128)(2,1)S(1)}, bf16[528,128]{1,0:T(8,128)(2,1)S(1)}, u32[]{:S(2)}, u32[]{:S(2)}) collective-permute-start(bf16[528,128]{1,0:T(8,128)(2,1)S(1)} %get-tuple-element.92), channel_id=1, source_target_pairs={{0,6},{1,7},{2,0},{3,1},{4,2},{5,3},{6,4},{7,5},{8,14},{9,15},{10,... | collective-permute-start | bytes 405512 | tf_op jit(solution)/shard_map/ppermute | solution.py:27
  13.6 3.7 %collective-permute-done = bf16[528,128]{1,0:T(8,128)(2,1)S(1)} collective-permute-done((bf16[528,128]{1,0:T(8,128)(2,1)S(1)}, bf16[528,128]{1,0:T(8,128)(2,1)S(1)}, u32[]{:S(2)}, u32[]{:S(2)}) %collective-permute-start) | collective-permute-done | bytes 135200 | tf_op jit(solution)/shard_map/ppermute | solution.py:27
  17.2 0.9 pad_maximum_fusion.4.mine_refs_0_
  18.3 2.0 %collective-permute-start.5 = (bf16[2,512,128]{2,1,0:T(8,128)(2,1)S(1)}, bf16[2,512,128]{2,1,0:T(8,128)(2,1)S(1)}, u32[]{:S(2)}, u32[]{:S(2)}) collective-permute-start(bf16[2,512,128]{2,1,0:T(8,128)(2,1)S(1)} %pad_maximum_fusion.7), channel_id=1, source_target_pairs={{0,2},{1,3},{2,4},{3,5},{4,6},{5,7},{6,0},{7,1},{8,10},{9,11},{10,... | collective-permute-start | bytes 786440 | tf_op jit(solution)/shard_map/ppermute | solution.py:27
  20.3 2.3 %collective-permute-start.6 = (bf16[2,512,128]{2,1,0:T(8,128)(2,1)S(1)}, bf16[2,512,128]{2,1,0:T(8,128)(2,1)S(1)}, u32[]{:S(2)}, u32[]{:S(2)}) collective-permute-start(bf16[2,512,128]{2,1,0:T(8,128)(2,1)S(1)} %pad_maximum_fusion.8), channel_id=1, source_target_pairs={{0,4},{1,5},{2,6},{3,7},{4,0},{5,1},{6,2},{7,3},{8,12},{9,13},{10,... | collective-permute-start | bytes 786440 | tf_op jit(solution)/shard_map/ppermute | solution.py:27
  23.0 2.3 %collective-permute-start.8 = (bf16[4,528,128]{2,1,0:T(8,128)(2,1)}, bf16[4,528,128]{2,1,0:T(8,128)(2,1)}, u32[]{:S(2)}, u32[]{:S(2)}) collective-permute-start(bf16[4,528,128]{2,1,0:T(8,128)(2,1)} %pad_maximum_fusion.4.mine_refs_0_), channel_id=1, source_target_pairs={{0,8},{8,0},{16,24},{24,16},{32,40},{40,32},{48,56},{56,48},{64,72... | collective-permute-start | bytes 1622024 | tf_op jit(solution)/shard_map/ppermute | solution.py:39
  25.3 0.7 fusion.3
  26.1 0.7 pad_maximum_fusion.6.in_refs_0_
  26.8 5.4 %collective-permute-done.3.mine_refs_1_ = bf16[4,528,128]{2,1,0:T(8,128)(2,1)} collective-permute-done((bf16[4,528,128]{2,1,0:T(8,128)(2,1)}, bf16[4,528,128]{2,1,0:T(8,128)(2,1)}, u32[]{:S(2)}, u32[]{:S(2)}) %collective-permute-start.3) | collective-permute-done | bytes 540704 | tf_op jit(solution)/shard_map/ppermute | solution.py:31
  32.2 0.5 collective-permute-done.6.in_refs_2_
  32.7 0.5 collective-permute-done.7.in_refs_3_
  33.2 2.2 %collective-permute-start.9 = (bf16[4,528,128]{2,1,0:T(8,128)(2,1)}, bf16[4,528,128]{2,1,0:T(8,128)(2,1)}, u32[]{:S(2)}, u32[]{:S(2)}) collective-permute-start(bf16[4,528,128]{2,1,0:T(8,128)(2,1)} %collective-permute-done.3.mine_refs_1_), channel_id=1, source_target_pairs={{0,8},{8,0},{16,24},{24,16},{32,40},{40,32},{48,56},{56,48},{64,72... | collective-permute-start | bytes 1622024 | tf_op jit(solution)/shard_map/ppermute | solution.py:39
  35.4 2.5 %shard_map.110.own_refs_0_ = bf16[128,4096]{1,0:T(8,128)(2,1)} custom-call(bf16[2,512,128]{2,1,0:T(8,128)(2,1)} %pad_maximum_fusion.6.in_refs_0_, bf16[2,512,128]{2,1,0:T(8,128)(2,1)} %copy-done.14, bf16[2,512,128]{2,1,0:T(8,128)(2,1)} %copy-done.15, bf16[2,512,128]{2,1,0:T(8,128)(2,1)} %copy-done.16), custom_call_target="tpu_custom_call" | custom-call | bytes 2097152 | tf_op jit(solution)/shard_map/pallas_call | solution.py:207
  37.9 0.7 collective-permute-start.12
  38.6 3.8 %collective-permute-start.11 = (bf16[128,4096]{1,0:T(8,128)(2,1)}, bf16[128,4096]{1,0:T(8,128)(2,1)S(1)}, u32[]{:S(2)}, u32[]{:S(2)}) collective-permute-start(bf16[128,4096]{1,0:T(8,128)(2,1)} %shard_map.110.own_refs_0_), channel_id=1, source_target_pairs={{0,96},{8,104},{16,112},{24,120},{32,0},{40,8},{48,16},{56,24},{64... | collective-permute-start | bytes 3145736 | tf_op jit(solution)/shard_map/ppermute | solution.py:35
  42.4 0.7 convert_reduce_fusion
  43.2 0.6 pad_add_fusion.1.info_ref
  43.8 27.8 %shard_map.109 = (bf16[512,512]{1,0:T(8,128)(2,1)}, bf16[4,512,128]{2,1,0:T(8,128)(2,1)}, bf16[8,512,128]{2,1,0:T(8,128)(2,1)}, bf16[8,512,128]{2,1,0:T(8,128)(2,1)}) custom-call(s32[17]{0:T(128)} %pad_add_fusion.1.info_ref, bf16[512,512]{1,0:T(8,128)(2,1)} %q_ref.1, bf16[512,512]{1,0:T(8,128)(2,1)} %g_ref.1, ...), custom_call_target="tpu_custom_call" | custom-call | flops 10737418240 | bytes 8388608 | tf_op jit(solution)/shard_map/pallas_call | solution.py:167
  72.2 1.4 collective-permute-start.19
  73.7 0.9 collective-permute-done.13
  74.6 1.6 collective-permute-done.14.other_refs_3_
  76.2 1.5 add_convert_fusion
  78.2 1.5 collective-permute-start.15
  79.6 11.3 %collective-permute-start.18 = (bf16[4,512,128]{2,1,0:T(8,128)(2,1)S(1)}, bf16[4,512,128]{2,1,0:T(8,128)(2,1)S(1)}, u32[]{:S(2)}, u32[]{:S(2)}) collective-permute-start(bf16[4,512,128]{2,1,0:T(8,128)(2,1)S(1)} %copy-done.1), channel_id=1, source_target_pairs={{0,1},{1,0},{2,3},{3,2},{4,5},{5,4},{6,7},{7,6},{8,9},{9,8},{10,11... | collective-permute-start | bytes 1572872 | tf_op jit(solution)/shard_map/ppermute | solution.py:31
  91.0 11.5 %collective-permute-done.18.grad_refs_3_ = bf16[4,512,128]{2,1,0:T(8,128)(2,1)S(1)} collective-permute-done((bf16[4,512,128]{2,1,0:T(8,128)(2,1)S(1)}, bf16[4,512,128]{2,1,0:T(8,128)(2,1)S(1)}, u32[]{:S(2)}, u32[]{:S(2)}) %collective-permute-start.18) | collective-permute-done | bytes 524320 | tf_op jit(solution)/shard_map/ppermute | solution.py:31
  102.4 1.4 collective-permute-start.22
  103.9 1.1 collective-permute-start.21
  105.3 11.4 %collective-permute-start.20 = (bf16[2,512,128]{2,1,0:T(8,128)(2,1)S(1)}, bf16[2,512,128]{2,1,0:T(8,128)(2,1)S(1)}, u32[]{:S(2)}, u32[]{:S(2)}) collective-permute-start(bf16[2,512,128]{2,1,0:T(8,128)(2,1)S(1)} %fusion.2), channel_id=1, source_target_pairs={{0,1},{1,0},{2,3},{3,2},{4,5},{5,4},{6,7},{7,6},{8,9},{9,8},{10,11... | collective-permute-start | bytes 786440 | tf_op jit(solution)/shard_map/ppermute | solution.py:31
  116.7 1.1 pad_maximum_fusion.1
  117.8 1.8 %collective-permute-start.23 = (bf16[8,512,128]{2,1,0:T(8,128)(2,1)}, bf16[8,512,128]{2,1,0:T(8,128)(2,1)}, u32[]{:S(2)}, u32[]{:S(2)}) collective-permute-start(bf16[8,512,128]{2,1,0:T(8,128)(2,1)} %pad_maximum_fusion.1), channel_id=1, source_target_pairs={{0,4},{1,5},{2,6},{3,7},{4,0},{5,1},{6,2},{7,3},{8,12},{9,13},{10,... | collective-permute-start | bytes 3145736 | tf_op jit(solution)/shard_map/ppermute | solution.py:27
  119.6 1.1 pad_maximum_fusion
  120.7 2.2 %collective-permute-done.20 = bf16[2,512,128]{2,1,0:T(8,128)(2,1)S(1)} collective-permute-done((bf16[2,512,128]{2,1,0:T(8,128)(2,1)S(1)}, bf16[2,512,128]{2,1,0:T(8,128)(2,1)S(1)}, u32[]{:S(2)}, u32[]{:S(2)}) %collective-permute-start.20) | collective-permute-done | bytes 262176 | tf_op jit(solution)/shard_map/ppermute | solution.py:31
  122.9 2.8 %collective-permute-start.24 = (bf16[8,512,128]{2,1,0:T(8,128)(2,1)}, bf16[8,512,128]{2,1,0:T(8,128)(2,1)S(1)}, u32[]{:S(2)}, u32[]{:S(2)}) collective-permute-start(bf16[8,512,128]{2,1,0:T(8,128)(2,1)} %pad_maximum_fusion), channel_id=1, source_target_pairs={{0,1},{1,0},{2,3},{3,2},{4,5},{5,4},{6,7},{7,6},{8,9},{9,8},{10,11... | collective-permute-start | bytes 3145736 | tf_op jit(solution)/shard_map/ppermute | solution.py:31
  125.8 1.0 collective-permute-start.27
  126.8 0.7 collective-permute-start.26
  127.5 0.8 collective-permute-start.25
  128.2 7.4 %shard_map.111.rest_0_ = f32[1024,512]{1,0:T(8,128)} custom-call(s32[2]{0:T(128)} %copy-done.17, bf16[128,4096]{1,0:T(8,128)(2,1)} %shard_map.110.own_refs_0_, bf16[128,4096]{1,0:T(8,128)(2,1)} %copy-done.3, bf16[128,4096]{1,0:T(8,128)(2,1)} %copy-done.4, bf16[128,4096]{1,0:T(8,128)(2,1)} %collective-permute-done.10.own_refs_3_, ...), custom_call_target="tpu_custom_call" | custom-call | flops 2147483648 | bytes 10485760 | tf_op jit(solution)/shard_map/pallas_call | solution.py:348
  135.6 7.9 %collective-permute-done.23.grad_refs_0_.grad_refs_2_ = bf16[8,512,128]{2,1,0:T(8,128)(2,1)} collective-permute-done((bf16[8,512,128]{2,1,0:T(8,128)(2,1)}, bf16[8,512,128]{2,1,0:T(8,128)(2,1)}, u32[]{:S(2)}, u32[]{:S(2)}) %collective-permute-start.23) | collective-permute-done | bytes 1048608 | tf_op jit(solution)/shard_map/ppermute | solution.py:27
  143.5 5.4 %collective-permute-done.27.rest_1__3_ = bf16[2,512,128]{2,1,0:T(8,128)(2,1)S(1)} collective-permute-done((bf16[2,512,128]{2,1,0:T(8,128)(2,1)S(1)}, bf16[2,512,128]{2,1,0:T(8,128)(2,1)S(1)}, u32[]{:S(2)}, u32[]{:S(2)}) %collective-permute-start.27) | collective-permute-done | bytes 262176 | tf_op jit(solution)/shard_map/ppermute | solution.py:27
  149.0 6.9 %collective-permute-done.25.rest_1__1_ = bf16[2,512,128]{2,1,0:T(8,128)(2,1)} collective-permute-done((bf16[2,512,128]{2,1,0:T(8,128)(2,1)S(1)}, bf16[2,512,128]{2,1,0:T(8,128)(2,1)}, u32[]{:S(2)}, u32[]{:S(2)}) %collective-permute-start.25) | collective-permute-done | bytes 262176 | tf_op jit(solution)/shard_map/ppermute | solution.py:27
  155.9 1.0 copy-done.7
  156.9 13.6 %shard_map.112 = (f32[1024,512]{1,0:T(8,128)}, f32[64,1024]{1,0:T(8,128)}, f32[64,1024]{1,0:T(8,128)}, bf16[64,512]{1,0:T(8,128)(2,1)}, bf16[64,512]{1,0:T(8,128)(2,1)}) custom-call(s32[2]{0:T(128)} %copy-done.17, bf16[128,4096]{1,0:T(8,128)(2,1)} %shard_map.110.own_refs_0_, bf16[128,4096]{1,0:T(8,128)(2,1)} %copy-done.3, bf16[128,4096]{1,0:T(8,128)(2,1)} %copy-done.4, ...), custom_call_target="tpu_custom_call" | custom-call | flops 2147483648 | bytes 10485760 | tf_op jit(solution)/shard_map/pallas_call | solution.py:348
  (78 shorter events, 2.5 us)
Async XLA Ops:
  2.3 15.9 %collective-permute-start.4 = (bf16[4,512,128]{2,1,0:T(8,128)(2,1)S(1)}, bf16[4,512,128]{2,1,0:T(8,128)(2,1)S(1)}, u32[]{:S(2)}, u32[]{:S(2)}) collective-permute-start(bf16[4,512,128]{2,1,0:T(8,128)(2,1)S(1)} %pad_maximum_fusion.5), channel_id=1, source_target_pairs={{0,1},{1,0},{2,3},{3,2},{4,5},{5,4},{6,7},{7,6},{8,9},{9,8},{10,11... | collective-permute-start | bytes 1572872 | tf_op jit(solution)/shard_map/ppermute | solution.py:31
  7.8 5.7 %collective-permute-start.1 = (bf16[528,128]{1,0:T(8,128)(2,1)S(1)}, bf16[528,128]{1,0:T(8,128)(2,1)S(1)}, u32[]{:S(2)}, u32[]{:S(2)}) collective-permute-start(bf16[528,128]{1,0:T(8,128)(2,1)S(1)} %get-tuple-element.92), channel_id=1, source_target_pairs={{0,4},{1,5},{2,6},{3,7},{4,0},{5,1},{6,2},{7,3},{8,12},{9,13},{10,... | collective-permute-start | bytes 405512 | tf_op jit(solution)/shard_map/ppermute | solution.py:27
  10.8 6.4 %collective-permute-start = (bf16[528,128]{1,0:T(8,128)(2,1)S(1)}, bf16[528,128]{1,0:T(8,128)(2,1)S(1)}, u32[]{:S(2)}, u32[]{:S(2)}) collective-permute-start(bf16[528,128]{1,0:T(8,128)(2,1)S(1)} %get-tuple-element.92), channel_id=1, source_target_pairs={{0,2},{1,3},{2,4},{3,5},{4,6},{5,7},{6,0},{7,1},{8,10},{9,11},{10,... | collective-permute-start | bytes 405512 | tf_op jit(solution)/shard_map/ppermute | solution.py:27
  11.2 6.0 %collective-permute-start.2 = (bf16[528,128]{1,0:T(8,128)(2,1)S(1)}, bf16[528,128]{1,0:T(8,128)(2,1)S(1)}, u32[]{:S(2)}, u32[]{:S(2)}) collective-permute-start(bf16[528,128]{1,0:T(8,128)(2,1)S(1)} %get-tuple-element.92), channel_id=1, source_target_pairs={{0,6},{1,7},{2,0},{3,1},{4,2},{5,3},{6,4},{7,5},{8,14},{9,15},{10,... | collective-permute-start | bytes 405512 | tf_op jit(solution)/shard_map/ppermute | solution.py:27
  18.1 14.1 %collective-permute-start.3 = (bf16[4,528,128]{2,1,0:T(8,128)(2,1)}, bf16[4,528,128]{2,1,0:T(8,128)(2,1)}, u32[]{:S(2)}, u32[]{:S(2)}) collective-permute-start(bf16[4,528,128]{2,1,0:T(8,128)(2,1)} %pad_maximum_fusion.4.mine_refs_0_), channel_id=1, source_target_pairs={{0,1},{1,0},{2,3},{3,2},{4,5},{5,4},{6,7},{7,6},{8,9},{9,8},{10,11... | collective-permute-start | bytes 1622024 | tf_op jit(solution)/shard_map/ppermute | solution.py:31
  18.3 13.9 %collective-permute-start.5 = (bf16[2,512,128]{2,1,0:T(8,128)(2,1)S(1)}, bf16[2,512,128]{2,1,0:T(8,128)(2,1)S(1)}, u32[]{:S(2)}, u32[]{:S(2)}) collective-permute-start(bf16[2,512,128]{2,1,0:T(8,128)(2,1)S(1)} %pad_maximum_fusion.7), channel_id=1, source_target_pairs={{0,2},{1,3},{2,4},{3,5},{4,6},{5,7},{6,0},{7,1},{8,10},{9,11},{10,... | collective-permute-start | bytes 786440 | tf_op jit(solution)/shard_map/ppermute | solution.py:27
  20.3 12.4 %collective-permute-start.6 = (bf16[2,512,128]{2,1,0:T(8,128)(2,1)S(1)}, bf16[2,512,128]{2,1,0:T(8,128)(2,1)S(1)}, u32[]{:S(2)}, u32[]{:S(2)}) collective-permute-start(bf16[2,512,128]{2,1,0:T(8,128)(2,1)S(1)} %pad_maximum_fusion.8), channel_id=1, source_target_pairs={{0,4},{1,5},{2,6},{3,7},{4,0},{5,1},{6,2},{7,3},{8,12},{9,13},{10,... | collective-permute-start | bytes 786440 | tf_op jit(solution)/shard_map/ppermute | solution.py:27
  22.6 10.6 %collective-permute-start.7 = (bf16[2,512,128]{2,1,0:T(8,128)(2,1)S(1)}, bf16[2,512,128]{2,1,0:T(8,128)(2,1)S(1)}, u32[]{:S(2)}, u32[]{:S(2)}) collective-permute-start(bf16[2,512,128]{2,1,0:T(8,128)(2,1)S(1)} %pad_maximum_fusion.9), channel_id=1, source_target_pairs={{0,6},{1,7},{2,0},{3,1},{4,2},{5,3},{6,4},{7,5},{8,14},{9,15},{10,... | collective-permute-start | bytes 786440 | tf_op jit(solution)/shard_map/ppermute | solution.py:27
  23.0 48.6 %copy-start.17 = (s32[2]{0:T(128)}, s32[2]{0:T(128)S(1)}, u32[]{:S(2)}) copy-start(s32[2]{0:T(128)S(1)} %pad_add_fusion.place_ref) | copy-start | bytes 28
  23.0 20.8 %collective-permute-start.8 = (bf16[4,528,128]{2,1,0:T(8,128)(2,1)}, bf16[4,528,128]{2,1,0:T(8,128)(2,1)}, u32[]{:S(2)}, u32[]{:S(2)}) collective-permute-start(bf16[4,528,128]{2,1,0:T(8,128)(2,1)} %pad_maximum_fusion.4.mine_refs_0_), channel_id=1, source_target_pairs={{0,8},{8,0},{16,24},{24,16},{32,40},{40,32},{48,56},{56,48},{64,72... | collective-permute-start | bytes 1622024 | tf_op jit(solution)/shard_map/ppermute | solution.py:39
  32.2 3.2 %copy-start.14 = (bf16[2,512,128]{2,1,0:T(8,128)(2,1)}, bf16[2,512,128]{2,1,0:T(8,128)(2,1)S(1)}, u32[]{:S(2)}) copy-start(bf16[2,512,128]{2,1,0:T(8,128)(2,1)S(1)} %collective-permute-done.5.in_refs_1_) | copy-start | bytes 786436
  32.7 2.7 %copy-start.15 = (bf16[2,512,128]{2,1,0:T(8,128)(2,1)}, bf16[2,512,128]{2,1,0:T(8,128)(2,1)S(1)}, u32[]{:S(2)}) copy-start(bf16[2,512,128]{2,1,0:T(8,128)(2,1)S(1)} %collective-permute-done.6.in_refs_2_) | copy-start | bytes 786436
  33.2 2.2 %copy-start.16 = (bf16[2,512,128]{2,1,0:T(8,128)(2,1)}, bf16[2,512,128]{2,1,0:T(8,128)(2,1)S(1)}, u32[]{:S(2)}) copy-start(bf16[2,512,128]{2,1,0:T(8,128)(2,1)S(1)} %collective-permute-done.7.in_refs_3_) | copy-start | bytes 786436
  33.2 10.6 %collective-permute-start.9 = (bf16[4,528,128]{2,1,0:T(8,128)(2,1)}, bf16[4,528,128]{2,1,0:T(8,128)(2,1)}, u32[]{:S(2)}, u32[]{:S(2)}) collective-permute-start(bf16[4,528,128]{2,1,0:T(8,128)(2,1)} %collective-permute-done.3.mine_refs_1_), channel_id=1, source_target_pairs={{0,8},{8,0},{16,24},{24,16},{32,40},{40,32},{48,56},{56,48},{64,72... | collective-permute-start | bytes 1622024 | tf_op jit(solution)/shard_map/ppermute | solution.py:39
  37.9 33.7 %collective-permute-start.12 = (bf16[128,4096]{1,0:T(8,128)(2,1)}, bf16[128,4096]{1,0:T(8,128)(2,1)S(1)}, u32[]{:S(2)}, u32[]{:S(2)}) collective-permute-start(bf16[128,4096]{1,0:T(8,128)(2,1)} %shard_map.110.own_refs_0_), channel_id=1, source_target_pairs={{0,8},{8,0},{16,24},{24,16},{32,40},{40,32},{48,56},{56,48},{64,72... | collective-permute-start | bytes 3145736 | tf_op jit(solution)/shard_map/ppermute | solution.py:39
  38.6 33.0 %collective-permute-start.11 = (bf16[128,4096]{1,0:T(8,128)(2,1)}, bf16[128,4096]{1,0:T(8,128)(2,1)S(1)}, u32[]{:S(2)}, u32[]{:S(2)}) collective-permute-start(bf16[128,4096]{1,0:T(8,128)(2,1)} %shard_map.110.own_refs_0_), channel_id=1, source_target_pairs={{0,96},{8,104},{16,112},{24,120},{32,0},{40,8},{48,16},{56,24},{64... | collective-permute-start | bytes 3145736 | tf_op jit(solution)/shard_map/ppermute | solution.py:35
  42.4 29.3 %collective-permute-start.10 = (bf16[128,4096]{1,0:T(8,128)(2,1)}, bf16[128,4096]{1,0:T(8,128)(2,1)}, u32[]{:S(2)}, u32[]{:S(2)}) collective-permute-start(bf16[128,4096]{1,0:T(8,128)(2,1)} %shard_map.110.own_refs_0_), channel_id=1, source_target_pairs={{0,32},{8,40},{16,48},{24,56},{32,64},{40,72},{48,80},{56,88},{64,... | collective-permute-start | bytes 3145736 | tf_op jit(solution)/shard_map/ppermute | solution.py:35
  43.8 28.4 %copy-start = (bf16[128,4096]{1,0:T(8,128)(2,1)S(1)}, bf16[128,4096]{1,0:T(8,128)(2,1)}, u32[]{:S(2)}) copy-start(bf16[128,4096]{1,0:T(8,128)(2,1)} %shard_map.110.own_refs_0_) | copy-start | bytes 3145732
  71.6 6.2 %copy-start.2 = (bf16[128,4096]{1,0:T(8,128)(2,1)}, bf16[128,4096]{1,0:T(8,128)(2,1)S(1)}, u32[]{:S(2)}) copy-start(bf16[128,4096]{1,0:T(8,128)(2,1)S(1)} %collective-permute-done.12.other_refs_0_) | copy-start | bytes 3145732
  71.6 30.8 %copy-start.3 = (bf16[128,4096]{1,0:T(8,128)(2,1)}, bf16[128,4096]{1,0:T(8,128)(2,1)S(1)}, u32[]{:S(2)}) copy-start(bf16[128,4096]{1,0:T(8,128)(2,1)S(1)} %collective-permute-done.11.own_refs_1_) | copy-start | bytes 3145732
  71.6 6.2 %copy-start.1 = (bf16[4,512,128]{2,1,0:T(8,128)(2,1)S(1)}, bf16[4,512,128]{2,1,0:T(8,128)(2,1)}, u32[]{:S(2)}) copy-start(bf16[4,512,128]{2,1,0:T(8,128)(2,1)} %get-tuple-element.53.grad_refs_0_) | copy-start | bytes 1572868
  71.7 3.0 %collective-permute-start.13 = (bf16[8,512,128]{2,1,0:T(8,128)(2,1)}, bf16[8,512,128]{2,1,0:T(8,128)(2,1)S(1)}, u32[]{:S(2)}, u32[]{:S(2)}) collective-permute-start(bf16[8,512,128]{2,1,0:T(8,128)(2,1)} %get-tuple-element.55), channel_id=1, source_target_pairs={{0,8},{8,0},{16,24},{24,16},{32,40},{40,32},{48,56},{56,48},{64,72... | collective-permute-start | bytes 3145736 | tf_op jit(solution)/shard_map/ppermute | solution.py:39
  72.0 4.2 %collective-permute-start.14 = (bf16[128,4096]{1,0:T(8,128)(2,1)}, bf16[128,4096]{1,0:T(8,128)(2,1)}, u32[]{:S(2)}, u32[]{:S(2)}) collective-permute-start(bf16[128,4096]{1,0:T(8,128)(2,1)} %collective-permute-done.10.own_refs_3_), channel_id=1, source_target_pairs={{0,8},{8,0},{16,24},{24,16},{32,40},{40,32},{48,56},{56,48},{64,72... | collective-permute-start | bytes 3145736 | tf_op jit(solution)/shard_map/ppermute | solution.py:39
  72.2 31.6 %collective-permute-start.19 = (bf16[128,4096]{1,0:T(8,128)(2,1)S(1)}, bf16[128,4096]{1,0:T(8,128)(2,1)S(1)}, u32[]{:S(2)}, u32[]{:S(2)}) collective-permute-start(bf16[128,4096]{1,0:T(8,128)(2,1)S(1)} %copy-done), channel_id=1, source_target_pairs={{0,64},{8,72},{16,80},{24,88},{32,96},{40,104},{48,112},{56,120},{... | collective-permute-start | bytes 3145736 | tf_op jit(solution)/shard_map/ppermute | solution.py:35
  77.9 25.9 %collective-permute-start.16 = (bf16[6,512,128]{2,1,0:T(8,128)(2,1)S(1)}, bf16[6,512,128]{2,1,0:T(8,128)(2,1)S(1)}, u32[]{:S(2)}, u32[]{:S(2)}) collective-permute-start(bf16[6,512,128]{2,1,0:T(8,128)(2,1)S(1)} %get-tuple-element.85), channel_id=1, source_target_pairs={{0,6},{1,7},{2,0},{3,1},{4,2},{5,3},{6,4},{7,5},{8,14},{9,15},{10,... | collective-permute-start | bytes 2359304 | tf_op jit(solution)/shard_map/ppermute | solution.py:27
  78.2 25.7 %collective-permute-start.15 = (bf16[6,512,128]{2,1,0:T(8,128)(2,1)S(1)}, bf16[6,512,128]{2,1,0:T(8,128)(2,1)S(1)}, u32[]{:S(2)}, u32[]{:S(2)}) collective-permute-start(bf16[6,512,128]{2,1,0:T(8,128)(2,1)S(1)} %get-tuple-element.86), channel_id=1, source_target_pairs={{0,2},{1,3},{2,4},{3,5},{4,6},{5,7},{6,0},{7,1},{8,10},{9,11},{10,... | collective-permute-start | bytes 2359304 | tf_op jit(solution)/shard_map/ppermute | solution.py:27
  79.6 22.8 %collective-permute-start.18 = (bf16[4,512,128]{2,1,0:T(8,128)(2,1)S(1)}, bf16[4,512,128]{2,1,0:T(8,128)(2,1)S(1)}, u32[]{:S(2)}, u32[]{:S(2)}) collective-permute-start(bf16[4,512,128]{2,1,0:T(8,128)(2,1)S(1)} %copy-done.1), channel_id=1, source_target_pairs={{0,1},{1,0},{2,3},{3,2},{4,5},{5,4},{6,7},{7,6},{8,9},{9,8},{10,11... | collective-permute-start | bytes 1572872 | tf_op jit(solution)/shard_map/ppermute | solution.py:31
  91.0 12.9 %collective-permute-start.17 = (bf16[2,512,128]{2,1,0:T(8,128)(2,1)S(1)}, bf16[2,512,128]{2,1,0:T(8,128)(2,1)S(1)}, u32[]{:S(2)}, u32[]{:S(2)}) collective-permute-start(bf16[2,512,128]{2,1,0:T(8,128)(2,1)S(1)} %get-tuple-element.82), channel_id=1, source_target_pairs={{0,4},{1,5},{2,6},{3,7},{4,0},{5,1},{6,2},{7,3},{8,12},{9,13},{10,... | collective-permute-start | bytes 786440 | tf_op jit(solution)/shard_map/ppermute | solution.py:27
  102.4 15.3 %copy-start.10 = (bf16[4,512,128]{2,1,0:T(8,128)(2,1)}, bf16[4,512,128]{2,1,0:T(8,128)(2,1)S(1)}, u32[]{:S(2)}) copy-start(bf16[4,512,128]{2,1,0:T(8,128)(2,1)S(1)} %collective-permute-done.18.grad_refs_3_) | copy-start | bytes 1572868
  102.4 18.2 %collective-permute-start.22 = (bf16[128,4096]{1,0:T(8,128)(2,1)S(1)}, bf16[128,4096]{1,0:T(8,128)(2,1)S(1)}, u32[]{:S(2)}, u32[]{:S(2)}) collective-permute-start(bf16[128,4096]{1,0:T(8,128)(2,1)S(1)} %collective-permute-done.11.own_refs_1_), channel_id=1, source_target_pairs={{0,8},{8,0},{16,24},{24,16},{32,40},{40,32},{48,56},{56,48},{64,72... | collective-permute-start | bytes 3145736 | tf_op jit(solution)/shard_map/ppermute | solution.py:39
  103.9 13.9 %copy-start.4 = (bf16[128,4096]{1,0:T(8,128)(2,1)}, bf16[128,4096]{1,0:T(8,128)(2,1)S(1)}, u32[]{:S(2)}) copy-start(bf16[128,4096]{1,0:T(8,128)(2,1)S(1)} %collective-permute-done.19.own_refs_2_) | copy-start | bytes 3145732
  103.9 1.4 copy-start.8
  103.9 1.4 copy-start.9
  103.9 18.9 %collective-permute-start.21 = (bf16[128,4096]{1,0:T(8,128)(2,1)S(1)}, bf16[128,4096]{1,0:T(8,128)(2,1)S(1)}, u32[]{:S(2)}, u32[]{:S(2)}) collective-permute-start(bf16[128,4096]{1,0:T(8,128)(2,1)S(1)} %collective-permute-done.19.own_refs_2_), channel_id=1, source_target_pairs={{0,8},{8,0},{16,24},{24,16},{32,40},{40,32},{48,56},{56,48},{64,72... | collective-permute-start | bytes 3145736 | tf_op jit(solution)/shard_map/ppermute | solution.py:39
  105.3 17.6 %collective-permute-start.20 = (bf16[2,512,128]{2,1,0:T(8,128)(2,1)S(1)}, bf16[2,512,128]{2,1,0:T(8,128)(2,1)S(1)}, u32[]{:S(2)}, u32[]{:S(2)}) collective-permute-start(bf16[2,512,128]{2,1,0:T(8,128)(2,1)S(1)} %fusion.2), channel_id=1, source_target_pairs={{0,1},{1,0},{2,3},{3,2},{4,5},{5,4},{6,7},{7,6},{8,9},{9,8},{10,11... | collective-permute-start | bytes 786440 | tf_op jit(solution)/shard_map/ppermute | solution.py:31
  117.8 25.7 %collective-permute-start.23 = (bf16[8,512,128]{2,1,0:T(8,128)(2,1)}, bf16[8,512,128]{2,1,0:T(8,128)(2,1)}, u32[]{:S(2)}, u32[]{:S(2)}) collective-permute-start(bf16[8,512,128]{2,1,0:T(8,128)(2,1)} %pad_maximum_fusion.1), channel_id=1, source_target_pairs={{0,4},{1,5},{2,6},{3,7},{4,0},{5,1},{6,2},{7,3},{8,12},{9,13},{10,... | collective-permute-start | bytes 3145736 | tf_op jit(solution)/shard_map/ppermute | solution.py:27
  120.7 7.6 %copy-start.5 = (bf16[128,4096]{1,0:T(8,128)(2,1)}, bf16[128,4096]{1,0:T(8,128)(2,1)S(1)}, u32[]{:S(2)}) copy-start(bf16[128,4096]{1,0:T(8,128)(2,1)S(1)} %collective-permute-done.22.other_refs_1_) | copy-start | bytes 3145732
  122.9 5.3 %copy-start.6 = (bf16[128,4096]{1,0:T(8,128)(2,1)}, bf16[128,4096]{1,0:T(8,128)(2,1)S(1)}, u32[]{:S(2)}) copy-start(bf16[128,4096]{1,0:T(8,128)(2,1)S(1)} %collective-permute-done.21.other_refs_2_) | copy-start | bytes 3145732
  122.9 33.0 %collective-permute-start.24 = (bf16[8,512,128]{2,1,0:T(8,128)(2,1)}, bf16[8,512,128]{2,1,0:T(8,128)(2,1)S(1)}, u32[]{:S(2)}, u32[]{:S(2)}) collective-permute-start(bf16[8,512,128]{2,1,0:T(8,128)(2,1)} %pad_maximum_fusion), channel_id=1, source_target_pairs={{0,1},{1,0},{2,3},{3,2},{4,5},{5,4},{6,7},{7,6},{8,9},{9,8},{10,11... | collective-permute-start | bytes 3145736 | tf_op jit(solution)/shard_map/ppermute | solution.py:31
  125.7 9.9 %copy-start.11 = (bf16[2,512,128]{2,1,0:T(8,128)(2,1)}, bf16[2,512,128]{2,1,0:T(8,128)(2,1)S(1)}, u32[]{:S(2)}) copy-start(bf16[2,512,128]{2,1,0:T(8,128)(2,1)S(1)} %add_convert_fusion.1.rest_1__0_) | copy-start | bytes 786436
  125.8 23.1 %collective-permute-start.27 = (bf16[2,512,128]{2,1,0:T(8,128)(2,1)S(1)}, bf16[2,512,128]{2,1,0:T(8,128)(2,1)S(1)}, u32[]{:S(2)}, u32[]{:S(2)}) collective-permute-start(bf16[2,512,128]{2,1,0:T(8,128)(2,1)S(1)} %add_convert_fusion.1.rest_1__0_), channel_id=1, source_target_pairs={{0,6},{1,7},{2,0},{3,1},{4,2},{5,3},{6,4},{7,5},{8,14},{9,15},{10,... | collective-permute-start | bytes 786440 | tf_op jit(solution)/shard_map/ppermute | solution.py:27
  126.8 22.2 %collective-permute-start.26 = (bf16[2,512,128]{2,1,0:T(8,128)(2,1)S(1)}, bf16[2,512,128]{2,1,0:T(8,128)(2,1)S(1)}, u32[]{:S(2)}, u32[]{:S(2)}) collective-permute-start(bf16[2,512,128]{2,1,0:T(8,128)(2,1)S(1)} %add_convert_fusion.1.rest_1__0_), channel_id=1, source_target_pairs={{0,4},{1,5},{2,6},{3,7},{4,0},{5,1},{6,2},{7,3},{8,12},{9,13},{10,... | collective-permute-start | bytes 786440 | tf_op jit(solution)/shard_map/ppermute | solution.py:27
  127.5 28.4 %collective-permute-start.25 = (bf16[2,512,128]{2,1,0:T(8,128)(2,1)S(1)}, bf16[2,512,128]{2,1,0:T(8,128)(2,1)}, u32[]{:S(2)}, u32[]{:S(2)}) collective-permute-start(bf16[2,512,128]{2,1,0:T(8,128)(2,1)S(1)} %add_convert_fusion.1.rest_1__0_), channel_id=1, source_target_pairs={{0,2},{1,3},{2,4},{3,5},{4,6},{5,7},{6,0},{7,1},{8,10},{9,11},{10,... | collective-permute-start | bytes 786440 | tf_op jit(solution)/shard_map/ppermute | solution.py:27
  148.9 7.0 %copy-start.12 = (bf16[2,512,128]{2,1,0:T(8,128)(2,1)}, bf16[2,512,128]{2,1,0:T(8,128)(2,1)S(1)}, u32[]{:S(2)}) copy-start(bf16[2,512,128]{2,1,0:T(8,128)(2,1)S(1)} %collective-permute-done.27.rest_1__3_) | copy-start | bytes 786436
  149.0 6.9 %copy-start.13 = (bf16[2,512,128]{2,1,0:T(8,128)(2,1)}, bf16[2,512,128]{2,1,0:T(8,128)(2,1)S(1)}, u32[]{:S(2)}) copy-start(bf16[2,512,128]{2,1,0:T(8,128)(2,1)S(1)} %collective-permute-done.26.rest_1__2_) | copy-start | bytes 786436
  155.9 1.0 copy-start.7

commit v7 on v6

--- a/solution.py
+++ b/solution.py
@@ -45,6 +45,21 @@
 
 def by_source(one, three, two):
     return [one, two, three]
+
+
+def in_strides(count, step, state):
+    done = 0
+    for stride in (4, 2, 1):
+
+        def several(j, state, done=done, stride=stride):
+            for i in range(stride):
+                state = step(done + j * stride + i, state)
+            return state
+
+        times = (count - done) // stride
+        state = lax.fori_loop(0, times, several, state)
+        done = done + times * stride
+    return state
 
 
 def attention_kernel(
@@ -80,19 +95,20 @@
             key_block = ks[pl.ds(at, RUN), :]
             value_block = vs[pl.ds(at, RUN), :]
             new_state = []
+            s_all = contract(key_block, qh[...], 1, 1) * (scale * LOG2E)
+            dp_all = contract(value_block, gh[...], 1, 1)
+            if diagonal:
+                key_at = lax.broadcasted_iota(jnp.int32, (RUN, RUN), 0)
+                query_at = lax.broadcasted_iota(jnp.int32, (RUN, RUN), 1)
+                visible = jnp.concatenate([key_at <= query_at] * heads, axis=1)
+                s_all = jnp.where(visible, s_all, LOW)
+            scores[pl.ds(at, RUN), :] = s_all
+            grads[pl.ds(at, RUN), :] = dp_all
             for h in range(heads):
                 row_max, denom, weighted = state[h]
                 cols = slice(h * RUN, (h + 1) * RUN)
-                s = contract(key_block, qh[cols, :], 1, 1) * (scale * LOG2E)
-                if diagonal:
-                    key_at = lax.broadcasted_iota(jnp.int32, (RUN, RUN), 0)
-                    query_at = lax.broadcasted_iota(jnp.int32, (RUN, RUN), 1)
-                    s = jnp.where(key_at <= query_at, s, LOW)
-                scores[pl.ds(at, RUN), cols] = s
-                dp = contract(value_block, gh[cols, :], 1, 1)
-                grads[pl.ds(at, RUN), cols] = dp
-                s3 = s.reshape(RUN // 8, 8, RUN)
-                dp3 = dp.reshape(RUN // 8, 8, RUN)
+                s3 = s_all[:, cols].reshape(RUN // 8, 8, RUN)
+                dp3 = dp_all[:, cols].reshape(RUN // 8, 8, RUN)
                 new_max = jnp.maximum(row_max, jnp.max(s3, axis=0))
                 fade = jnp.exp2(row_max - new_max)
                 expo = jnp.exp2(s3 - new_max[None])
@@ -109,7 +125,7 @@
 
         zeros = jnp.zeros((8, RUN), jnp.float32)
         state = tuple((jnp.full((8, RUN), LOW, jnp.float32), zeros, zeros) for _ in range(heads))
-        state = lax.fori_loop(0, run, lambda j, st: stat_step(j, st, False), state)
+        state = in_strides(run, lambda j, st: stat_step(j, st, False), state)
         state = stat_step(run, state, True)
         lse, dots = [], []
         for h in range(heads):
@@ -124,19 +140,22 @@
         def grad_step(j, carry):
             at = pl.multiple_of(j * RUN, RUN)
             key_cols = kt[:, pl.ds(at, RUN)]
-            dk, dv = 0.0, 0.0
+            probs_low, grad_scores = [], []
             for h in range(heads):
                 cols = slice(h * RUN, (h + 1) * RUN)
                 p = jnp.exp2(scores[pl.ds(at, RUN), cols] - lse[h])
-                ds = (p * (grads[pl.ds(at, RUN), cols] - dots[h])).astype(jnp.bfloat16)
-                dv += contract(p.astype(jnp.bfloat16), gh[cols, :], 1, 0)
-                dk += contract(ds, qh[cols, :], 1, 0)
-                dqt[:, cols] += contract(key_cols, ds, 1, 0)
+                ds = p * (grads[pl.ds(at, RUN), cols] - dots[h])
+                probs_low.append(p.astype(jnp.bfloat16))
+                grad_scores.append(ds.astype(jnp.bfloat16))
+            ds_all = jnp.concatenate(grad_scores, axis=1)
+            dv = contract(jnp.concatenate(probs_low, axis=1), gh[...], 1, 0)
+            dk = contract(ds_all, qh[...], 1, 0)
+            dqt[...] += contract(key_cols, ds_all, 1, 0)
             dka[pl.ds(at, RUN), :] += dk
             dva[pl.ds(at, RUN), :] += dv
             return carry
 
-        lax.fori_loop(0, run + 1, grad_step, 0)
+        in_strides(run + 1, grad_step, 0)
         for h in range(heads):
             cols = slice(h * RUN, (h + 1) * RUN)
             dq = (dqt[:, cols] * scale).T.astype(jnp.bfloat16)
@@ -238,10 +257,8 @@
     tall = own_refs[0].shape[0]
     tokens, wide = grad_refs[0].shape[1:]
     heads = grads.shape[1] // wide
-    half = len(EARLY) * tokens
-    order = LATE + EARLY if last else EARLY
-    spans = consecutive(order)
-    first_spans = sum(1 for at, _, _ in spans if at < len(EARLY))
+    slots = LATE if last else EARLY
+    spans = [[0, 0, 8]] if last else consecutive(EARLY)
     grad_copies = [
         pltpu.make_async_copy(
             ref.at[start + h],
@@ -259,10 +276,10 @@
         shared_copies = [
             pltpu.make_async_copy(
                 shared_refs[slot % 4].at[slot // 4],
-                shared.at[pl.ds(i * tokens, tokens)],
-                shared_sems.at[i],
+                shared.at[pl.ds(slot * tokens, tokens)],
+                shared_sems.at[slot],
             )
-            for i, slot in enumerate(order)
+            for slot in range(8)
         ]
     for away in range(4):
         for n, (at, slot, many) in enumerate(spans):
@@ -273,25 +290,45 @@
                     inputs.at[away, pl.ds(down, tall), pl.ds(at * tokens, many * tokens)],
                     in_sems.at[away, n, which],
                 )
-                in_copies[away, n, which].start()
         if last:
             sum_copies.append(
                 pltpu.make_async_copy(
                     sum_ref.at[pl.ds(row[away], 2 * tall)], sums.at[away], sum_sems.at[away]
                 )
             )
+
+    def fetch(away):
+        for n in range(len(spans)):
+            for which in range(2):
+                in_copies[away, n, which].start()
+        if last:
             sum_copies[away].start()
-            if away == 0:
-                for copy in shared_copies:
-                    copy.start()
+
+    fetch(0)
+    for copy in shared_copies:
+        copy.start()
+    fetch(1)
     for copy in grad_copies:
         copy.wait()
     norm = 1.0 / math.sqrt(8 * tokens)
     for away in range(4):
-        for n in range(first_spans):
+        for n in range(len(spans)):
             for which in range(2):
                 in_copies[away, n, which].wait()
-        total = contract(inputs[away, :, :half], grads[...], 1, 0)
+        if away + 2 < 4:
+            fetch(away + 2)
+        if last:
+            total = sum(
+                contract(
+                    inputs[away, :, slot * tokens : (slot + many) * tokens],
+                    grads[at * tokens : (at + many) * tokens],
+                    1,
+                    0,
+                )
+                for at, slot, many in consecutive(slots)
+            )
+        else:
+            total = contract(inputs[away], grads[...], 1, 0)
         if last:
             sum_copies[away].wait()
             total = (total + sums[away]) * norm
@@ -306,15 +343,11 @@
             if away == 0:
                 for copy in shared_copies:
                     copy.wait()
-            for n in range(first_spans, len(spans)):
-                for which in range(2):
-                    in_copies[away, n, which].wait()
             part = (contract(inputs[away], shared[...], 1, 0) * norm).T
             wk_ref[:, pl.ds(row[away], 2 * tall)] = part[: tall // 2]
             wv_ref[:, pl.ds(row[away], 2 * tall)] = part[tall // 2 :]
     if last:
-        at = order.index(0) * tokens
-        here = shared[at : at + tokens].T
+        here = shared[:tokens].T
         k_ref[...] = here[: here.shape[0] // 2]
         v_ref[...] = here[here.shape[0] // 2 :]
     for copy in out_copies:
@@ -333,17 +366,17 @@
     wq = jax.ShapeDtypeStruct((8 * tall, cols), f32)
     narrow = jax.ShapeDtypeStruct((tall // 2, 8 * tall), f32)
     narrow_in = jax.ShapeDtypeStruct((tall // 2, tokens), bf16)
-    order = LATE + EARLY if last else EARLY
+    spans = 1 if last else len(consecutive(EARLY))
     scratch = [
-        pltpu.VMEM((4, 2 * tall, len(order) * tokens), bf16),
+        pltpu.VMEM((4, 2 * tall, (8 if last else len(EARLY)) * tokens), bf16),
         pltpu.VMEM((len(grads) * tokens, cols), bf16),
         pltpu.VMEM((4, 2 * tall, cols), f32),
     ]
     if last:
         scratch += [pltpu.VMEM((across, tall), bf16)]
-    scratch += [sem((4, len(consecutive(order)), 2)), sem((len(grads), heads))]
+    scratch += [sem((4, spans, 2)), sem((len(grads), heads))]
     if last:
-        scratch += [sem((4,)), sem((len(order),))]
+        scratch += [sem((4,)), sem((8,))]
     scratch += [sem((4,))]
     return pl.pallas_call(
         functools.partial(weight_kernel, last, tuple(start for _, start in grads)),

time: 169 us -> 159 us (0.941); the launches traced: 171 us -> 159 us
  waiting for transfers between devices: 46.7 us -> 69.9 us
  starting transfers between devices: 59 us -> 38.9 us
  Pallas kernels: 51.2 us -> 36.3 us
    ppermute x5, starting transfers between devices: 29.3 us -> 9.56 us  [swap_x(): return lax.ppermute(value, 'ctx', [(i, i ^ 1) for i in range(8)])]
    pallas_call x1, Pallas kernels: 27.8 us -> 15.7 us  [attention(): pl.pallas_call(functools.partial(attention_kernel, heads), out_shape=(jax...]
    ppermute x3, waiting for transfers between devices: 0.01 us -> 10.2 us  [along_z(): lax.ppermute(value, 'dp', [(i, (i + 4 * step) % 16) for i in range(16)])]
    ppermute x13, waiting for transfers between devices: 25.1 us -> 34.5 us  [along_y(): lax.ppermute(value, 'ctx', [(i, (i + 2 * step) % 8) for i in range(8)])]
    pallas_call x2, Pallas kernels: 21 us -> 18.1 us  [weights(): pl.pallas_call(functools.partial(weight_kernel, last, tuple((start for _,...]
    ppermute x5, waiting for transfers between devices: 19 us -> 21.1 us  [swap_x(): return lax.ppermute(value, 'ctx', [(i, i ^ 1) for i in range(8)])]
  transfers between devices with their start and end apart: 28 -> 28, of which waited for: 13 -> 18; matrix products, arithmetic and copies ran while one was open for 6% -> 6% of each run, Pallas kernels for 22% -> 16%
where the time goes in v7:
time: 159 us
  waiting for transfers between devices  69.9 us (44%)
  starting transfers between devices  38.9 us (24%)
  Pallas kernels  36.3 us (23%)
  other arithmetic  8.97 us (6%)
  local copies, waits for them, and re-layouts  3.58 us (2%)
    ppermute x13, waiting for transfers between devices, along_y(): lax.ppermute(value, 'ctx', [(i, (i + 2 * step) % 8) for i in range(8)])  34.5 us
    ppermute x5, waiting for transfers between devices, swap_x(): return lax.ppermute(value, 'ctx', [(i, i ^ 1) for i in range(8)])  21.1 us
    pallas_call x2, Pallas kernels, weights(): pl.pallas_call(functools.partial(weight_kernel, last, tuple((start for _,...  18.1 us
    ppermute x13, starting transfers between devices, along_y(): lax.ppermute(value, 'ctx', [(i, (i + 2 * step) % 8) for i in range(8)])  16.4 us
    pallas_call x1, Pallas kernels, attention(): pl.pallas_call(functools.partial(attention_kernel, heads), out_shape=(jax...  15.7 us
    ppermute x3, waiting for transfers between devices, along_z(): lax.ppermute(value, 'dp', [(i, (i + 4 * step) % 16) for i in range(16)])  10.2 us
    ppermute x5, starting transfers between devices, swap_x(): return lax.ppermute(value, 'ctx', [(i, i ^ 1) for i in range(8)])  9.56 us
    ppermute x7, starting transfers between devices, swap_cores(): return lax.ppermute(value, 'dp', [(i, i ^ 1) for i in range(16)])  9.17 us
  transfers between devices with their start and end apart: 28, of which 18 were waited for; matrix products, arithmetic and copies ran while one was open for 6% of the time, Pallas kernels for 16%

profile of v7, /device:TPU:1, one launch (start us, length us, event | category | flops | bytes accessed | tf_op | source)
XLA Modules:
  0.0 158.8 jit_solution(10364964298702643587)
XLA Ops:
  0.8 1.4 dynamic-slice_bitcast_fusion
  2.3 3.7 %collective-permute-start.4 = (bf16[4,512,128]{2,1,0:T(8,128)(2,1)S(1)}, bf16[4,512,128]{2,1,0:T(8,128)(2,1)S(1)}, u32[]{:S(2)}, u32[]{:S(2)}) collective-permute-start(bf16[4,512,128]{2,1,0:T(8,128)(2,1)S(1)} %pad_maximum_fusion.5), channel_id=1, source_target_pairs={{0,1},{1,0},{2,3},{3,2},{4,5},{5,4},{6,7},{7,6},{8,9},{9,8},{10,11... | collective-permute-start | bytes 1572872 | tf_op jit(solution)/shard_map/ppermute | solution.py:31
  5.9 0.8 slice.48
  6.8 1.0 dynamic-slice_select_fusion
  7.8 3.0 %collective-permute-start.1 = (bf16[528,128]{1,0:T(8,128)(2,1)S(1)}, bf16[528,128]{1,0:T(8,128)(2,1)S(1)}, u32[]{:S(2)}, u32[]{:S(2)}) collective-permute-start(bf16[528,128]{1,0:T(8,128)(2,1)S(1)} %get-tuple-element.92), channel_id=1, source_target_pairs={{0,4},{1,5},{2,6},{3,7},{4,0},{5,1},{6,2},{7,3},{8,12},{9,13},{10,... | collective-permute-start | bytes 405512 | tf_op jit(solution)/shard_map/ppermute | solution.py:27
  11.2 2.3 %collective-permute-start.2 = (bf16[528,128]{1,0:T(8,128)(2,1)S(1)}, bf16[528,128]{1,0:T(8,128)(2,1)S(1)}, u32[]{:S(2)}, u32[]{:S(2)}) collective-permute-start(bf16[528,128]{1,0:T(8,128)(2,1)S(1)} %get-tuple-element.92), channel_id=1, source_target_pairs={{0,6},{1,7},{2,0},{3,1},{4,2},{5,3},{6,4},{7,5},{8,14},{9,15},{10,... | collective-permute-start | bytes 405512 | tf_op jit(solution)/shard_map/ppermute | solution.py:27
  13.6 3.7 %collective-permute-done = bf16[528,128]{1,0:T(8,128)(2,1)S(1)} collective-permute-done((bf16[528,128]{1,0:T(8,128)(2,1)S(1)}, bf16[528,128]{1,0:T(8,128)(2,1)S(1)}, u32[]{:S(2)}, u32[]{:S(2)}) %collective-permute-start) | collective-permute-done | bytes 135200 | tf_op jit(solution)/shard_map/ppermute | solution.py:27
  17.2 0.9 pad_maximum_fusion.4.mine_refs_0_
  18.3 2.0 %collective-permute-start.5 = (bf16[2,512,128]{2,1,0:T(8,128)(2,1)S(1)}, bf16[2,512,128]{2,1,0:T(8,128)(2,1)S(1)}, u32[]{:S(2)}, u32[]{:S(2)}) collective-permute-start(bf16[2,512,128]{2,1,0:T(8,128)(2,1)S(1)} %pad_maximum_fusion.7), channel_id=1, source_target_pairs={{0,2},{1,3},{2,4},{3,5},{4,6},{5,7},{6,0},{7,1},{8,10},{9,11},{10,... | collective-permute-start | bytes 786440 | tf_op jit(solution)/shard_map/ppermute | solution.py:27
  20.3 2.3 %collective-permute-start.6 = (bf16[2,512,128]{2,1,0:T(8,128)(2,1)S(1)}, bf16[2,512,128]{2,1,0:T(8,128)(2,1)S(1)}, u32[]{:S(2)}, u32[]{:S(2)}) collective-permute-start(bf16[2,512,128]{2,1,0:T(8,128)(2,1)S(1)} %pad_maximum_fusion.8), channel_id=1, source_target_pairs={{0,4},{1,5},{2,6},{3,7},{4,0},{5,1},{6,2},{7,3},{8,12},{9,13},{10,... | collective-permute-start | bytes 786440 | tf_op jit(solution)/shard_map/ppermute | solution.py:27
  23.0 2.3 %collective-permute-start.8 = (bf16[4,528,128]{2,1,0:T(8,128)(2,1)}, bf16[4,528,128]{2,1,0:T(8,128)(2,1)}, u32[]{:S(2)}, u32[]{:S(2)}) collective-permute-start(bf16[4,528,128]{2,1,0:T(8,128)(2,1)} %pad_maximum_fusion.4.mine_refs_0_), channel_id=1, source_target_pairs={{0,8},{8,0},{16,24},{24,16},{32,40},{40,32},{48,56},{56,48},{64,72... | collective-permute-start | bytes 1622024 | tf_op jit(solution)/shard_map/ppermute | solution.py:39
  25.3 0.7 fusion.3
  26.1 0.7 pad_maximum_fusion.6.in_refs_0_
  26.8 5.4 %collective-permute-done.3.mine_refs_1_ = bf16[4,528,128]{2,1,0:T(8,128)(2,1)} collective-permute-done((bf16[4,528,128]{2,1,0:T(8,128)(2,1)}, bf16[4,528,128]{2,1,0:T(8,128)(2,1)}, u32[]{:S(2)}, u32[]{:S(2)}) %collective-permute-start.3) | collective-permute-done | bytes 540704 | tf_op jit(solution)/shard_map/ppermute | solution.py:31
  33.2 2.2 %collective-permute-start.9 = (bf16[4,528,128]{2,1,0:T(8,128)(2,1)}, bf16[4,528,128]{2,1,0:T(8,128)(2,1)}, u32[]{:S(2)}, u32[]{:S(2)}) collective-permute-start(bf16[4,528,128]{2,1,0:T(8,128)(2,1)} %collective-permute-done.3.mine_refs_1_), channel_id=1, source_target_pairs={{0,8},{8,0},{16,24},{24,16},{32,40},{40,32},{48,56},{56,48},{64,72... | collective-permute-start | bytes 1622024 | tf_op jit(solution)/shard_map/ppermute | solution.py:39
  35.4 2.5 %shard_map.110.own_refs_0_ = bf16[128,4096]{1,0:T(8,128)(2,1)} custom-call(bf16[2,512,128]{2,1,0:T(8,128)(2,1)} %pad_maximum_fusion.6.in_refs_0_, bf16[2,512,128]{2,1,0:T(8,128)(2,1)} %copy-done.14, bf16[2,512,128]{2,1,0:T(8,128)(2,1)} %copy-done.15, bf16[2,512,128]{2,1,0:T(8,128)(2,1)} %copy-done.16), custom_call_target="tpu_custom_call" | custom-call | bytes 2097152 | tf_op jit(solution)/shard_map/pallas_call | solution.py:226
  37.9 0.7 collective-permute-start.12
  38.6 3.8 %collective-permute-start.11 = (bf16[128,4096]{1,0:T(8,128)(2,1)}, bf16[128,4096]{1,0:T(8,128)(2,1)S(1)}, u32[]{:S(2)}, u32[]{:S(2)}) collective-permute-start(bf16[128,4096]{1,0:T(8,128)(2,1)} %shard_map.110.own_refs_0_), channel_id=1, source_target_pairs={{0,96},{8,104},{16,112},{24,120},{32,0},{40,8},{48,16},{56,24},{64... | collective-permute-start | bytes 3145736 | tf_op jit(solution)/shard_map/ppermute | solution.py:35
  42.4 0.7 convert_reduce_fusion
  43.2 0.6 pad_add_fusion.1.info_ref
  43.8 15.7 %shard_map.109 = (bf16[512,512]{1,0:T(8,128)(2,1)}, bf16[4,512,128]{2,1,0:T(8,128)(2,1)}, bf16[8,512,128]{2,1,0:T(8,128)(2,1)}, bf16[8,512,128]{2,1,0:T(8,128)(2,1)}) custom-call(s32[17]{0:T(128)} %pad_add_fusion.1.info_ref, bf16[512,512]{1,0:T(8,128)(2,1)} %q_ref.1, bf16[512,512]{1,0:T(8,128)(2,1)} %g_ref.1, ...), custom_call_target="tpu_custom_call" | custom-call | flops 10737418240 | bytes 8388608 | tf_op jit(solution)/shard_map/pallas_call | solution.py:186
  59.5 5.8 %collective-permute-done.11.own_refs_1_ = bf16[128,4096]{1,0:T(8,128)(2,1)S(1)} collective-permute-done((bf16[128,4096]{1,0:T(8,128)(2,1)}, bf16[128,4096]{1,0:T(8,128)(2,1)S(1)}, u32[]{:S(2)}, u32[]{:S(2)}) %collective-permute-start.11) | collective-permute-done | bytes 1048608 | tf_op jit(solution)/shard_map/ppermute | solution.py:35
  65.3 3.1 %collective-permute-done.10.own_refs_3_ = bf16[128,4096]{1,0:T(8,128)(2,1)} collective-permute-done((bf16[128,4096]{1,0:T(8,128)(2,1)}, bf16[128,4096]{1,0:T(8,128)(2,1)}, u32[]{:S(2)}, u32[]{:S(2)}) %collective-permute-start.10) | collective-permute-done | bytes 1048608 | tf_op jit(solution)/shard_map/ppermute | solution.py:35
  68.4 1.1 collective-permute-start.13
  69.5 3.9 %collective-permute-done.13 = bf16[8,512,128]{2,1,0:T(8,128)(2,1)S(1)} collective-permute-done((bf16[8,512,128]{2,1,0:T(8,128)(2,1)}, bf16[8,512,128]{2,1,0:T(8,128)(2,1)S(1)}, u32[]{:S(2)}, u32[]{:S(2)}) %collective-permute-start.13) | collective-permute-done | bytes 1048608 | tf_op jit(solution)/shard_map/ppermute | solution.py:39
  73.6 1.5 add_convert_fusion
  75.3 2.7 %collective-permute-start.16 = (bf16[6,512,128]{2,1,0:T(8,128)(2,1)S(1)}, bf16[6,512,128]{2,1,0:T(8,128)(2,1)S(1)}, u32[]{:S(2)}, u32[]{:S(2)}) collective-permute-start(bf16[6,512,128]{2,1,0:T(8,128)(2,1)S(1)} %get-tuple-element.85), channel_id=1, source_target_pairs={{0,6},{1,7},{2,0},{3,1},{4,2},{5,3},{6,4},{7,5},{8,14},{9,15},{10,... | collective-permute-start | bytes 2359304 | tf_op jit(solution)/shard_map/ppermute | solution.py:27
  78.0 1.9 %collective-permute-start.18 = (bf16[4,512,128]{2,1,0:T(8,128)(2,1)S(1)}, bf16[4,512,128]{2,1,0:T(8,128)(2,1)S(1)}, u32[]{:S(2)}, u32[]{:S(2)}) collective-permute-start(bf16[4,512,128]{2,1,0:T(8,128)(2,1)S(1)} %copy-done.1), channel_id=1, source_target_pairs={{0,1},{1,0},{2,3},{3,2},{4,5},{5,4},{6,7},{7,6},{8,9},{9,8},{10,11... | collective-permute-start | bytes 1572872 | tf_op jit(solution)/shard_map/ppermute | solution.py:31
  80.0 1.3 collective-permute-start.17
  81.2 11.3 %collective-permute-done.18.grad_refs_3_ = bf16[4,512,128]{2,1,0:T(8,128)(2,1)S(1)} collective-permute-done((bf16[4,512,128]{2,1,0:T(8,128)(2,1)S(1)}, bf16[4,512,128]{2,1,0:T(8,128)(2,1)S(1)}, u32[]{:S(2)}, u32[]{:S(2)}) %collective-permute-start.18) | collective-permute-done | bytes 524320 | tf_op jit(solution)/shard_map/ppermute | solution.py:31
  92.5 1.4 collective-permute-start.22
  93.9 1.3 collective-permute-done.19.own_refs_2_
  95.2 7.2 %collective-permute-done.17 = bf16[2,512,128]{2,1,0:T(8,128)(2,1)S(1)} collective-permute-done((bf16[2,512,128]{2,1,0:T(8,128)(2,1)S(1)}, bf16[2,512,128]{2,1,0:T(8,128)(2,1)S(1)}, u32[]{:S(2)}, u32[]{:S(2)}) %collective-permute-start.17) | collective-permute-done | bytes 262176 | tf_op jit(solution)/shard_map/ppermute | solution.py:27
  102.4 1.0 collective-permute-done.15.grad_refs_1_
  103.4 1.4 collective-permute-start.21
  105.1 2.0 %collective-permute-start.20 = (bf16[2,512,128]{2,1,0:T(8,128)(2,1)S(1)}, bf16[2,512,128]{2,1,0:T(8,128)(2,1)S(1)}, u32[]{:S(2)}, u32[]{:S(2)}) collective-permute-start(bf16[2,512,128]{2,1,0:T(8,128)(2,1)S(1)} %fusion.2), channel_id=1, source_target_pairs={{0,1},{1,0},{2,3},{3,2},{4,5},{5,4},{6,7},{7,6},{8,9},{9,8},{10,11... | collective-permute-start | bytes 786440 | tf_op jit(solution)/shard_map/ppermute | solution.py:31
  107.1 1.1 pad_maximum_fusion.1
  108.5 1.1 pad_maximum_fusion
  109.7 4.4 %collective-permute-done.20 = bf16[2,512,128]{2,1,0:T(8,128)(2,1)S(1)} collective-permute-done((bf16[2,512,128]{2,1,0:T(8,128)(2,1)S(1)}, bf16[2,512,128]{2,1,0:T(8,128)(2,1)S(1)}, u32[]{:S(2)}, u32[]{:S(2)}) %collective-permute-start.20) | collective-permute-done | bytes 262176 | tf_op jit(solution)/shard_map/ppermute | solution.py:31
  114.1 1.9 %collective-permute-start.24 = (bf16[8,512,128]{2,1,0:T(8,128)(2,1)}, bf16[8,512,128]{2,1,0:T(8,128)(2,1)S(1)}, u32[]{:S(2)}, u32[]{:S(2)}) collective-permute-start(bf16[8,512,128]{2,1,0:T(8,128)(2,1)} %pad_maximum_fusion), channel_id=1, source_target_pairs={{0,1},{1,0},{2,3},{3,2},{4,5},{5,4},{6,7},{7,6},{8,9},{9,8},{10,11... | collective-permute-start | bytes 3145736 | tf_op jit(solution)/shard_map/ppermute | solution.py:31
  116.7 1.2 collective-permute-start.25
  117.9 6.8 %shard_map.111.rest_0_ = f32[1024,512]{1,0:T(8,128)} custom-call(s32[2]{0:T(128)} %copy-done.17, bf16[128,4096]{1,0:T(8,128)(2,1)} %shard_map.110.own_refs_0_, bf16[128,4096]{1,0:T(8,128)(2,1)} %copy-done.3, bf16[128,4096]{1,0:T(8,128)(2,1)} %copy-done.4, bf16[128,4096]{1,0:T(8,128)(2,1)} %collective-permute-done.10.own_refs_3_, ...), custom_call_target="tpu_custom_call" | custom-call | flops 2147483648 | bytes 10485760 | tf_op jit(solution)/shard_map/pallas_call | solution.py:381
  124.7 9.1 %collective-permute-done.23.grad_refs_0_.grad_refs_2_ = bf16[8,512,128]{2,1,0:T(8,128)(2,1)} collective-permute-done((bf16[8,512,128]{2,1,0:T(8,128)(2,1)}, bf16[8,512,128]{2,1,0:T(8,128)(2,1)}, u32[]{:S(2)}, u32[]{:S(2)}) %collective-permute-start.23) | collective-permute-done | bytes 1048608 | tf_op jit(solution)/shard_map/ppermute | solution.py:27
  133.9 4.3 %collective-permute-done.27.rest_1__3_ = bf16[2,512,128]{2,1,0:T(8,128)(2,1)S(1)} collective-permute-done((bf16[2,512,128]{2,1,0:T(8,128)(2,1)S(1)}, bf16[2,512,128]{2,1,0:T(8,128)(2,1)S(1)}, u32[]{:S(2)}, u32[]{:S(2)}) %collective-permute-start.27) | collective-permute-done | bytes 262176 | tf_op jit(solution)/shard_map/ppermute | solution.py:27
  138.2 1.2 collective-permute-done.26.rest_1__2_
  139.4 6.9 %collective-permute-done.25.rest_1__1_ = bf16[2,512,128]{2,1,0:T(8,128)(2,1)} collective-permute-done((bf16[2,512,128]{2,1,0:T(8,128)(2,1)S(1)}, bf16[2,512,128]{2,1,0:T(8,128)(2,1)}, u32[]{:S(2)}, u32[]{:S(2)}) %collective-permute-start.25) | collective-permute-done | bytes 262176 | tf_op jit(solution)/shard_map/ppermute | solution.py:27
  146.3 1.0 copy-done.7
  147.3 11.3 %shard_map.112 = (f32[1024,512]{1,0:T(8,128)}, f32[64,1024]{1,0:T(8,128)}, f32[64,1024]{1,0:T(8,128)}, bf16[64,512]{1,0:T(8,128)(2,1)}, bf16[64,512]{1,0:T(8,128)(2,1)}) custom-call(s32[2]{0:T(128)} %copy-done.17, bf16[128,4096]{1,0:T(8,128)(2,1)} %shard_map.110.own_refs_0_, bf16[128,4096]{1,0:T(8,128)(2,1)} %copy-done.3, bf16[128,4096]{1,0:T(8,128)(2,1)} %copy-done.4, ...), custom_call_target="tpu_custom_call" | custom-call | flops 2147483648 | bytes 10485760 | tf_op jit(solution)/shard_map/pallas_call | solution.py:381
  (78 shorter events, 4.0 us)
Async XLA Ops:
  2.3 15.9 %collective-permute-start.4 = (bf16[4,512,128]{2,1,0:T(8,128)(2,1)S(1)}, bf16[4,512,128]{2,1,0:T(8,128)(2,1)S(1)}, u32[]{:S(2)}, u32[]{:S(2)}) collective-permute-start(bf16[4,512,128]{2,1,0:T(8,128)(2,1)S(1)} %pad_maximum_fusion.5), channel_id=1, source_target_pairs={{0,1},{1,0},{2,3},{3,2},{4,5},{5,4},{6,7},{7,6},{8,9},{9,8},{10,11... | collective-permute-start | bytes 1572872 | tf_op jit(solution)/shard_map/ppermute | solution.py:31
  7.8 5.7 %collective-permute-start.1 = (bf16[528,128]{1,0:T(8,128)(2,1)S(1)}, bf16[528,128]{1,0:T(8,128)(2,1)S(1)}, u32[]{:S(2)}, u32[]{:S(2)}) collective-permute-start(bf16[528,128]{1,0:T(8,128)(2,1)S(1)} %get-tuple-element.92), channel_id=1, source_target_pairs={{0,4},{1,5},{2,6},{3,7},{4,0},{5,1},{6,2},{7,3},{8,12},{9,13},{10,... | collective-permute-start | bytes 405512 | tf_op jit(solution)/shard_map/ppermute | solution.py:27
  10.8 6.4 %collective-permute-start = (bf16[528,128]{1,0:T(8,128)(2,1)S(1)}, bf16[528,128]{1,0:T(8,128)(2,1)S(1)}, u32[]{:S(2)}, u32[]{:S(2)}) collective-permute-start(bf16[528,128]{1,0:T(8,128)(2,1)S(1)} %get-tuple-element.92), channel_id=1, source_target_pairs={{0,2},{1,3},{2,4},{3,5},{4,6},{5,7},{6,0},{7,1},{8,10},{9,11},{10,... | collective-permute-start | bytes 405512 | tf_op jit(solution)/shard_map/ppermute | solution.py:27
  11.2 6.0 %collective-permute-start.2 = (bf16[528,128]{1,0:T(8,128)(2,1)S(1)}, bf16[528,128]{1,0:T(8,128)(2,1)S(1)}, u32[]{:S(2)}, u32[]{:S(2)}) collective-permute-start(bf16[528,128]{1,0:T(8,128)(2,1)S(1)} %get-tuple-element.92), channel_id=1, source_target_pairs={{0,6},{1,7},{2,0},{3,1},{4,2},{5,3},{6,4},{7,5},{8,14},{9,15},{10,... | collective-permute-start | bytes 405512 | tf_op jit(solution)/shard_map/ppermute | solution.py:27
  18.1 14.1 %collective-permute-start.3 = (bf16[4,528,128]{2,1,0:T(8,128)(2,1)}, bf16[4,528,128]{2,1,0:T(8,128)(2,1)}, u32[]{:S(2)}, u32[]{:S(2)}) collective-permute-start(bf16[4,528,128]{2,1,0:T(8,128)(2,1)} %pad_maximum_fusion.4.mine_refs_0_), channel_id=1, source_target_pairs={{0,1},{1,0},{2,3},{3,2},{4,5},{5,4},{6,7},{7,6},{8,9},{9,8},{10,11... | collective-permute-start | bytes 1622024 | tf_op jit(solution)/shard_map/ppermute | solution.py:31
  18.3 13.9 %collective-permute-start.5 = (bf16[2,512,128]{2,1,0:T(8,128)(2,1)S(1)}, bf16[2,512,128]{2,1,0:T(8,128)(2,1)S(1)}, u32[]{:S(2)}, u32[]{:S(2)}) collective-permute-start(bf16[2,512,128]{2,1,0:T(8,128)(2,1)S(1)} %pad_maximum_fusion.7), channel_id=1, source_target_pairs={{0,2},{1,3},{2,4},{3,5},{4,6},{5,7},{6,0},{7,1},{8,10},{9,11},{10,... | collective-permute-start | bytes 786440 | tf_op jit(solution)/shard_map/ppermute | solution.py:27
  20.3 12.4 %collective-permute-start.6 = (bf16[2,512,128]{2,1,0:T(8,128)(2,1)S(1)}, bf16[2,512,128]{2,1,0:T(8,128)(2,1)S(1)}, u32[]{:S(2)}, u32[]{:S(2)}) collective-permute-start(bf16[2,512,128]{2,1,0:T(8,128)(2,1)S(1)} %pad_maximum_fusion.8), channel_id=1, source_target_pairs={{0,4},{1,5},{2,6},{3,7},{4,0},{5,1},{6,2},{7,3},{8,12},{9,13},{10,... | collective-permute-start | bytes 786440 | tf_op jit(solution)/shard_map/ppermute | solution.py:27
  22.6 10.6 %collective-permute-start.7 = (bf16[2,512,128]{2,1,0:T(8,128)(2,1)S(1)}, bf16[2,512,128]{2,1,0:T(8,128)(2,1)S(1)}, u32[]{:S(2)}, u32[]{:S(2)}) collective-permute-start(bf16[2,512,128]{2,1,0:T(8,128)(2,1)S(1)} %pad_maximum_fusion.9), channel_id=1, source_target_pairs={{0,6},{1,7},{2,0},{3,1},{4,2},{5,3},{6,4},{7,5},{8,14},{9,15},{10,... | collective-permute-start | bytes 786440 | tf_op jit(solution)/shard_map/ppermute | solution.py:27
  23.0 36.5 %copy-start.17 = (s32[2]{0:T(128)}, s32[2]{0:T(128)S(1)}, u32[]{:S(2)}) copy-start(s32[2]{0:T(128)S(1)} %pad_add_fusion.place_ref) | copy-start | bytes 28
  23.0 20.8 %collective-permute-start.8 = (bf16[4,528,128]{2,1,0:T(8,128)(2,1)}, bf16[4,528,128]{2,1,0:T(8,128)(2,1)}, u32[]{:S(2)}, u32[]{:S(2)}) collective-permute-start(bf16[4,528,128]{2,1,0:T(8,128)(2,1)} %pad_maximum_fusion.4.mine_refs_0_), channel_id=1, source_target_pairs={{0,8},{8,0},{16,24},{24,16},{32,40},{40,32},{48,56},{56,48},{64,72... | collective-permute-start | bytes 1622024 | tf_op jit(solution)/shard_map/ppermute | solution.py:39
  32.2 3.2 %copy-start.14 = (bf16[2,512,128]{2,1,0:T(8,128)(2,1)}, bf16[2,512,128]{2,1,0:T(8,128)(2,1)S(1)}, u32[]{:S(2)}) copy-start(bf16[2,512,128]{2,1,0:T(8,128)(2,1)S(1)} %collective-permute-done.5.in_refs_1_) | copy-start | bytes 786436
  32.7 2.7 %copy-start.15 = (bf16[2,512,128]{2,1,0:T(8,128)(2,1)}, bf16[2,512,128]{2,1,0:T(8,128)(2,1)S(1)}, u32[]{:S(2)}) copy-start(bf16[2,512,128]{2,1,0:T(8,128)(2,1)S(1)} %collective-permute-done.6.in_refs_2_) | copy-start | bytes 786436
  33.2 2.2 %copy-start.16 = (bf16[2,512,128]{2,1,0:T(8,128)(2,1)}, bf16[2,512,128]{2,1,0:T(8,128)(2,1)S(1)}, u32[]{:S(2)}) copy-start(bf16[2,512,128]{2,1,0:T(8,128)(2,1)S(1)} %collective-permute-done.7.in_refs_3_) | copy-start | bytes 786436
  33.2 10.6 %collective-permute-start.9 = (bf16[4,528,128]{2,1,0:T(8,128)(2,1)}, bf16[4,528,128]{2,1,0:T(8,128)(2,1)}, u32[]{:S(2)}, u32[]{:S(2)}) collective-permute-start(bf16[4,528,128]{2,1,0:T(8,128)(2,1)} %collective-permute-done.3.mine_refs_1_), channel_id=1, source_target_pairs={{0,8},{8,0},{16,24},{24,16},{32,40},{40,32},{48,56},{56,48},{64,72... | collective-permute-start | bytes 1622024 | tf_op jit(solution)/shard_map/ppermute | solution.py:39
  37.9 21.6 %collective-permute-start.12 = (bf16[128,4096]{1,0:T(8,128)(2,1)}, bf16[128,4096]{1,0:T(8,128)(2,1)S(1)}, u32[]{:S(2)}, u32[]{:S(2)}) collective-permute-start(bf16[128,4096]{1,0:T(8,128)(2,1)} %shard_map.110.own_refs_0_), channel_id=1, source_target_pairs={{0,8},{8,0},{16,24},{24,16},{32,40},{40,32},{48,56},{56,48},{64,72... | collective-permute-start | bytes 3145736 | tf_op jit(solution)/shard_map/ppermute | solution.py:39
  38.6 26.7 %collective-permute-start.11 = (bf16[128,4096]{1,0:T(8,128)(2,1)}, bf16[128,4096]{1,0:T(8,128)(2,1)S(1)}, u32[]{:S(2)}, u32[]{:S(2)}) collective-permute-start(bf16[128,4096]{1,0:T(8,128)(2,1)} %shard_map.110.own_refs_0_), channel_id=1, source_target_pairs={{0,96},{8,104},{16,112},{24,120},{32,0},{40,8},{48,16},{56,24},{64... | collective-permute-start | bytes 3145736 | tf_op jit(solution)/shard_map/ppermute | solution.py:35
  42.4 26.0 %collective-permute-start.10 = (bf16[128,4096]{1,0:T(8,128)(2,1)}, bf16[128,4096]{1,0:T(8,128)(2,1)}, u32[]{:S(2)}, u32[]{:S(2)}) collective-permute-start(bf16[128,4096]{1,0:T(8,128)(2,1)} %shard_map.110.own_refs_0_), channel_id=1, source_target_pairs={{0,32},{8,40},{16,48},{24,56},{32,64},{40,72},{48,80},{56,88},{64,... | collective-permute-start | bytes 3145736 | tf_op jit(solution)/shard_map/ppermute | solution.py:35
  43.8 25.7 %copy-start = (bf16[128,4096]{1,0:T(8,128)(2,1)S(1)}, bf16[128,4096]{1,0:T(8,128)(2,1)}, u32[]{:S(2)}) copy-start(bf16[128,4096]{1,0:T(8,128)(2,1)} %shard_map.110.own_refs_0_) | copy-start | bytes 3145732
  59.5 15.7 %copy-start.2 = (bf16[128,4096]{1,0:T(8,128)(2,1)}, bf16[128,4096]{1,0:T(8,128)(2,1)S(1)}, u32[]{:S(2)}) copy-start(bf16[128,4096]{1,0:T(8,128)(2,1)S(1)} %collective-permute-done.12.other_refs_0_) | copy-start | bytes 3145732
  65.3 27.2 %copy-start.3 = (bf16[128,4096]{1,0:T(8,128)(2,1)}, bf16[128,4096]{1,0:T(8,128)(2,1)S(1)}, u32[]{:S(2)}) copy-start(bf16[128,4096]{1,0:T(8,128)(2,1)S(1)} %collective-permute-done.11.own_refs_1_) | copy-start | bytes 3145732
  68.4 6.8 %copy-start.1 = (bf16[4,512,128]{2,1,0:T(8,128)(2,1)S(1)}, bf16[4,512,128]{2,1,0:T(8,128)(2,1)}, u32[]{:S(2)}) copy-start(bf16[4,512,128]{2,1,0:T(8,128)(2,1)} %get-tuple-element.53.grad_refs_0_) | copy-start | bytes 1572868
  68.4 5.1 %collective-permute-start.13 = (bf16[8,512,128]{2,1,0:T(8,128)(2,1)}, bf16[8,512,128]{2,1,0:T(8,128)(2,1)S(1)}, u32[]{:S(2)}, u32[]{:S(2)}) collective-permute-start(bf16[8,512,128]{2,1,0:T(8,128)(2,1)} %get-tuple-element.55), channel_id=1, source_target_pairs={{0,8},{8,0},{16,24},{24,16},{32,40},{40,32},{48,56},{56,48},{64,72... | collective-permute-start | bytes 3145736 | tf_op jit(solution)/shard_map/ppermute | solution.py:39
  69.5 4.1 %collective-permute-start.14 = (bf16[128,4096]{1,0:T(8,128)(2,1)}, bf16[128,4096]{1,0:T(8,128)(2,1)}, u32[]{:S(2)}, u32[]{:S(2)}) collective-permute-start(bf16[128,4096]{1,0:T(8,128)(2,1)} %collective-permute-done.10.own_refs_3_), channel_id=1, source_target_pairs={{0,8},{8,0},{16,24},{24,16},{32,40},{40,32},{48,56},{56,48},{64,72... | collective-permute-start | bytes 3145736 | tf_op jit(solution)/shard_map/ppermute | solution.py:39
  69.5 25.7 %collective-permute-start.19 = (bf16[128,4096]{1,0:T(8,128)(2,1)S(1)}, bf16[128,4096]{1,0:T(8,128)(2,1)S(1)}, u32[]{:S(2)}, u32[]{:S(2)}) collective-permute-start(bf16[128,4096]{1,0:T(8,128)(2,1)S(1)} %copy-done), channel_id=1, source_target_pairs={{0,64},{8,72},{16,80},{24,88},{32,96},{40,104},{48,112},{56,120},{... | collective-permute-start | bytes 3145736 | tf_op jit(solution)/shard_map/ppermute | solution.py:35
  75.3 27.1 %collective-permute-start.16 = (bf16[6,512,128]{2,1,0:T(8,128)(2,1)S(1)}, bf16[6,512,128]{2,1,0:T(8,128)(2,1)S(1)}, u32[]{:S(2)}, u32[]{:S(2)}) collective-permute-start(bf16[6,512,128]{2,1,0:T(8,128)(2,1)S(1)} %get-tuple-element.85), channel_id=1, source_target_pairs={{0,6},{1,7},{2,0},{3,1},{4,2},{5,3},{6,4},{7,5},{8,14},{9,15},{10,... | collective-permute-start | bytes 2359304 | tf_op jit(solution)/shard_map/ppermute | solution.py:27
  78.0 25.4 %collective-permute-start.15 = (bf16[6,512,128]{2,1,0:T(8,128)(2,1)S(1)}, bf16[6,512,128]{2,1,0:T(8,128)(2,1)S(1)}, u32[]{:S(2)}, u32[]{:S(2)}) collective-permute-start(bf16[6,512,128]{2,1,0:T(8,128)(2,1)S(1)} %get-tuple-element.86), channel_id=1, source_target_pairs={{0,2},{1,3},{2,4},{3,5},{4,6},{5,7},{6,0},{7,1},{8,10},{9,11},{10,... | collective-permute-start | bytes 2359304 | tf_op jit(solution)/shard_map/ppermute | solution.py:27
  78.0 14.4 %collective-permute-start.18 = (bf16[4,512,128]{2,1,0:T(8,128)(2,1)S(1)}, bf16[4,512,128]{2,1,0:T(8,128)(2,1)S(1)}, u32[]{:S(2)}, u32[]{:S(2)}) collective-permute-start(bf16[4,512,128]{2,1,0:T(8,128)(2,1)S(1)} %copy-done.1), channel_id=1, source_target_pairs={{0,1},{1,0},{2,3},{3,2},{4,5},{5,4},{6,7},{7,6},{8,9},{9,8},{10,11... | collective-permute-start | bytes 1572872 | tf_op jit(solution)/shard_map/ppermute | solution.py:31
  80.0 22.4 %collective-permute-start.17 = (bf16[2,512,128]{2,1,0:T(8,128)(2,1)S(1)}, bf16[2,512,128]{2,1,0:T(8,128)(2,1)S(1)}, u32[]{:S(2)}, u32[]{:S(2)}) collective-permute-start(bf16[2,512,128]{2,1,0:T(8,128)(2,1)S(1)} %get-tuple-element.82), channel_id=1, source_target_pairs={{0,4},{1,5},{2,6},{3,7},{4,0},{5,1},{6,2},{7,3},{8,12},{9,13},{10,... | collective-permute-start | bytes 786440 | tf_op jit(solution)/shard_map/ppermute | solution.py:27
  92.5 15.7 %copy-start.10 = (bf16[4,512,128]{2,1,0:T(8,128)(2,1)}, bf16[4,512,128]{2,1,0:T(8,128)(2,1)S(1)}, u32[]{:S(2)}) copy-start(bf16[4,512,128]{2,1,0:T(8,128)(2,1)S(1)} %collective-permute-done.18.grad_refs_3_) | copy-start | bytes 1572868
  92.5 17.2 %collective-permute-start.22 = (bf16[128,4096]{1,0:T(8,128)(2,1)S(1)}, bf16[128,4096]{1,0:T(8,128)(2,1)S(1)}, u32[]{:S(2)}, u32[]{:S(2)}) collective-permute-start(bf16[128,4096]{1,0:T(8,128)(2,1)S(1)} %collective-permute-done.11.own_refs_1_), channel_id=1, source_target_pairs={{0,8},{8,0},{16,24},{24,16},{32,40},{40,32},{48,56},{56,48},{64,72... | collective-permute-start | bytes 3145736 | tf_op jit(solution)/shard_map/ppermute | solution.py:39
  95.2 12.9 %copy-start.4 = (bf16[128,4096]{1,0:T(8,128)(2,1)}, bf16[128,4096]{1,0:T(8,128)(2,1)S(1)}, u32[]{:S(2)}) copy-start(bf16[128,4096]{1,0:T(8,128)(2,1)S(1)} %collective-permute-done.19.own_refs_2_) | copy-start | bytes 3145732
  102.4 2.7 %copy-start.8 = (bf16[6,512,128]{2,1,0:T(8,128)(2,1)}, bf16[6,512,128]{2,1,0:T(8,128)(2,1)S(1)}, u32[]{:S(2)}) copy-start(bf16[6,512,128]{2,1,0:T(8,128)(2,1)S(1)} %collective-permute-done.16.grad_refs_2_) | copy-start | bytes 2359300
  103.4 1.7 %copy-start.9 = (bf16[6,512,128]{2,1,0:T(8,128)(2,1)}, bf16[6,512,128]{2,1,0:T(8,128)(2,1)S(1)}, u32[]{:S(2)}) copy-start(bf16[6,512,128]{2,1,0:T(8,128)(2,1)S(1)} %collective-permute-done.15.grad_refs_1_) | copy-start | bytes 2359300
  103.4 10.7 %collective-permute-start.21 = (bf16[128,4096]{1,0:T(8,128)(2,1)S(1)}, bf16[128,4096]{1,0:T(8,128)(2,1)S(1)}, u32[]{:S(2)}, u32[]{:S(2)}) collective-permute-start(bf16[128,4096]{1,0:T(8,128)(2,1)S(1)} %collective-permute-done.19.own_refs_2_), channel_id=1, source_target_pairs={{0,8},{8,0},{16,24},{24,16},{32,40},{40,32},{48,56},{56,48},{64,72... | collective-permute-start | bytes 3145736 | tf_op jit(solution)/shard_map/ppermute | solution.py:39
  105.1 9.0 %collective-permute-start.20 = (bf16[2,512,128]{2,1,0:T(8,128)(2,1)S(1)}, bf16[2,512,128]{2,1,0:T(8,128)(2,1)S(1)}, u32[]{:S(2)}, u32[]{:S(2)}) collective-permute-start(bf16[2,512,128]{2,1,0:T(8,128)(2,1)S(1)} %fusion.2), channel_id=1, source_target_pairs={{0,1},{1,0},{2,3},{3,2},{4,5},{5,4},{6,7},{7,6},{8,9},{9,8},{10,11... | collective-permute-start | bytes 786440 | tf_op jit(solution)/shard_map/ppermute | solution.py:31
  108.1 25.7 %collective-permute-start.23 = (bf16[8,512,128]{2,1,0:T(8,128)(2,1)}, bf16[8,512,128]{2,1,0:T(8,128)(2,1)}, u32[]{:S(2)}, u32[]{:S(2)}) collective-permute-start(bf16[8,512,128]{2,1,0:T(8,128)(2,1)} %pad_maximum_fusion.1), channel_id=1, source_target_pairs={{0,4},{1,5},{2,6},{3,7},{4,0},{5,1},{6,2},{7,3},{8,12},{9,13},{10,... | collective-permute-start | bytes 3145736 | tf_op jit(solution)/shard_map/ppermute | solution.py:27
  109.6 8.2 %copy-start.5 = (bf16[128,4096]{1,0:T(8,128)(2,1)}, bf16[128,4096]{1,0:T(8,128)(2,1)S(1)}, u32[]{:S(2)}) copy-start(bf16[128,4096]{1,0:T(8,128)(2,1)S(1)} %collective-permute-done.22.other_refs_1_) | copy-start | bytes 3145732
  114.1 3.8 %copy-start.6 = (bf16[128,4096]{1,0:T(8,128)(2,1)}, bf16[128,4096]{1,0:T(8,128)(2,1)S(1)}, u32[]{:S(2)}) copy-start(bf16[128,4096]{1,0:T(8,128)(2,1)S(1)} %collective-permute-done.21.other_refs_2_) | copy-start | bytes 3145732
  114.1 32.2 %collective-permute-start.24 = (bf16[8,512,128]{2,1,0:T(8,128)(2,1)}, bf16[8,512,128]{2,1,0:T(8,128)(2,1)S(1)}, u32[]{:S(2)}, u32[]{:S(2)}) collective-permute-start(bf16[8,512,128]{2,1,0:T(8,128)(2,1)} %pad_maximum_fusion), channel_id=1, source_target_pairs={{0,1},{1,0},{2,3},{3,2},{4,5},{5,4},{6,7},{7,6},{8,9},{9,8},{10,11... | collective-permute-start | bytes 3145736 | tf_op jit(solution)/shard_map/ppermute | solution.py:31
  116.1 8.6 %copy-start.11 = (bf16[2,512,128]{2,1,0:T(8,128)(2,1)}, bf16[2,512,128]{2,1,0:T(8,128)(2,1)S(1)}, u32[]{:S(2)}) copy-start(bf16[2,512,128]{2,1,0:T(8,128)(2,1)S(1)} %add_convert_fusion.1.rest_1__0_) | copy-start | bytes 786436
  116.1 22.0 %collective-permute-start.27 = (bf16[2,512,128]{2,1,0:T(8,128)(2,1)S(1)}, bf16[2,512,128]{2,1,0:T(8,128)(2,1)S(1)}, u32[]{:S(2)}, u32[]{:S(2)}) collective-permute-start(bf16[2,512,128]{2,1,0:T(8,128)(2,1)S(1)} %add_convert_fusion.1.rest_1__0_), channel_id=1, source_target_pairs={{0,6},{1,7},{2,0},{3,1},{4,2},{5,3},{6,4},{7,5},{8,14},{9,15},{10,... | collective-permute-start | bytes 786440 | tf_op jit(solution)/shard_map/ppermute | solution.py:27
  116.4 22.9 %collective-permute-start.26 = (bf16[2,512,128]{2,1,0:T(8,128)(2,1)S(1)}, bf16[2,512,128]{2,1,0:T(8,128)(2,1)S(1)}, u32[]{:S(2)}, u32[]{:S(2)}) collective-permute-start(bf16[2,512,128]{2,1,0:T(8,128)(2,1)S(1)} %add_convert_fusion.1.rest_1__0_), channel_id=1, source_target_pairs={{0,4},{1,5},{2,6},{3,7},{4,0},{5,1},{6,2},{7,3},{8,12},{9,13},{10,... | collective-permute-start | bytes 786440 | tf_op jit(solution)/shard_map/ppermute | solution.py:27
  116.7 29.6 %collective-permute-start.25 = (bf16[2,512,128]{2,1,0:T(8,128)(2,1)S(1)}, bf16[2,512,128]{2,1,0:T(8,128)(2,1)}, u32[]{:S(2)}, u32[]{:S(2)}) collective-permute-start(bf16[2,512,128]{2,1,0:T(8,128)(2,1)S(1)} %add_convert_fusion.1.rest_1__0_), channel_id=1, source_target_pairs={{0,2},{1,3},{2,4},{3,5},{4,6},{5,7},{6,0},{7,1},{8,10},{9,11},{10,... | collective-permute-start | bytes 786440 | tf_op jit(solution)/shard_map/ppermute | solution.py:27
  138.2 8.1 %copy-start.12 = (bf16[2,512,128]{2,1,0:T(8,128)(2,1)}, bf16[2,512,128]{2,1,0:T(8,128)(2,1)S(1)}, u32[]{:S(2)}) copy-start(bf16[2,512,128]{2,1,0:T(8,128)(2,1)S(1)} %collective-permute-done.27.rest_1__3_) | copy-start | bytes 786436
  139.4 6.9 %copy-start.13 = (bf16[2,512,128]{2,1,0:T(8,128)(2,1)}, bf16[2,512,128]{2,1,0:T(8,128)(2,1)S(1)}, u32[]{:S(2)}) copy-start(bf16[2,512,128]{2,1,0:T(8,128)(2,1)S(1)} %collective-permute-done.26.rest_1__2_) | copy-start | bytes 786436
  146.3 1.0 copy-start.7

commit v8 on v7

--- a/solution.py
+++ b/solution.py
@@ -445,31 +445,35 @@
         (grad_heads, keep, give, slab_own, slab_back, slab_ahead, own_other)
     )
 
-    give, back_other = lax.optimization_barrier((swap_cores(give), swap_cores(slab_back)))
-    summed = (keep.astype(jnp.float32) + give.astype(jnp.float32)).astype(jnp.bfloat16)
+    from_1, from_3 = along_y(grad_heads, 1), along_y(grad_heads, 3)
+    from_x = swap_x(grad_heads)
+    summed = (keep.astype(jnp.float32) + swap_cores(give).astype(jnp.float32)).astype(jnp.bfloat16)
     summed = summed.reshape(2, 4, count, HD)
-    from_1 = along_y(jnp.concatenate([grad_heads, summed[:, 3]]), 1)
-    from_3 = along_y(jnp.concatenate([grad_heads, summed[:, 1]]), 3)
-    rows_2 = along_y(summed[:, 2], 2)
-    from_x = swap_x(grad_heads)
+    rows_1, rows_3 = along_y(summed[:, 3], 1), along_y(summed[:, 1], 3)
+    from_1, from_3, from_x, to_2, slab_own = lax.optimization_barrier(
+        (from_1, from_3, from_x, summed[:, 2], slab_own)
+    )
+    rows_2 = along_y(to_2, 2)
+    from_x13 = swap_x(jnp.concatenate([from_1, from_3]))
     slab_far = along_z(slab_own, 2)
-    from_1, from_3, rows_2, from_x, slab_far = lax.optimization_barrier(
-        (from_1, from_3, rows_2, from_x, slab_far)
-    )
     rows_y = summed[:, 0].astype(jnp.float32)
-    for term in (from_1[heads:], from_3[heads:], rows_2):
+    for term in (rows_1, rows_3, rows_2):
         rows_y = rows_y + term.astype(jnp.float32)
     rows_y = rows_y.astype(jnp.bfloat16)
+    to_2 = jnp.concatenate([grad_heads, from_x])
+    rows_y, to_2, slab_back = lax.optimization_barrier((rows_y, to_2, slab_back))
     rows_x = swap_x(rows_y)
-    from_2 = along_y(jnp.concatenate([grad_heads, from_x]), 2)
-    far_other, ahead_other = swap_cores(slab_far), swap_cores(slab_ahead)
-    to_x = jnp.concatenate([from_1[:heads], from_3[:heads]])
-    rows_x, far_other, ahead_other, to_x = lax.optimization_barrier(
-        (rows_x, far_other, ahead_other, to_x)
-    )
-    from_x13 = swap_x(to_x)
+    from_2 = along_y(to_2, 2)
+    back_other = swap_cores(slab_back)
+    rows_x, slab_far, back_other, slab_ahead, from_x13 = lax.optimization_barrier(
+        (rows_x, slab_far, back_other, slab_ahead, from_x13)
+    )
     both = (rows_y.astype(jnp.float32) + rows_x.astype(jnp.float32)[::-1]).astype(jnp.bfloat16)
     shared = [both] + by_source(*to_all_y(both))
+
+    ahead_other = swap_cores(slab_ahead)
+    ahead_other, slab_far = lax.optimization_barrier((ahead_other, slab_far))
+    far_other = swap_cores(slab_far)
 
     slabs = [slab_own, slab_ahead, slab_far, slab_back]
     slabs_other = [own_other, ahead_other, far_other, back_other]

time: 159 us -> 176 us (1.11)
  waiting for transfers between devices: 69.9 us -> 79.2 us
  Pallas kernels: 36.3 us -> 43.2 us
  starting transfers between devices: 38.9 us -> 42.8 us
  other arithmetic: 8.97 us -> 5.62 us
    ppermute x13 -> x15, waiting for transfers between devices: 34.5 us -> 44 us  [along_y(): lax.ppermute(value, 'ctx', [(i, (i + 2 * step) % 8) for i in range(8)])]
    ppermute x5, waiting for transfers between devices: 21.1 us -> 30.3 us  [swap_x(): return lax.ppermute(value, 'ctx', [(i, i ^ 1) for i in range(8)])]
    ppermute x3, waiting for transfers between devices: 10.2 us -> 2.57 us  [along_z(): lax.ppermute(value, 'dp', [(i, (i + 4 * step) % 16) for i in range(16)])]
    pallas_call x1, Pallas kernels: 15.7 us -> 22.7 us  [attention(): pl.pallas_call(functools.partial(attention_kernel, heads), out_shape=(jax...]
    ppermute x13 -> x15, starting transfers between devices: 16.4 us -> 19.3 us  [along_y(): lax.ppermute(value, 'ctx', [(i, (i + 2 * step) % 8) for i in range(8)])]
    ppermute x7, starting transfers between devices: 9.17 us -> 11.1 us  [swap_cores(): return lax.ppermute(value, 'dp', [(i, i ^ 1) for i in range(16)])]
    ppermute x7, waiting for transfers between devices: 4.13 us -> 2.3 us  [swap_cores(): return lax.ppermute(value, 'dp', [(i, i ^ 1) for i in range(16)])]
  transfers between devices with their start and end apart: 28 -> 30, of which waited for: 18 -> 17; matrix products, arithmetic and copies ran while one was open for 6% -> 4% of each run, Pallas kernels for 16% -> 18%
where the time goes in v8:
time: 176 us
  waiting for transfers between devices  79.2 us (45%)
  Pallas kernels  43.2 us (25%)
  starting transfers between devices  42.8 us (24%)
  other arithmetic  5.62 us (3%)
  local copies, waits for them, and re-layouts  3.48 us (2%)
    ppermute x15, waiting for transfers between devices, along_y(): lax.ppermute(value, 'ctx', [(i, (i + 2 * step) % 8) for i in range(8)])  44 us
    ppermute x5, waiting for transfers between devices, swap_x(): return lax.ppermute(value, 'ctx', [(i, i ^ 1) for i in range(8)])  30.3 us
    pallas_call x1, Pallas kernels, attention(): pl.pallas_call(functools.partial(attention_kernel, heads), out_shape=(jax...  22.7 us
    ppermute x15, starting transfers between devices, along_y(): lax.ppermute(value, 'ctx', [(i, (i + 2 * step) % 8) for i in range(8)])  19.3 us
    pallas_call x2, Pallas kernels, weights(): pl.pallas_call(functools.partial(weight_kernel, last, tuple((start for _,...  18.1 us
    ppermute x7, starting transfers between devices, swap_cores(): return lax.ppermute(value, 'dp', [(i, i ^ 1) for i in range(16)])  11.1 us
    ppermute x5, starting transfers between devices, swap_x(): return lax.ppermute(value, 'ctx', [(i, i ^ 1) for i in range(8)])  8.66 us
    ppermute x3, starting transfers between devices, along_z(): lax.ppermute(value, 'dp', [(i, (i + 4 * step) % 16) for i in range(16)])  3.76 us
  transfers between devices with their start and end apart: 30, of which 17 were waited for; matrix products, arithmetic and copies ran while one was open for 4% of the time, Pallas kernels for 18%

profile of v8, /device:TPU:1, one launch (start us, length us, event | category | flops | bytes accessed | tf_op | source)
XLA Modules:
  0.0 175.6 jit_solution(10565889074481017097)
XLA Ops:
  0.8 1.4 dynamic-slice_bitcast_fusion
  2.3 3.7 %collective-permute-start.4 = (bf16[4,512,128]{2,1,0:T(8,128)(2,1)S(1)}, bf16[4,512,128]{2,1,0:T(8,128)(2,1)S(1)}, u32[]{:S(2)}, u32[]{:S(2)}) collective-permute-start(bf16[4,512,128]{2,1,0:T(8,128)(2,1)S(1)} %pad_maximum_fusion.3), channel_id=1, source_target_pairs={{0,1},{1,0},{2,3},{3,2},{4,5},{5,4},{6,7},{7,6},{8,9},{9,8},{10,11... | collective-permute-start | bytes 1572872 | tf_op jit(solution)/shard_map/ppermute | solution.py:31
  5.9 0.8 slice.36
  6.8 1.0 dynamic-slice_select_fusion
  7.8 3.0 %collective-permute-start.1 = (bf16[528,128]{1,0:T(8,128)(2,1)S(1)}, bf16[528,128]{1,0:T(8,128)(2,1)S(1)}, u32[]{:S(2)}, u32[]{:S(2)}) collective-permute-start(bf16[528,128]{1,0:T(8,128)(2,1)S(1)} %get-tuple-element.98), channel_id=1, source_target_pairs={{0,4},{1,5},{2,6},{3,7},{4,0},{5,1},{6,2},{7,3},{8,12},{9,13},{10,... | collective-permute-start | bytes 405512 | tf_op jit(solution)/shard_map/ppermute | solution.py:27
  11.2 2.3 %collective-permute-start.2 = (bf16[528,128]{1,0:T(8,128)(2,1)S(1)}, bf16[528,128]{1,0:T(8,128)(2,1)S(1)}, u32[]{:S(2)}, u32[]{:S(2)}) collective-permute-start(bf16[528,128]{1,0:T(8,128)(2,1)S(1)} %get-tuple-element.98), channel_id=1, source_target_pairs={{0,6},{1,7},{2,0},{3,1},{4,2},{5,3},{6,4},{7,5},{8,14},{9,15},{10,... | collective-permute-start | bytes 405512 | tf_op jit(solution)/shard_map/ppermute | solution.py:27
  13.6 3.7 %collective-permute-done = bf16[528,128]{1,0:T(8,128)(2,1)S(1)} collective-permute-done((bf16[528,128]{1,0:T(8,128)(2,1)S(1)}, bf16[528,128]{1,0:T(8,128)(2,1)S(1)}, u32[]{:S(2)}, u32[]{:S(2)}) %collective-permute-start) | collective-permute-done | bytes 135200 | tf_op jit(solution)/shard_map/ppermute | solution.py:27
  17.6 2.0 %collective-permute-start.5 = (bf16[2,512,128]{2,1,0:T(8,128)(2,1)S(1)}, bf16[2,512,128]{2,1,0:T(8,128)(2,1)S(1)}, u32[]{:S(2)}, u32[]{:S(2)}) collective-permute-start(bf16[2,512,128]{2,1,0:T(8,128)(2,1)S(1)} %pad_maximum_fusion.5), channel_id=1, source_target_pairs={{0,2},{1,3},{2,4},{3,5},{4,6},{5,7},{6,0},{7,1},{8,10},{9,11},{10,... | collective-permute-start | bytes 786440 | tf_op jit(solution)/shard_map/ppermute | solution.py:27
  19.6 2.3 %collective-permute-start.6 = (bf16[2,512,128]{2,1,0:T(8,128)(2,1)S(1)}, bf16[2,512,128]{2,1,0:T(8,128)(2,1)S(1)}, u32[]{:S(2)}, u32[]{:S(2)}) collective-permute-start(bf16[2,512,128]{2,1,0:T(8,128)(2,1)S(1)} %pad_maximum_fusion.6), channel_id=1, source_target_pairs={{0,4},{1,5},{2,6},{3,7},{4,0},{5,1},{6,2},{7,3},{8,12},{9,13},{10,... | collective-permute-start | bytes 786440 | tf_op jit(solution)/shard_map/ppermute | solution.py:27
  21.9 1.0 collective-permute-start.7
  22.9 2.4 %collective-permute-start.8 = (bf16[4,528,128]{2,1,0:T(8,128)(2,1)S(1)}, bf16[4,528,128]{2,1,0:T(8,128)(2,1)}, u32[]{:S(2)}, u32[]{:S(2)}) collective-permute-start(bf16[4,528,128]{2,1,0:T(8,128)(2,1)S(1)} %pad_maximum_fusion.2.mine_refs_0_), channel_id=1, source_target_pairs={{0,8},{8,0},{16,24},{24,16},{32,40},{40,32},{48,56},{56,48},{64,72... | collective-permute-start | bytes 1622024 | tf_op jit(solution)/shard_map/ppermute | solution.py:39
  25.4 0.7 pad_maximum_fusion.4.in_refs_0_
  26.2 5.0 %collective-permute-done.3.mine_refs_1_ = bf16[4,528,128]{2,1,0:T(8,128)(2,1)S(1)} collective-permute-done((bf16[4,528,128]{2,1,0:T(8,128)(2,1)S(1)}, bf16[4,528,128]{2,1,0:T(8,128)(2,1)S(1)}, u32[]{:S(2)}, u32[]{:S(2)}) %collective-permute-start.3) | collective-permute-done | bytes 540704 | tf_op jit(solution)/shard_map/ppermute | solution.py:31
  31.2 0.7 collective-permute-done.6.in_refs_2_
  32.1 2.6 %collective-permute-start.9 = (bf16[4,528,128]{2,1,0:T(8,128)(2,1)S(1)}, bf16[4,528,128]{2,1,0:T(8,128)(2,1)}, u32[]{:S(2)}, u32[]{:S(2)}) collective-permute-start(bf16[4,528,128]{2,1,0:T(8,128)(2,1)S(1)} %collective-permute-done.3.mine_refs_1_), channel_id=1, source_target_pairs={{0,8},{8,0},{16,24},{24,16},{32,40},{40,32},{48,56},{56,48},{64,72... | collective-permute-start | bytes 1622024 | tf_op jit(solution)/shard_map/ppermute | solution.py:39
  34.7 2.5 %shard_map.110.own_refs_0_ = bf16[128,4096]{1,0:T(8,128)(2,1)} custom-call(bf16[2,512,128]{2,1,0:T(8,128)(2,1)} %pad_maximum_fusion.4.in_refs_0_, bf16[2,512,128]{2,1,0:T(8,128)(2,1)} %copy-done.16, bf16[2,512,128]{2,1,0:T(8,128)(2,1)} %copy-done.17, bf16[2,512,128]{2,1,0:T(8,128)(2,1)} %copy-done.18), custom_call_target="tpu_custom_call" | custom-call | bytes 2097152 | tf_op jit(solution)/shard_map/pallas_call | solution.py:226
  37.2 0.7 collective-permute-start.12
  37.9 3.8 %collective-permute-start.11 = (bf16[128,4096]{1,0:T(8,128)(2,1)}, bf16[128,4096]{1,0:T(8,128)(2,1)S(1)}, u32[]{:S(2)}, u32[]{:S(2)}) collective-permute-start(bf16[128,4096]{1,0:T(8,128)(2,1)} %shard_map.110.own_refs_0_), channel_id=1, source_target_pairs={{0,96},{8,104},{16,112},{24,120},{32,0},{40,8},{48,16},{56,24},{64... | collective-permute-start | bytes 3145736 | tf_op jit(solution)/shard_map/ppermute | solution.py:35
  42.4 22.7 %shard_map.109 = (bf16[512,512]{1,0:T(8,128)(2,1)}, bf16[4,512,128]{2,1,0:T(8,128)(2,1)}, bf16[8,512,128]{2,1,0:T(8,128)(2,1)}, bf16[8,512,128]{2,1,0:T(8,128)(2,1)}) custom-call(s32[17]{0:T(128)} %pad_add_fusion.1.info_ref, bf16[512,512]{1,0:T(8,128)(2,1)} %q_ref.1, bf16[512,512]{1,0:T(8,128)(2,1)} %g_ref.1, bf16[4,528,128]{2,1,0:T(8,128)(2,1)} %copy-done.13, ...), custom_call_target="tpu_custom_call" | custom-call | flops 10737418240 | bytes 8388608 | tf_op jit(solution)/shard_map/pallas_call | solution.py:186
  65.1 2.6 %collective-permute-done.10.own_refs_3_ = bf16[128,4096]{1,0:T(8,128)(2,1)} collective-permute-done((bf16[128,4096]{1,0:T(8,128)(2,1)}, bf16[128,4096]{1,0:T(8,128)(2,1)}, u32[]{:S(2)}, u32[]{:S(2)}) %collective-permute-start.10) | collective-permute-done | bytes 1048608 | tf_op jit(solution)/shard_map/ppermute | solution.py:35
  67.6 1.1 collective-permute-start.16
  68.7 2.7 %collective-permute-start.15 = (bf16[4,512,128]{2,1,0:T(8,128)(2,1)}, bf16[4,512,128]{2,1,0:T(8,128)(2,1)S(1)}, u32[]{:S(2)}, u32[]{:S(2)}) collective-permute-start(bf16[4,512,128]{2,1,0:T(8,128)(2,1)} %get-tuple-element.55.grad_refs_0_), channel_id=1, source_target_pairs={{0,1},{1,0},{2,3},{3,2},{4,5},{5,4},{6,7},{7,6},{8,9},{9,8},{10,11... | collective-permute-start | bytes 1572872 | tf_op jit(solution)/shard_map/ppermute | solution.py:31
  71.5 1.8 %collective-permute-start.14 = (bf16[4,512,128]{2,1,0:T(8,128)(2,1)}, bf16[4,512,128]{2,1,0:T(8,128)(2,1)S(1)}, u32[]{:S(2)}, u32[]{:S(2)}) collective-permute-start(bf16[4,512,128]{2,1,0:T(8,128)(2,1)} %get-tuple-element.55.grad_refs_0_), channel_id=1, source_target_pairs={{0,6},{1,7},{2,0},{3,1},{4,2},{5,3},{6,4},{7,5},{8,14},{9,15},{10,... | collective-permute-start | bytes 1572872 | tf_op jit(solution)/shard_map/ppermute | solution.py:27
  73.3 1.5 add_convert_fusion
  74.9 9.1 %collective-permute-done.15.grad_refs_3_ = bf16[4,512,128]{2,1,0:T(8,128)(2,1)S(1)} collective-permute-done((bf16[4,512,128]{2,1,0:T(8,128)(2,1)}, bf16[4,512,128]{2,1,0:T(8,128)(2,1)S(1)}, u32[]{:S(2)}, u32[]{:S(2)}) %collective-permute-start.15) | collective-permute-done | bytes 524320 | tf_op jit(solution)/shard_map/ppermute | solution.py:31
  84.0 0.9 collective-permute-done.14.grad_refs_2_
  84.9 2.7 %collective-permute-done.13.grad_refs_1_ = bf16[4,512,128]{2,1,0:T(8,128)(2,1)S(1)} collective-permute-done((bf16[4,512,128]{2,1,0:T(8,128)(2,1)}, bf16[4,512,128]{2,1,0:T(8,128)(2,1)S(1)}, u32[]{:S(2)}, u32[]{:S(2)}) %collective-permute-start.13) | collective-permute-done | bytes 524320 | tf_op jit(solution)/shard_map/ppermute | solution.py:27
  87.7 1.0 collective-permute-start.17
  88.6 1.7 collective-permute-start.18
  90.4 1.4 collective-permute-start.23
  91.9 1.1 pad_maximum_fusion
  92.9 2.7 %collective-permute-done.19 = bf16[2,512,128]{2,1,0:T(8,128)(2,1)S(1)} collective-permute-done((bf16[2,512,128]{2,1,0:T(8,128)(2,1)S(1)}, bf16[2,512,128]{2,1,0:T(8,128)(2,1)S(1)}, u32[]{:S(2)}, u32[]{:S(2)}) %collective-permute-start.19) | collective-permute-done | bytes 262176 | tf_op jit(solution)/shard_map/ppermute | solution.py:27
  95.6 6.7 %collective-permute-done.17 = bf16[2,512,128]{2,1,0:T(8,128)(2,1)S(1)} collective-permute-done((bf16[2,512,128]{2,1,0:T(8,128)(2,1)S(1)}, bf16[2,512,128]{2,1,0:T(8,128)(2,1)S(1)}, u32[]{:S(2)}, u32[]{:S(2)}) %collective-permute-start.17) | collective-permute-done | bytes 262176 | tf_op jit(solution)/shard_map/ppermute | solution.py:27
  102.5 0.9 collective-permute-start.22
  104.1 16.2 %collective-permute-done.20 = bf16[2,512,128]{2,1,0:T(8,128)(2,1)S(1)} collective-permute-done((bf16[2,512,128]{2,1,0:T(8,128)(2,1)S(1)}, bf16[2,512,128]{2,1,0:T(8,128)(2,1)S(1)}, u32[]{:S(2)}, u32[]{:S(2)}) %collective-permute-start.20) | collective-permute-done | bytes 262176 | tf_op jit(solution)/shard_map/ppermute | solution.py:31
  120.3 3.0 %collective-permute-start.24 = (bf16[128,4096]{1,0:T(8,128)(2,1)S(1)}, bf16[128,4096]{1,0:T(8,128)(2,1)S(1)}, u32[]{:S(2)}, u32[]{:S(2)}) collective-permute-start(bf16[128,4096]{1,0:T(8,128)(2,1)S(1)} %collective-permute-done.11.own_refs_1_), channel_id=1, source_target_pairs={{0,8},{8,0},{16,24},{24,16},{32,40},{40,32},{48,56},{56,48},{64,72... | collective-permute-start | bytes 3145736 | tf_op jit(solution)/shard_map/ppermute | solution.py:39
  123.3 2.3 %collective-permute-done.24.other_refs_1_ = bf16[128,4096]{1,0:T(8,128)(2,1)S(1)} collective-permute-done((bf16[128,4096]{1,0:T(8,128)(2,1)S(1)}, bf16[128,4096]{1,0:T(8,128)(2,1)S(1)}, u32[]{:S(2)}, u32[]{:S(2)}) %collective-permute-start.24) | collective-permute-done | bytes 1048608 | tf_op jit(solution)/shard_map/ppermute | solution.py:39
  126.0 1.8 %collective-permute-start.26 = (bf16[8,512,128]{2,1,0:T(8,128)(2,1)}, bf16[8,512,128]{2,1,0:T(8,128)(2,1)}, u32[]{:S(2)}, u32[]{:S(2)}) collective-permute-start(bf16[8,512,128]{2,1,0:T(8,128)(2,1)} %pad_maximum_fusion), channel_id=1, source_target_pairs={{0,4},{1,5},{2,6},{3,7},{4,0},{5,1},{6,2},{7,3},{8,12},{9,13},{10,... | collective-permute-start | bytes 3145736 | tf_op jit(solution)/shard_map/ppermute | solution.py:27
  127.9 0.7 collective-permute-start.29
  128.6 0.7 collective-permute-start.28
  129.3 0.8 collective-permute-start.27
  130.0 1.0 copy-done.7
  131.0 6.8 %shard_map.111.rest_0_ = f32[1024,512]{1,0:T(8,128)} custom-call(s32[2]{0:T(128)} %copy-done.19, bf16[128,4096]{1,0:T(8,128)(2,1)} %shard_map.110.own_refs_0_, bf16[128,4096]{1,0:T(8,128)(2,1)} %copy-done.2, bf16[128,4096]{1,0:T(8,128)(2,1)} %copy-done.4, bf16[128,4096]{1,0:T(8,128)(2,1)} %collective-permute-done.10.own_refs_3_, ...), custom_call_target="tpu_custom_call" | custom-call | flops 2147483648 | bytes 10485760 | tf_op jit(solution)/shard_map/pallas_call | solution.py:381
  137.8 14.7 %collective-permute-done.26.grad_refs_0_.grad_refs_2_ = bf16[8,512,128]{2,1,0:T(8,128)(2,1)} collective-permute-done((bf16[8,512,128]{2,1,0:T(8,128)(2,1)}, bf16[8,512,128]{2,1,0:T(8,128)(2,1)}, u32[]{:S(2)}, u32[]{:S(2)}) %collective-permute-start.26) | collective-permute-done | bytes 1048608 | tf_op jit(solution)/shard_map/ppermute | solution.py:27
  152.5 3.7 %collective-permute-done.29.rest_1__3_ = bf16[2,512,128]{2,1,0:T(8,128)(2,1)S(1)} collective-permute-done((bf16[2,512,128]{2,1,0:T(8,128)(2,1)S(1)}, bf16[2,512,128]{2,1,0:T(8,128)(2,1)S(1)}, u32[]{:S(2)}, u32[]{:S(2)}) %collective-permute-start.29) | collective-permute-done | bytes 262176 | tf_op jit(solution)/shard_map/ppermute | solution.py:27
  156.2 1.8 %collective-permute-done.28.rest_1__2_ = bf16[2,512,128]{2,1,0:T(8,128)(2,1)S(1)} collective-permute-done((bf16[2,512,128]{2,1,0:T(8,128)(2,1)S(1)}, bf16[2,512,128]{2,1,0:T(8,128)(2,1)S(1)}, u32[]{:S(2)}, u32[]{:S(2)}) %collective-permute-start.28) | collective-permute-done | bytes 262176 | tf_op jit(solution)/shard_map/ppermute | solution.py:27
  158.0 6.1 %collective-permute-done.27.rest_1__1_ = bf16[2,512,128]{2,1,0:T(8,128)(2,1)} collective-permute-done((bf16[2,512,128]{2,1,0:T(8,128)(2,1)S(1)}, bf16[2,512,128]{2,1,0:T(8,128)(2,1)}, u32[]{:S(2)}, u32[]{:S(2)}) %collective-permute-start.27) | collective-permute-done | bytes 262176 | tf_op jit(solution)/shard_map/ppermute | solution.py:27
  164.1 11.3 %shard_map.112 = (f32[1024,512]{1,0:T(8,128)}, f32[64,1024]{1,0:T(8,128)}, f32[64,1024]{1,0:T(8,128)}, bf16[64,512]{1,0:T(8,128)(2,1)}, bf16[64,512]{1,0:T(8,128)(2,1)}) custom-call(s32[2]{0:T(128)} %copy-done.19, bf16[128,4096]{1,0:T(8,128)(2,1)} %shard_map.110.own_refs_0_, bf16[128,4096]{1,0:T(8,128)(2,1)} %copy-done.2, bf16[128,4096]{1,0:T(8,128)(2,1)} %copy-done.4, ...), custom_call_target="tpu_custom_call" | custom-call | flops 2147483648 | bytes 10485760 | tf_op jit(solution)/shard_map/pallas_call | solution.py:381
  (85 shorter events, 3.6 us)
Async XLA Ops:
  2.3 15.2 %collective-permute-start.4 = (bf16[4,512,128]{2,1,0:T(8,128)(2,1)S(1)}, bf16[4,512,128]{2,1,0:T(8,128)(2,1)S(1)}, u32[]{:S(2)}, u32[]{:S(2)}) collective-permute-start(bf16[4,512,128]{2,1,0:T(8,128)(2,1)S(1)} %pad_maximum_fusion.3), channel_id=1, source_target_pairs={{0,1},{1,0},{2,3},{3,2},{4,5},{5,4},{6,7},{7,6},{8,9},{9,8},{10,11... | collective-permute-start | bytes 1572872 | tf_op jit(solution)/shard_map/ppermute | solution.py:31
  7.8 5.7 %collective-permute-start.1 = (bf16[528,128]{1,0:T(8,128)(2,1)S(1)}, bf16[528,128]{1,0:T(8,128)(2,1)S(1)}, u32[]{:S(2)}, u32[]{:S(2)}) collective-permute-start(bf16[528,128]{1,0:T(8,128)(2,1)S(1)} %get-tuple-element.98), channel_id=1, source_target_pairs={{0,4},{1,5},{2,6},{3,7},{4,0},{5,1},{6,2},{7,3},{8,12},{9,13},{10,... | collective-permute-start | bytes 405512 | tf_op jit(solution)/shard_map/ppermute | solution.py:27
  10.8 6.4 %collective-permute-start = (bf16[528,128]{1,0:T(8,128)(2,1)S(1)}, bf16[528,128]{1,0:T(8,128)(2,1)S(1)}, u32[]{:S(2)}, u32[]{:S(2)}) collective-permute-start(bf16[528,128]{1,0:T(8,128)(2,1)S(1)} %get-tuple-element.98), channel_id=1, source_target_pairs={{0,2},{1,3},{2,4},{3,5},{4,6},{5,7},{6,0},{7,1},{8,10},{9,11},{10,... | collective-permute-start | bytes 405512 | tf_op jit(solution)/shard_map/ppermute | solution.py:27
  11.2 6.0 %collective-permute-start.2 = (bf16[528,128]{1,0:T(8,128)(2,1)S(1)}, bf16[528,128]{1,0:T(8,128)(2,1)S(1)}, u32[]{:S(2)}, u32[]{:S(2)}) collective-permute-start(bf16[528,128]{1,0:T(8,128)(2,1)S(1)} %get-tuple-element.98), channel_id=1, source_target_pairs={{0,6},{1,7},{2,0},{3,1},{4,2},{5,3},{6,4},{7,5},{8,14},{9,15},{10,... | collective-permute-start | bytes 405512 | tf_op jit(solution)/shard_map/ppermute | solution.py:27
  17.3 19.9 %copy-start.13 = (bf16[4,528,128]{2,1,0:T(8,128)(2,1)}, bf16[4,528,128]{2,1,0:T(8,128)(2,1)S(1)}, u32[]{:S(2)}) copy-start(bf16[4,528,128]{2,1,0:T(8,128)(2,1)S(1)} %pad_maximum_fusion.2.mine_refs_0_) | copy-start | bytes 1622020
  17.3 13.9 %collective-permute-start.3 = (bf16[4,528,128]{2,1,0:T(8,128)(2,1)S(1)}, bf16[4,528,128]{2,1,0:T(8,128)(2,1)S(1)}, u32[]{:S(2)}, u32[]{:S(2)}) collective-permute-start(bf16[4,528,128]{2,1,0:T(8,128)(2,1)S(1)} %pad_maximum_fusion.2.mine_refs_0_), channel_id=1, source_target_pairs={{0,1},{1,0},{2,3},{3,2},{4,5},{5,4},{6,7},{7,6},{8,9},{9,8},{10,11... | collective-permute-start | bytes 1622024 | tf_op jit(solution)/shard_map/ppermute | solution.py:31
  17.6 13.6 %collective-permute-start.5 = (bf16[2,512,128]{2,1,0:T(8,128)(2,1)S(1)}, bf16[2,512,128]{2,1,0:T(8,128)(2,1)S(1)}, u32[]{:S(2)}, u32[]{:S(2)}) collective-permute-start(bf16[2,512,128]{2,1,0:T(8,128)(2,1)S(1)} %pad_maximum_fusion.5), channel_id=1, source_target_pairs={{0,2},{1,3},{2,4},{3,5},{4,6},{5,7},{6,0},{7,1},{8,10},{9,11},{10,... | collective-permute-start | bytes 786440 | tf_op jit(solution)/shard_map/ppermute | solution.py:27
  19.6 12.3 %collective-permute-start.6 = (bf16[2,512,128]{2,1,0:T(8,128)(2,1)S(1)}, bf16[2,512,128]{2,1,0:T(8,128)(2,1)S(1)}, u32[]{:S(2)}, u32[]{:S(2)}) collective-permute-start(bf16[2,512,128]{2,1,0:T(8,128)(2,1)S(1)} %pad_maximum_fusion.6), channel_id=1, source_target_pairs={{0,4},{1,5},{2,6},{3,7},{4,0},{5,1},{6,2},{7,3},{8,12},{9,13},{10,... | collective-permute-start | bytes 786440 | tf_op jit(solution)/shard_map/ppermute | solution.py:27
  21.9 10.2 %collective-permute-start.7 = (bf16[2,512,128]{2,1,0:T(8,128)(2,1)S(1)}, bf16[2,512,128]{2,1,0:T(8,128)(2,1)S(1)}, u32[]{:S(2)}, u32[]{:S(2)}) collective-permute-start(bf16[2,512,128]{2,1,0:T(8,128)(2,1)S(1)} %pad_maximum_fusion.7), channel_id=1, source_target_pairs={{0,6},{1,7},{2,0},{3,1},{4,2},{5,3},{6,4},{7,5},{8,14},{9,15},{10,... | collective-permute-start | bytes 786440 | tf_op jit(solution)/shard_map/ppermute | solution.py:27
  22.9 42.1 %copy-start.19 = (s32[2]{0:T(128)}, s32[2]{0:T(128)S(1)}, u32[]{:S(2)}) copy-start(s32[2]{0:T(128)S(1)} %pad_add_fusion.place_ref) | copy-start | bytes 28
  22.9 19.5 %collective-permute-start.8 = (bf16[4,528,128]{2,1,0:T(8,128)(2,1)S(1)}, bf16[4,528,128]{2,1,0:T(8,128)(2,1)}, u32[]{:S(2)}, u32[]{:S(2)}) collective-permute-start(bf16[4,528,128]{2,1,0:T(8,128)(2,1)S(1)} %pad_maximum_fusion.2.mine_refs_0_), channel_id=1, source_target_pairs={{0,8},{8,0},{16,24},{24,16},{32,40},{40,32},{48,56},{56,48},{64,72... | collective-permute-start | bytes 1622024 | tf_op jit(solution)/shard_map/ppermute | solution.py:39
  31.2 11.2 %copy-start.20 = (bf16[4,528,128]{2,1,0:T(8,128)(2,1)}, bf16[4,528,128]{2,1,0:T(8,128)(2,1)S(1)}, u32[]{:S(2)}) copy-start(bf16[4,528,128]{2,1,0:T(8,128)(2,1)S(1)} %collective-permute-done.3.mine_refs_1_) | copy-start | bytes 1622020
  31.2 3.5 %copy-start.16 = (bf16[2,512,128]{2,1,0:T(8,128)(2,1)}, bf16[2,512,128]{2,1,0:T(8,128)(2,1)S(1)}, u32[]{:S(2)}) copy-start(bf16[2,512,128]{2,1,0:T(8,128)(2,1)S(1)} %collective-permute-done.5.in_refs_1_) | copy-start | bytes 786436
  32.1 10.3 %collective-permute-start.9 = (bf16[4,528,128]{2,1,0:T(8,128)(2,1)S(1)}, bf16[4,528,128]{2,1,0:T(8,128)(2,1)}, u32[]{:S(2)}, u32[]{:S(2)}) collective-permute-start(bf16[4,528,128]{2,1,0:T(8,128)(2,1)S(1)} %collective-permute-done.3.mine_refs_1_), channel_id=1, source_target_pairs={{0,8},{8,0},{16,24},{24,16},{32,40},{40,32},{48,56},{56,48},{64,72... | collective-permute-start | bytes 1622024 | tf_op jit(solution)/shard_map/ppermute | solution.py:39
  37.2 27.9 %collective-permute-start.12 = (bf16[128,4096]{1,0:T(8,128)(2,1)}, bf16[128,4096]{1,0:T(8,128)(2,1)S(1)}, u32[]{:S(2)}, u32[]{:S(2)}) collective-permute-start(bf16[128,4096]{1,0:T(8,128)(2,1)} %shard_map.110.own_refs_0_), channel_id=1, source_target_pairs={{0,8},{8,0},{16,24},{24,16},{32,40},{40,32},{48,56},{56,48},{64,72... | collective-permute-start | bytes 3145736 | tf_op jit(solution)/shard_map/ppermute | solution.py:39
  37.9 27.2 %collective-permute-start.11 = (bf16[128,4096]{1,0:T(8,128)(2,1)}, bf16[128,4096]{1,0:T(8,128)(2,1)S(1)}, u32[]{:S(2)}, u32[]{:S(2)}) collective-permute-start(bf16[128,4096]{1,0:T(8,128)(2,1)} %shard_map.110.own_refs_0_), channel_id=1, source_target_pairs={{0,96},{8,104},{16,112},{24,120},{32,0},{40,8},{48,16},{56,24},{64... | collective-permute-start | bytes 3145736 | tf_op jit(solution)/shard_map/ppermute | solution.py:35
  41.6 26.0 %collective-permute-start.10 = (bf16[128,4096]{1,0:T(8,128)(2,1)}, bf16[128,4096]{1,0:T(8,128)(2,1)}, u32[]{:S(2)}, u32[]{:S(2)}) collective-permute-start(bf16[128,4096]{1,0:T(8,128)(2,1)} %shard_map.110.own_refs_0_), channel_id=1, source_target_pairs={{0,32},{8,40},{16,48},{24,56},{32,64},{40,72},{48,80},{56,88},{64,... | collective-permute-start | bytes 3145736 | tf_op jit(solution)/shard_map/ppermute | solution.py:35
  65.0 9.9 %copy-start.1 = (bf16[128,4096]{1,0:T(8,128)(2,1)}, bf16[128,4096]{1,0:T(8,128)(2,1)S(1)}, u32[]{:S(2)}) copy-start(bf16[128,4096]{1,0:T(8,128)(2,1)S(1)} %collective-permute-done.12.other_refs_0_) | copy-start | bytes 3145732
  65.1 55.2 %copy-start.2 = (bf16[128,4096]{1,0:T(8,128)(2,1)}, bf16[128,4096]{1,0:T(8,128)(2,1)S(1)}, u32[]{:S(2)}) copy-start(bf16[128,4096]{1,0:T(8,128)(2,1)S(1)} %collective-permute-done.11.own_refs_1_) | copy-start | bytes 3145732
  67.6 5.7 %collective-permute-start.16 = (bf16[8,512,128]{2,1,0:T(8,128)(2,1)}, bf16[8,512,128]{2,1,0:T(8,128)(2,1)S(1)}, u32[]{:S(2)}, u32[]{:S(2)}) collective-permute-start(bf16[8,512,128]{2,1,0:T(8,128)(2,1)} %get-tuple-element.57), channel_id=1, source_target_pairs={{0,8},{8,0},{16,24},{24,16},{32,40},{40,32},{48,56},{56,48},{64,72... | collective-permute-start | bytes 3145736 | tf_op jit(solution)/shard_map/ppermute | solution.py:39
  68.7 15.3 %collective-permute-start.15 = (bf16[4,512,128]{2,1,0:T(8,128)(2,1)}, bf16[4,512,128]{2,1,0:T(8,128)(2,1)S(1)}, u32[]{:S(2)}, u32[]{:S(2)}) collective-permute-start(bf16[4,512,128]{2,1,0:T(8,128)(2,1)} %get-tuple-element.55.grad_refs_0_), channel_id=1, source_target_pairs={{0,1},{1,0},{2,3},{3,2},{4,5},{5,4},{6,7},{7,6},{8,9},{9,8},{10,11... | collective-permute-start | bytes 1572872 | tf_op jit(solution)/shard_map/ppermute | solution.py:31
  71.5 13.4 %collective-permute-start.14 = (bf16[4,512,128]{2,1,0:T(8,128)(2,1)}, bf16[4,512,128]{2,1,0:T(8,128)(2,1)S(1)}, u32[]{:S(2)}, u32[]{:S(2)}) collective-permute-start(bf16[4,512,128]{2,1,0:T(8,128)(2,1)} %get-tuple-element.55.grad_refs_0_), channel_id=1, source_target_pairs={{0,6},{1,7},{2,0},{3,1},{4,2},{5,3},{6,4},{7,5},{8,14},{9,15},{10,... | collective-permute-start | bytes 1572872 | tf_op jit(solution)/shard_map/ppermute | solution.py:27
  73.3 14.3 %collective-permute-start.13 = (bf16[4,512,128]{2,1,0:T(8,128)(2,1)}, bf16[4,512,128]{2,1,0:T(8,128)(2,1)S(1)}, u32[]{:S(2)}, u32[]{:S(2)}) collective-permute-start(bf16[4,512,128]{2,1,0:T(8,128)(2,1)} %get-tuple-element.55.grad_refs_0_), channel_id=1, source_target_pairs={{0,2},{1,3},{2,4},{3,5},{4,6},{5,7},{6,0},{7,1},{8,10},{9,11},{10,... | collective-permute-start | bytes 1572872 | tf_op jit(solution)/shard_map/ppermute | solution.py:27
  74.8 17.0 %copy-start = (bf16[128,4096]{1,0:T(8,128)(2,1)S(1)}, bf16[128,4096]{1,0:T(8,128)(2,1)}, u32[]{:S(2)}) copy-start(bf16[128,4096]{1,0:T(8,128)(2,1)} %shard_map.110.own_refs_0_) | copy-start | bytes 3145732
  74.8 17.0 %copy-start.8 = (bf16[4,512,128]{2,1,0:T(8,128)(2,1)S(1)}, bf16[4,512,128]{2,1,0:T(8,128)(2,1)}, u32[]{:S(2)}) copy-start(bf16[4,512,128]{2,1,0:T(8,128)(2,1)} %get-tuple-element.55.grad_refs_0_) | copy-start | bytes 1572868
  84.0 8.9 %copy-start.9 = (bf16[4,512,128]{2,1,0:T(8,128)(2,1)}, bf16[4,512,128]{2,1,0:T(8,128)(2,1)S(1)}, u32[]{:S(2)}) copy-start(bf16[4,512,128]{2,1,0:T(8,128)(2,1)S(1)} %collective-permute-done.15.grad_refs_3_) | copy-start | bytes 1572868
  84.9 8.0 %copy-start.10 = (bf16[4,512,128]{2,1,0:T(8,128)(2,1)}, bf16[4,512,128]{2,1,0:T(8,128)(2,1)S(1)}, u32[]{:S(2)}) copy-start(bf16[4,512,128]{2,1,0:T(8,128)(2,1)S(1)} %collective-permute-done.14.grad_refs_2_) | copy-start | bytes 1572868
  87.7 5.3 %copy-start.11 = (bf16[4,512,128]{2,1,0:T(8,128)(2,1)}, bf16[4,512,128]{2,1,0:T(8,128)(2,1)S(1)}, u32[]{:S(2)}) copy-start(bf16[4,512,128]{2,1,0:T(8,128)(2,1)S(1)} %collective-permute-done.13.grad_refs_1_) | copy-start | bytes 1572868
  87.7 8.0 %collective-permute-start.19 = (bf16[2,512,128]{2,1,0:T(8,128)(2,1)S(1)}, bf16[2,512,128]{2,1,0:T(8,128)(2,1)S(1)}, u32[]{:S(2)}, u32[]{:S(2)}) collective-permute-start(bf16[2,512,128]{2,1,0:T(8,128)(2,1)S(1)} %get-tuple-element.60), channel_id=1, source_target_pairs={{0,4},{1,5},{2,6},{3,7},{4,0},{5,1},{6,2},{7,3},{8,12},{9,13},{10,... | collective-permute-start | bytes 786440 | tf_op jit(solution)/shard_map/ppermute | solution.py:27
  87.7 14.7 %collective-permute-start.17 = (bf16[2,512,128]{2,1,0:T(8,128)(2,1)S(1)}, bf16[2,512,128]{2,1,0:T(8,128)(2,1)S(1)}, u32[]{:S(2)}, u32[]{:S(2)}) collective-permute-start(bf16[2,512,128]{2,1,0:T(8,128)(2,1)S(1)} %get-tuple-element.90), channel_id=1, source_target_pairs={{0,2},{1,3},{2,4},{3,5},{4,6},{5,7},{6,0},{7,1},{8,10},{9,11},{10,... | collective-permute-start | bytes 786440 | tf_op jit(solution)/shard_map/ppermute | solution.py:27
  88.6 13.7 %collective-permute-start.18 = (bf16[2,512,128]{2,1,0:T(8,128)(2,1)S(1)}, bf16[2,512,128]{2,1,0:T(8,128)(2,1)S(1)}, u32[]{:S(2)}, u32[]{:S(2)}) collective-permute-start(bf16[2,512,128]{2,1,0:T(8,128)(2,1)S(1)} %get-tuple-element.92), channel_id=1, source_target_pairs={{0,6},{1,7},{2,0},{3,1},{4,2},{5,3},{6,4},{7,5},{8,14},{9,15},{10,... | collective-permute-start | bytes 786440 | tf_op jit(solution)/shard_map/ppermute | solution.py:27
  90.4 29.8 %collective-permute-start.23 = (bf16[8,512,128]{2,1,0:T(8,128)(2,1)S(1)}, bf16[8,512,128]{2,1,0:T(8,128)(2,1)S(1)}, u32[]{:S(2)}, u32[]{:S(2)}) collective-permute-start(bf16[8,512,128]{2,1,0:T(8,128)(2,1)S(1)} %pad_maximum_fusion.1), channel_id=1, source_target_pairs={{0,1},{1,0},{2,3},{3,2},{4,5},{5,4},{6,7},{7,6},{8,9},{9,8},{10,11... | collective-permute-start | bytes 3145736 | tf_op jit(solution)/shard_map/ppermute | solution.py:31
  91.8 28.4 %collective-permute-start.21 = (bf16[128,4096]{1,0:T(8,128)(2,1)S(1)}, bf16[128,4096]{1,0:T(8,128)(2,1)S(1)}, u32[]{:S(2)}, u32[]{:S(2)}) collective-permute-start(bf16[128,4096]{1,0:T(8,128)(2,1)S(1)} %copy-done), channel_id=1, source_target_pairs={{0,64},{8,72},{16,80},{24,88},{32,96},{40,104},{48,112},{56,120},{... | collective-permute-start | bytes 3145736 | tf_op jit(solution)/shard_map/ppermute | solution.py:35
  102.5 17.8 %collective-permute-start.22 = (bf16[128,4096]{1,0:T(8,128)(2,1)}, bf16[128,4096]{1,0:T(8,128)(2,1)S(1)}, u32[]{:S(2)}, u32[]{:S(2)}) collective-permute-start(bf16[128,4096]{1,0:T(8,128)(2,1)} %collective-permute-done.10.own_refs_3_), channel_id=1, source_target_pairs={{0,8},{8,0},{16,24},{24,16},{32,40},{40,32},{48,56},{56,48},{64,72... | collective-permute-start | bytes 3145736 | tf_op jit(solution)/shard_map/ppermute | solution.py:39
  103.4 16.8 %collective-permute-start.20 = (bf16[2,512,128]{2,1,0:T(8,128)(2,1)S(1)}, bf16[2,512,128]{2,1,0:T(8,128)(2,1)S(1)}, u32[]{:S(2)}, u32[]{:S(2)}) collective-permute-start(bf16[2,512,128]{2,1,0:T(8,128)(2,1)S(1)} %fusion.2), channel_id=1, source_target_pairs={{0,1},{1,0},{2,3},{3,2},{4,5},{5,4},{6,7},{7,6},{8,9},{9,8},{10,11... | collective-permute-start | bytes 786440 | tf_op jit(solution)/shard_map/ppermute | solution.py:31
  120.3 17.5 %copy-start.3 = (bf16[8,512,128]{2,1,0:T(8,128)(2,1)}, bf16[8,512,128]{2,1,0:T(8,128)(2,1)S(1)}, u32[]{:S(2)}) copy-start(bf16[8,512,128]{2,1,0:T(8,128)(2,1)S(1)} %collective-permute-done.23.grad_refs_1_.grad_refs_3_) | copy-start | bytes 3145732
  120.3 5.3 %copy-start.4 = (bf16[128,4096]{1,0:T(8,128)(2,1)}, bf16[128,4096]{1,0:T(8,128)(2,1)S(1)}, u32[]{:S(2)}) copy-start(bf16[128,4096]{1,0:T(8,128)(2,1)S(1)} %collective-permute-done.21.own_refs_2_) | copy-start | bytes 3145732
  120.3 5.7 %copy-start.5 = (bf16[128,4096]{1,0:T(8,128)(2,1)}, bf16[128,4096]{1,0:T(8,128)(2,1)S(1)}, u32[]{:S(2)}) copy-start(bf16[128,4096]{1,0:T(8,128)(2,1)S(1)} %collective-permute-done.22.other_refs_3_) | copy-start | bytes 3145732
  120.3 5.3 %collective-permute-start.24 = (bf16[128,4096]{1,0:T(8,128)(2,1)S(1)}, bf16[128,4096]{1,0:T(8,128)(2,1)S(1)}, u32[]{:S(2)}, u32[]{:S(2)}) collective-permute-start(bf16[128,4096]{1,0:T(8,128)(2,1)S(1)} %collective-permute-done.11.own_refs_1_), channel_id=1, source_target_pairs={{0,8},{8,0},{16,24},{24,16},{32,40},{40,32},{48,56},{56,48},{64,72... | collective-permute-start | bytes 3145736 | tf_op jit(solution)/shard_map/ppermute | solution.py:39
  125.6 4.4 %copy-start.6 = (bf16[128,4096]{1,0:T(8,128)(2,1)}, bf16[128,4096]{1,0:T(8,128)(2,1)S(1)}, u32[]{:S(2)}) copy-start(bf16[128,4096]{1,0:T(8,128)(2,1)S(1)} %collective-permute-done.24.other_refs_1_) | copy-start | bytes 3145732
  125.6 4.4 %collective-permute-start.25 = (bf16[128,4096]{1,0:T(8,128)(2,1)S(1)}, bf16[128,4096]{1,0:T(8,128)(2,1)S(1)}, u32[]{:S(2)}, u32[]{:S(2)}) collective-permute-start(bf16[128,4096]{1,0:T(8,128)(2,1)S(1)} %collective-permute-done.21.own_refs_2_), channel_id=1, source_target_pairs={{0,8},{8,0},{16,24},{24,16},{32,40},{40,32},{48,56},{56,48},{64,72... | collective-permute-start | bytes 3145736 | tf_op jit(solution)/shard_map/ppermute | solution.py:39
  126.0 26.5 %collective-permute-start.26 = (bf16[8,512,128]{2,1,0:T(8,128)(2,1)}, bf16[8,512,128]{2,1,0:T(8,128)(2,1)}, u32[]{:S(2)}, u32[]{:S(2)}) collective-permute-start(bf16[8,512,128]{2,1,0:T(8,128)(2,1)} %pad_maximum_fusion), channel_id=1, source_target_pairs={{0,4},{1,5},{2,6},{3,7},{4,0},{5,1},{6,2},{7,3},{8,12},{9,13},{10,... | collective-permute-start | bytes 3145736 | tf_op jit(solution)/shard_map/ppermute | solution.py:27
  127.9 10.0 %copy-start.12 = (bf16[2,512,128]{2,1,0:T(8,128)(2,1)}, bf16[2,512,128]{2,1,0:T(8,128)(2,1)S(1)}, u32[]{:S(2)}) copy-start(bf16[2,512,128]{2,1,0:T(8,128)(2,1)S(1)} %add_convert_fusion.1.rest_1__0_) | copy-start | bytes 786436
  127.9 28.3 %collective-permute-start.29 = (bf16[2,512,128]{2,1,0:T(8,128)(2,1)S(1)}, bf16[2,512,128]{2,1,0:T(8,128)(2,1)S(1)}, u32[]{:S(2)}, u32[]{:S(2)}) collective-permute-start(bf16[2,512,128]{2,1,0:T(8,128)(2,1)S(1)} %add_convert_fusion.1.rest_1__0_), channel_id=1, source_target_pairs={{0,6},{1,7},{2,0},{3,1},{4,2},{5,3},{6,4},{7,5},{8,14},{9,15},{10,... | collective-permute-start | bytes 786440 | tf_op jit(solution)/shard_map/ppermute | solution.py:27
  128.6 29.4 %collective-permute-start.28 = (bf16[2,512,128]{2,1,0:T(8,128)(2,1)S(1)}, bf16[2,512,128]{2,1,0:T(8,128)(2,1)S(1)}, u32[]{:S(2)}, u32[]{:S(2)}) collective-permute-start(bf16[2,512,128]{2,1,0:T(8,128)(2,1)S(1)} %add_convert_fusion.1.rest_1__0_), channel_id=1, source_target_pairs={{0,4},{1,5},{2,6},{3,7},{4,0},{5,1},{6,2},{7,3},{8,12},{9,13},{10,... | collective-permute-start | bytes 786440 | tf_op jit(solution)/shard_map/ppermute | solution.py:27
  129.3 34.9 %collective-permute-start.27 = (bf16[2,512,128]{2,1,0:T(8,128)(2,1)S(1)}, bf16[2,512,128]{2,1,0:T(8,128)(2,1)}, u32[]{:S(2)}, u32[]{:S(2)}) collective-permute-start(bf16[2,512,128]{2,1,0:T(8,128)(2,1)S(1)} %add_convert_fusion.1.rest_1__0_), channel_id=1, source_target_pairs={{0,2},{1,3},{2,4},{3,5},{4,6},{5,7},{6,0},{7,1},{8,10},{9,11},{10,... | collective-permute-start | bytes 786440 | tf_op jit(solution)/shard_map/ppermute | solution.py:27
  156.2 8.0 %copy-start.14 = (bf16[2,512,128]{2,1,0:T(8,128)(2,1)}, bf16[2,512,128]{2,1,0:T(8,128)(2,1)S(1)}, u32[]{:S(2)}) copy-start(bf16[2,512,128]{2,1,0:T(8,128)(2,1)S(1)} %collective-permute-done.29.rest_1__3_) | copy-start | bytes 786436
  158.0 6.1 %copy-start.15 = (bf16[2,512,128]{2,1,0:T(8,128)(2,1)}, bf16[2,512,128]{2,1,0:T(8,128)(2,1)S(1)}, u32[]{:S(2)}) copy-start(bf16[2,512,128]{2,1,0:T(8,128)(2,1)S(1)} %collective-permute-done.28.rest_1__2_) | copy-start | bytes 786436
  (3 other events, 6.4 us)

commit v9 on v8

--- a/solution.py
+++ b/solution.py
@@ -450,29 +450,27 @@
     summed = (keep.astype(jnp.float32) + swap_cores(give).astype(jnp.float32)).astype(jnp.bfloat16)
     summed = summed.reshape(2, 4, count, HD)
     rows_1, rows_3 = along_y(summed[:, 3], 1), along_y(summed[:, 1], 3)
-    from_1, from_3, from_x, to_2, slab_own = lax.optimization_barrier(
-        (from_1, from_3, from_x, summed[:, 2], slab_own)
-    )
+    from_x, to_2 = lax.optimization_barrier((from_x, summed[:, 2]))
     rows_2 = along_y(to_2, 2)
-    from_x13 = swap_x(jnp.concatenate([from_1, from_3]))
+    from_1, from_3, rows_1, rows_3, rows_2, slab_own, slab_back, slab_ahead = lax.optimization_barrier(
+        (from_1, from_3, rows_1, rows_3, rows_2, slab_own, slab_back, slab_ahead)
+    )
     slab_far = along_z(slab_own, 2)
     rows_y = summed[:, 0].astype(jnp.float32)
     for term in (rows_1, rows_3, rows_2):
         rows_y = rows_y + term.astype(jnp.float32)
     rows_y = rows_y.astype(jnp.bfloat16)
-    to_2 = jnp.concatenate([grad_heads, from_x])
-    rows_y, to_2, slab_back = lax.optimization_barrier((rows_y, to_2, slab_back))
     rows_x = swap_x(rows_y)
-    from_2 = along_y(to_2, 2)
-    back_other = swap_cores(slab_back)
-    rows_x, slab_far, back_other, slab_ahead, from_x13 = lax.optimization_barrier(
-        (rows_x, slab_far, back_other, slab_ahead, from_x13)
-    )
+    from_2 = along_y(jnp.concatenate([grad_heads, from_x]), 2)
+    back_other, ahead_other = swap_cores(slab_back), swap_cores(slab_ahead)
+    to_x = jnp.concatenate([from_1, from_3])
+    rows_x, back_other, ahead_other, to_x = lax.optimization_barrier(
+        (rows_x, back_other, ahead_other, to_x)
+    )
+    from_x13 = swap_x(to_x)
     both = (rows_y.astype(jnp.float32) + rows_x.astype(jnp.float32)[::-1]).astype(jnp.bfloat16)
     shared = [both] + by_source(*to_all_y(both))
 
-    ahead_other = swap_cores(slab_ahead)
-    ahead_other, slab_far = lax.optimization_barrier((ahead_other, slab_far))
     far_other = swap_cores(slab_far)
 
     slabs = [slab_own, slab_ahead, slab_far, slab_back]

time: 176 us -> 179 us (1.017)
  starting transfers between devices: 42.8 us -> 45.2 us
    ppermute x3, waiting for transfers between devices: 2.57 us -> 25.2 us  [along_z(): lax.ppermute(value, 'dp', [(i, (i + 4 * step) % 16) for i in range(16)])]
    ppermute x5, waiting for transfers between devices: 30.3 us -> 14.1 us  [swap_x(): return lax.ppermute(value, 'ctx', [(i, i ^ 1) for i in range(8)])]
    ppermute x15, waiting for transfers between devices: 44 us -> 39.8 us  [along_y(): lax.ppermute(value, 'ctx', [(i, (i + 2 * step) % 8) for i in range(8)])]
    ppermute x5, starting transfers between devices: 8.66 us -> 11.8 us  [swap_x(): return lax.ppermute(value, 'ctx', [(i, i ^ 1) for i in range(8)])]
    ppermute x7, waiting for transfers between devices: 2.3 us -> 0.02 us  [swap_cores(): return lax.ppermute(value, 'dp', [(i, i ^ 1) for i in range(16)])]
    ppermute x7, starting transfers between devices: 11.1 us -> 9.23 us  [swap_cores(): return lax.ppermute(value, 'dp', [(i, i ^ 1) for i in range(16)])]
  transfers between devices with their start and end apart: 30 -> 30, of which waited for: 17 -> 15; matrix products, arithmetic and copies ran while one was open for 4% -> 4% of each run, Pallas kernels for 18% -> 18%
where the time goes in v9:
time: 179 us; the launch traced here: 178 us
  waiting for transfers between devices  79.1 us (44%)
  starting transfers between devices  45.2 us (25%)
  Pallas kernels  42.8 us (24%)
  other arithmetic  5.63 us (3%)
  local copies, waits for them, and re-layouts  4.41 us (2%)
    ppermute x15, waiting for transfers between devices, along_y(): lax.ppermute(value, 'ctx', [(i, (i + 2 * step) % 8) for i in range(8)])  39.8 us
    ppermute x3, waiting for transfers between devices, along_z(): lax.ppermute(value, 'dp', [(i, (i + 4 * step) % 16) for i in range(16)])  25.2 us
    pallas_call x1, Pallas kernels, attention(): pl.pallas_call(functools.partial(attention_kernel, heads), out_shape=(jax...  22.2 us
    ppermute x15, starting transfers between devices, along_y(): lax.ppermute(value, 'ctx', [(i, (i + 2 * step) % 8) for i in range(8)])  20.4 us
    pallas_call x2, Pallas kernels, weights(): pl.pallas_call(functools.partial(weight_kernel, last, tuple((start for _,...  18.1 us
    ppermute x5, waiting for transfers between devices, swap_x(): return lax.ppermute(value, 'ctx', [(i, i ^ 1) for i in range(8)])  14.1 us
    ppermute x5, starting transfers between devices, swap_x(): return lax.ppermute(value, 'ctx', [(i, i ^ 1) for i in range(8)])  11.8 us
    ppermute x7, starting transfers between devices, swap_cores(): return lax.ppermute(value, 'dp', [(i, i ^ 1) for i in range(16)])  9.23 us
  transfers between devices with their start and end apart: 30, of which 15 were waited for; matrix products, arithmetic and copies ran while one was open for 4% of the time, Pallas kernels for 18%

profile of v9, /device:TPU:1, one launch (start us, length us, event | category | flops | bytes accessed | tf_op | source)
XLA Modules:
  0.0 178.4 jit_solution(829672130791143688)
XLA Ops:
  0.8 1.4 dynamic-slice_bitcast_fusion
  2.3 3.7 %collective-permute-start.4 = (bf16[4,512,128]{2,1,0:T(8,128)(2,1)S(1)}, bf16[4,512,128]{2,1,0:T(8,128)(2,1)S(1)}, u32[]{:S(2)}, u32[]{:S(2)}) collective-permute-start(bf16[4,512,128]{2,1,0:T(8,128)(2,1)S(1)} %pad_maximum_fusion.3), channel_id=1, source_target_pairs={{0,1},{1,0},{2,3},{3,2},{4,5},{5,4},{6,7},{7,6},{8,9},{9,8},{10,11... | collective-permute-start | bytes 1572872 | tf_op jit(solution)/shard_map/ppermute | solution.py:31
  5.9 0.8 slice.36
  6.8 1.0 dynamic-slice_select_fusion
  7.8 3.0 %collective-permute-start.1 = (bf16[528,128]{1,0:T(8,128)(2,1)S(1)}, bf16[528,128]{1,0:T(8,128)(2,1)S(1)}, u32[]{:S(2)}, u32[]{:S(2)}) collective-permute-start(bf16[528,128]{1,0:T(8,128)(2,1)S(1)} %get-tuple-element.96), channel_id=1, source_target_pairs={{0,4},{1,5},{2,6},{3,7},{4,0},{5,1},{6,2},{7,3},{8,12},{9,13},{10,... | collective-permute-start | bytes 405512 | tf_op jit(solution)/shard_map/ppermute | solution.py:27
  11.2 2.3 %collective-permute-start.2 = (bf16[528,128]{1,0:T(8,128)(2,1)S(1)}, bf16[528,128]{1,0:T(8,128)(2,1)S(1)}, u32[]{:S(2)}, u32[]{:S(2)}) collective-permute-start(bf16[528,128]{1,0:T(8,128)(2,1)S(1)} %get-tuple-element.96), channel_id=1, source_target_pairs={{0,6},{1,7},{2,0},{3,1},{4,2},{5,3},{6,4},{7,5},{8,14},{9,15},{10,... | collective-permute-start | bytes 405512 | tf_op jit(solution)/shard_map/ppermute | solution.py:27
  13.6 3.7 %collective-permute-done = bf16[528,128]{1,0:T(8,128)(2,1)S(1)} collective-permute-done((bf16[528,128]{1,0:T(8,128)(2,1)S(1)}, bf16[528,128]{1,0:T(8,128)(2,1)S(1)}, u32[]{:S(2)}, u32[]{:S(2)}) %collective-permute-start) | collective-permute-done | bytes 135200 | tf_op jit(solution)/shard_map/ppermute | solution.py:27
  17.6 2.0 %collective-permute-start.5 = (bf16[2,512,128]{2,1,0:T(8,128)(2,1)S(1)}, bf16[2,512,128]{2,1,0:T(8,128)(2,1)S(1)}, u32[]{:S(2)}, u32[]{:S(2)}) collective-permute-start(bf16[2,512,128]{2,1,0:T(8,128)(2,1)S(1)} %pad_maximum_fusion.5), channel_id=1, source_target_pairs={{0,2},{1,3},{2,4},{3,5},{4,6},{5,7},{6,0},{7,1},{8,10},{9,11},{10,... | collective-permute-start | bytes 786440 | tf_op jit(solution)/shard_map/ppermute | solution.py:27
  19.6 2.3 %collective-permute-start.6 = (bf16[2,512,128]{2,1,0:T(8,128)(2,1)S(1)}, bf16[2,512,128]{2,1,0:T(8,128)(2,1)S(1)}, u32[]{:S(2)}, u32[]{:S(2)}) collective-permute-start(bf16[2,512,128]{2,1,0:T(8,128)(2,1)S(1)} %pad_maximum_fusion.6), channel_id=1, source_target_pairs={{0,4},{1,5},{2,6},{3,7},{4,0},{5,1},{6,2},{7,3},{8,12},{9,13},{10,... | collective-permute-start | bytes 786440 | tf_op jit(solution)/shard_map/ppermute | solution.py:27
  21.9 1.0 collective-permute-start.7
  22.9 2.4 %collective-permute-start.8 = (bf16[4,528,128]{2,1,0:T(8,128)(2,1)S(1)}, bf16[4,528,128]{2,1,0:T(8,128)(2,1)}, u32[]{:S(2)}, u32[]{:S(2)}) collective-permute-start(bf16[4,528,128]{2,1,0:T(8,128)(2,1)S(1)} %pad_maximum_fusion.2.mine_refs_0_), channel_id=1, source_target_pairs={{0,8},{8,0},{16,24},{24,16},{32,40},{40,32},{48,56},{56,48},{64,72... | collective-permute-start | bytes 1622024 | tf_op jit(solution)/shard_map/ppermute | solution.py:39
  25.4 0.7 pad_maximum_fusion.4.in_refs_0_
  26.2 5.0 %collective-permute-done.3.mine_refs_1_ = bf16[4,528,128]{2,1,0:T(8,128)(2,1)S(1)} collective-permute-done((bf16[4,528,128]{2,1,0:T(8,128)(2,1)S(1)}, bf16[4,528,128]{2,1,0:T(8,128)(2,1)S(1)}, u32[]{:S(2)}, u32[]{:S(2)}) %collective-permute-start.3) | collective-permute-done | bytes 540704 | tf_op jit(solution)/shard_map/ppermute | solution.py:31
  31.2 0.7 collective-permute-done.6.in_refs_2_
  32.1 2.6 %collective-permute-start.9 = (bf16[4,528,128]{2,1,0:T(8,128)(2,1)S(1)}, bf16[4,528,128]{2,1,0:T(8,128)(2,1)}, u32[]{:S(2)}, u32[]{:S(2)}) collective-permute-start(bf16[4,528,128]{2,1,0:T(8,128)(2,1)S(1)} %collective-permute-done.3.mine_refs_1_), channel_id=1, source_target_pairs={{0,8},{8,0},{16,24},{24,16},{32,40},{40,32},{48,56},{56,48},{64,72... | collective-permute-start | bytes 1622024 | tf_op jit(solution)/shard_map/ppermute | solution.py:39
  34.7 2.5 %shard_map.110.own_refs_0_ = bf16[128,4096]{1,0:T(8,128)(2,1)} custom-call(bf16[2,512,128]{2,1,0:T(8,128)(2,1)} %pad_maximum_fusion.4.in_refs_0_, bf16[2,512,128]{2,1,0:T(8,128)(2,1)} %copy-done.16, bf16[2,512,128]{2,1,0:T(8,128)(2,1)} %copy-done.17, bf16[2,512,128]{2,1,0:T(8,128)(2,1)} %copy-done.18), custom_call_target="tpu_custom_call" | custom-call | bytes 2097152 | tf_op jit(solution)/shard_map/pallas_call | solution.py:226
  37.2 0.7 collective-permute-start.12
  37.9 3.8 %collective-permute-start.11 = (bf16[128,4096]{1,0:T(8,128)(2,1)}, bf16[128,4096]{1,0:T(8,128)(2,1)S(1)}, u32[]{:S(2)}, u32[]{:S(2)}) collective-permute-start(bf16[128,4096]{1,0:T(8,128)(2,1)} %shard_map.110.own_refs_0_), channel_id=1, source_target_pairs={{0,96},{8,104},{16,112},{24,120},{32,0},{40,8},{48,16},{56,24},{64... | collective-permute-start | bytes 3145736 | tf_op jit(solution)/shard_map/ppermute | solution.py:35
  41.7 0.6 pad_add_fusion.1.info_ref
  42.4 22.2 %shard_map.109 = (bf16[512,512]{1,0:T(8,128)(2,1)}, bf16[4,512,128]{2,1,0:T(8,128)(2,1)}, bf16[8,512,128]{2,1,0:T(8,128)(2,1)}, bf16[8,512,128]{2,1,0:T(8,128)(2,1)}) custom-call(s32[17]{0:T(128)} %pad_add_fusion.1.info_ref, bf16[512,512]{1,0:T(8,128)(2,1)} %q_ref.1, bf16[512,512]{1,0:T(8,128)(2,1)} %g_ref.1, bf16[4,528,128]{2,1,0:T(8,128)(2,1)} %copy-done.13, ...), custom_call_target="tpu_custom_call" | custom-call | flops 10737418240 | bytes 8388608 | tf_op jit(solution)/shard_map/pallas_call | solution.py:186
  64.6 3.0 %collective-permute-done.10.own_refs_3_ = bf16[128,4096]{1,0:T(8,128)(2,1)} collective-permute-done((bf16[128,4096]{1,0:T(8,128)(2,1)}, bf16[128,4096]{1,0:T(8,128)(2,1)}, u32[]{:S(2)}, u32[]{:S(2)}) %collective-permute-start.10) | collective-permute-done | bytes 1048608 | tf_op jit(solution)/shard_map/ppermute | solution.py:35
  67.6 1.1 collective-permute-start.15
  68.7 2.7 %collective-permute-start.18 = (bf16[4,512,128]{2,1,0:T(8,128)(2,1)}, bf16[4,512,128]{2,1,0:T(8,128)(2,1)S(1)}, u32[]{:S(2)}, u32[]{:S(2)}) collective-permute-start(bf16[4,512,128]{2,1,0:T(8,128)(2,1)} %get-tuple-element.54.grad_refs_0_), channel_id=1, source_target_pairs={{0,1},{1,0},{2,3},{3,2},{4,5},{5,4},{6,7},{7,6},{8,9},{9,8},{10,11... | collective-permute-start | bytes 1572872 | tf_op jit(solution)/shard_map/ppermute | solution.py:31
  71.5 1.8 %collective-permute-start.14 = (bf16[4,512,128]{2,1,0:T(8,128)(2,1)}, bf16[4,512,128]{2,1,0:T(8,128)(2,1)S(1)}, u32[]{:S(2)}, u32[]{:S(2)}) collective-permute-start(bf16[4,512,128]{2,1,0:T(8,128)(2,1)} %get-tuple-element.54.grad_refs_0_), channel_id=1, source_target_pairs={{0,6},{1,7},{2,0},{3,1},{4,2},{5,3},{6,4},{7,5},{8,14},{9,15},{10,... | collective-permute-start | bytes 1572872 | tf_op jit(solution)/shard_map/ppermute | solution.py:27
  73.3 1.5 add_convert_fusion
  74.9 9.1 %collective-permute-done.18.grad_refs_3_ = bf16[4,512,128]{2,1,0:T(8,128)(2,1)S(1)} collective-permute-done((bf16[4,512,128]{2,1,0:T(8,128)(2,1)}, bf16[4,512,128]{2,1,0:T(8,128)(2,1)S(1)}, u32[]{:S(2)}, u32[]{:S(2)}) %collective-permute-start.18) | collective-permute-done | bytes 524320 | tf_op jit(solution)/shard_map/ppermute | solution.py:31
  84.0 2.1 %collective-permute-start.19 = (bf16[2,512,128]{2,1,0:T(8,128)(2,1)S(1)}, bf16[2,512,128]{2,1,0:T(8,128)(2,1)S(1)}, u32[]{:S(2)}, u32[]{:S(2)}) collective-permute-start(bf16[2,512,128]{2,1,0:T(8,128)(2,1)S(1)} %get-tuple-element.57), channel_id=1, source_target_pairs={{0,4},{1,5},{2,6},{3,7},{4,0},{5,1},{6,2},{7,3},{8,12},{9,13},{10,... | collective-permute-start | bytes 786440 | tf_op jit(solution)/shard_map/ppermute | solution.py:27
  86.1 1.3 collective-permute-start.17
  87.7 5.0 %collective-permute-done.19 = bf16[2,512,128]{2,1,0:T(8,128)(2,1)S(1)} collective-permute-done((bf16[2,512,128]{2,1,0:T(8,128)(2,1)S(1)}, bf16[2,512,128]{2,1,0:T(8,128)(2,1)S(1)}, u32[]{:S(2)}, u32[]{:S(2)}) %collective-permute-start.19) | collective-permute-done | bytes 262176 | tf_op jit(solution)/shard_map/ppermute | solution.py:27
  92.7 5.2 %collective-permute-done.17 = bf16[2,512,128]{2,1,0:T(8,128)(2,1)S(1)} collective-permute-done((bf16[2,512,128]{2,1,0:T(8,128)(2,1)S(1)}, bf16[2,512,128]{2,1,0:T(8,128)(2,1)S(1)}, u32[]{:S(2)}, u32[]{:S(2)}) %collective-permute-start.17) | collective-permute-done | bytes 262176 | tf_op jit(solution)/shard_map/ppermute | solution.py:27
  97.9 1.7 collective-permute-done.16
  99.6 0.8 collective-permute-start.23
  100.6 2.4 %collective-permute-start.21 = (bf16[2,512,128]{2,1,0:T(8,128)(2,1)S(1)}, bf16[2,512,128]{2,1,0:T(8,128)(2,1)S(1)}, u32[]{:S(2)}, u32[]{:S(2)}) collective-permute-start(bf16[2,512,128]{2,1,0:T(8,128)(2,1)S(1)} %fusion.2), channel_id=1, source_target_pairs={{0,1},{1,0},{2,3},{3,2},{4,5},{5,4},{6,7},{7,6},{8,9},{9,8},{10,11... | collective-permute-start | bytes 786440 | tf_op jit(solution)/shard_map/ppermute | solution.py:31
  103.0 22.1 %collective-permute-done.20.own_refs_2_ = bf16[128,4096]{1,0:T(8,128)(2,1)S(1)} collective-permute-done((bf16[128,4096]{1,0:T(8,128)(2,1)S(1)}, bf16[128,4096]{1,0:T(8,128)(2,1)S(1)}, u32[]{:S(2)}, u32[]{:S(2)}) %collective-permute-start.20) | collective-permute-done | bytes 1048608 | tf_op jit(solution)/shard_map/ppermute | solution.py:35
  125.2 1.6 collective-permute-start.24
  126.7 1.1 pad_maximum_fusion.1
  127.8 1.9 %collective-permute-start.25 = (bf16[8,512,128]{2,1,0:T(8,128)(2,1)}, bf16[8,512,128]{2,1,0:T(8,128)(2,1)}, u32[]{:S(2)}, u32[]{:S(2)}) collective-permute-start(bf16[8,512,128]{2,1,0:T(8,128)(2,1)} %pad_maximum_fusion.1), channel_id=1, source_target_pairs={{0,4},{1,5},{2,6},{3,7},{4,0},{5,1},{6,2},{7,3},{8,12},{9,13},{10,... | collective-permute-start | bytes 3145736 | tf_op jit(solution)/shard_map/ppermute | solution.py:27
  129.9 2.8 %collective-permute-start.26 = (bf16[8,512,128]{2,1,0:T(8,128)(2,1)S(1)}, bf16[8,512,128]{2,1,0:T(8,128)(2,1)S(1)}, u32[]{:S(2)}, u32[]{:S(2)}) collective-permute-start(bf16[8,512,128]{2,1,0:T(8,128)(2,1)S(1)} %pad_maximum_fusion), channel_id=1, source_target_pairs={{0,1},{1,0},{2,3},{3,2},{4,5},{5,4},{6,7},{7,6},{8,9},{9,8},{10,11... | collective-permute-start | bytes 3145736 | tf_op jit(solution)/shard_map/ppermute | solution.py:31
  132.8 1.1 collective-permute-start.29
  133.9 1.0 collective-permute-start.28
  135.0 0.9 copy-done.6
  135.9 6.8 %shard_map.111.rest_0_ = f32[1024,512]{1,0:T(8,128)} custom-call(s32[2]{0:T(128)} %copy-done.19, bf16[128,4096]{1,0:T(8,128)(2,1)} %shard_map.110.own_refs_0_, bf16[128,4096]{1,0:T(8,128)(2,1)} %copy-done.2, bf16[128,4096]{1,0:T(8,128)(2,1)} %copy-done.3, bf16[128,4096]{1,0:T(8,128)(2,1)} %collective-permute-done.10.own_refs_3_, ...), custom_call_target="tpu_custom_call" | custom-call | flops 2147483648 | bytes 10485760 | tf_op jit(solution)/shard_map/pallas_call | solution.py:381
  142.7 11.6 %collective-permute-done.25.grad_refs_0_.grad_refs_2_ = bf16[8,512,128]{2,1,0:T(8,128)(2,1)} collective-permute-done((bf16[8,512,128]{2,1,0:T(8,128)(2,1)}, bf16[8,512,128]{2,1,0:T(8,128)(2,1)}, u32[]{:S(2)}, u32[]{:S(2)}) %collective-permute-start.25) | collective-permute-done | bytes 1048608 | tf_op jit(solution)/shard_map/ppermute | solution.py:27
  154.4 4.8 %collective-permute-done.29.rest_1__3_ = bf16[2,512,128]{2,1,0:T(8,128)(2,1)S(1)} collective-permute-done((bf16[2,512,128]{2,1,0:T(8,128)(2,1)S(1)}, bf16[2,512,128]{2,1,0:T(8,128)(2,1)S(1)}, u32[]{:S(2)}, u32[]{:S(2)}) %collective-permute-start.29) | collective-permute-done | bytes 262176 | tf_op jit(solution)/shard_map/ppermute | solution.py:27
  159.2 0.7 collective-permute-done.28.rest_1__2_
  159.9 6.0 %collective-permute-done.27.rest_1__1_ = bf16[2,512,128]{2,1,0:T(8,128)(2,1)} collective-permute-done((bf16[2,512,128]{2,1,0:T(8,128)(2,1)S(1)}, bf16[2,512,128]{2,1,0:T(8,128)(2,1)}, u32[]{:S(2)}, u32[]{:S(2)}) %collective-permute-start.27) | collective-permute-done | bytes 262176 | tf_op jit(solution)/shard_map/ppermute | solution.py:27
  165.9 1.0 copy-done.7
  167.0 11.3 %shard_map.112 = (f32[1024,512]{1,0:T(8,128)}, f32[64,1024]{1,0:T(8,128)}, f32[64,1024]{1,0:T(8,128)}, bf16[64,512]{1,0:T(8,128)(2,1)}, bf16[64,512]{1,0:T(8,128)(2,1)}) custom-call(s32[2]{0:T(128)} %copy-done.19, bf16[128,4096]{1,0:T(8,128)(2,1)} %shard_map.110.own_refs_0_, bf16[128,4096]{1,0:T(8,128)(2,1)} %copy-done.2, bf16[128,4096]{1,0:T(8,128)(2,1)} %copy-done.3, ...), custom_call_target="tpu_custom_call" | custom-call | flops 2147483648 | bytes 10485760 | tf_op jit(solution)/shard_map/pallas_call | solution.py:381
  (85 shorter events, 2.4 us)
Async XLA Ops:
  2.3 15.2 %collective-permute-start.4 = (bf16[4,512,128]{2,1,0:T(8,128)(2,1)S(1)}, bf16[4,512,128]{2,1,0:T(8,128)(2,1)S(1)}, u32[]{:S(2)}, u32[]{:S(2)}) collective-permute-start(bf16[4,512,128]{2,1,0:T(8,128)(2,1)S(1)} %pad_maximum_fusion.3), channel_id=1, source_target_pairs={{0,1},{1,0},{2,3},{3,2},{4,5},{5,4},{6,7},{7,6},{8,9},{9,8},{10,11... | collective-permute-start | bytes 1572872 | tf_op jit(solution)/shard_map/ppermute | solution.py:31
  7.8 5.7 %collective-permute-start.1 = (bf16[528,128]{1,0:T(8,128)(2,1)S(1)}, bf16[528,128]{1,0:T(8,128)(2,1)S(1)}, u32[]{:S(2)}, u32[]{:S(2)}) collective-permute-start(bf16[528,128]{1,0:T(8,128)(2,1)S(1)} %get-tuple-element.96), channel_id=1, source_target_pairs={{0,4},{1,5},{2,6},{3,7},{4,0},{5,1},{6,2},{7,3},{8,12},{9,13},{10,... | collective-permute-start | bytes 405512 | tf_op jit(solution)/shard_map/ppermute | solution.py:27
  10.8 6.4 %collective-permute-start = (bf16[528,128]{1,0:T(8,128)(2,1)S(1)}, bf16[528,128]{1,0:T(8,128)(2,1)S(1)}, u32[]{:S(2)}, u32[]{:S(2)}) collective-permute-start(bf16[528,128]{1,0:T(8,128)(2,1)S(1)} %get-tuple-element.96), channel_id=1, source_target_pairs={{0,2},{1,3},{2,4},{3,5},{4,6},{5,7},{6,0},{7,1},{8,10},{9,11},{10,... | collective-permute-start | bytes 405512 | tf_op jit(solution)/shard_map/ppermute | solution.py:27
  11.2 6.0 %collective-permute-start.2 = (bf16[528,128]{1,0:T(8,128)(2,1)S(1)}, bf16[528,128]{1,0:T(8,128)(2,1)S(1)}, u32[]{:S(2)}, u32[]{:S(2)}) collective-permute-start(bf16[528,128]{1,0:T(8,128)(2,1)S(1)} %get-tuple-element.96), channel_id=1, source_target_pairs={{0,6},{1,7},{2,0},{3,1},{4,2},{5,3},{6,4},{7,5},{8,14},{9,15},{10,... | collective-permute-start | bytes 405512 | tf_op jit(solution)/shard_map/ppermute | solution.py:27
  17.3 19.9 %copy-start.13 = (bf16[4,528,128]{2,1,0:T(8,128)(2,1)}, bf16[4,528,128]{2,1,0:T(8,128)(2,1)S(1)}, u32[]{:S(2)}) copy-start(bf16[4,528,128]{2,1,0:T(8,128)(2,1)S(1)} %pad_maximum_fusion.2.mine_refs_0_) | copy-start | bytes 1622020
  17.3 13.9 %collective-permute-start.3 = (bf16[4,528,128]{2,1,0:T(8,128)(2,1)S(1)}, bf16[4,528,128]{2,1,0:T(8,128)(2,1)S(1)}, u32[]{:S(2)}, u32[]{:S(2)}) collective-permute-start(bf16[4,528,128]{2,1,0:T(8,128)(2,1)S(1)} %pad_maximum_fusion.2.mine_refs_0_), channel_id=1, source_target_pairs={{0,1},{1,0},{2,3},{3,2},{4,5},{5,4},{6,7},{7,6},{8,9},{9,8},{10,11... | collective-permute-start | bytes 1622024 | tf_op jit(solution)/shard_map/ppermute | solution.py:31
  17.6 13.6 %collective-permute-start.5 = (bf16[2,512,128]{2,1,0:T(8,128)(2,1)S(1)}, bf16[2,512,128]{2,1,0:T(8,128)(2,1)S(1)}, u32[]{:S(2)}, u32[]{:S(2)}) collective-permute-start(bf16[2,512,128]{2,1,0:T(8,128)(2,1)S(1)} %pad_maximum_fusion.5), channel_id=1, source_target_pairs={{0,2},{1,3},{2,4},{3,5},{4,6},{5,7},{6,0},{7,1},{8,10},{9,11},{10,... | collective-permute-start | bytes 786440 | tf_op jit(solution)/shard_map/ppermute | solution.py:27
  19.6 12.3 %collective-permute-start.6 = (bf16[2,512,128]{2,1,0:T(8,128)(2,1)S(1)}, bf16[2,512,128]{2,1,0:T(8,128)(2,1)S(1)}, u32[]{:S(2)}, u32[]{:S(2)}) collective-permute-start(bf16[2,512,128]{2,1,0:T(8,128)(2,1)S(1)} %pad_maximum_fusion.6), channel_id=1, source_target_pairs={{0,4},{1,5},{2,6},{3,7},{4,0},{5,1},{6,2},{7,3},{8,12},{9,13},{10,... | collective-permute-start | bytes 786440 | tf_op jit(solution)/shard_map/ppermute | solution.py:27
  21.9 10.2 %collective-permute-start.7 = (bf16[2,512,128]{2,1,0:T(8,128)(2,1)S(1)}, bf16[2,512,128]{2,1,0:T(8,128)(2,1)S(1)}, u32[]{:S(2)}, u32[]{:S(2)}) collective-permute-start(bf16[2,512,128]{2,1,0:T(8,128)(2,1)S(1)} %pad_maximum_fusion.7), channel_id=1, source_target_pairs={{0,6},{1,7},{2,0},{3,1},{4,2},{5,3},{6,4},{7,5},{8,14},{9,15},{10,... | collective-permute-start | bytes 786440 | tf_op jit(solution)/shard_map/ppermute | solution.py:27
  22.9 41.6 %copy-start.19 = (s32[2]{0:T(128)}, s32[2]{0:T(128)S(1)}, u32[]{:S(2)}) copy-start(s32[2]{0:T(128)S(1)} %pad_add_fusion.place_ref) | copy-start | bytes 28
  22.9 19.5 %collective-permute-start.8 = (bf16[4,528,128]{2,1,0:T(8,128)(2,1)S(1)}, bf16[4,528,128]{2,1,0:T(8,128)(2,1)}, u32[]{:S(2)}, u32[]{:S(2)}) collective-permute-start(bf16[4,528,128]{2,1,0:T(8,128)(2,1)S(1)} %pad_maximum_fusion.2.mine_refs_0_), channel_id=1, source_target_pairs={{0,8},{8,0},{16,24},{24,16},{32,40},{40,32},{48,56},{56,48},{64,72... | collective-permute-start | bytes 1622024 | tf_op jit(solution)/shard_map/ppermute | solution.py:39
  31.2 11.2 %copy-start.20 = (bf16[4,528,128]{2,1,0:T(8,128)(2,1)}, bf16[4,528,128]{2,1,0:T(8,128)(2,1)S(1)}, u32[]{:S(2)}) copy-start(bf16[4,528,128]{2,1,0:T(8,128)(2,1)S(1)} %collective-permute-done.3.mine_refs_1_) | copy-start | bytes 1622020
  31.2 3.5 %copy-start.16 = (bf16[2,512,128]{2,1,0:T(8,128)(2,1)}, bf16[2,512,128]{2,1,0:T(8,128)(2,1)S(1)}, u32[]{:S(2)}) copy-start(bf16[2,512,128]{2,1,0:T(8,128)(2,1)S(1)} %collective-permute-done.5.in_refs_1_) | copy-start | bytes 786436
  31.9 2.8 %copy-start.17 = (bf16[2,512,128]{2,1,0:T(8,128)(2,1)}, bf16[2,512,128]{2,1,0:T(8,128)(2,1)S(1)}, u32[]{:S(2)}) copy-start(bf16[2,512,128]{2,1,0:T(8,128)(2,1)S(1)} %collective-permute-done.6.in_refs_2_) | copy-start | bytes 786436
  32.1 10.3 %collective-permute-start.9 = (bf16[4,528,128]{2,1,0:T(8,128)(2,1)S(1)}, bf16[4,528,128]{2,1,0:T(8,128)(2,1)}, u32[]{:S(2)}, u32[]{:S(2)}) collective-permute-start(bf16[4,528,128]{2,1,0:T(8,128)(2,1)S(1)} %collective-permute-done.3.mine_refs_1_), channel_id=1, source_target_pairs={{0,8},{8,0},{16,24},{24,16},{32,40},{40,32},{48,56},{56,48},{64,72... | collective-permute-start | bytes 1622024 | tf_op jit(solution)/shard_map/ppermute | solution.py:39
  37.2 27.4 %collective-permute-start.12 = (bf16[128,4096]{1,0:T(8,128)(2,1)}, bf16[128,4096]{1,0:T(8,128)(2,1)S(1)}, u32[]{:S(2)}, u32[]{:S(2)}) collective-permute-start(bf16[128,4096]{1,0:T(8,128)(2,1)} %shard_map.110.own_refs_0_), channel_id=1, source_target_pairs={{0,8},{8,0},{16,24},{24,16},{32,40},{40,32},{48,56},{56,48},{64,72... | collective-permute-start | bytes 3145736 | tf_op jit(solution)/shard_map/ppermute | solution.py:39
  37.9 26.7 %collective-permute-start.11 = (bf16[128,4096]{1,0:T(8,128)(2,1)}, bf16[128,4096]{1,0:T(8,128)(2,1)S(1)}, u32[]{:S(2)}, u32[]{:S(2)}) collective-permute-start(bf16[128,4096]{1,0:T(8,128)(2,1)} %shard_map.110.own_refs_0_), channel_id=1, source_target_pairs={{0,96},{8,104},{16,112},{24,120},{32,0},{40,8},{48,16},{56,24},{64... | collective-permute-start | bytes 3145736 | tf_op jit(solution)/shard_map/ppermute | solution.py:35
  41.6 26.0 %collective-permute-start.10 = (bf16[128,4096]{1,0:T(8,128)(2,1)}, bf16[128,4096]{1,0:T(8,128)(2,1)}, u32[]{:S(2)}, u32[]{:S(2)}) collective-permute-start(bf16[128,4096]{1,0:T(8,128)(2,1)} %shard_map.110.own_refs_0_), channel_id=1, source_target_pairs={{0,32},{8,40},{16,48},{24,56},{32,64},{40,72},{48,80},{56,88},{64,... | collective-permute-start | bytes 3145736 | tf_op jit(solution)/shard_map/ppermute | solution.py:35
  64.6 10.3 %copy-start.1 = (bf16[128,4096]{1,0:T(8,128)(2,1)}, bf16[128,4096]{1,0:T(8,128)(2,1)S(1)}, u32[]{:S(2)}) copy-start(bf16[128,4096]{1,0:T(8,128)(2,1)S(1)} %collective-permute-done.12.other_refs_0_) | copy-start | bytes 3145732
  64.6 35.0 %copy-start.2 = (bf16[128,4096]{1,0:T(8,128)(2,1)}, bf16[128,4096]{1,0:T(8,128)(2,1)S(1)}, u32[]{:S(2)}) copy-start(bf16[128,4096]{1,0:T(8,128)(2,1)S(1)} %collective-permute-done.11.own_refs_1_) | copy-start | bytes 3145732
  67.6 32.0 %copy-start = (bf16[128,4096]{1,0:T(8,128)(2,1)S(1)}, bf16[128,4096]{1,0:T(8,128)(2,1)}, u32[]{:S(2)}) copy-start(bf16[128,4096]{1,0:T(8,128)(2,1)} %shard_map.110.own_refs_0_) | copy-start | bytes 3145732
  67.6 5.7 %collective-permute-start.15 = (bf16[8,512,128]{2,1,0:T(8,128)(2,1)}, bf16[8,512,128]{2,1,0:T(8,128)(2,1)S(1)}, u32[]{:S(2)}, u32[]{:S(2)}) collective-permute-start(bf16[8,512,128]{2,1,0:T(8,128)(2,1)} %get-tuple-element.56), channel_id=1, source_target_pairs={{0,8},{8,0},{16,24},{24,16},{32,40},{40,32},{48,56},{56,48},{64,72... | collective-permute-start | bytes 3145736 | tf_op jit(solution)/shard_map/ppermute | solution.py:39
  68.7 15.3 %collective-permute-start.18 = (bf16[4,512,128]{2,1,0:T(8,128)(2,1)}, bf16[4,512,128]{2,1,0:T(8,128)(2,1)S(1)}, u32[]{:S(2)}, u32[]{:S(2)}) collective-permute-start(bf16[4,512,128]{2,1,0:T(8,128)(2,1)} %get-tuple-element.54.grad_refs_0_), channel_id=1, source_target_pairs={{0,1},{1,0},{2,3},{3,2},{4,5},{5,4},{6,7},{7,6},{8,9},{9,8},{10,11... | collective-permute-start | bytes 1572872 | tf_op jit(solution)/shard_map/ppermute | solution.py:31
  71.5 16.1 %collective-permute-start.14 = (bf16[4,512,128]{2,1,0:T(8,128)(2,1)}, bf16[4,512,128]{2,1,0:T(8,128)(2,1)S(1)}, u32[]{:S(2)}, u32[]{:S(2)}) collective-permute-start(bf16[4,512,128]{2,1,0:T(8,128)(2,1)} %get-tuple-element.54.grad_refs_0_), channel_id=1, source_target_pairs={{0,6},{1,7},{2,0},{3,1},{4,2},{5,3},{6,4},{7,5},{8,14},{9,15},{10,... | collective-permute-start | bytes 1572872 | tf_op jit(solution)/shard_map/ppermute | solution.py:27
  73.3 14.3 %collective-permute-start.13 = (bf16[4,512,128]{2,1,0:T(8,128)(2,1)}, bf16[4,512,128]{2,1,0:T(8,128)(2,1)S(1)}, u32[]{:S(2)}, u32[]{:S(2)}) collective-permute-start(bf16[4,512,128]{2,1,0:T(8,128)(2,1)} %get-tuple-element.54.grad_refs_0_), channel_id=1, source_target_pairs={{0,2},{1,3},{2,4},{3,5},{4,6},{5,7},{6,0},{7,1},{8,10},{9,11},{10,... | collective-permute-start | bytes 1572872 | tf_op jit(solution)/shard_map/ppermute | solution.py:27
  74.8 51.9 %copy-start.8 = (bf16[4,512,128]{2,1,0:T(8,128)(2,1)S(1)}, bf16[4,512,128]{2,1,0:T(8,128)(2,1)}, u32[]{:S(2)}) copy-start(bf16[4,512,128]{2,1,0:T(8,128)(2,1)} %get-tuple-element.54.grad_refs_0_) | copy-start | bytes 1572868
  84.0 45.8 %copy-start.9 = (bf16[4,512,128]{2,1,0:T(8,128)(2,1)}, bf16[4,512,128]{2,1,0:T(8,128)(2,1)S(1)}, u32[]{:S(2)}) copy-start(bf16[4,512,128]{2,1,0:T(8,128)(2,1)S(1)} %collective-permute-done.18.grad_refs_3_) | copy-start | bytes 1572868
  84.0 8.6 %collective-permute-start.19 = (bf16[2,512,128]{2,1,0:T(8,128)(2,1)S(1)}, bf16[2,512,128]{2,1,0:T(8,128)(2,1)S(1)}, u32[]{:S(2)}, u32[]{:S(2)}) collective-permute-start(bf16[2,512,128]{2,1,0:T(8,128)(2,1)S(1)} %get-tuple-element.57), channel_id=1, source_target_pairs={{0,4},{1,5},{2,6},{3,7},{4,0},{5,1},{6,2},{7,3},{8,12},{9,13},{10,... | collective-permute-start | bytes 786440 | tf_op jit(solution)/shard_map/ppermute | solution.py:27
  86.1 11.8 %collective-permute-start.17 = (bf16[2,512,128]{2,1,0:T(8,128)(2,1)S(1)}, bf16[2,512,128]{2,1,0:T(8,128)(2,1)S(1)}, u32[]{:S(2)}, u32[]{:S(2)}) collective-permute-start(bf16[2,512,128]{2,1,0:T(8,128)(2,1)S(1)} %get-tuple-element.89), channel_id=1, source_target_pairs={{0,6},{1,7},{2,0},{3,1},{4,2},{5,3},{6,4},{7,5},{8,14},{9,15},{10,... | collective-permute-start | bytes 786440 | tf_op jit(solution)/shard_map/ppermute | solution.py:27
  87.4 12.2 %collective-permute-start.16 = (bf16[2,512,128]{2,1,0:T(8,128)(2,1)S(1)}, bf16[2,512,128]{2,1,0:T(8,128)(2,1)S(1)}, u32[]{:S(2)}, u32[]{:S(2)}) collective-permute-start(bf16[2,512,128]{2,1,0:T(8,128)(2,1)S(1)} %get-tuple-element.90), channel_id=1, source_target_pairs={{0,2},{1,3},{2,4},{3,5},{4,6},{5,7},{6,0},{7,1},{8,10},{9,11},{10,... | collective-permute-start | bytes 786440 | tf_op jit(solution)/shard_map/ppermute | solution.py:27
  87.6 42.2 %copy-start.10 = (bf16[4,512,128]{2,1,0:T(8,128)(2,1)}, bf16[4,512,128]{2,1,0:T(8,128)(2,1)S(1)}, u32[]{:S(2)}) copy-start(bf16[4,512,128]{2,1,0:T(8,128)(2,1)S(1)} %collective-permute-done.14.grad_refs_2_) | copy-start | bytes 1572868
  87.7 42.1 %copy-start.11 = (bf16[4,512,128]{2,1,0:T(8,128)(2,1)}, bf16[4,512,128]{2,1,0:T(8,128)(2,1)S(1)}, u32[]{:S(2)}) copy-start(bf16[4,512,128]{2,1,0:T(8,128)(2,1)S(1)} %collective-permute-done.13.grad_refs_1_) | copy-start | bytes 1572868
  99.6 25.5 %collective-permute-start.20 = (bf16[128,4096]{1,0:T(8,128)(2,1)S(1)}, bf16[128,4096]{1,0:T(8,128)(2,1)S(1)}, u32[]{:S(2)}, u32[]{:S(2)}) collective-permute-start(bf16[128,4096]{1,0:T(8,128)(2,1)S(1)} %copy-done), channel_id=1, source_target_pairs={{0,64},{8,72},{16,80},{24,88},{32,96},{40,104},{48,112},{56,120},{... | collective-permute-start | bytes 3145736 | tf_op jit(solution)/shard_map/ppermute | solution.py:35
  99.6 30.2 %collective-permute-start.23 = (bf16[128,4096]{1,0:T(8,128)(2,1)S(1)}, bf16[128,4096]{1,0:T(8,128)(2,1)S(1)}, u32[]{:S(2)}, u32[]{:S(2)}) collective-permute-start(bf16[128,4096]{1,0:T(8,128)(2,1)S(1)} %collective-permute-done.11.own_refs_1_), channel_id=1, source_target_pairs={{0,8},{8,0},{16,24},{24,16},{32,40},{40,32},{48,56},{56,48},{64,72... | collective-permute-start | bytes 3145736 | tf_op jit(solution)/shard_map/ppermute | solution.py:39
  100.4 29.4 %collective-permute-start.22 = (bf16[128,4096]{1,0:T(8,128)(2,1)}, bf16[128,4096]{1,0:T(8,128)(2,1)S(1)}, u32[]{:S(2)}, u32[]{:S(2)}) collective-permute-start(bf16[128,4096]{1,0:T(8,128)(2,1)} %collective-permute-done.10.own_refs_3_), channel_id=1, source_target_pairs={{0,8},{8,0},{16,24},{24,16},{32,40},{40,32},{48,56},{56,48},{64,72... | collective-permute-start | bytes 3145736 | tf_op jit(solution)/shard_map/ppermute | solution.py:39
  100.6 29.2 %collective-permute-start.21 = (bf16[2,512,128]{2,1,0:T(8,128)(2,1)S(1)}, bf16[2,512,128]{2,1,0:T(8,128)(2,1)S(1)}, u32[]{:S(2)}, u32[]{:S(2)}) collective-permute-start(bf16[2,512,128]{2,1,0:T(8,128)(2,1)S(1)} %fusion.2), channel_id=1, source_target_pairs={{0,1},{1,0},{2,3},{3,2},{4,5},{5,4},{6,7},{7,6},{8,9},{9,8},{10,11... | collective-permute-start | bytes 786440 | tf_op jit(solution)/shard_map/ppermute | solution.py:31
  125.1 4.6 %copy-start.3 = (bf16[128,4096]{1,0:T(8,128)(2,1)}, bf16[128,4096]{1,0:T(8,128)(2,1)S(1)}, u32[]{:S(2)}) copy-start(bf16[128,4096]{1,0:T(8,128)(2,1)S(1)} %collective-permute-done.20.own_refs_2_) | copy-start | bytes 3145732
  125.2 9.8 %collective-permute-start.24 = (bf16[128,4096]{1,0:T(8,128)(2,1)S(1)}, bf16[128,4096]{1,0:T(8,128)(2,1)S(1)}, u32[]{:S(2)}, u32[]{:S(2)}) collective-permute-start(bf16[128,4096]{1,0:T(8,128)(2,1)S(1)} %collective-permute-done.20.own_refs_2_), channel_id=1, source_target_pairs={{0,8},{8,0},{16,24},{24,16},{32,40},{40,32},{48,56},{56,48},{64,72... | collective-permute-start | bytes 3145736 | tf_op jit(solution)/shard_map/ppermute | solution.py:39
  127.8 26.6 %collective-permute-start.25 = (bf16[8,512,128]{2,1,0:T(8,128)(2,1)}, bf16[8,512,128]{2,1,0:T(8,128)(2,1)}, u32[]{:S(2)}, u32[]{:S(2)}) collective-permute-start(bf16[8,512,128]{2,1,0:T(8,128)(2,1)} %pad_maximum_fusion.1), channel_id=1, source_target_pairs={{0,4},{1,5},{2,6},{3,7},{4,0},{5,1},{6,2},{7,3},{8,12},{9,13},{10,... | collective-permute-start | bytes 3145736 | tf_op jit(solution)/shard_map/ppermute | solution.py:27
  129.8 5.1 %copy-start.4 = (bf16[128,4096]{1,0:T(8,128)(2,1)}, bf16[128,4096]{1,0:T(8,128)(2,1)S(1)}, u32[]{:S(2)}) copy-start(bf16[128,4096]{1,0:T(8,128)(2,1)S(1)} %collective-permute-done.23.other_refs_1_) | copy-start | bytes 3145732
  129.8 5.1 %copy-start.5 = (bf16[128,4096]{1,0:T(8,128)(2,1)}, bf16[128,4096]{1,0:T(8,128)(2,1)S(1)}, u32[]{:S(2)}) copy-start(bf16[128,4096]{1,0:T(8,128)(2,1)S(1)} %collective-permute-done.22.other_refs_3_) | copy-start | bytes 3145732
  129.9 36.1 %collective-permute-start.26 = (bf16[8,512,128]{2,1,0:T(8,128)(2,1)S(1)}, bf16[8,512,128]{2,1,0:T(8,128)(2,1)S(1)}, u32[]{:S(2)}, u32[]{:S(2)}) collective-permute-start(bf16[8,512,128]{2,1,0:T(8,128)(2,1)S(1)} %pad_maximum_fusion), channel_id=1, source_target_pairs={{0,1},{1,0},{2,3},{3,2},{4,5},{5,4},{6,7},{7,6},{8,9},{9,8},{10,11... | collective-permute-start | bytes 3145736 | tf_op jit(solution)/shard_map/ppermute | solution.py:31
  132.8 9.9 %copy-start.12 = (bf16[2,512,128]{2,1,0:T(8,128)(2,1)}, bf16[2,512,128]{2,1,0:T(8,128)(2,1)S(1)}, u32[]{:S(2)}) copy-start(bf16[2,512,128]{2,1,0:T(8,128)(2,1)S(1)} %add_convert_fusion.1.rest_1__0_) | copy-start | bytes 786436
  132.8 26.4 %collective-permute-start.29 = (bf16[2,512,128]{2,1,0:T(8,128)(2,1)S(1)}, bf16[2,512,128]{2,1,0:T(8,128)(2,1)S(1)}, u32[]{:S(2)}, u32[]{:S(2)}) collective-permute-start(bf16[2,512,128]{2,1,0:T(8,128)(2,1)S(1)} %add_convert_fusion.1.rest_1__0_), channel_id=1, source_target_pairs={{0,6},{1,7},{2,0},{3,1},{4,2},{5,3},{6,4},{7,5},{8,14},{9,15},{10,... | collective-permute-start | bytes 786440 | tf_op jit(solution)/shard_map/ppermute | solution.py:27
  133.9 26.0 %collective-permute-start.28 = (bf16[2,512,128]{2,1,0:T(8,128)(2,1)S(1)}, bf16[2,512,128]{2,1,0:T(8,128)(2,1)S(1)}, u32[]{:S(2)}, u32[]{:S(2)}) collective-permute-start(bf16[2,512,128]{2,1,0:T(8,128)(2,1)S(1)} %add_convert_fusion.1.rest_1__0_), channel_id=1, source_target_pairs={{0,4},{1,5},{2,6},{3,7},{4,0},{5,1},{6,2},{7,3},{8,12},{9,13},{10,... | collective-permute-start | bytes 786440 | tf_op jit(solution)/shard_map/ppermute | solution.py:27
  134.9 31.0 %collective-permute-start.27 = (bf16[2,512,128]{2,1,0:T(8,128)(2,1)S(1)}, bf16[2,512,128]{2,1,0:T(8,128)(2,1)}, u32[]{:S(2)}, u32[]{:S(2)}) collective-permute-start(bf16[2,512,128]{2,1,0:T(8,128)(2,1)S(1)} %add_convert_fusion.1.rest_1__0_), channel_id=1, source_target_pairs={{0,2},{1,3},{2,4},{3,5},{4,6},{5,7},{6,0},{7,1},{8,10},{9,11},{10,... | collective-permute-start | bytes 786440 | tf_op jit(solution)/shard_map/ppermute | solution.py:27
  159.2 6.7 %copy-start.14 = (bf16[2,512,128]{2,1,0:T(8,128)(2,1)}, bf16[2,512,128]{2,1,0:T(8,128)(2,1)S(1)}, u32[]{:S(2)}) copy-start(bf16[2,512,128]{2,1,0:T(8,128)(2,1)S(1)} %collective-permute-done.29.rest_1__3_) | copy-start | bytes 786436
  159.9 6.0 %copy-start.15 = (bf16[2,512,128]{2,1,0:T(8,128)(2,1)}, bf16[2,512,128]{2,1,0:T(8,128)(2,1)S(1)}, u32[]{:S(2)}) copy-start(bf16[2,512,128]{2,1,0:T(8,128)(2,1)S(1)} %collective-permute-done.28.rest_1__2_) | copy-start | bytes 786436
  (3 other events, 4.6 us)

commit v10 on v7

--- a/solution.py
+++ b/solution.py
@@ -63,18 +63,19 @@
 
 
 def attention_kernel(
-    heads, info_ref, q_ref, g_ref, mine_refs, other_refs, dq_ref, dqh_ref, keep_ref, give_ref,
+    heads, place_ref, here_ref, there_ref, q_ref, g_ref, mine_refs, other_refs, dq_ref, dqh_ref, keep_ref, give_ref,
     ks, vs, kt, scores, grads, dka, dva, qh, gh, dqt,
 ):
     per_ref = mine_refs[0].shape[0]
     slots = per_ref * len(mine_refs)
     runs_per_slot = 2
     scale = 1.0 / math.sqrt(HD)
-    core = info_ref[2 * slots]
+    core = place_ref[0]
+    runs = [ref[i] for ref in (here_ref, there_ref) for i in range(slots)]
     for b in range(slots * runs_per_slot):
         slot, part = b // runs_per_slot, b % runs_per_slot
         rows = slice(part * RUN, (part + 1) * RUN)
-        at = pl.multiple_of(info_ref[b] * RUN, RUN)
+        at = pl.multiple_of(runs[b] * RUN, RUN)
         first = mine_refs[slot // per_ref][slot % per_ref, rows, :]
         second = other_refs[slot // per_ref][slot % per_ref, rows, :]
         key_block = jnp.where(core == 0, first, second)
@@ -84,7 +85,7 @@
     dka[...] = jnp.zeros_like(dka)
     dva[...] = jnp.zeros_like(dva)
     for half in range(2):
-        run = info_ref[half]
+        run = runs[half]
         rows = slice(half * RUN, (half + 1) * RUN)
         for h in range(heads):
             qh[h * RUN : (h + 1) * RUN, :] = q_ref[rows, h * HD : (h + 1) * HD]
@@ -165,7 +166,7 @@
     for b in range(slots * runs_per_slot):
         slot, part = b // runs_per_slot, b % runs_per_slot
         rows = slice(part * RUN, (part + 1) * RUN)
-        at = pl.multiple_of(info_ref[b] * RUN, RUN)
+        at = pl.multiple_of(runs[b] * RUN, RUN)
         dk = dka[pl.ds(at, RUN), :] * scale
         dv = dva[pl.ds(at, RUN), :]
         low = jnp.concatenate([dk[:, :half_head], dv[:, :half_head]], axis=1)
@@ -174,7 +175,7 @@
         give_ref[slot, rows, :] = jnp.where(core == 0, high, low).astype(jnp.bfloat16)
 
 
-def attention(info, queries, grad_output, mine, other):
+def attention(place, here, there, queries, grad_output, mine, other):
     slots = mine[0].shape[0] * len(mine)
     count = slots * 2 * RUN
     heads = queries.shape[1] // HD
@@ -191,7 +192,7 @@
             shared,
             shared,
         ),
-        in_specs=[smem, vmem, vmem, [vmem] * len(mine), [vmem] * len(other)],
+        in_specs=[smem, smem, smem, vmem, vmem, [vmem] * len(mine), [vmem] * len(other)],
         out_specs=(vmem, vmem, vmem, vmem),
         scratch_shapes=[
             pltpu.VMEM((count, HD), jnp.bfloat16),
@@ -209,7 +210,7 @@
         cost_estimate=pl.CostEstimate(
             flops=5 * 4 * pairs * HD, bytes_accessed=8 * 1024 * 1024, transcendentals=2 * pairs
         ),
-    )(info, queries, grad_output, mine, other)
+    )(place, here, there, queries, grad_output, mine, other)
 
 
 def turn_kernel(in_refs, out_ref):
@@ -247,18 +248,36 @@
     return spans
 
 
-def weight_kernel(last, starts, place_ref, own_refs, other_refs, grad_refs, *rest):
+def slab_copies(core, own_refs, other_refs, inputs, sems, spans, tokens):
+    tall = own_refs[0].shape[0]
+    copies = []
+    for away in range(4):
+        copies.append([])
+        for n, (at, slot, many) in enumerate(spans):
+            for which, ref in enumerate((own_refs[away], other_refs[away])):
+                down = pl.multiple_of((core if which == 0 else 1 - core) * tall, tall)
+                copies[away].append(
+                    pltpu.make_async_copy(
+                        ref.at[:, pl.ds(slot * tokens, many * tokens)],
+                        inputs.at[away, pl.ds(down, tall), pl.ds(at * tokens, many * tokens)],
+                        sems.at[away, n, which],
+                    )
+                )
+    return copies
+
+
+def pair_rows(z, tall):
+    return [pl.multiple_of(lax.rem(z + away, 4) * 2 * tall, 2 * tall) for away in range(4)]
+
+
+def query_weight_kernel(last, starts, place_ref, own_refs, other_refs, grad_refs, *rest):
     if last:
-        (sum_ref, shared_refs, wq_ref, wk_ref, wv_ref, k_ref, v_ref,
-         inputs, grads, sums, shared, in_sems, grad_sems, sum_sems, shared_sems, out_sems) = rest
+        sum_ref, out_ref, inputs, grads, sums, in_sems, grad_sems, out_sems, sum_sems = rest
     else:
-        wq_ref, inputs, grads, sums, in_sems, grad_sems, out_sems = rest
-    core, z = place_ref[0], place_ref[1]
+        out_ref, inputs, grads, sums, in_sems, grad_sems, out_sems = rest
     tall = own_refs[0].shape[0]
     tokens, wide = grad_refs[0].shape[1:]
-    heads = grads.shape[1] // wide
-    slots = LATE if last else EARLY
-    spans = [[0, 0, 8]] if last else consecutive(EARLY)
+    spans = consecutive(LATE if last else EARLY)
     grad_copies = [
         pltpu.make_async_copy(
             ref.at[start + h],
@@ -266,124 +285,68 @@
             grad_sems.at[i, h],
         )
         for i, (ref, start) in enumerate(zip(grad_refs, starts))
-        for h in range(heads)
+        for h in range(grads.shape[1] // wide)
     ]
     for copy in grad_copies:
         copy.start()
-    row = [pl.multiple_of(lax.rem(z + away, 4) * 2 * tall, 2 * tall) for away in range(4)]
-    in_copies, sum_copies, shared_copies, out_copies = {}, [], [], []
-    if last:
-        shared_copies = [
-            pltpu.make_async_copy(
-                shared_refs[slot % 4].at[slot // 4],
-                shared.at[pl.ds(slot * tokens, tokens)],
-                shared_sems.at[slot],
-            )
-            for slot in range(8)
-        ]
+    row = pair_rows(place_ref[1], tall)
+    in_copies = slab_copies(place_ref[0], own_refs, other_refs, inputs, in_sems, spans, tokens)
+    out_copies = []
     for away in range(4):
-        for n, (at, slot, many) in enumerate(spans):
-            for which, ref in enumerate((own_refs[away], other_refs[away])):
-                down = pl.multiple_of((core if which == 0 else 1 - core) * tall, tall)
-                in_copies[away, n, which] = pltpu.make_async_copy(
-                    ref.at[:, pl.ds(slot * tokens, many * tokens)],
-                    inputs.at[away, pl.ds(down, tall), pl.ds(at * tokens, many * tokens)],
-                    in_sems.at[away, n, which],
-                )
         if last:
-            sum_copies.append(
+            in_copies[away].append(
                 pltpu.make_async_copy(
                     sum_ref.at[pl.ds(row[away], 2 * tall)], sums.at[away], sum_sems.at[away]
                 )
             )
-
-    def fetch(away):
-        for n in range(len(spans)):
-            for which in range(2):
-                in_copies[away, n, which].start()
-        if last:
-            sum_copies[away].start()
-
-    fetch(0)
-    for copy in shared_copies:
-        copy.start()
-    fetch(1)
+        out_copies.append(
+            pltpu.make_async_copy(
+                sums.at[away], out_ref.at[pl.ds(row[away], 2 * tall)], out_sems.at[away]
+            )
+        )
+    for away in range(2):
+        for copy in in_copies[away]:
+            copy.start()
     for copy in grad_copies:
         copy.wait()
-    norm = 1.0 / math.sqrt(8 * tokens)
     for away in range(4):
-        for n in range(len(spans)):
-            for which in range(2):
-                in_copies[away, n, which].wait()
+        for copy in in_copies[away]:
+            copy.wait()
         if away + 2 < 4:
-            fetch(away + 2)
+            for copy in in_copies[away + 2]:
+                copy.start()
+        total = contract(inputs[away], grads[...], 1, 0)
         if last:
-            total = sum(
-                contract(
-                    inputs[away, :, slot * tokens : (slot + many) * tokens],
-                    grads[at * tokens : (at + many) * tokens],
-                    1,
-                    0,
-                )
-                for at, slot, many in consecutive(slots)
-            )
-        else:
-            total = contract(inputs[away], grads[...], 1, 0)
-        if last:
-            sum_copies[away].wait()
-            total = (total + sums[away]) * norm
+            total = (total + sums[away]) * (1.0 / math.sqrt(8 * tokens))
         sums[away] = total
-        out_copies.append(
-            pltpu.make_async_copy(
-                sums.at[away], wq_ref.at[pl.ds(row[away], 2 * tall)], out_sems.at[away]
-            )
-        )
         out_copies[away].start()
-        if last:
-            if away == 0:
-                for copy in shared_copies:
-                    copy.wait()
-            part = (contract(inputs[away], shared[...], 1, 0) * norm).T
-            wk_ref[:, pl.ds(row[away], 2 * tall)] = part[: tall // 2]
-            wv_ref[:, pl.ds(row[away], 2 * tall)] = part[tall // 2 :]
-    if last:
-        here = shared[:tokens].T
-        k_ref[...] = here[: here.shape[0] // 2]
-        v_ref[...] = here[here.shape[0] // 2 :]
     for copy in out_copies:
         copy.wait()
 
 
-def weights(place, own, other, grads, heads, total=None, shared=None):
+def query_weights(place, own, other, grads, heads, total=None):
     last = total is not None
     smem = pl.BlockSpec(memory_space=pltpu.SMEM)
-    vmem = pl.BlockSpec(memory_space=pltpu.VMEM)
     hbm = pl.BlockSpec(memory_space=pl.ANY)
-    tall, across = own[0].shape
+    tall = own[0].shape[0]
     tokens, wide = grads[0][0].shape[1:]
     cols = heads * wide
     f32, bf16, sem = jnp.float32, jnp.bfloat16, pltpu.SemaphoreType.DMA
-    wq = jax.ShapeDtypeStruct((8 * tall, cols), f32)
-    narrow = jax.ShapeDtypeStruct((tall // 2, 8 * tall), f32)
-    narrow_in = jax.ShapeDtypeStruct((tall // 2, tokens), bf16)
-    spans = 1 if last else len(consecutive(EARLY))
-    scratch = [
-        pltpu.VMEM((4, 2 * tall, (8 if last else len(EARLY)) * tokens), bf16),
-        pltpu.VMEM((len(grads) * tokens, cols), bf16),
-        pltpu.VMEM((4, 2 * tall, cols), f32),
-    ]
-    if last:
-        scratch += [pltpu.VMEM((across, tall), bf16)]
-    scratch += [sem((4, spans, 2)), sem((len(grads), heads))]
-    if last:
-        scratch += [sem((4,)), sem((8,))]
-    scratch += [sem((4,))]
+    spans = len(consecutive(LATE if last else EARLY))
     return pl.pallas_call(
-        functools.partial(weight_kernel, last, tuple(start for _, start in grads)),
-        out_shape=(wq, narrow, narrow, narrow_in, narrow_in) if last else wq,
-        in_specs=[smem, [hbm] * 4, [hbm] * 4, [hbm] * 4] + ([hbm, [hbm] * 4] if last else []),
-        out_specs=(hbm, vmem, vmem, vmem, vmem) if last else hbm,
-        scratch_shapes=scratch,
+        functools.partial(query_weight_kernel, last, tuple(start for _, start in grads)),
+        out_shape=jax.ShapeDtypeStruct((8 * tall, cols), f32),
+        in_specs=[smem, [hbm] * 4, [hbm] * 4, [hbm] * 4] + ([hbm] if last else []),
+        out_specs=hbm,
+        scratch_shapes=[
+            pltpu.VMEM((4, 2 * tall, len(grads) * tokens), bf16),
+            pltpu.VMEM((len(grads) * tokens, cols), bf16),
+            pltpu.VMEM((4, 2 * tall, cols), f32),
+            sem((4, spans, 2)),
+            sem((len(grads), heads)),
+            sem((4,)),
+        ]
+        + ([sem((4,))] if last else []),
         compiler_params=pltpu.CompilerParams(vmem_limit_bytes=VMEM_BYTES),
         cost_estimate=pl.CostEstimate(
             flops=8 * tokens * cols * 8 * tall, bytes_accessed=10 * 1024 * 1024, transcendentals=0
@@ -393,8 +356,76 @@
         list(own),
         list(other),
         [array for array, _ in grads],
-        *((total, list(shared)) if last else ()),
-    )
+        *((total,) if last else ()),
+    )
+
+
+def shared_weight_kernel(
+    place_ref, own_refs, other_refs, shared_refs, wk_ref, wv_ref, k_ref, v_ref,
+    inputs, shared, in_sems, shared_sems,
+):
+    tall = own_refs[0].shape[0]
+    tokens = shared_refs[0].shape[1]
+    half = tall // 2
+    shared_copies = [
+        pltpu.make_async_copy(
+            shared_refs[slot % 4].at[slot // 4],
+            shared.at[pl.ds(slot * tokens, tokens)],
+            shared_sems.at[slot],
+        )
+        for slot in range(8)
+    ]
+    for copy in shared_copies:
+        copy.start()
+    row = pair_rows(place_ref[1], tall)
+    in_copies = slab_copies(
+        place_ref[0], own_refs, other_refs, inputs, in_sems, [[0, 0, 8]], tokens
+    )
+    for away in range(2):
+        for copy in in_copies[away]:
+            copy.start()
+    for copy in shared_copies:
+        copy.wait()
+    here = shared[:tokens].T
+    k_ref[...] = here[:half]
+    v_ref[...] = here[half:]
+    for away in range(4):
+        for copy in in_copies[away]:
+            copy.wait()
+        if away + 2 < 4:
+            for copy in in_copies[away + 2]:
+                copy.start()
+        part = contract(inputs[away], shared[...], 1, 0) * (1.0 / math.sqrt(8 * tokens))
+        part = part.T
+        wk_ref[:, pl.ds(row[away], 2 * tall)] = part[:half]
+        wv_ref[:, pl.ds(row[away], 2 * tall)] = part[half:]
+
+
+def shared_weights(place, own, other, shared):
+    smem = pl.BlockSpec(memory_space=pltpu.SMEM)
+    vmem = pl.BlockSpec(memory_space=pltpu.VMEM)
+    hbm = pl.BlockSpec(memory_space=pl.ANY)
+    tall, across = own[0].shape
+    tokens = shared[0].shape[1]
+    f32, bf16, sem = jnp.float32, jnp.bfloat16, pltpu.SemaphoreType.DMA
+    narrow = jax.ShapeDtypeStruct((tall // 2, 8 * tall), f32)
+    narrow_in = jax.ShapeDtypeStruct((tall // 2, tokens), bf16)
+    return pl.pallas_call(
+        shared_weight_kernel,
+        out_shape=(narrow, narrow, narrow_in, narrow_in),
+        in_specs=[smem, [hbm] * 4, [hbm] * 4, [hbm] * 4],
+        out_specs=(vmem, vmem, vmem, vmem),
+        scratch_shapes=[
+            pltpu.VMEM((4, 2 * tall, across), bf16),
+            pltpu.VMEM((across, tall), bf16),
+            sem((4, 1, 2)),
+            sem((8,)),
+        ],
+        compiler_params=pltpu.CompilerParams(vmem_limit_bytes=VMEM_BYTES),
+        cost_estimate=pl.CostEstimate(
+            flops=2 * across * tall * 8 * tall, bytes_accessed=10 * 1024 * 1024, transcendentals=0
+        ),
+    )(place, list(own), list(other), list(shared))
 
 
 def local(layer_input, queries, key_vectors, value_vectors, grad_output, positions):
@@ -425,20 +456,24 @@
     column_other = swap_cores(column)
     pairs = [jnp.stack([block(dy, 0), from_x[dy]]) for dy in range(4)]
     moved = [along_y(pairs[dy], dy) for dy in range(1, 4)]
+    slab_own = turn([pairs[0]] + moved)
     info = column[:, count, :2].reshape(8).astype(jnp.int32)
-    partner_column, info, place, kept, *moved = lax.optimization_barrier(
-        (partner_column, info, place, pairs[0], *moved)
-    )
-    pairs = [kept] + moved
+    partner_column, info, place, slab_own = lax.optimization_barrier(
+        (partner_column, info, place, slab_own)
+    )
     partner_other = swap_cores(partner_column)
     partner_info = partner_column[:, count, :2].reshape(8).astype(jnp.int32)
-    info = jnp.concatenate([info, partner_info, place[:1]])
-    slab_own = turn(pairs)
     slab_back, slab_ahead = along_z(slab_own, 1), along_z(slab_own, 3)
     own_other = swap_cores(slab_own)
 
     grad_query, grad_heads, keep, give = attention(
-        info, queries, grad_output, [column, partner_column], [column_other, partner_other]
+        place,
+        info,
+        partner_info,
+        queries,
+        grad_output,
+        [column, partner_column],
+        [column_other, partner_other],
     )
     heads = grad_heads.shape[0]
     grad_heads, keep, give, slab_own, slab_back, slab_ahead, own_other = lax.optimization_barrier(
@@ -475,10 +510,9 @@
     slabs_other = [own_other, ahead_other, far_other, back_other]
     early = [(grad_heads, 0), (from_1, 0), (from_3, 0), (from_x, 0)]
     late = [(from_2, 0), (from_x13, 0), (from_2, heads), (from_x13, heads)]
-    partial = weights(place, slabs, slabs_other, early, heads)
-    grad_wq, grad_wk, grad_wv, grad_key, grad_value = weights(
-        place, slabs, slabs_other, late, heads, partial, shared
-    )
+    partial = query_weights(place, slabs, slabs_other, early, heads)
+    grad_wq = query_weights(place, slabs, slabs_other, late, heads, partial)
+    grad_wk, grad_wv, grad_key, grad_value = shared_weights(place, slabs, slabs_other, shared)
     return grad_query, grad_key.T, grad_value.T, grad_wq, grad_wk.T, grad_wv.T
 
 

time: 159 us -> 160 us (level); the launches traced: 159 us -> 158 us
  waiting for transfers between devices: 69.9 us -> 53.5 us
  Pallas kernels: 36.3 us -> 44.9 us
  starting transfers between devices: 38.9 us -> 43.9 us
  local copies, waits for them, and re-layouts: 3.58 us -> 5.4 us
    ppermute x5, waiting for transfers between devices: 21.1 us -> 13 us  [swap_x(): return lax.ppermute(value, 'ctx', [(i, i ^ 1) for i in range(8)])]
    ppermute x3, waiting for transfers between devices: 10.2 us -> 2.33 us  [along_z(): lax.ppermute(value, 'dp', [(i, (i + 4 * step) % 16) for i in range(16)])]
    pallas_call x1, Pallas kernels: 15.7 us -> 21.3 us  [attention(): pl.pallas_call(functools.partial(attention_kernel, heads), out_shape=(jax...]
    pallas_call x2 -> x3, Pallas kernels: 18.1 us -> 21.2 us  [the longest x2 14 us: query_weights(): pl.pallas_call(functools.partial(query_weight_kernel, last, tuple((start...]
    ppermute x7, waiting for transfers between devices: 4.13 us -> 1.21 us  [swap_cores(): return lax.ppermute(value, 'dp', [(i, i ^ 1) for i in range(16)])]
    ppermute x3, starting transfers between devices: 3.76 us -> 6.46 us  [along_z(): lax.ppermute(value, 'dp', [(i, (i + 4 * step) % 16) for i in range(16)])]
    ppermute x5, starting transfers between devices: 9.56 us -> 12.1 us  [swap_x(): return lax.ppermute(value, 'ctx', [(i, i ^ 1) for i in range(8)])]
    ppermute x13, waiting for transfers between devices: 34.5 us -> 37 us  [along_y(): lax.ppermute(value, 'ctx', [(i, (i + 2 * step) % 8) for i in range(8)])]
  transfers between devices with their start and end apart: 28 -> 28, of which waited for: 18 -> 15; matrix products, arithmetic and copies ran while one was open for 6% -> 7% of each run, Pallas kernels for 16% -> 24%
where the time goes in v10:
time: 160 us; the launch traced here: 158 us
  waiting for transfers between devices  53.5 us (33%)
  Pallas kernels  44.9 us (28%)
  starting transfers between devices  43.9 us (27%)
  other arithmetic  8.93 us (6%)
  local copies, waits for them, and re-layouts  5.4 us (3%)
    ppermute x13, waiting for transfers between devices, along_y(): lax.ppermute(value, 'ctx', [(i, (i + 2 * step) % 8) for i in range(8)])  37 us
    pallas_call x1, Pallas kernels, attention(): pl.pallas_call(functools.partial(attention_kernel, heads), out_shape=(jax...  21.3 us
    ppermute x13, starting transfers between devices, along_y(): lax.ppermute(value, 'ctx', [(i, (i + 2 * step) % 8) for i in range(8)])  17.2 us
    pallas_call x2, Pallas kernels, query_weights(): pl.pallas_call(functools.partial(query_weight_kernel, last, tuple((start...  14 us
    ppermute x5, waiting for transfers between devices, swap_x(): return lax.ppermute(value, 'ctx', [(i, i ^ 1) for i in range(8)])  13 us
    ppermute x5, starting transfers between devices, swap_x(): return lax.ppermute(value, 'ctx', [(i, i ^ 1) for i in range(8)])  12.1 us
    ppermute x7, starting transfers between devices, swap_cores(): return lax.ppermute(value, 'dp', [(i, i ^ 1) for i in range(16)])  8.12 us
    pallas_call x1, Pallas kernels, shared_weights(): pl.pallas_call(shared_weight_kernel, out_shape=(narrow, narrow, narrow_in...  7.14 us
  transfers between devices with their start and end apart: 28, of which 15 were waited for; matrix products, arithmetic and copies ran while one was open for 7% of the time, Pallas kernels for 24%

profile of v10, /device:TPU:1, one launch (start us, length us, event | category | flops | bytes accessed | tf_op | source)
XLA Modules:
  0.0 157.9 jit_solution(11318843084248656005)
XLA Ops:
  0.8 1.4 dynamic-slice_bitcast_fusion
  2.3 3.7 %collective-permute-start.4 = (bf16[4,512,128]{2,1,0:T(8,128)(2,1)S(1)}, bf16[4,512,128]{2,1,0:T(8,128)(2,1)S(1)}, u32[]{:S(2)}, u32[]{:S(2)}) collective-permute-start(bf16[4,512,128]{2,1,0:T(8,128)(2,1)S(1)} %pad_maximum_fusion.5), channel_id=1, source_target_pairs={{0,1},{1,0},{2,3},{3,2},{4,5},{5,4},{6,7},{7,6},{8,9},{9,8},{10,11... | collective-permute-start | bytes 1572872 | tf_op jit(solution)/shard_map/ppermute | solution.py:31
  5.9 0.8 slice.45
  6.8 1.0 dynamic-slice_select_fusion
  7.8 1.4 collective-permute-start
  9.2 2.6 %collective-permute-start.1 = (bf16[528,128]{1,0:T(8,128)(2,1)S(1)}, bf16[528,128]{1,0:T(8,128)(2,1)S(1)}, u32[]{:S(2)}, u32[]{:S(2)}) collective-permute-start(bf16[528,128]{1,0:T(8,128)(2,1)S(1)} %get-tuple-element.84), channel_id=1, source_target_pairs={{0,4},{1,5},{2,6},{3,7},{4,0},{5,1},{6,2},{7,3},{8,12},{9,13},{10,... | collective-permute-start | bytes 405512 | tf_op jit(solution)/shard_map/ppermute | solution.py:27
  11.8 1.1 collective-permute-start.2
  13.4 4.0 %collective-permute-done.1 = bf16[528,128]{1,0:T(8,128)(2,1)S(1)} collective-permute-done((bf16[528,128]{1,0:T(8,128)(2,1)S(1)}, bf16[528,128]{1,0:T(8,128)(2,1)S(1)}, u32[]{:S(2)}, u32[]{:S(2)}) %collective-permute-start.1) | collective-permute-done | bytes 135200 | tf_op jit(solution)/shard_map/ppermute | solution.py:27
  17.4 0.9 pad_maximum_fusion.4.mine_refs_0_
  18.4 2.5 %collective-permute-start.7 = (bf16[2,512,128]{2,1,0:T(8,128)(2,1)S(1)}, bf16[2,512,128]{2,1,0:T(8,128)(2,1)S(1)}, u32[]{:S(2)}, u32[]{:S(2)}) collective-permute-start(bf16[2,512,128]{2,1,0:T(8,128)(2,1)S(1)} %pad_maximum_fusion.9), channel_id=1, source_target_pairs={{0,6},{1,7},{2,0},{3,1},{4,2},{5,3},{6,4},{7,5},{8,14},{9,15},{10,... | collective-permute-start | bytes 786440 | tf_op jit(solution)/shard_map/ppermute | solution.py:27
  21.0 0.7 collective-permute-start.6
  22.4 3.2 %collective-permute-start.8 = (bf16[4,528,128]{2,1,0:T(8,128)(2,1)}, bf16[4,528,128]{2,1,0:T(8,128)(2,1)}, u32[]{:S(2)}, u32[]{:S(2)}) collective-permute-start(bf16[4,528,128]{2,1,0:T(8,128)(2,1)} %pad_maximum_fusion.4.mine_refs_0_), channel_id=1, source_target_pairs={{0,8},{8,0},{16,24},{24,16},{32,40},{40,32},{48,56},{56,48},{64,72... | collective-permute-start | bytes 1622024 | tf_op jit(solution)/shard_map/ppermute | solution.py:39
  25.7 0.7 fusion.3
  27.0 0.7 pad_maximum_fusion.6.in_refs_0_
  27.7 0.9 collective-permute-done.6.in_refs_2_
  28.6 7.8 %collective-permute-done.5.in_refs_1_ = bf16[2,512,128]{2,1,0:T(8,128)(2,1)S(1)} collective-permute-done((bf16[2,512,128]{2,1,0:T(8,128)(2,1)S(1)}, bf16[2,512,128]{2,1,0:T(8,128)(2,1)S(1)}, u32[]{:S(2)}, u32[]{:S(2)}) %collective-permute-start.5) | collective-permute-done | bytes 262176 | tf_op jit(solution)/shard_map/ppermute | solution.py:27
  36.4 0.7 copy-done.16
  37.1 2.5 %shard_map.109.own_refs_0_ = bf16[128,4096]{1,0:T(8,128)(2,1)} custom-call(bf16[2,512,128]{2,1,0:T(8,128)(2,1)} %pad_maximum_fusion.6.in_refs_0_, bf16[2,512,128]{2,1,0:T(8,128)(2,1)} %copy-done.16, bf16[2,512,128]{2,1,0:T(8,128)(2,1)} %copy-done.15, bf16[2,512,128]{2,1,0:T(8,128)(2,1)} %copy-done.14), custom_call_target="tpu_custom_call" | custom-call | bytes 2097152 | tf_op jit(solution)/shard_map/pallas_call | solution.py:227
  40.1 1.7 %collective-permute-start.10 = (bf16[128,4096]{1,0:T(8,128)(2,1)}, bf16[128,4096]{1,0:T(8,128)(2,1)S(1)}, u32[]{:S(2)}, u32[]{:S(2)}) collective-permute-start(bf16[128,4096]{1,0:T(8,128)(2,1)} %shard_map.109.own_refs_0_), channel_id=1, source_target_pairs={{0,32},{8,40},{16,48},{24,56},{32,64},{40,72},{48,80},{56,88},{64,... | collective-permute-start | bytes 3145736 | tf_op jit(solution)/shard_map/ppermute | solution.py:35
  41.8 2.1 %collective-permute-start.11 = (bf16[128,4096]{1,0:T(8,128)(2,1)}, bf16[128,4096]{1,0:T(8,128)(2,1)S(1)}, u32[]{:S(2)}, u32[]{:S(2)}) collective-permute-start(bf16[128,4096]{1,0:T(8,128)(2,1)} %shard_map.109.own_refs_0_), channel_id=1, source_target_pairs={{0,96},{8,104},{16,112},{24,120},{32,0},{40,8},{48,16},{56,24},{64... | collective-permute-start | bytes 3145736 | tf_op jit(solution)/shard_map/ppermute | solution.py:35
  44.4 0.7 convert_reduce_fusion
  45.7 21.3 %shard_map.110 = (bf16[512,512]{1,0:T(8,128)(2,1)}, bf16[4,512,128]{2,1,0:T(8,128)(2,1)}, bf16[8,512,128]{2,1,0:T(8,128)(2,1)}, bf16[8,512,128]{2,1,0:T(8,128)(2,1)}) custom-call(s32[2]{0:T(128)} %pad_add_fusion.place_ref, s32[8]{0:T(128)} %reshape.23.here_ref, s32[8]{0:T(128)} %reshape.24.there_ref, bf16[512,512]{1,0:T(8,128)(2,1)} %q_ref.1, ...), custom_call_target="tpu_custom_call" | custom-call | flops 10737418240 | bytes 8388608 | tf_op jit(solution)/shard_map/pallas_call | solution.py:187
  67.6 0.7 collective-permute-start.13
  68.5 2.6 %collective-permute-start.19 = (bf16[128,4096]{1,0:T(8,128)(2,1)S(1)}, bf16[128,4096]{1,0:T(8,128)(2,1)S(1)}, u32[]{:S(2)}, u32[]{:S(2)}) collective-permute-start(bf16[128,4096]{1,0:T(8,128)(2,1)S(1)} %copy-done), channel_id=1, source_target_pairs={{0,64},{8,72},{16,80},{24,88},{32,96},{40,104},{48,112},{56,120},{... | collective-permute-start | bytes 3145736 | tf_op jit(solution)/shard_map/ppermute | solution.py:35
  71.4 0.8 collective-permute-done.14.other_refs_3_
  72.3 1.5 add_convert_fusion
  74.1 2.7 %collective-permute-start.16 = (bf16[6,512,128]{2,1,0:T(8,128)(2,1)S(1)}, bf16[6,512,128]{2,1,0:T(8,128)(2,1)S(1)}, u32[]{:S(2)}, u32[]{:S(2)}) collective-permute-start(bf16[6,512,128]{2,1,0:T(8,128)(2,1)S(1)} %get-tuple-element.77), channel_id=1, source_target_pairs={{0,6},{1,7},{2,0},{3,1},{4,2},{5,3},{6,4},{7,5},{8,14},{9,15},{10,... | collective-permute-start | bytes 2359304 | tf_op jit(solution)/shard_map/ppermute | solution.py:27
  76.7 2.7 %collective-permute-start.18 = (bf16[4,512,128]{2,1,0:T(8,128)(2,1)S(1)}, bf16[4,512,128]{2,1,0:T(8,128)(2,1)S(1)}, u32[]{:S(2)}, u32[]{:S(2)}) collective-permute-start(bf16[4,512,128]{2,1,0:T(8,128)(2,1)S(1)} %copy-done.6), channel_id=1, source_target_pairs={{0,1},{1,0},{2,3},{3,2},{4,5},{5,4},{6,7},{7,6},{8,9},{9,8},{10,11... | collective-permute-start | bytes 1572872 | tf_op jit(solution)/shard_map/ppermute | solution.py:31
  79.9 10.9 %collective-permute-done.18.grad_refs_3_ = bf16[4,512,128]{2,1,0:T(8,128)(2,1)S(1)} collective-permute-done((bf16[4,512,128]{2,1,0:T(8,128)(2,1)S(1)}, bf16[4,512,128]{2,1,0:T(8,128)(2,1)S(1)}, u32[]{:S(2)}, u32[]{:S(2)}) %collective-permute-start.18) | collective-permute-done | bytes 524320 | tf_op jit(solution)/shard_map/ppermute | solution.py:31
  90.7 1.8 %collective-permute-start.22 = (bf16[128,4096]{1,0:T(8,128)(2,1)S(1)}, bf16[128,4096]{1,0:T(8,128)(2,1)S(1)}, u32[]{:S(2)}, u32[]{:S(2)}) collective-permute-start(bf16[128,4096]{1,0:T(8,128)(2,1)S(1)} %collective-permute-done.11.own_refs_1_), channel_id=1, source_target_pairs={{0,8},{8,0},{16,24},{24,16},{32,40},{40,32},{48,56},{56,48},{64,72... | collective-permute-start | bytes 3145736 | tf_op jit(solution)/shard_map/ppermute | solution.py:39
  92.6 1.7 %collective-permute-done.19.own_refs_2_ = bf16[128,4096]{1,0:T(8,128)(2,1)S(1)} collective-permute-done((bf16[128,4096]{1,0:T(8,128)(2,1)S(1)}, bf16[128,4096]{1,0:T(8,128)(2,1)S(1)}, u32[]{:S(2)}, u32[]{:S(2)}) %collective-permute-start.19) | collective-permute-done | bytes 1048608 | tf_op jit(solution)/shard_map/ppermute | solution.py:35
  94.3 4.3 %collective-permute-done.17 = bf16[2,512,128]{2,1,0:T(8,128)(2,1)S(1)} collective-permute-done((bf16[2,512,128]{2,1,0:T(8,128)(2,1)S(1)}, bf16[2,512,128]{2,1,0:T(8,128)(2,1)S(1)}, u32[]{:S(2)}, u32[]{:S(2)}) %collective-permute-start.17) | collective-permute-done | bytes 262176 | tf_op jit(solution)/shard_map/ppermute | solution.py:27
  98.6 1.1 collective-permute-done.15.grad_refs_1_
  99.6 1.3 collective-permute-start.21
  101.2 2.8 %collective-permute-start.20 = (bf16[2,512,128]{2,1,0:T(8,128)(2,1)S(1)}, bf16[2,512,128]{2,1,0:T(8,128)(2,1)S(1)}, u32[]{:S(2)}, u32[]{:S(2)}) collective-permute-start(bf16[2,512,128]{2,1,0:T(8,128)(2,1)S(1)} %fusion.2), channel_id=1, source_target_pairs={{0,1},{1,0},{2,3},{3,2},{4,5},{5,4},{6,7},{7,6},{8,9},{9,8},{10,11... | collective-permute-start | bytes 786440 | tf_op jit(solution)/shard_map/ppermute | solution.py:31
  104.0 1.1 pad_maximum_fusion.1
  105.1 1.5 collective-permute-start.26
  106.6 1.1 pad_maximum_fusion
  107.7 2.1 %collective-permute-done.20 = bf16[2,512,128]{2,1,0:T(8,128)(2,1)S(1)} collective-permute-done((bf16[2,512,128]{2,1,0:T(8,128)(2,1)S(1)}, bf16[2,512,128]{2,1,0:T(8,128)(2,1)S(1)}, u32[]{:S(2)}, u32[]{:S(2)}) %collective-permute-start.20) | collective-permute-done | bytes 262176 | tf_op jit(solution)/shard_map/ppermute | solution.py:31
  109.8 2.9 %collective-permute-start.27 = (bf16[8,512,128]{2,1,0:T(8,128)(2,1)}, bf16[8,512,128]{2,1,0:T(8,128)(2,1)S(1)}, u32[]{:S(2)}, u32[]{:S(2)}) collective-permute-start(bf16[8,512,128]{2,1,0:T(8,128)(2,1)} %pad_maximum_fusion), channel_id=1, source_target_pairs={{0,1},{1,0},{2,3},{3,2},{4,5},{5,4},{6,7},{7,6},{8,9},{9,8},{10,11... | collective-permute-start | bytes 3145736 | tf_op jit(solution)/shard_map/ppermute | solution.py:31
  112.8 0.9 collective-permute-start.23
  113.7 3.3 %collective-permute-start.24 = (bf16[2,512,128]{2,1,0:T(8,128)(2,1)S(1)}, bf16[2,512,128]{2,1,0:T(8,128)(2,1)S(1)}, u32[]{:S(2)}, u32[]{:S(2)}) collective-permute-start(bf16[2,512,128]{2,1,0:T(8,128)(2,1)S(1)} %add_convert_fusion.1.shared_refs_0_), channel_id=1, source_target_pairs={{0,4},{1,5},{2,6},{3,7},{4,0},{5,1},{6,2},{7,3},{8,12},{9,13},{10,... | collective-permute-start | bytes 786440 | tf_op jit(solution)/shard_map/ppermute | solution.py:27
  117.0 6.8 %shard_map.112.rest_0_ = f32[1024,512]{1,0:T(8,128)} custom-call(s32[2]{0:T(128)} %pad_add_fusion.place_ref, bf16[128,4096]{1,0:T(8,128)(2,1)} %shard_map.109.own_refs_0_, bf16[128,4096]{1,0:T(8,128)(2,1)} %copy-done.2, bf16[128,4096]{1,0:T(8,128)(2,1)} %copy-done.3, bf16[128,4096]{1,0:T(8,128)(2,1)} %copy-done.1, ...), custom_call_target="tpu_custom_call" | custom-call | flops 2147483648 | bytes 10485760 | tf_op jit(solution)/shard_map/pallas_call | solution.py:336
  123.9 15.0 %collective-permute-done.23.shared_refs_1_ = bf16[2,512,128]{2,1,0:T(8,128)(2,1)S(1)} collective-permute-done((bf16[2,512,128]{2,1,0:T(8,128)(2,1)S(1)}, bf16[2,512,128]{2,1,0:T(8,128)(2,1)S(1)}, u32[]{:S(2)}, u32[]{:S(2)}) %collective-permute-start.23) | collective-permute-done | bytes 262176 | tf_op jit(solution)/shard_map/ppermute | solution.py:27
  138.9 2.8 %collective-permute-done.24.shared_refs_2_ = bf16[2,512,128]{2,1,0:T(8,128)(2,1)S(1)} collective-permute-done((bf16[2,512,128]{2,1,0:T(8,128)(2,1)S(1)}, bf16[2,512,128]{2,1,0:T(8,128)(2,1)S(1)}, u32[]{:S(2)}, u32[]{:S(2)}) %collective-permute-start.24) | collective-permute-done | bytes 262176 | tf_op jit(solution)/shard_map/ppermute | solution.py:27
  142.4 7.1 %shard_map.111 = (f32[64,1024]{1,0:T(8,128)}, f32[64,1024]{1,0:T(8,128)}, bf16[64,512]{1,0:T(8,128)(2,1)}, bf16[64,512]{1,0:T(8,128)(2,1)}) custom-call(s32[2]{0:T(128)} %pad_add_fusion.place_ref, bf16[128,4096]{1,0:T(8,128)(2,1)} %shard_map.109.own_refs_0_, bf16[128,4096]{1,0:T(8,128)(2,1)} %copy-done.2, bf16[128,4096]{1,0:T(8,128)(2,1)} %copy-done.3, ...), custom_call_target="tpu_custom_call" | custom-call | flops 1073741824 | bytes 10485760 | tf_op jit(solution)/shard_map/pallas_call | solution.py:413
  149.6 1.0 copy-done.7
  150.6 7.2 %shard_map.113 = f32[1024,512]{1,0:T(8,128)} custom-call(s32[2]{0:T(128)} %pad_add_fusion.place_ref, bf16[128,4096]{1,0:T(8,128)(2,1)} %shard_map.109.own_refs_0_, bf16[128,4096]{1,0:T(8,128)(2,1)} %copy-done.2, bf16[128,4096]{1,0:T(8,128)(2,1)} %copy-done.3, bf16[128,4096]{1,0:T(8,128)(2,1)} %copy-done.1, ...), custom_call_target="tpu_custom_call" | custom-call | flops 2147483648 | bytes 10485760 | tf_op jit(solution)/shard_map/pallas_call | solution.py:336
  (76 shorter events, 6.5 us)
Async XLA Ops:
  2.3 16.1 %collective-permute-start.4 = (bf16[4,512,128]{2,1,0:T(8,128)(2,1)S(1)}, bf16[4,512,128]{2,1,0:T(8,128)(2,1)S(1)}, u32[]{:S(2)}, u32[]{:S(2)}) collective-permute-start(bf16[4,512,128]{2,1,0:T(8,128)(2,1)S(1)} %pad_maximum_fusion.5), channel_id=1, source_target_pairs={{0,1},{1,0},{2,3},{3,2},{4,5},{5,4},{6,7},{7,6},{8,9},{9,8},{10,11... | collective-permute-start | bytes 1572872 | tf_op jit(solution)/shard_map/ppermute | solution.py:31
  7.8 5.5 %collective-permute-start = (bf16[528,128]{1,0:T(8,128)(2,1)S(1)}, bf16[528,128]{1,0:T(8,128)(2,1)S(1)}, u32[]{:S(2)}, u32[]{:S(2)}) collective-permute-start(bf16[528,128]{1,0:T(8,128)(2,1)S(1)} %get-tuple-element.84), channel_id=1, source_target_pairs={{0,2},{1,3},{2,4},{3,5},{4,6},{5,7},{6,0},{7,1},{8,10},{9,11},{10,... | collective-permute-start | bytes 405512 | tf_op jit(solution)/shard_map/ppermute | solution.py:27
  9.2 8.2 %collective-permute-start.1 = (bf16[528,128]{1,0:T(8,128)(2,1)S(1)}, bf16[528,128]{1,0:T(8,128)(2,1)S(1)}, u32[]{:S(2)}, u32[]{:S(2)}) collective-permute-start(bf16[528,128]{1,0:T(8,128)(2,1)S(1)} %get-tuple-element.84), channel_id=1, source_target_pairs={{0,4},{1,5},{2,6},{3,7},{4,0},{5,1},{6,2},{7,3},{8,12},{9,13},{10,... | collective-permute-start | bytes 405512 | tf_op jit(solution)/shard_map/ppermute | solution.py:27
  11.8 5.6 %collective-permute-start.2 = (bf16[528,128]{1,0:T(8,128)(2,1)S(1)}, bf16[528,128]{1,0:T(8,128)(2,1)S(1)}, u32[]{:S(2)}, u32[]{:S(2)}) collective-permute-start(bf16[528,128]{1,0:T(8,128)(2,1)S(1)} %get-tuple-element.84), channel_id=1, source_target_pairs={{0,6},{1,7},{2,0},{3,1},{4,2},{5,3},{6,4},{7,5},{8,14},{9,15},{10,... | collective-permute-start | bytes 405512 | tf_op jit(solution)/shard_map/ppermute | solution.py:27
  18.3 21.3 %collective-permute-start.3 = (bf16[4,528,128]{2,1,0:T(8,128)(2,1)}, bf16[4,528,128]{2,1,0:T(8,128)(2,1)}, u32[]{:S(2)}, u32[]{:S(2)}) collective-permute-start(bf16[4,528,128]{2,1,0:T(8,128)(2,1)} %pad_maximum_fusion.4.mine_refs_0_), channel_id=1, source_target_pairs={{0,1},{1,0},{2,3},{3,2},{4,5},{5,4},{6,7},{7,6},{8,9},{9,8},{10,11... | collective-permute-start | bytes 1622024 | tf_op jit(solution)/shard_map/ppermute | solution.py:31
  18.4 9.3 %collective-permute-start.7 = (bf16[2,512,128]{2,1,0:T(8,128)(2,1)S(1)}, bf16[2,512,128]{2,1,0:T(8,128)(2,1)S(1)}, u32[]{:S(2)}, u32[]{:S(2)}) collective-permute-start(bf16[2,512,128]{2,1,0:T(8,128)(2,1)S(1)} %pad_maximum_fusion.9), channel_id=1, source_target_pairs={{0,6},{1,7},{2,0},{3,1},{4,2},{5,3},{6,4},{7,5},{8,14},{9,15},{10,... | collective-permute-start | bytes 786440 | tf_op jit(solution)/shard_map/ppermute | solution.py:27
  21.0 7.6 %collective-permute-start.6 = (bf16[2,512,128]{2,1,0:T(8,128)(2,1)S(1)}, bf16[2,512,128]{2,1,0:T(8,128)(2,1)S(1)}, u32[]{:S(2)}, u32[]{:S(2)}) collective-permute-start(bf16[2,512,128]{2,1,0:T(8,128)(2,1)S(1)} %pad_maximum_fusion.8), channel_id=1, source_target_pairs={{0,4},{1,5},{2,6},{3,7},{4,0},{5,1},{6,2},{7,3},{8,12},{9,13},{10,... | collective-permute-start | bytes 786440 | tf_op jit(solution)/shard_map/ppermute | solution.py:27
  21.7 14.7 %collective-permute-start.5 = (bf16[2,512,128]{2,1,0:T(8,128)(2,1)S(1)}, bf16[2,512,128]{2,1,0:T(8,128)(2,1)S(1)}, u32[]{:S(2)}, u32[]{:S(2)}) collective-permute-start(bf16[2,512,128]{2,1,0:T(8,128)(2,1)S(1)} %pad_maximum_fusion.7), channel_id=1, source_target_pairs={{0,2},{1,3},{2,4},{3,5},{4,6},{5,7},{6,0},{7,1},{8,10},{9,11},{10,... | collective-permute-start | bytes 786440 | tf_op jit(solution)/shard_map/ppermute | solution.py:27
  22.4 23.3 %collective-permute-start.8 = (bf16[4,528,128]{2,1,0:T(8,128)(2,1)}, bf16[4,528,128]{2,1,0:T(8,128)(2,1)}, u32[]{:S(2)}, u32[]{:S(2)}) collective-permute-start(bf16[4,528,128]{2,1,0:T(8,128)(2,1)} %pad_maximum_fusion.4.mine_refs_0_), channel_id=1, source_target_pairs={{0,8},{8,0},{16,24},{24,16},{32,40},{40,32},{48,56},{56,48},{64,72... | collective-permute-start | bytes 1622024 | tf_op jit(solution)/shard_map/ppermute | solution.py:39
  27.7 8.7 %copy-start.14 = (bf16[2,512,128]{2,1,0:T(8,128)(2,1)}, bf16[2,512,128]{2,1,0:T(8,128)(2,1)S(1)}, u32[]{:S(2)}) copy-start(bf16[2,512,128]{2,1,0:T(8,128)(2,1)S(1)} %collective-permute-done.7.in_refs_3_) | copy-start | bytes 786436
  28.6 7.8 %copy-start.15 = (bf16[2,512,128]{2,1,0:T(8,128)(2,1)}, bf16[2,512,128]{2,1,0:T(8,128)(2,1)S(1)}, u32[]{:S(2)}) copy-start(bf16[2,512,128]{2,1,0:T(8,128)(2,1)S(1)} %collective-permute-done.6.in_refs_2_) | copy-start | bytes 786436
  36.4 0.7 copy-start.16
  39.6 6.1 %collective-permute-start.9 = (bf16[4,528,128]{2,1,0:T(8,128)(2,1)}, bf16[4,528,128]{2,1,0:T(8,128)(2,1)}, u32[]{:S(2)}, u32[]{:S(2)}) collective-permute-start(bf16[4,528,128]{2,1,0:T(8,128)(2,1)} %collective-permute-done.3.mine_refs_1_), channel_id=1, source_target_pairs={{0,8},{8,0},{16,24},{24,16},{32,40},{40,32},{48,56},{56,48},{64,72... | collective-permute-start | bytes 1622024 | tf_op jit(solution)/shard_map/ppermute | solution.py:39
  40.1 27.5 %collective-permute-start.10 = (bf16[128,4096]{1,0:T(8,128)(2,1)}, bf16[128,4096]{1,0:T(8,128)(2,1)S(1)}, u32[]{:S(2)}, u32[]{:S(2)}) collective-permute-start(bf16[128,4096]{1,0:T(8,128)(2,1)} %shard_map.109.own_refs_0_), channel_id=1, source_target_pairs={{0,32},{8,40},{16,48},{24,56},{32,64},{40,72},{48,80},{56,88},{64,... | collective-permute-start | bytes 3145736 | tf_op jit(solution)/shard_map/ppermute | solution.py:35
  41.8 25.8 %collective-permute-start.11 = (bf16[128,4096]{1,0:T(8,128)(2,1)}, bf16[128,4096]{1,0:T(8,128)(2,1)S(1)}, u32[]{:S(2)}, u32[]{:S(2)}) collective-permute-start(bf16[128,4096]{1,0:T(8,128)(2,1)} %shard_map.109.own_refs_0_), channel_id=1, source_target_pairs={{0,96},{8,104},{16,112},{24,120},{32,0},{40,8},{48,16},{56,24},{64... | collective-permute-start | bytes 3145736 | tf_op jit(solution)/shard_map/ppermute | solution.py:35
  43.9 23.7 %collective-permute-start.12 = (bf16[128,4096]{1,0:T(8,128)(2,1)}, bf16[128,4096]{1,0:T(8,128)(2,1)}, u32[]{:S(2)}, u32[]{:S(2)}) collective-permute-start(bf16[128,4096]{1,0:T(8,128)(2,1)} %shard_map.109.own_refs_0_), channel_id=1, source_target_pairs={{0,8},{8,0},{16,24},{24,16},{32,40},{40,32},{48,56},{56,48},{64,72... | collective-permute-start | bytes 3145736 | tf_op jit(solution)/shard_map/ppermute | solution.py:39
  45.7 22.8 %copy-start = (bf16[128,4096]{1,0:T(8,128)(2,1)S(1)}, bf16[128,4096]{1,0:T(8,128)(2,1)}, u32[]{:S(2)}) copy-start(bf16[128,4096]{1,0:T(8,128)(2,1)} %shard_map.109.own_refs_0_) | copy-start | bytes 3145732
  67.6 6.2 %copy-start.1 = (bf16[128,4096]{1,0:T(8,128)(2,1)}, bf16[128,4096]{1,0:T(8,128)(2,1)S(1)}, u32[]{:S(2)}) copy-start(bf16[128,4096]{1,0:T(8,128)(2,1)S(1)} %collective-permute-done.10.own_refs_3_) | copy-start | bytes 3145732
  67.6 23.1 %copy-start.2 = (bf16[128,4096]{1,0:T(8,128)(2,1)}, bf16[128,4096]{1,0:T(8,128)(2,1)S(1)}, u32[]{:S(2)}) copy-start(bf16[128,4096]{1,0:T(8,128)(2,1)S(1)} %collective-permute-done.11.own_refs_1_) | copy-start | bytes 3145732
  67.6 6.2 %copy-start.6 = (bf16[4,512,128]{2,1,0:T(8,128)(2,1)S(1)}, bf16[4,512,128]{2,1,0:T(8,128)(2,1)}, u32[]{:S(2)}) copy-start(bf16[4,512,128]{2,1,0:T(8,128)(2,1)} %get-tuple-element.46.grad_refs_0_) | copy-start | bytes 1572868
  67.6 3.8 %collective-permute-start.13 = (bf16[8,512,128]{2,1,0:T(8,128)(2,1)}, bf16[8,512,128]{2,1,0:T(8,128)(2,1)S(1)}, u32[]{:S(2)}, u32[]{:S(2)}) collective-permute-start(bf16[8,512,128]{2,1,0:T(8,128)(2,1)} %get-tuple-element.48), channel_id=1, source_target_pairs={{0,8},{8,0},{16,24},{24,16},{32,40},{40,32},{48,56},{56,48},{64,72... | collective-permute-start | bytes 3145736 | tf_op jit(solution)/shard_map/ppermute | solution.py:39
  68.4 3.9 %collective-permute-start.14 = (bf16[128,4096]{1,0:T(8,128)(2,1)S(1)}, bf16[128,4096]{1,0:T(8,128)(2,1)}, u32[]{:S(2)}, u32[]{:S(2)}) collective-permute-start(bf16[128,4096]{1,0:T(8,128)(2,1)S(1)} %collective-permute-done.10.own_refs_3_), channel_id=1, source_target_pairs={{0,8},{8,0},{16,24},{24,16},{32,40},{40,32},{48,56},{56,48},{64,72... | collective-permute-start | bytes 3145736 | tf_op jit(solution)/shard_map/ppermute | solution.py:39
  68.5 25.8 %collective-permute-start.19 = (bf16[128,4096]{1,0:T(8,128)(2,1)S(1)}, bf16[128,4096]{1,0:T(8,128)(2,1)S(1)}, u32[]{:S(2)}, u32[]{:S(2)}) collective-permute-start(bf16[128,4096]{1,0:T(8,128)(2,1)S(1)} %copy-done), channel_id=1, source_target_pairs={{0,64},{8,72},{16,80},{24,88},{32,96},{40,104},{48,112},{56,120},{... | collective-permute-start | bytes 3145736 | tf_op jit(solution)/shard_map/ppermute | solution.py:35
  74.0 25.7 %collective-permute-start.15 = (bf16[6,512,128]{2,1,0:T(8,128)(2,1)S(1)}, bf16[6,512,128]{2,1,0:T(8,128)(2,1)S(1)}, u32[]{:S(2)}, u32[]{:S(2)}) collective-permute-start(bf16[6,512,128]{2,1,0:T(8,128)(2,1)S(1)} %get-tuple-element.78), channel_id=1, source_target_pairs={{0,2},{1,3},{2,4},{3,5},{4,6},{5,7},{6,0},{7,1},{8,10},{9,11},{10,... | collective-permute-start | bytes 2359304 | tf_op jit(solution)/shard_map/ppermute | solution.py:27
  74.1 25.6 %collective-permute-start.16 = (bf16[6,512,128]{2,1,0:T(8,128)(2,1)S(1)}, bf16[6,512,128]{2,1,0:T(8,128)(2,1)S(1)}, u32[]{:S(2)}, u32[]{:S(2)}) collective-permute-start(bf16[6,512,128]{2,1,0:T(8,128)(2,1)S(1)} %get-tuple-element.77), channel_id=1, source_target_pairs={{0,6},{1,7},{2,0},{3,1},{4,2},{5,3},{6,4},{7,5},{8,14},{9,15},{10,... | collective-permute-start | bytes 2359304 | tf_op jit(solution)/shard_map/ppermute | solution.py:27
  76.7 14.0 %collective-permute-start.18 = (bf16[4,512,128]{2,1,0:T(8,128)(2,1)S(1)}, bf16[4,512,128]{2,1,0:T(8,128)(2,1)S(1)}, u32[]{:S(2)}, u32[]{:S(2)}) collective-permute-start(bf16[4,512,128]{2,1,0:T(8,128)(2,1)S(1)} %copy-done.6), channel_id=1, source_target_pairs={{0,1},{1,0},{2,3},{3,2},{4,5},{5,4},{6,7},{7,6},{8,9},{9,8},{10,11... | collective-permute-start | bytes 1572872 | tf_op jit(solution)/shard_map/ppermute | solution.py:31
  79.5 19.1 %collective-permute-start.17 = (bf16[2,512,128]{2,1,0:T(8,128)(2,1)S(1)}, bf16[2,512,128]{2,1,0:T(8,128)(2,1)S(1)}, u32[]{:S(2)}, u32[]{:S(2)}) collective-permute-start(bf16[2,512,128]{2,1,0:T(8,128)(2,1)S(1)} %get-tuple-element.74), channel_id=1, source_target_pairs={{0,4},{1,5},{2,6},{3,7},{4,0},{5,1},{6,2},{7,3},{8,12},{9,13},{10,... | collective-permute-start | bytes 786440 | tf_op jit(solution)/shard_map/ppermute | solution.py:27
  90.7 14.3 %copy-start.10 = (bf16[4,512,128]{2,1,0:T(8,128)(2,1)}, bf16[4,512,128]{2,1,0:T(8,128)(2,1)S(1)}, u32[]{:S(2)}) copy-start(bf16[4,512,128]{2,1,0:T(8,128)(2,1)S(1)} %collective-permute-done.18.grad_refs_3_) | copy-start | bytes 1572868
  90.7 17.0 %collective-permute-start.22 = (bf16[128,4096]{1,0:T(8,128)(2,1)S(1)}, bf16[128,4096]{1,0:T(8,128)(2,1)S(1)}, u32[]{:S(2)}, u32[]{:S(2)}) collective-permute-start(bf16[128,4096]{1,0:T(8,128)(2,1)S(1)} %collective-permute-done.11.own_refs_1_), channel_id=1, source_target_pairs={{0,8},{8,0},{16,24},{24,16},{32,40},{40,32},{48,56},{56,48},{64,72... | collective-permute-start | bytes 3145736 | tf_op jit(solution)/shard_map/ppermute | solution.py:39
  94.3 10.8 %copy-start.3 = (bf16[128,4096]{1,0:T(8,128)(2,1)}, bf16[128,4096]{1,0:T(8,128)(2,1)S(1)}, u32[]{:S(2)}) copy-start(bf16[128,4096]{1,0:T(8,128)(2,1)S(1)} %collective-permute-done.19.own_refs_2_) | copy-start | bytes 3145732
  99.6 1.5 copy-start.8
  99.6 1.5 copy-start.9
  99.6 10.2 %collective-permute-start.21 = (bf16[128,4096]{1,0:T(8,128)(2,1)S(1)}, bf16[128,4096]{1,0:T(8,128)(2,1)S(1)}, u32[]{:S(2)}, u32[]{:S(2)}) collective-permute-start(bf16[128,4096]{1,0:T(8,128)(2,1)S(1)} %collective-permute-done.19.own_refs_2_), channel_id=1, source_target_pairs={{0,8},{8,0},{16,24},{24,16},{32,40},{40,32},{48,56},{56,48},{64,72... | collective-permute-start | bytes 3145736 | tf_op jit(solution)/shard_map/ppermute | solution.py:39
  101.2 8.7 %collective-permute-start.20 = (bf16[2,512,128]{2,1,0:T(8,128)(2,1)S(1)}, bf16[2,512,128]{2,1,0:T(8,128)(2,1)S(1)}, u32[]{:S(2)}, u32[]{:S(2)}) collective-permute-start(bf16[2,512,128]{2,1,0:T(8,128)(2,1)S(1)} %fusion.2), channel_id=1, source_target_pairs={{0,1},{1,0},{2,3},{3,2},{4,5},{5,4},{6,7},{7,6},{8,9},{9,8},{10,11... | collective-permute-start | bytes 786440 | tf_op jit(solution)/shard_map/ppermute | solution.py:31
  105.1 44.5 %collective-permute-start.26 = (bf16[8,512,128]{2,1,0:T(8,128)(2,1)}, bf16[8,512,128]{2,1,0:T(8,128)(2,1)}, u32[]{:S(2)}, u32[]{:S(2)}) collective-permute-start(bf16[8,512,128]{2,1,0:T(8,128)(2,1)} %pad_maximum_fusion.1), channel_id=1, source_target_pairs={{0,4},{1,5},{2,6},{3,7},{4,0},{5,1},{6,2},{7,3},{8,12},{9,13},{10,... | collective-permute-start | bytes 3145736 | tf_op jit(solution)/shard_map/ppermute | solution.py:27
  107.7 9.3 %copy-start.4 = (bf16[128,4096]{1,0:T(8,128)(2,1)}, bf16[128,4096]{1,0:T(8,128)(2,1)S(1)}, u32[]{:S(2)}) copy-start(bf16[128,4096]{1,0:T(8,128)(2,1)S(1)} %collective-permute-done.22.other_refs_1_) | copy-start | bytes 3145732
  109.8 7.2 %copy-start.5 = (bf16[128,4096]{1,0:T(8,128)(2,1)}, bf16[128,4096]{1,0:T(8,128)(2,1)S(1)}, u32[]{:S(2)}) copy-start(bf16[128,4096]{1,0:T(8,128)(2,1)S(1)} %collective-permute-done.21.other_refs_2_) | copy-start | bytes 3145732
  109.8 39.7 %collective-permute-start.27 = (bf16[8,512,128]{2,1,0:T(8,128)(2,1)}, bf16[8,512,128]{2,1,0:T(8,128)(2,1)S(1)}, u32[]{:S(2)}, u32[]{:S(2)}) collective-permute-start(bf16[8,512,128]{2,1,0:T(8,128)(2,1)} %pad_maximum_fusion), channel_id=1, source_target_pairs={{0,1},{1,0},{2,3},{3,2},{4,5},{5,4},{6,7},{7,6},{8,9},{9,8},{10,11... | collective-permute-start | bytes 3145736 | tf_op jit(solution)/shard_map/ppermute | solution.py:31
  112.8 11.0 %copy-start.11 = (bf16[2,512,128]{2,1,0:T(8,128)(2,1)}, bf16[2,512,128]{2,1,0:T(8,128)(2,1)S(1)}, u32[]{:S(2)}) copy-start(bf16[2,512,128]{2,1,0:T(8,128)(2,1)S(1)} %add_convert_fusion.1.shared_refs_0_) | copy-start | bytes 786436
  112.8 26.1 %collective-permute-start.23 = (bf16[2,512,128]{2,1,0:T(8,128)(2,1)S(1)}, bf16[2,512,128]{2,1,0:T(8,128)(2,1)S(1)}, u32[]{:S(2)}, u32[]{:S(2)}) collective-permute-start(bf16[2,512,128]{2,1,0:T(8,128)(2,1)S(1)} %add_convert_fusion.1.shared_refs_0_), channel_id=1, source_target_pairs={{0,2},{1,3},{2,4},{3,5},{4,6},{5,7},{6,0},{7,1},{8,10},{9,11},{10,... | collective-permute-start | bytes 786440 | tf_op jit(solution)/shard_map/ppermute | solution.py:27
  113.7 28.0 %collective-permute-start.24 = (bf16[2,512,128]{2,1,0:T(8,128)(2,1)S(1)}, bf16[2,512,128]{2,1,0:T(8,128)(2,1)S(1)}, u32[]{:S(2)}, u32[]{:S(2)}) collective-permute-start(bf16[2,512,128]{2,1,0:T(8,128)(2,1)S(1)} %add_convert_fusion.1.shared_refs_0_), channel_id=1, source_target_pairs={{0,4},{1,5},{2,6},{3,7},{4,0},{5,1},{6,2},{7,3},{8,12},{9,13},{10,... | collective-permute-start | bytes 786440 | tf_op jit(solution)/shard_map/ppermute | solution.py:27
  117.0 25.3 %collective-permute-start.25 = (bf16[2,512,128]{2,1,0:T(8,128)(2,1)S(1)}, bf16[2,512,128]{2,1,0:T(8,128)(2,1)}, u32[]{:S(2)}, u32[]{:S(2)}) collective-permute-start(bf16[2,512,128]{2,1,0:T(8,128)(2,1)S(1)} %add_convert_fusion.1.shared_refs_0_), channel_id=1, source_target_pairs={{0,6},{1,7},{2,0},{3,1},{4,2},{5,3},{6,4},{7,5},{8,14},{9,15},{10,... | collective-permute-start | bytes 786440 | tf_op jit(solution)/shard_map/ppermute | solution.py:27
  138.9 3.4 %copy-start.12 = (bf16[2,512,128]{2,1,0:T(8,128)(2,1)}, bf16[2,512,128]{2,1,0:T(8,128)(2,1)S(1)}, u32[]{:S(2)}) copy-start(bf16[2,512,128]{2,1,0:T(8,128)(2,1)S(1)} %collective-permute-done.23.shared_refs_1_) | copy-start | bytes 786436
  141.7 0.7 copy-start.13
  149.6 1.0 copy-start.7

commit v11 on v10

--- a/solution.py
+++ b/solution.py
@@ -71,7 +71,7 @@
     runs_per_slot = 2
     scale = 1.0 / math.sqrt(HD)
     core = place_ref[0]
-    runs = [ref[i] for ref in (here_ref, there_ref) for i in range(slots)]
+    runs = [ref[i, j] for ref in (here_ref, there_ref) for i in range(per_ref) for j in range(2)]
     for b in range(slots * runs_per_slot):
         slot, part = b // runs_per_slot, b % runs_per_slot
         rows = slice(part * RUN, (part + 1) * RUN)
@@ -456,13 +456,13 @@
     column_other = swap_cores(column)
     pairs = [jnp.stack([block(dy, 0), from_x[dy]]) for dy in range(4)]
     moved = [along_y(pairs[dy], dy) for dy in range(1, 4)]
-    slab_own = turn([pairs[0]] + moved)
-    info = column[:, count, :2].reshape(8).astype(jnp.int32)
-    partner_column, info, place, slab_own = lax.optimization_barrier(
-        (partner_column, info, place, slab_own)
+    info = column[:, count, :2].astype(jnp.int32)
+    partner_column, info, place, kept, *moved = lax.optimization_barrier(
+        (partner_column, info, place, pairs[0], *moved)
     )
     partner_other = swap_cores(partner_column)
-    partner_info = partner_column[:, count, :2].reshape(8).astype(jnp.int32)
+    partner_info = partner_column[:, count, :2].astype(jnp.int32)
+    slab_own = turn([kept] + moved)
     slab_back, slab_ahead = along_z(slab_own, 1), along_z(slab_own, 3)
     own_other = swap_cores(slab_own)
 
@@ -512,6 +512,7 @@
     late = [(from_2, 0), (from_x13, 0), (from_2, heads), (from_x13, heads)]
     partial = query_weights(place, slabs, slabs_other, early, heads)
     grad_wq = query_weights(place, slabs, slabs_other, late, heads, partial)
+    place, grad_wq = lax.optimization_barrier((place, grad_wq))
     grad_wk, grad_wv, grad_key, grad_value = shared_weights(place, slabs, slabs_other, shared)
     return grad_query, grad_key.T, grad_value.T, grad_wq, grad_wk.T, grad_wv.T
 

time: 160 us -> 157 us (0.981)
  waiting for transfers between devices: 53.5 us -> 60.5 us
  starting transfers between devices: 43.9 us -> 38.8 us
  Pallas kernels: 44.9 us -> 42 us
    ppermute x13, waiting for transfers between devices: 37 us -> 20.3 us  [along_y(): lax.ppermute(value, 'ctx', [(i, (i + 2 * step) % 8) for i in range(8)])]
    ppermute x5, waiting for transfers between devices: 13 us -> 28.4 us  [swap_x(): return lax.ppermute(value, 'ctx', [(i, i ^ 1) for i in range(8)])]
    ppermute x3, waiting for transfers between devices: 2.33 us -> 7.68 us  [along_z(): lax.ppermute(value, 'dp', [(i, (i + 4 * step) % 16) for i in range(16)])]
    ppermute x7, waiting for transfers between devices: 1.21 us -> 4.13 us  [swap_cores(): return lax.ppermute(value, 'dp', [(i, i ^ 1) for i in range(16)])]
    pallas_call x1, Pallas kernels: 21.3 us -> 18.4 us  [attention(): pl.pallas_call(functools.partial(attention_kernel, heads), out_shape=(jax...]
    ppermute x3, starting transfers between devices: 6.46 us -> 3.76 us  [along_z(): lax.ppermute(value, 'dp', [(i, (i + 4 * step) % 16) for i in range(16)])]
    ppermute x13, starting transfers between devices: 17.2 us -> 15.5 us  [along_y(): lax.ppermute(value, 'ctx', [(i, (i + 2 * step) % 8) for i in range(8)])]
  transfers between devices with their start and end apart: 28 -> 28, of which waited for: 15 -> 14; matrix products, arithmetic and copies ran while one was open for 7% -> 6% of each run, Pallas kernels for 24% -> 22%
where the time goes in v11:
time: 157 us; the launch traced here: 155 us
  waiting for transfers between devices  60.5 us (39%)
  Pallas kernels  42 us (27%)
  starting transfers between devices  38.8 us (25%)
  other arithmetic  7.91 us (5%)
  local copies, waits for them, and re-layouts  4.93 us (3%)
    ppermute x5, waiting for transfers between devices, swap_x(): return lax.ppermute(value, 'ctx', [(i, i ^ 1) for i in range(8)])  28.4 us
    ppermute x13, waiting for transfers between devices, along_y(): lax.ppermute(value, 'ctx', [(i, (i + 2 * step) % 8) for i in range(8)])  20.3 us
    pallas_call x1, Pallas kernels, attention(): pl.pallas_call(functools.partial(attention_kernel, heads), out_shape=(jax...  18.4 us
    ppermute x13, starting transfers between devices, along_y(): lax.ppermute(value, 'ctx', [(i, (i + 2 * step) % 8) for i in range(8)])  15.5 us
    pallas_call x2, Pallas kernels, query_weights(): pl.pallas_call(functools.partial(query_weight_kernel, last, tuple((start...  14 us
    ppermute x5, starting transfers between devices, swap_x(): return lax.ppermute(value, 'ctx', [(i, i ^ 1) for i in range(8)])  11.9 us
    ppermute x7, starting transfers between devices, swap_cores(): return lax.ppermute(value, 'dp', [(i, i ^ 1) for i in range(16)])  7.68 us
    ppermute x3, waiting for transfers between devices, along_z(): lax.ppermute(value, 'dp', [(i, (i + 4 * step) % 16) for i in range(16)])  7.68 us
  transfers between devices with their start and end apart: 28, of which 14 were waited for; matrix products, arithmetic and copies ran while one was open for 6% of the time, Pallas kernels for 22%

profile of v11, /device:TPU:1, one launch (start us, length us, event | category | flops | bytes accessed | tf_op | source)
XLA Modules:
  0.0 155.4 jit_solution(11146395763551827695)
XLA Ops:
  0.8 1.4 dynamic-slice_bitcast_fusion
  2.3 3.7 %collective-permute-start.4 = (bf16[4,512,128]{2,1,0:T(8,128)(2,1)S(1)}, bf16[4,512,128]{2,1,0:T(8,128)(2,1)S(1)}, u32[]{:S(2)}, u32[]{:S(2)}) collective-permute-start(bf16[4,512,128]{2,1,0:T(8,128)(2,1)S(1)} %pad_maximum_fusion.5), channel_id=1, source_target_pairs={{0,1},{1,0},{2,3},{3,2},{4,5},{5,4},{6,7},{7,6},{8,9},{9,8},{10,11... | collective-permute-start | bytes 1572872 | tf_op jit(solution)/shard_map/ppermute | solution.py:31
  5.9 0.8 slice.45
  6.8 1.0 dynamic-slice_select_fusion
  7.8 3.0 %collective-permute-start.1 = (bf16[528,128]{1,0:T(8,128)(2,1)S(1)}, bf16[528,128]{1,0:T(8,128)(2,1)S(1)}, u32[]{:S(2)}, u32[]{:S(2)}) collective-permute-start(bf16[528,128]{1,0:T(8,128)(2,1)S(1)} %get-tuple-element.94), channel_id=1, source_target_pairs={{0,4},{1,5},{2,6},{3,7},{4,0},{5,1},{6,2},{7,3},{8,12},{9,13},{10,... | collective-permute-start | bytes 405512 | tf_op jit(solution)/shard_map/ppermute | solution.py:27
  11.2 2.3 %collective-permute-start.2 = (bf16[528,128]{1,0:T(8,128)(2,1)S(1)}, bf16[528,128]{1,0:T(8,128)(2,1)S(1)}, u32[]{:S(2)}, u32[]{:S(2)}) collective-permute-start(bf16[528,128]{1,0:T(8,128)(2,1)S(1)} %get-tuple-element.94), channel_id=1, source_target_pairs={{0,6},{1,7},{2,0},{3,1},{4,2},{5,3},{6,4},{7,5},{8,14},{9,15},{10,... | collective-permute-start | bytes 405512 | tf_op jit(solution)/shard_map/ppermute | solution.py:27
  13.5 0.6 pad_add_fusion.place_ref
  14.1 3.1 %collective-permute-done = bf16[528,128]{1,0:T(8,128)(2,1)S(1)} collective-permute-done((bf16[528,128]{1,0:T(8,128)(2,1)S(1)}, bf16[528,128]{1,0:T(8,128)(2,1)S(1)}, u32[]{:S(2)}, u32[]{:S(2)}) %collective-permute-start) | collective-permute-done | bytes 135200 | tf_op jit(solution)/shard_map/ppermute | solution.py:27
  17.3 1.6 %collective-permute-start.8 = (bf16[4,528,128]{2,1,0:T(8,128)(2,1)S(1)}, bf16[4,528,128]{2,1,0:T(8,128)(2,1)}, u32[]{:S(2)}, u32[]{:S(2)}) collective-permute-start(bf16[4,528,128]{2,1,0:T(8,128)(2,1)S(1)} %pad_maximum_fusion.4.mine_refs_0_), channel_id=1, source_target_pairs={{0,8},{8,0},{16,24},{24,16},{32,40},{40,32},{48,56},{56,48},{64,72... | collective-permute-start | bytes 1622024 | tf_op jit(solution)/shard_map/ppermute | solution.py:39
  19.1 1.2 collective-permute-start.5
  20.3 3.1 %collective-permute-start.6 = (bf16[2,512,128]{2,1,0:T(8,128)(2,1)S(1)}, bf16[2,512,128]{2,1,0:T(8,128)(2,1)S(1)}, u32[]{:S(2)}, u32[]{:S(2)}) collective-permute-start(bf16[2,512,128]{2,1,0:T(8,128)(2,1)S(1)} %pad_maximum_fusion.8), channel_id=1, source_target_pairs={{0,4},{1,5},{2,6},{3,7},{4,0},{5,1},{6,2},{7,3},{8,12},{9,13},{10,... | collective-permute-start | bytes 786440 | tf_op jit(solution)/shard_map/ppermute | solution.py:27
  23.6 0.7 pad_maximum_fusion.6.in_refs_0_
  24.4 9.9 %collective-permute-done.3.mine_refs_1_ = bf16[4,528,128]{2,1,0:T(8,128)(2,1)} collective-permute-done((bf16[4,528,128]{2,1,0:T(8,128)(2,1)S(1)}, bf16[4,528,128]{2,1,0:T(8,128)(2,1)}, u32[]{:S(2)}, u32[]{:S(2)}) %collective-permute-start.3) | collective-permute-done | bytes 540704 | tf_op jit(solution)/shard_map/ppermute | solution.py:31
  34.3 0.7 collective-permute-done.6.in_refs_2_
  35.0 1.3 collective-permute-start.9
  36.3 2.5 %shard_map.110.own_refs_0_ = bf16[128,4096]{1,0:T(8,128)(2,1)} custom-call(bf16[2,512,128]{2,1,0:T(8,128)(2,1)} %pad_maximum_fusion.6.in_refs_0_, bf16[2,512,128]{2,1,0:T(8,128)(2,1)} %copy-done.15, bf16[2,512,128]{2,1,0:T(8,128)(2,1)} %copy-done.16, bf16[2,512,128]{2,1,0:T(8,128)(2,1)} %copy-done.17), custom_call_target="tpu_custom_call" | custom-call | bytes 2097152 | tf_op jit(solution)/shard_map/pallas_call | solution.py:227
  38.8 0.7 collective-permute-start.12
  39.5 3.8 %collective-permute-start.11 = (bf16[128,4096]{1,0:T(8,128)(2,1)}, bf16[128,4096]{1,0:T(8,128)(2,1)S(1)}, u32[]{:S(2)}, u32[]{:S(2)}) collective-permute-start(bf16[128,4096]{1,0:T(8,128)(2,1)} %shard_map.110.own_refs_0_), channel_id=1, source_target_pairs={{0,96},{8,104},{16,112},{24,120},{32,0},{40,8},{48,16},{56,24},{64... | collective-permute-start | bytes 3145736 | tf_op jit(solution)/shard_map/ppermute | solution.py:35
  43.2 1.3 slice_convert_fusion.1
  44.5 0.7 copy.26.here_ref
  45.2 18.4 %shard_map.109 = (bf16[512,512]{1,0:T(8,128)(2,1)}, bf16[4,512,128]{2,1,0:T(8,128)(2,1)}, bf16[8,512,128]{2,1,0:T(8,128)(2,1)}, bf16[8,512,128]{2,1,0:T(8,128)(2,1)}) custom-call(s32[2]{0:T(128)} %pad_add_fusion.place_ref, s32[4,2]{1,0:T(4,128)} %copy.26.here_ref, s32[4,2]{1,0:T(4,128)} %bitcast.55, bf16[512,512]{1,0:T(8,128)(2,1)} %q_ref.1, ...), custom_call_target="tpu_custom_call" | custom-call | flops 10737418240 | bytes 8388608 | tf_op jit(solution)/shard_map/pallas_call | solution.py:187
  63.6 2.6 %collective-permute-done.11.own_refs_1_ = bf16[128,4096]{1,0:T(8,128)(2,1)S(1)} collective-permute-done((bf16[128,4096]{1,0:T(8,128)(2,1)}, bf16[128,4096]{1,0:T(8,128)(2,1)S(1)}, u32[]{:S(2)}, u32[]{:S(2)}) %collective-permute-start.11) | collective-permute-done | bytes 1048608 | tf_op jit(solution)/shard_map/ppermute | solution.py:35
  66.1 3.1 %collective-permute-done.10.own_refs_3_ = bf16[128,4096]{1,0:T(8,128)(2,1)} collective-permute-done((bf16[128,4096]{1,0:T(8,128)(2,1)}, bf16[128,4096]{1,0:T(8,128)(2,1)}, u32[]{:S(2)}, u32[]{:S(2)}) %collective-permute-start.10) | collective-permute-done | bytes 1048608 | tf_op jit(solution)/shard_map/ppermute | solution.py:35
  69.2 1.1 collective-permute-start.13
  70.3 3.9 %collective-permute-done.13 = bf16[8,512,128]{2,1,0:T(8,128)(2,1)S(1)} collective-permute-done((bf16[8,512,128]{2,1,0:T(8,128)(2,1)}, bf16[8,512,128]{2,1,0:T(8,128)(2,1)S(1)}, u32[]{:S(2)}, u32[]{:S(2)}) %collective-permute-start.13) | collective-permute-done | bytes 1048608 | tf_op jit(solution)/shard_map/ppermute | solution.py:39
  74.5 1.5 add_convert_fusion
  76.2 2.0 %collective-permute-start.16 = (bf16[6,512,128]{2,1,0:T(8,128)(2,1)S(1)}, bf16[6,512,128]{2,1,0:T(8,128)(2,1)S(1)}, u32[]{:S(2)}, u32[]{:S(2)}) collective-permute-start(bf16[6,512,128]{2,1,0:T(8,128)(2,1)S(1)} %get-tuple-element.87), channel_id=1, source_target_pairs={{0,6},{1,7},{2,0},{3,1},{4,2},{5,3},{6,4},{7,5},{8,14},{9,15},{10,... | collective-permute-start | bytes 2359304 | tf_op jit(solution)/shard_map/ppermute | solution.py:27
  78.2 2.6 %collective-permute-start.18 = (bf16[4,512,128]{2,1,0:T(8,128)(2,1)S(1)}, bf16[4,512,128]{2,1,0:T(8,128)(2,1)S(1)}, u32[]{:S(2)}, u32[]{:S(2)}) collective-permute-start(bf16[4,512,128]{2,1,0:T(8,128)(2,1)S(1)} %copy-done.6), channel_id=1, source_target_pairs={{0,1},{1,0},{2,3},{3,2},{4,5},{5,4},{6,7},{7,6},{8,9},{9,8},{10,11... | collective-permute-start | bytes 1572872 | tf_op jit(solution)/shard_map/ppermute | solution.py:31
  80.8 1.3 collective-permute-start.17
  82.1 10.4 %collective-permute-done.18.grad_refs_3_ = bf16[4,512,128]{2,1,0:T(8,128)(2,1)S(1)} collective-permute-done((bf16[4,512,128]{2,1,0:T(8,128)(2,1)S(1)}, bf16[4,512,128]{2,1,0:T(8,128)(2,1)S(1)}, u32[]{:S(2)}, u32[]{:S(2)}) %collective-permute-start.18) | collective-permute-done | bytes 524320 | tf_op jit(solution)/shard_map/ppermute | solution.py:31
  92.5 1.5 collective-permute-start.22
  94.0 2.0 %collective-permute-done.19.own_refs_2_ = bf16[128,4096]{1,0:T(8,128)(2,1)S(1)} collective-permute-done((bf16[128,4096]{1,0:T(8,128)(2,1)S(1)}, bf16[128,4096]{1,0:T(8,128)(2,1)S(1)}, u32[]{:S(2)}, u32[]{:S(2)}) %collective-permute-start.19) | collective-permute-done | bytes 1048608 | tf_op jit(solution)/shard_map/ppermute | solution.py:35
  96.1 6.3 %collective-permute-done.17 = bf16[2,512,128]{2,1,0:T(8,128)(2,1)S(1)} collective-permute-done((bf16[2,512,128]{2,1,0:T(8,128)(2,1)S(1)}, bf16[2,512,128]{2,1,0:T(8,128)(2,1)S(1)}, u32[]{:S(2)}, u32[]{:S(2)}) %collective-permute-start.17) | collective-permute-done | bytes 262176 | tf_op jit(solution)/shard_map/ppermute | solution.py:27
  102.4 1.0 collective-permute-done.15.grad_refs_1_
  103.4 1.5 collective-permute-start.21
  105.2 2.7 %collective-permute-start.20 = (bf16[2,512,128]{2,1,0:T(8,128)(2,1)S(1)}, bf16[2,512,128]{2,1,0:T(8,128)(2,1)S(1)}, u32[]{:S(2)}, u32[]{:S(2)}) collective-permute-start(bf16[2,512,128]{2,1,0:T(8,128)(2,1)S(1)} %fusion.2), channel_id=1, source_target_pairs={{0,1},{1,0},{2,3},{3,2},{4,5},{5,4},{6,7},{7,6},{8,9},{9,8},{10,11... | collective-permute-start | bytes 786440 | tf_op jit(solution)/shard_map/ppermute | solution.py:31
  107.9 1.1 pad_maximum_fusion.1
  109.4 1.1 pad_maximum_fusion
  110.5 3.6 %collective-permute-done.20 = bf16[2,512,128]{2,1,0:T(8,128)(2,1)S(1)} collective-permute-done((bf16[2,512,128]{2,1,0:T(8,128)(2,1)S(1)}, bf16[2,512,128]{2,1,0:T(8,128)(2,1)S(1)}, u32[]{:S(2)}, u32[]{:S(2)}) %collective-permute-start.20) | collective-permute-done | bytes 262176 | tf_op jit(solution)/shard_map/ppermute | solution.py:31
  114.1 2.7 %collective-permute-start.24 = (bf16[8,512,128]{2,1,0:T(8,128)(2,1)}, bf16[8,512,128]{2,1,0:T(8,128)(2,1)S(1)}, u32[]{:S(2)}, u32[]{:S(2)}) collective-permute-start(bf16[8,512,128]{2,1,0:T(8,128)(2,1)} %pad_maximum_fusion), channel_id=1, source_target_pairs={{0,1},{1,0},{2,3},{3,2},{4,5},{5,4},{6,7},{7,6},{8,9},{9,8},{10,11... | collective-permute-start | bytes 3145736 | tf_op jit(solution)/shard_map/ppermute | solution.py:31
  117.5 1.2 collective-permute-start.25
  118.7 6.8 %shard_map.111.rest_0_ = f32[1024,512]{1,0:T(8,128)} custom-call(s32[2]{0:T(128)} %pad_add_fusion.place_ref, bf16[128,4096]{1,0:T(8,128)(2,1)} %shard_map.110.own_refs_0_, bf16[128,4096]{1,0:T(8,128)(2,1)} %copy-done.2, bf16[128,4096]{1,0:T(8,128)(2,1)} %copy-done.3, bf16[128,4096]{1,0:T(8,128)(2,1)} %collective-permute-done.10.own_refs_3_, ...), custom_call_target="tpu_custom_call" | custom-call | flops 2147483648 | bytes 10485760 | tf_op jit(solution)/shard_map/pallas_call | solution.py:336
  125.6 9.1 %collective-permute-done.23.grad_refs_0_.grad_refs_2_ = bf16[8,512,128]{2,1,0:T(8,128)(2,1)} collective-permute-done((bf16[8,512,128]{2,1,0:T(8,128)(2,1)}, bf16[8,512,128]{2,1,0:T(8,128)(2,1)}, u32[]{:S(2)}, u32[]{:S(2)}) %collective-permute-start.23) | collective-permute-done | bytes 1048608 | tf_op jit(solution)/shard_map/ppermute | solution.py:27
  134.7 4.4 %collective-permute-done.24.grad_refs_1_.grad_refs_3_ = bf16[8,512,128]{2,1,0:T(8,128)(2,1)S(1)} collective-permute-done((bf16[8,512,128]{2,1,0:T(8,128)(2,1)}, bf16[8,512,128]{2,1,0:T(8,128)(2,1)S(1)}, u32[]{:S(2)}, u32[]{:S(2)}) %collective-permute-start.24) | collective-permute-done | bytes 1048608 | tf_op jit(solution)/shard_map/ppermute | solution.py:31
  139.1 1.0 copy-done.7
  140.1 7.2 %shard_map.112 = f32[1024,512]{1,0:T(8,128)} custom-call(s32[2]{0:T(128)} %pad_add_fusion.place_ref, bf16[128,4096]{1,0:T(8,128)(2,1)} %shard_map.110.own_refs_0_, bf16[128,4096]{1,0:T(8,128)(2,1)} %copy-done.2, bf16[128,4096]{1,0:T(8,128)(2,1)} %copy-done.3, bf16[128,4096]{1,0:T(8,128)(2,1)} %collective-permute-done.10.own_refs_3_, ...), custom_call_target="tpu_custom_call" | custom-call | flops 2147483648 | bytes 10485760 | tf_op jit(solution)/shard_map/pallas_call | solution.py:336
  147.4 0.7 copy-done.13
  148.1 7.1 %shard_map.113 = (f32[64,1024]{1,0:T(8,128)}, f32[64,1024]{1,0:T(8,128)}, bf16[64,512]{1,0:T(8,128)(2,1)}, bf16[64,512]{1,0:T(8,128)(2,1)}) custom-call(s32[2]{0:T(128)} %pad_add_fusion.place_ref, bf16[128,4096]{1,0:T(8,128)(2,1)} %shard_map.110.own_refs_0_, bf16[128,4096]{1,0:T(8,128)(2,1)} %copy-done.2, bf16[128,4096]{1,0:T(8,128)(2,1)} %copy-done.3, ...), custom_call_target="tpu_custom_call" | custom-call | flops 1073741824 | bytes 10485760 | tf_op jit(solution)/shard_map/pallas_call | solution.py:413
  (78 shorter events, 2.9 us)
Async XLA Ops:
  2.3 16.8 %collective-permute-start.4 = (bf16[4,512,128]{2,1,0:T(8,128)(2,1)S(1)}, bf16[4,512,128]{2,1,0:T(8,128)(2,1)S(1)}, u32[]{:S(2)}, u32[]{:S(2)}) collective-permute-start(bf16[4,512,128]{2,1,0:T(8,128)(2,1)S(1)} %pad_maximum_fusion.5), channel_id=1, source_target_pairs={{0,1},{1,0},{2,3},{3,2},{4,5},{5,4},{6,7},{7,6},{8,9},{9,8},{10,11... | collective-permute-start | bytes 1572872 | tf_op jit(solution)/shard_map/ppermute | solution.py:31
  7.8 6.3 %collective-permute-start.1 = (bf16[528,128]{1,0:T(8,128)(2,1)S(1)}, bf16[528,128]{1,0:T(8,128)(2,1)S(1)}, u32[]{:S(2)}, u32[]{:S(2)}) collective-permute-start(bf16[528,128]{1,0:T(8,128)(2,1)S(1)} %get-tuple-element.94), channel_id=1, source_target_pairs={{0,4},{1,5},{2,6},{3,7},{4,0},{5,1},{6,2},{7,3},{8,12},{9,13},{10,... | collective-permute-start | bytes 405512 | tf_op jit(solution)/shard_map/ppermute | solution.py:27
  10.8 6.4 %collective-permute-start = (bf16[528,128]{1,0:T(8,128)(2,1)S(1)}, bf16[528,128]{1,0:T(8,128)(2,1)S(1)}, u32[]{:S(2)}, u32[]{:S(2)}) collective-permute-start(bf16[528,128]{1,0:T(8,128)(2,1)S(1)} %get-tuple-element.94), channel_id=1, source_target_pairs={{0,2},{1,3},{2,4},{3,5},{4,6},{5,7},{6,0},{7,1},{8,10},{9,11},{10,... | collective-permute-start | bytes 405512 | tf_op jit(solution)/shard_map/ppermute | solution.py:27
  11.2 6.0 %collective-permute-start.2 = (bf16[528,128]{1,0:T(8,128)(2,1)S(1)}, bf16[528,128]{1,0:T(8,128)(2,1)S(1)}, u32[]{:S(2)}, u32[]{:S(2)}) collective-permute-start(bf16[528,128]{1,0:T(8,128)(2,1)S(1)} %get-tuple-element.94), channel_id=1, source_target_pairs={{0,6},{1,7},{2,0},{3,1},{4,2},{5,3},{6,4},{7,5},{8,14},{9,15},{10,... | collective-permute-start | bytes 405512 | tf_op jit(solution)/shard_map/ppermute | solution.py:27
  17.3 21.5 %copy-start.12 = (bf16[4,528,128]{2,1,0:T(8,128)(2,1)}, bf16[4,528,128]{2,1,0:T(8,128)(2,1)S(1)}, u32[]{:S(2)}) copy-start(bf16[4,528,128]{2,1,0:T(8,128)(2,1)S(1)} %pad_maximum_fusion.4.mine_refs_0_) | copy-start | bytes 1622020
  17.3 27.9 %collective-permute-start.8 = (bf16[4,528,128]{2,1,0:T(8,128)(2,1)S(1)}, bf16[4,528,128]{2,1,0:T(8,128)(2,1)}, u32[]{:S(2)}, u32[]{:S(2)}) collective-permute-start(bf16[4,528,128]{2,1,0:T(8,128)(2,1)S(1)} %pad_maximum_fusion.4.mine_refs_0_), channel_id=1, source_target_pairs={{0,8},{8,0},{16,24},{24,16},{32,40},{40,32},{48,56},{56,48},{64,72... | collective-permute-start | bytes 1622024 | tf_op jit(solution)/shard_map/ppermute | solution.py:39
  18.9 15.4 %collective-permute-start.3 = (bf16[4,528,128]{2,1,0:T(8,128)(2,1)S(1)}, bf16[4,528,128]{2,1,0:T(8,128)(2,1)}, u32[]{:S(2)}, u32[]{:S(2)}) collective-permute-start(bf16[4,528,128]{2,1,0:T(8,128)(2,1)S(1)} %pad_maximum_fusion.4.mine_refs_0_), channel_id=1, source_target_pairs={{0,1},{1,0},{2,3},{3,2},{4,5},{5,4},{6,7},{7,6},{8,9},{9,8},{10,11... | collective-permute-start | bytes 1622024 | tf_op jit(solution)/shard_map/ppermute | solution.py:31
  19.1 15.2 %collective-permute-start.5 = (bf16[2,512,128]{2,1,0:T(8,128)(2,1)S(1)}, bf16[2,512,128]{2,1,0:T(8,128)(2,1)S(1)}, u32[]{:S(2)}, u32[]{:S(2)}) collective-permute-start(bf16[2,512,128]{2,1,0:T(8,128)(2,1)S(1)} %pad_maximum_fusion.7), channel_id=1, source_target_pairs={{0,2},{1,3},{2,4},{3,5},{4,6},{5,7},{6,0},{7,1},{8,10},{9,11},{10,... | collective-permute-start | bytes 786440 | tf_op jit(solution)/shard_map/ppermute | solution.py:27
  20.3 14.7 %collective-permute-start.6 = (bf16[2,512,128]{2,1,0:T(8,128)(2,1)S(1)}, bf16[2,512,128]{2,1,0:T(8,128)(2,1)S(1)}, u32[]{:S(2)}, u32[]{:S(2)}) collective-permute-start(bf16[2,512,128]{2,1,0:T(8,128)(2,1)S(1)} %pad_maximum_fusion.8), channel_id=1, source_target_pairs={{0,4},{1,5},{2,6},{3,7},{4,0},{5,1},{6,2},{7,3},{8,12},{9,13},{10,... | collective-permute-start | bytes 786440 | tf_op jit(solution)/shard_map/ppermute | solution.py:27
  23.5 11.5 %collective-permute-start.7 = (bf16[2,512,128]{2,1,0:T(8,128)(2,1)S(1)}, bf16[2,512,128]{2,1,0:T(8,128)(2,1)S(1)}, u32[]{:S(2)}, u32[]{:S(2)}) collective-permute-start(bf16[2,512,128]{2,1,0:T(8,128)(2,1)S(1)} %pad_maximum_fusion.9), channel_id=1, source_target_pairs={{0,6},{1,7},{2,0},{3,1},{4,2},{5,3},{6,4},{7,5},{8,14},{9,15},{10,... | collective-permute-start | bytes 786440 | tf_op jit(solution)/shard_map/ppermute | solution.py:27
  34.3 2.0 %copy-start.15 = (bf16[2,512,128]{2,1,0:T(8,128)(2,1)}, bf16[2,512,128]{2,1,0:T(8,128)(2,1)S(1)}, u32[]{:S(2)}) copy-start(bf16[2,512,128]{2,1,0:T(8,128)(2,1)S(1)} %collective-permute-done.5.in_refs_1_) | copy-start | bytes 786436
  35.0 1.3 copy-start.16
  35.0 1.3 copy-start.17
  35.0 10.2 %collective-permute-start.9 = (bf16[4,528,128]{2,1,0:T(8,128)(2,1)}, bf16[4,528,128]{2,1,0:T(8,128)(2,1)}, u32[]{:S(2)}, u32[]{:S(2)}) collective-permute-start(bf16[4,528,128]{2,1,0:T(8,128)(2,1)} %collective-permute-done.3.mine_refs_1_), channel_id=1, source_target_pairs={{0,8},{8,0},{16,24},{24,16},{32,40},{40,32},{48,56},{56,48},{64,72... | collective-permute-start | bytes 1622024 | tf_op jit(solution)/shard_map/ppermute | solution.py:39
  38.8 24.8 %collective-permute-start.12 = (bf16[128,4096]{1,0:T(8,128)(2,1)}, bf16[128,4096]{1,0:T(8,128)(2,1)S(1)}, u32[]{:S(2)}, u32[]{:S(2)}) collective-permute-start(bf16[128,4096]{1,0:T(8,128)(2,1)} %shard_map.110.own_refs_0_), channel_id=1, source_target_pairs={{0,8},{8,0},{16,24},{24,16},{32,40},{40,32},{48,56},{56,48},{64,72... | collective-permute-start | bytes 3145736 | tf_op jit(solution)/shard_map/ppermute | solution.py:39
  39.5 26.7 %collective-permute-start.11 = (bf16[128,4096]{1,0:T(8,128)(2,1)}, bf16[128,4096]{1,0:T(8,128)(2,1)S(1)}, u32[]{:S(2)}, u32[]{:S(2)}) collective-permute-start(bf16[128,4096]{1,0:T(8,128)(2,1)} %shard_map.110.own_refs_0_), channel_id=1, source_target_pairs={{0,96},{8,104},{16,112},{24,120},{32,0},{40,8},{48,16},{56,24},{64... | collective-permute-start | bytes 3145736 | tf_op jit(solution)/shard_map/ppermute | solution.py:35
  43.2 26.0 %collective-permute-start.10 = (bf16[128,4096]{1,0:T(8,128)(2,1)}, bf16[128,4096]{1,0:T(8,128)(2,1)}, u32[]{:S(2)}, u32[]{:S(2)}) collective-permute-start(bf16[128,4096]{1,0:T(8,128)(2,1)} %shard_map.110.own_refs_0_), channel_id=1, source_target_pairs={{0,32},{8,40},{16,48},{24,56},{32,64},{40,72},{48,80},{56,88},{64,... | collective-permute-start | bytes 3145736 | tf_op jit(solution)/shard_map/ppermute | solution.py:35
  45.2 25.2 %copy-start = (bf16[128,4096]{1,0:T(8,128)(2,1)S(1)}, bf16[128,4096]{1,0:T(8,128)(2,1)}, u32[]{:S(2)}) copy-start(bf16[128,4096]{1,0:T(8,128)(2,1)} %shard_map.110.own_refs_0_) | copy-start | bytes 3145732
  63.5 12.5 %copy-start.1 = (bf16[128,4096]{1,0:T(8,128)(2,1)}, bf16[128,4096]{1,0:T(8,128)(2,1)S(1)}, u32[]{:S(2)}) copy-start(bf16[128,4096]{1,0:T(8,128)(2,1)S(1)} %collective-permute-done.12.other_refs_0_) | copy-start | bytes 3145732
  66.1 26.4 %copy-start.2 = (bf16[128,4096]{1,0:T(8,128)(2,1)}, bf16[128,4096]{1,0:T(8,128)(2,1)S(1)}, u32[]{:S(2)}) copy-start(bf16[128,4096]{1,0:T(8,128)(2,1)S(1)} %collective-permute-done.11.own_refs_1_) | copy-start | bytes 3145732
  69.2 6.8 %copy-start.6 = (bf16[4,512,128]{2,1,0:T(8,128)(2,1)S(1)}, bf16[4,512,128]{2,1,0:T(8,128)(2,1)}, u32[]{:S(2)}) copy-start(bf16[4,512,128]{2,1,0:T(8,128)(2,1)} %get-tuple-element.54.grad_refs_0_) | copy-start | bytes 1572868
  69.2 5.1 %collective-permute-start.13 = (bf16[8,512,128]{2,1,0:T(8,128)(2,1)}, bf16[8,512,128]{2,1,0:T(8,128)(2,1)S(1)}, u32[]{:S(2)}, u32[]{:S(2)}) collective-permute-start(bf16[8,512,128]{2,1,0:T(8,128)(2,1)} %get-tuple-element.56), channel_id=1, source_target_pairs={{0,8},{8,0},{16,24},{24,16},{32,40},{40,32},{48,56},{56,48},{64,72... | collective-permute-start | bytes 3145736 | tf_op jit(solution)/shard_map/ppermute | solution.py:39
  70.3 4.1 %collective-permute-start.14 = (bf16[128,4096]{1,0:T(8,128)(2,1)}, bf16[128,4096]{1,0:T(8,128)(2,1)}, u32[]{:S(2)}, u32[]{:S(2)}) collective-permute-start(bf16[128,4096]{1,0:T(8,128)(2,1)} %collective-permute-done.10.own_refs_3_), channel_id=1, source_target_pairs={{0,8},{8,0},{16,24},{24,16},{32,40},{40,32},{48,56},{56,48},{64,72... | collective-permute-start | bytes 3145736 | tf_op jit(solution)/shard_map/ppermute | solution.py:39
  70.3 25.7 %collective-permute-start.19 = (bf16[128,4096]{1,0:T(8,128)(2,1)S(1)}, bf16[128,4096]{1,0:T(8,128)(2,1)S(1)}, u32[]{:S(2)}, u32[]{:S(2)}) collective-permute-start(bf16[128,4096]{1,0:T(8,128)(2,1)S(1)} %copy-done), channel_id=1, source_target_pairs={{0,64},{8,72},{16,80},{24,88},{32,96},{40,104},{48,112},{56,120},{... | collective-permute-start | bytes 3145736 | tf_op jit(solution)/shard_map/ppermute | solution.py:35
  76.2 26.3 %collective-permute-start.16 = (bf16[6,512,128]{2,1,0:T(8,128)(2,1)S(1)}, bf16[6,512,128]{2,1,0:T(8,128)(2,1)S(1)}, u32[]{:S(2)}, u32[]{:S(2)}) collective-permute-start(bf16[6,512,128]{2,1,0:T(8,128)(2,1)S(1)} %get-tuple-element.87), channel_id=1, source_target_pairs={{0,6},{1,7},{2,0},{3,1},{4,2},{5,3},{6,4},{7,5},{8,14},{9,15},{10,... | collective-permute-start | bytes 2359304 | tf_op jit(solution)/shard_map/ppermute | solution.py:27
  78.2 25.3 %collective-permute-start.15 = (bf16[6,512,128]{2,1,0:T(8,128)(2,1)S(1)}, bf16[6,512,128]{2,1,0:T(8,128)(2,1)S(1)}, u32[]{:S(2)}, u32[]{:S(2)}) collective-permute-start(bf16[6,512,128]{2,1,0:T(8,128)(2,1)S(1)} %get-tuple-element.88), channel_id=1, source_target_pairs={{0,2},{1,3},{2,4},{3,5},{4,6},{5,7},{6,0},{7,1},{8,10},{9,11},{10,... | collective-permute-start | bytes 2359304 | tf_op jit(solution)/shard_map/ppermute | solution.py:27
  78.2 14.3 %collective-permute-start.18 = (bf16[4,512,128]{2,1,0:T(8,128)(2,1)S(1)}, bf16[4,512,128]{2,1,0:T(8,128)(2,1)S(1)}, u32[]{:S(2)}, u32[]{:S(2)}) collective-permute-start(bf16[4,512,128]{2,1,0:T(8,128)(2,1)S(1)} %copy-done.6), channel_id=1, source_target_pairs={{0,1},{1,0},{2,3},{3,2},{4,5},{5,4},{6,7},{7,6},{8,9},{9,8},{10,11... | collective-permute-start | bytes 1572872 | tf_op jit(solution)/shard_map/ppermute | solution.py:31
  80.8 21.6 %collective-permute-start.17 = (bf16[2,512,128]{2,1,0:T(8,128)(2,1)S(1)}, bf16[2,512,128]{2,1,0:T(8,128)(2,1)S(1)}, u32[]{:S(2)}, u32[]{:S(2)}) collective-permute-start(bf16[2,512,128]{2,1,0:T(8,128)(2,1)S(1)} %get-tuple-element.84), channel_id=1, source_target_pairs={{0,4},{1,5},{2,6},{3,7},{4,0},{5,1},{6,2},{7,3},{8,12},{9,13},{10,... | collective-permute-start | bytes 786440 | tf_op jit(solution)/shard_map/ppermute | solution.py:27
  92.5 16.5 %copy-start.10 = (bf16[4,512,128]{2,1,0:T(8,128)(2,1)}, bf16[4,512,128]{2,1,0:T(8,128)(2,1)S(1)}, u32[]{:S(2)}) copy-start(bf16[4,512,128]{2,1,0:T(8,128)(2,1)S(1)} %collective-permute-done.18.grad_refs_3_) | copy-start | bytes 1572868
  92.5 18.0 %collective-permute-start.22 = (bf16[128,4096]{1,0:T(8,128)(2,1)S(1)}, bf16[128,4096]{1,0:T(8,128)(2,1)S(1)}, u32[]{:S(2)}, u32[]{:S(2)}) collective-permute-start(bf16[128,4096]{1,0:T(8,128)(2,1)S(1)} %collective-permute-done.11.own_refs_1_), channel_id=1, source_target_pairs={{0,8},{8,0},{16,24},{24,16},{32,40},{40,32},{48,56},{56,48},{64,72... | collective-permute-start | bytes 3145736 | tf_op jit(solution)/shard_map/ppermute | solution.py:39
  96.0 12.9 %copy-start.3 = (bf16[128,4096]{1,0:T(8,128)(2,1)}, bf16[128,4096]{1,0:T(8,128)(2,1)S(1)}, u32[]{:S(2)}) copy-start(bf16[128,4096]{1,0:T(8,128)(2,1)S(1)} %collective-permute-done.19.own_refs_2_) | copy-start | bytes 3145732
  102.4 2.8 %copy-start.8 = (bf16[6,512,128]{2,1,0:T(8,128)(2,1)}, bf16[6,512,128]{2,1,0:T(8,128)(2,1)S(1)}, u32[]{:S(2)}) copy-start(bf16[6,512,128]{2,1,0:T(8,128)(2,1)S(1)} %collective-permute-done.16.grad_refs_2_) | copy-start | bytes 2359300
  103.4 1.8 %copy-start.9 = (bf16[6,512,128]{2,1,0:T(8,128)(2,1)}, bf16[6,512,128]{2,1,0:T(8,128)(2,1)S(1)}, u32[]{:S(2)}) copy-start(bf16[6,512,128]{2,1,0:T(8,128)(2,1)S(1)} %collective-permute-done.15.grad_refs_1_) | copy-start | bytes 2359300
  103.4 10.7 %collective-permute-start.21 = (bf16[128,4096]{1,0:T(8,128)(2,1)S(1)}, bf16[128,4096]{1,0:T(8,128)(2,1)S(1)}, u32[]{:S(2)}, u32[]{:S(2)}) collective-permute-start(bf16[128,4096]{1,0:T(8,128)(2,1)S(1)} %collective-permute-done.19.own_refs_2_), channel_id=1, source_target_pairs={{0,8},{8,0},{16,24},{24,16},{32,40},{40,32},{48,56},{56,48},{64,72... | collective-permute-start | bytes 3145736 | tf_op jit(solution)/shard_map/ppermute | solution.py:39
  105.2 8.9 %collective-permute-start.20 = (bf16[2,512,128]{2,1,0:T(8,128)(2,1)S(1)}, bf16[2,512,128]{2,1,0:T(8,128)(2,1)S(1)}, u32[]{:S(2)}, u32[]{:S(2)}) collective-permute-start(bf16[2,512,128]{2,1,0:T(8,128)(2,1)S(1)} %fusion.2), channel_id=1, source_target_pairs={{0,1},{1,0},{2,3},{3,2},{4,5},{5,4},{6,7},{7,6},{8,9},{9,8},{10,11... | collective-permute-start | bytes 786440 | tf_op jit(solution)/shard_map/ppermute | solution.py:31
  109.0 25.7 %collective-permute-start.23 = (bf16[8,512,128]{2,1,0:T(8,128)(2,1)}, bf16[8,512,128]{2,1,0:T(8,128)(2,1)}, u32[]{:S(2)}, u32[]{:S(2)}) collective-permute-start(bf16[8,512,128]{2,1,0:T(8,128)(2,1)} %pad_maximum_fusion.1), channel_id=1, source_target_pairs={{0,4},{1,5},{2,6},{3,7},{4,0},{5,1},{6,2},{7,3},{8,12},{9,13},{10,... | collective-permute-start | bytes 3145736 | tf_op jit(solution)/shard_map/ppermute | solution.py:27
  110.5 8.2 %copy-start.4 = (bf16[128,4096]{1,0:T(8,128)(2,1)}, bf16[128,4096]{1,0:T(8,128)(2,1)S(1)}, u32[]{:S(2)}) copy-start(bf16[128,4096]{1,0:T(8,128)(2,1)S(1)} %collective-permute-done.22.other_refs_1_) | copy-start | bytes 3145732
  114.1 4.6 %copy-start.5 = (bf16[128,4096]{1,0:T(8,128)(2,1)}, bf16[128,4096]{1,0:T(8,128)(2,1)S(1)}, u32[]{:S(2)}) copy-start(bf16[128,4096]{1,0:T(8,128)(2,1)S(1)} %collective-permute-done.21.other_refs_2_) | copy-start | bytes 3145732
  114.1 25.0 %collective-permute-start.24 = (bf16[8,512,128]{2,1,0:T(8,128)(2,1)}, bf16[8,512,128]{2,1,0:T(8,128)(2,1)S(1)}, u32[]{:S(2)}, u32[]{:S(2)}) collective-permute-start(bf16[8,512,128]{2,1,0:T(8,128)(2,1)} %pad_maximum_fusion), channel_id=1, source_target_pairs={{0,1},{1,0},{2,3},{3,2},{4,5},{5,4},{6,7},{7,6},{8,9},{9,8},{10,11... | collective-permute-start | bytes 3145736 | tf_op jit(solution)/shard_map/ppermute | solution.py:31
  116.9 8.6 %copy-start.11 = (bf16[2,512,128]{2,1,0:T(8,128)(2,1)}, bf16[2,512,128]{2,1,0:T(8,128)(2,1)S(1)}, u32[]{:S(2)}) copy-start(bf16[2,512,128]{2,1,0:T(8,128)(2,1)S(1)} %add_convert_fusion.1.shared_refs_0_) | copy-start | bytes 786436
  117.0 30.4 %collective-permute-start.27 = (bf16[2,512,128]{2,1,0:T(8,128)(2,1)S(1)}, bf16[2,512,128]{2,1,0:T(8,128)(2,1)S(1)}, u32[]{:S(2)}, u32[]{:S(2)}) collective-permute-start(bf16[2,512,128]{2,1,0:T(8,128)(2,1)S(1)} %add_convert_fusion.1.shared_refs_0_), channel_id=1, source_target_pairs={{0,6},{1,7},{2,0},{3,1},{4,2},{5,3},{6,4},{7,5},{8,14},{9,15},{10,... | collective-permute-start | bytes 786440 | tf_op jit(solution)/shard_map/ppermute | solution.py:27
  117.3 30.1 %collective-permute-start.26 = (bf16[2,512,128]{2,1,0:T(8,128)(2,1)S(1)}, bf16[2,512,128]{2,1,0:T(8,128)(2,1)S(1)}, u32[]{:S(2)}, u32[]{:S(2)}) collective-permute-start(bf16[2,512,128]{2,1,0:T(8,128)(2,1)S(1)} %add_convert_fusion.1.shared_refs_0_), channel_id=1, source_target_pairs={{0,4},{1,5},{2,6},{3,7},{4,0},{5,1},{6,2},{7,3},{8,12},{9,13},{10,... | collective-permute-start | bytes 786440 | tf_op jit(solution)/shard_map/ppermute | solution.py:27
  117.5 29.8 %collective-permute-start.25 = (bf16[2,512,128]{2,1,0:T(8,128)(2,1)S(1)}, bf16[2,512,128]{2,1,0:T(8,128)(2,1)}, u32[]{:S(2)}, u32[]{:S(2)}) collective-permute-start(bf16[2,512,128]{2,1,0:T(8,128)(2,1)S(1)} %add_convert_fusion.1.shared_refs_0_), channel_id=1, source_target_pairs={{0,2},{1,3},{2,4},{3,5},{4,6},{5,7},{6,0},{7,1},{8,10},{9,11},{10,... | collective-permute-start | bytes 786440 | tf_op jit(solution)/shard_map/ppermute | solution.py:27
  139.1 1.0 copy-start.7
  147.3 0.7 copy-start.13
  147.3 0.8 copy-start.14

commit v12 on v7

--- a/solution.py
+++ b/solution.py
@@ -15,6 +15,7 @@
 LOW = -1e30
 LOG2E = 1.4426950408889634
 VMEM_BYTES = 60 * 1024 * 1024
+WEIGHT_VMEM_BYTES = 20 * 1024 * 1024
 
 
 def contract(left, right, left_dim, right_dim):
@@ -384,7 +385,7 @@
         in_specs=[smem, [hbm] * 4, [hbm] * 4, [hbm] * 4] + ([hbm, [hbm] * 4] if last else []),
         out_specs=(hbm, vmem, vmem, vmem, vmem) if last else hbm,
         scratch_shapes=scratch,
-        compiler_params=pltpu.CompilerParams(vmem_limit_bytes=VMEM_BYTES),
+        compiler_params=pltpu.CompilerParams(vmem_limit_bytes=WEIGHT_VMEM_BYTES),
         cost_estimate=pl.CostEstimate(
             flops=8 * tokens * cols * 8 * tall, bytes_accessed=10 * 1024 * 1024, transcendentals=0
         ),

time: 159 us -> 156 us (0.981)
  waiting for transfers between devices: 69.9 us -> 65.2 us
  Pallas kernels: 36.3 us -> 40 us
  other arithmetic: 8.97 us -> 6.97 us
    pallas_call x1, Pallas kernels: 15.7 us -> 22.1 us  [attention(): pl.pallas_call(functools.partial(attention_kernel, heads), out_shape=(jax...]
    ppermute x3, waiting for transfers between devices: 10.2 us -> 4.43 us  [along_z(): lax.ppermute(value, 'dp', [(i, (i + 4 * step) % 16) for i in range(16)])]
    pallas_call x2, Pallas kernels: 18.1 us -> 15.4 us  [weights(): pl.pallas_call(functools.partial(weight_kernel, last, tuple((start for _,...]
  transfers between devices with their start and end apart: 28 -> 28, of which waited for: 18 -> 17; matrix products, arithmetic and copies ran while one was open for 6% -> 5% of each run, Pallas kernels for 16% -> 19%
where the time goes in v12:
time: 156 us
  waiting for transfers between devices  65.2 us (42%)
  starting transfers between devices  40.1 us (26%)
  Pallas kernels  40 us (26%)
  other arithmetic  6.97 us (4%)
  local copies, waits for them, and re-layouts  2.52 us (2%)
    ppermute x13, waiting for transfers between devices, along_y(): lax.ppermute(value, 'ctx', [(i, (i + 2 * step) % 8) for i in range(8)])  34.3 us
    ppermute x5, waiting for transfers between devices, swap_x(): return lax.ppermute(value, 'ctx', [(i, i ^ 1) for i in range(8)])  22.5 us
    pallas_call x1, Pallas kernels, attention(): pl.pallas_call(functools.partial(attention_kernel, heads), out_shape=(jax...  22.1 us
    ppermute x13, starting transfers between devices, along_y(): lax.ppermute(value, 'ctx', [(i, (i + 2 * step) % 8) for i in range(8)])  15.9 us
    pallas_call x2, Pallas kernels, weights(): pl.pallas_call(functools.partial(weight_kernel, last, tuple((start for _,...  15.4 us
    ppermute x5, starting transfers between devices, swap_x(): return lax.ppermute(value, 'ctx', [(i, i ^ 1) for i in range(8)])  11.1 us
    ppermute x7, starting transfers between devices, swap_cores(): return lax.ppermute(value, 'dp', [(i, i ^ 1) for i in range(16)])  9.43 us
    ppermute x3, waiting for transfers between devices, along_z(): lax.ppermute(value, 'dp', [(i, (i + 4 * step) % 16) for i in range(16)])  4.43 us
  transfers between devices with their start and end apart: 28, of which 17 were waited for; matrix products, arithmetic and copies ran while one was open for 5% of the time, Pallas kernels for 19%

profile of v12, /device:TPU:1, one launch (start us, length us, event | category | flops | bytes accessed | tf_op | source)
XLA Modules:
  0.0 156.0 jit_solution(10810136833843888429)
XLA Ops:
  0.8 1.4 dynamic-slice_bitcast_fusion
  2.3 3.7 %collective-permute-start.4 = (bf16[4,512,128]{2,1,0:T(8,128)(2,1)S(1)}, bf16[4,512,128]{2,1,0:T(8,128)(2,1)S(1)}, u32[]{:S(2)}, u32[]{:S(2)}) collective-permute-start(bf16[4,512,128]{2,1,0:T(8,128)(2,1)S(1)} %pad_maximum_fusion.5), channel_id=1, source_target_pairs={{0,1},{1,0},{2,3},{3,2},{4,5},{5,4},{6,7},{7,6},{8,9},{9,8},{10,11... | collective-permute-start | bytes 1572872 | tf_op jit(solution)/shard_map/ppermute | solution.py:32
  5.9 0.8 slice.48
  6.8 1.0 dynamic-slice_select_fusion
  7.8 3.0 %collective-permute-start.1 = (bf16[528,128]{1,0:T(8,128)(2,1)S(1)}, bf16[528,128]{1,0:T(8,128)(2,1)S(1)}, u32[]{:S(2)}, u32[]{:S(2)}) collective-permute-start(bf16[528,128]{1,0:T(8,128)(2,1)S(1)} %get-tuple-element.92), channel_id=1, source_target_pairs={{0,4},{1,5},{2,6},{3,7},{4,0},{5,1},{6,2},{7,3},{8,12},{9,13},{10,... | collective-permute-start | bytes 405512 | tf_op jit(solution)/shard_map/ppermute | solution.py:28
  10.8 0.4 collective-permute-start
  11.2 2.3 %collective-permute-start.2 = (bf16[528,128]{1,0:T(8,128)(2,1)S(1)}, bf16[528,128]{1,0:T(8,128)(2,1)S(1)}, u32[]{:S(2)}, u32[]{:S(2)}) collective-permute-start(bf16[528,128]{1,0:T(8,128)(2,1)S(1)} %get-tuple-element.92), channel_id=1, source_target_pairs={{0,6},{1,7},{2,0},{3,1},{4,2},{5,3},{6,4},{7,5},{8,14},{9,15},{10,... | collective-permute-start | bytes 405512 | tf_op jit(solution)/shard_map/ppermute | solution.py:28
  13.6 3.7 %collective-permute-done = bf16[528,128]{1,0:T(8,128)(2,1)S(1)} collective-permute-done((bf16[528,128]{1,0:T(8,128)(2,1)S(1)}, bf16[528,128]{1,0:T(8,128)(2,1)S(1)}, u32[]{:S(2)}, u32[]{:S(2)}) %collective-permute-start) | collective-permute-done | bytes 135200 | tf_op jit(solution)/shard_map/ppermute | solution.py:28
  17.2 0.9 pad_maximum_fusion.4.mine_refs_0_
  18.3 2.0 %collective-permute-start.5 = (bf16[2,512,128]{2,1,0:T(8,128)(2,1)S(1)}, bf16[2,512,128]{2,1,0:T(8,128)(2,1)S(1)}, u32[]{:S(2)}, u32[]{:S(2)}) collective-permute-start(bf16[2,512,128]{2,1,0:T(8,128)(2,1)S(1)} %pad_maximum_fusion.7), channel_id=1, source_target_pairs={{0,2},{1,3},{2,4},{3,5},{4,6},{5,7},{6,0},{7,1},{8,10},{9,11},{10,... | collective-permute-start | bytes 786440 | tf_op jit(solution)/shard_map/ppermute | solution.py:28
  20.3 2.3 %collective-permute-start.6 = (bf16[2,512,128]{2,1,0:T(8,128)(2,1)S(1)}, bf16[2,512,128]{2,1,0:T(8,128)(2,1)S(1)}, u32[]{:S(2)}, u32[]{:S(2)}) collective-permute-start(bf16[2,512,128]{2,1,0:T(8,128)(2,1)S(1)} %pad_maximum_fusion.8), channel_id=1, source_target_pairs={{0,4},{1,5},{2,6},{3,7},{4,0},{5,1},{6,2},{7,3},{8,12},{9,13},{10,... | collective-permute-start | bytes 786440 | tf_op jit(solution)/shard_map/ppermute | solution.py:28
  23.0 2.4 %collective-permute-start.8 = (bf16[4,528,128]{2,1,0:T(8,128)(2,1)}, bf16[4,528,128]{2,1,0:T(8,128)(2,1)}, u32[]{:S(2)}, u32[]{:S(2)}) collective-permute-start(bf16[4,528,128]{2,1,0:T(8,128)(2,1)} %pad_maximum_fusion.4.mine_refs_0_), channel_id=1, source_target_pairs={{0,8},{8,0},{16,24},{24,16},{32,40},{40,32},{48,56},{56,48},{64,72... | collective-permute-start | bytes 1622024 | tf_op jit(solution)/shard_map/ppermute | solution.py:40
  25.3 0.7 fusion.3
  26.1 0.7 pad_maximum_fusion.6.in_refs_0_
  26.8 5.4 %collective-permute-done.3.mine_refs_1_ = bf16[4,528,128]{2,1,0:T(8,128)(2,1)} collective-permute-done((bf16[4,528,128]{2,1,0:T(8,128)(2,1)}, bf16[4,528,128]{2,1,0:T(8,128)(2,1)}, u32[]{:S(2)}, u32[]{:S(2)}) %collective-permute-start.3) | collective-permute-done | bytes 540704 | tf_op jit(solution)/shard_map/ppermute | solution.py:32
  32.2 0.5 collective-permute-done.6.in_refs_2_
  32.7 0.5 collective-permute-done.7.in_refs_3_
  33.2 2.2 %collective-permute-start.9 = (bf16[4,528,128]{2,1,0:T(8,128)(2,1)}, bf16[4,528,128]{2,1,0:T(8,128)(2,1)}, u32[]{:S(2)}, u32[]{:S(2)}) collective-permute-start(bf16[4,528,128]{2,1,0:T(8,128)(2,1)} %collective-permute-done.3.mine_refs_1_), channel_id=1, source_target_pairs={{0,8},{8,0},{16,24},{24,16},{32,40},{40,32},{48,56},{56,48},{64,72... | collective-permute-start | bytes 1622024 | tf_op jit(solution)/shard_map/ppermute | solution.py:40
  35.4 2.5 %shard_map.110.own_refs_0_ = bf16[128,4096]{1,0:T(8,128)(2,1)} custom-call(bf16[2,512,128]{2,1,0:T(8,128)(2,1)} %pad_maximum_fusion.6.in_refs_0_, bf16[2,512,128]{2,1,0:T(8,128)(2,1)} %copy-done.2, bf16[2,512,128]{2,1,0:T(8,128)(2,1)} %copy-done.3, bf16[2,512,128]{2,1,0:T(8,128)(2,1)} %copy-done.4), custom_call_target="tpu_custom_call" | custom-call | bytes 2097152 | tf_op jit(solution)/shard_map/pallas_call | solution.py:227
  37.9 0.7 collective-permute-start.12
  38.6 3.8 %collective-permute-start.11 = (bf16[128,4096]{1,0:T(8,128)(2,1)}, bf16[128,4096]{1,0:T(8,128)(2,1)S(1)}, u32[]{:S(2)}, u32[]{:S(2)}) collective-permute-start(bf16[128,4096]{1,0:T(8,128)(2,1)} %shard_map.110.own_refs_0_), channel_id=1, source_target_pairs={{0,96},{8,104},{16,112},{24,120},{32,0},{40,8},{48,16},{56,24},{64... | collective-permute-start | bytes 3145736 | tf_op jit(solution)/shard_map/ppermute | solution.py:36
  42.3 0.7 convert_reduce_fusion
  43.2 0.6 pad_add_fusion.1.info_ref
  43.8 22.1 %shard_map.109 = (bf16[512,512]{1,0:T(8,128)(2,1)}, bf16[4,512,128]{2,1,0:T(8,128)(2,1)}, bf16[8,512,128]{2,1,0:T(8,128)(2,1)}, bf16[8,512,128]{2,1,0:T(8,128)(2,1)}) custom-call(s32[17]{0:T(128)} %pad_add_fusion.1.info_ref, bf16[512,512]{1,0:T(8,128)(2,1)} %q_ref.1, bf16[512,512]{1,0:T(8,128)(2,1)} %g_ref.1, ...), custom_call_target="tpu_custom_call" | custom-call | flops 10737418240 | bytes 8388608 | tf_op jit(solution)/shard_map/pallas_call | solution.py:187
  65.9 2.5 %collective-permute-done.10.own_refs_3_ = bf16[128,4096]{1,0:T(8,128)(2,1)} collective-permute-done((bf16[128,4096]{1,0:T(8,128)(2,1)}, bf16[128,4096]{1,0:T(8,128)(2,1)}, u32[]{:S(2)}, u32[]{:S(2)}) %collective-permute-start.10) | collective-permute-done | bytes 1048608 | tf_op jit(solution)/shard_map/ppermute | solution.py:36
  68.3 1.1 collective-permute-start.13
  69.5 2.5 %collective-permute-done.13 = bf16[8,512,128]{2,1,0:T(8,128)(2,1)S(1)} collective-permute-done((bf16[8,512,128]{2,1,0:T(8,128)(2,1)}, bf16[8,512,128]{2,1,0:T(8,128)(2,1)S(1)}, u32[]{:S(2)}, u32[]{:S(2)}) %collective-permute-start.13) | collective-permute-done | bytes 1048608 | tf_op jit(solution)/shard_map/ppermute | solution.py:40
  71.9 1.5 collective-permute-done.14.other_refs_3_
  73.4 1.5 add_convert_fusion
  75.1 2.2 %collective-permute-start.16 = (bf16[6,512,128]{2,1,0:T(8,128)(2,1)S(1)}, bf16[6,512,128]{2,1,0:T(8,128)(2,1)S(1)}, u32[]{:S(2)}, u32[]{:S(2)}) collective-permute-start(bf16[6,512,128]{2,1,0:T(8,128)(2,1)S(1)} %get-tuple-element.85), channel_id=1, source_target_pairs={{0,6},{1,7},{2,0},{3,1},{4,2},{5,3},{6,4},{7,5},{8,14},{9,15},{10,... | collective-permute-start | bytes 2359304 | tf_op jit(solution)/shard_map/ppermute | solution.py:28
  77.4 2.4 %collective-permute-start.18 = (bf16[4,512,128]{2,1,0:T(8,128)(2,1)S(1)}, bf16[4,512,128]{2,1,0:T(8,128)(2,1)S(1)}, u32[]{:S(2)}, u32[]{:S(2)}) collective-permute-start(bf16[4,512,128]{2,1,0:T(8,128)(2,1)S(1)} %copy-done.1), channel_id=1, source_target_pairs={{0,1},{1,0},{2,3},{3,2},{4,5},{5,4},{6,7},{7,6},{8,9},{9,8},{10,11... | collective-permute-start | bytes 1572872 | tf_op jit(solution)/shard_map/ppermute | solution.py:32
  79.8 1.3 collective-permute-start.17
  81.0 10.7 %collective-permute-done.18.grad_refs_3_ = bf16[4,512,128]{2,1,0:T(8,128)(2,1)S(1)} collective-permute-done((bf16[4,512,128]{2,1,0:T(8,128)(2,1)S(1)}, bf16[4,512,128]{2,1,0:T(8,128)(2,1)S(1)}, u32[]{:S(2)}, u32[]{:S(2)}) %collective-permute-start.18) | collective-permute-done | bytes 524320 | tf_op jit(solution)/shard_map/ppermute | solution.py:32
  91.7 1.5 collective-permute-start.22
  93.2 2.0 %collective-permute-done.19.own_refs_2_ = bf16[128,4096]{1,0:T(8,128)(2,1)S(1)} collective-permute-done((bf16[128,4096]{1,0:T(8,128)(2,1)S(1)}, bf16[128,4096]{1,0:T(8,128)(2,1)S(1)}, u32[]{:S(2)}, u32[]{:S(2)}) %collective-permute-start.19) | collective-permute-done | bytes 1048608 | tf_op jit(solution)/shard_map/ppermute | solution.py:36
  95.2 6.4 %collective-permute-done.17 = bf16[2,512,128]{2,1,0:T(8,128)(2,1)S(1)} collective-permute-done((bf16[2,512,128]{2,1,0:T(8,128)(2,1)S(1)}, bf16[2,512,128]{2,1,0:T(8,128)(2,1)S(1)}, u32[]{:S(2)}, u32[]{:S(2)}) %collective-permute-start.17) | collective-permute-done | bytes 262176 | tf_op jit(solution)/shard_map/ppermute | solution.py:28
  101.6 1.0 collective-permute-done.15.grad_refs_1_
  102.6 1.5 collective-permute-start.21
  104.4 2.5 %collective-permute-start.20 = (bf16[2,512,128]{2,1,0:T(8,128)(2,1)S(1)}, bf16[2,512,128]{2,1,0:T(8,128)(2,1)S(1)}, u32[]{:S(2)}, u32[]{:S(2)}) collective-permute-start(bf16[2,512,128]{2,1,0:T(8,128)(2,1)S(1)} %fusion.2), channel_id=1, source_target_pairs={{0,1},{1,0},{2,3},{3,2},{4,5},{5,4},{6,7},{7,6},{8,9},{9,8},{10,11... | collective-permute-start | bytes 786440 | tf_op jit(solution)/shard_map/ppermute | solution.py:32
  107.5 6.5 %collective-permute-done.20 = bf16[2,512,128]{2,1,0:T(8,128)(2,1)S(1)} collective-permute-done((bf16[2,512,128]{2,1,0:T(8,128)(2,1)S(1)}, bf16[2,512,128]{2,1,0:T(8,128)(2,1)S(1)}, u32[]{:S(2)}, u32[]{:S(2)}) %collective-permute-start.20) | collective-permute-done | bytes 262176 | tf_op jit(solution)/shard_map/ppermute | solution.py:32
  113.9 2.4 %collective-permute-start.24 = (bf16[8,512,128]{2,1,0:T(8,128)(2,1)S(1)}, bf16[8,512,128]{2,1,0:T(8,128)(2,1)S(1)}, u32[]{:S(2)}, u32[]{:S(2)}) collective-permute-start(bf16[8,512,128]{2,1,0:T(8,128)(2,1)S(1)} %pad_maximum_fusion), channel_id=1, source_target_pairs={{0,1},{1,0},{2,3},{3,2},{4,5},{5,4},{6,7},{7,6},{8,9},{9,8},{10,11... | collective-permute-start | bytes 3145736 | tf_op jit(solution)/shard_map/ppermute | solution.py:32
  117.1 1.1 collective-permute-start.25
  118.2 4.5 %shard_map.111.rest_0_ = f32[1024,512]{1,0:T(8,128)S(1)} custom-call(s32[2]{0:T(128)S(1)} %pad_add_fusion.place_ref, bf16[128,4096]{1,0:T(8,128)(2,1)S(1)} %copy-done, bf16[128,4096]{1,0:T(8,128)(2,1)S(1)} %collective-permute-done.11.own_refs_1_, bf16[128,4096]{1,0:T(8,128)(2,1)S(1)} %collective-permute-done.19.own_refs_2_, ...), custom_call_target="tpu_custom_call" | custom-call | flops 2147483648 | bytes 10485760 | tf_op jit(solution)/shard_map/pallas_call | solution.py:382
  122.7 10.3 %collective-permute-done.23.grad_refs_0_.grad_refs_2_ = bf16[8,512,128]{2,1,0:T(8,128)(2,1)S(1)} collective-permute-done((bf16[8,512,128]{2,1,0:T(8,128)(2,1)S(1)}, bf16[8,512,128]{2,1,0:T(8,128)(2,1)S(1)}, u32[]{:S(2)}, u32[]{:S(2)}) %collective-permute-start.23) | collective-permute-done | bytes 1048608 | tf_op jit(solution)/shard_map/ppermute | solution.py:28
  133.1 3.2 %collective-permute-done.27.rest_1__3_ = bf16[2,512,128]{2,1,0:T(8,128)(2,1)S(1)} collective-permute-done((bf16[2,512,128]{2,1,0:T(8,128)(2,1)S(1)}, bf16[2,512,128]{2,1,0:T(8,128)(2,1)S(1)}, u32[]{:S(2)}, u32[]{:S(2)}) %collective-permute-start.27) | collective-permute-done | bytes 262176 | tf_op jit(solution)/shard_map/ppermute | solution.py:28
  136.3 2.4 %collective-permute-done.26.rest_1__2_ = bf16[2,512,128]{2,1,0:T(8,128)(2,1)S(1)} collective-permute-done((bf16[2,512,128]{2,1,0:T(8,128)(2,1)S(1)}, bf16[2,512,128]{2,1,0:T(8,128)(2,1)S(1)}, u32[]{:S(2)}, u32[]{:S(2)}) %collective-permute-start.26) | collective-permute-done | bytes 262176 | tf_op jit(solution)/shard_map/ppermute | solution.py:28
  138.7 6.2 %collective-permute-done.25.rest_1__1_ = bf16[2,512,128]{2,1,0:T(8,128)(2,1)S(1)} collective-permute-done((bf16[2,512,128]{2,1,0:T(8,128)(2,1)S(1)}, bf16[2,512,128]{2,1,0:T(8,128)(2,1)S(1)}, u32[]{:S(2)}, u32[]{:S(2)}) %collective-permute-start.25) | collective-permute-done | bytes 262176 | tf_op jit(solution)/shard_map/ppermute | solution.py:28
  144.9 10.9 %shard_map.112 = (f32[1024,512]{1,0:T(8,128)}, f32[64,1024]{1,0:T(8,128)}, f32[64,1024]{1,0:T(8,128)}, bf16[64,512]{1,0:T(8,128)(2,1)}, bf16[64,512]{1,0:T(8,128)(2,1)}) custom-call(s32[2]{0:T(128)S(1)} %pad_add_fusion.place_ref, bf16[128,4096]{1,0:T(8,128)(2,1)S(1)} %copy-done, bf16[128,4096]{1,0:T(8,128)(2,1)S(1)} %collective-permute-done.11.own_refs_1_, ...), custom_call_target="tpu_custom_call" | custom-call | flops 2147483648 | bytes 10485760 | tf_op jit(solution)/shard_map/pallas_call | solution.py:382
  (52 shorter events, 2.7 us)
Async XLA Ops:
  2.3 15.9 %collective-permute-start.4 = (bf16[4,512,128]{2,1,0:T(8,128)(2,1)S(1)}, bf16[4,512,128]{2,1,0:T(8,128)(2,1)S(1)}, u32[]{:S(2)}, u32[]{:S(2)}) collective-permute-start(bf16[4,512,128]{2,1,0:T(8,128)(2,1)S(1)} %pad_maximum_fusion.5), channel_id=1, source_target_pairs={{0,1},{1,0},{2,3},{3,2},{4,5},{5,4},{6,7},{7,6},{8,9},{9,8},{10,11... | collective-permute-start | bytes 1572872 | tf_op jit(solution)/shard_map/ppermute | solution.py:32
  7.8 5.7 %collective-permute-start.1 = (bf16[528,128]{1,0:T(8,128)(2,1)S(1)}, bf16[528,128]{1,0:T(8,128)(2,1)S(1)}, u32[]{:S(2)}, u32[]{:S(2)}) collective-permute-start(bf16[528,128]{1,0:T(8,128)(2,1)S(1)} %get-tuple-element.92), channel_id=1, source_target_pairs={{0,4},{1,5},{2,6},{3,7},{4,0},{5,1},{6,2},{7,3},{8,12},{9,13},{10,... | collective-permute-start | bytes 405512 | tf_op jit(solution)/shard_map/ppermute | solution.py:28
  10.8 6.4 %collective-permute-start = (bf16[528,128]{1,0:T(8,128)(2,1)S(1)}, bf16[528,128]{1,0:T(8,128)(2,1)S(1)}, u32[]{:S(2)}, u32[]{:S(2)}) collective-permute-start(bf16[528,128]{1,0:T(8,128)(2,1)S(1)} %get-tuple-element.92), channel_id=1, source_target_pairs={{0,2},{1,3},{2,4},{3,5},{4,6},{5,7},{6,0},{7,1},{8,10},{9,11},{10,... | collective-permute-start | bytes 405512 | tf_op jit(solution)/shard_map/ppermute | solution.py:28
  11.2 6.0 %collective-permute-start.2 = (bf16[528,128]{1,0:T(8,128)(2,1)S(1)}, bf16[528,128]{1,0:T(8,128)(2,1)S(1)}, u32[]{:S(2)}, u32[]{:S(2)}) collective-permute-start(bf16[528,128]{1,0:T(8,128)(2,1)S(1)} %get-tuple-element.92), channel_id=1, source_target_pairs={{0,6},{1,7},{2,0},{3,1},{4,2},{5,3},{6,4},{7,5},{8,14},{9,15},{10,... | collective-permute-start | bytes 405512 | tf_op jit(solution)/shard_map/ppermute | solution.py:28
  18.1 14.1 %collective-permute-start.3 = (bf16[4,528,128]{2,1,0:T(8,128)(2,1)}, bf16[4,528,128]{2,1,0:T(8,128)(2,1)}, u32[]{:S(2)}, u32[]{:S(2)}) collective-permute-start(bf16[4,528,128]{2,1,0:T(8,128)(2,1)} %pad_maximum_fusion.4.mine_refs_0_), channel_id=1, source_target_pairs={{0,1},{1,0},{2,3},{3,2},{4,5},{5,4},{6,7},{7,6},{8,9},{9,8},{10,11... | collective-permute-start | bytes 1622024 | tf_op jit(solution)/shard_map/ppermute | solution.py:32
  18.3 13.9 %collective-permute-start.5 = (bf16[2,512,128]{2,1,0:T(8,128)(2,1)S(1)}, bf16[2,512,128]{2,1,0:T(8,128)(2,1)S(1)}, u32[]{:S(2)}, u32[]{:S(2)}) collective-permute-start(bf16[2,512,128]{2,1,0:T(8,128)(2,1)S(1)} %pad_maximum_fusion.7), channel_id=1, source_target_pairs={{0,2},{1,3},{2,4},{3,5},{4,6},{5,7},{6,0},{7,1},{8,10},{9,11},{10,... | collective-permute-start | bytes 786440 | tf_op jit(solution)/shard_map/ppermute | solution.py:28
  20.3 12.4 %collective-permute-start.6 = (bf16[2,512,128]{2,1,0:T(8,128)(2,1)S(1)}, bf16[2,512,128]{2,1,0:T(8,128)(2,1)S(1)}, u32[]{:S(2)}, u32[]{:S(2)}) collective-permute-start(bf16[2,512,128]{2,1,0:T(8,128)(2,1)S(1)} %pad_maximum_fusion.8), channel_id=1, source_target_pairs={{0,4},{1,5},{2,6},{3,7},{4,0},{5,1},{6,2},{7,3},{8,12},{9,13},{10,... | collective-permute-start | bytes 786440 | tf_op jit(solution)/shard_map/ppermute | solution.py:28
  22.6 10.6 %collective-permute-start.7 = (bf16[2,512,128]{2,1,0:T(8,128)(2,1)S(1)}, bf16[2,512,128]{2,1,0:T(8,128)(2,1)S(1)}, u32[]{:S(2)}, u32[]{:S(2)}) collective-permute-start(bf16[2,512,128]{2,1,0:T(8,128)(2,1)S(1)} %pad_maximum_fusion.9), channel_id=1, source_target_pairs={{0,6},{1,7},{2,0},{3,1},{4,2},{5,3},{6,4},{7,5},{8,14},{9,15},{10,... | collective-permute-start | bytes 786440 | tf_op jit(solution)/shard_map/ppermute | solution.py:28
  23.0 20.8 %collective-permute-start.8 = (bf16[4,528,128]{2,1,0:T(8,128)(2,1)}, bf16[4,528,128]{2,1,0:T(8,128)(2,1)}, u32[]{:S(2)}, u32[]{:S(2)}) collective-permute-start(bf16[4,528,128]{2,1,0:T(8,128)(2,1)} %pad_maximum_fusion.4.mine_refs_0_), channel_id=1, source_target_pairs={{0,8},{8,0},{16,24},{24,16},{32,40},{40,32},{48,56},{56,48},{64,72... | collective-permute-start | bytes 1622024 | tf_op jit(solution)/shard_map/ppermute | solution.py:40
  32.2 3.2 %copy-start.2 = (bf16[2,512,128]{2,1,0:T(8,128)(2,1)}, bf16[2,512,128]{2,1,0:T(8,128)(2,1)S(1)}, u32[]{:S(2)}) copy-start(bf16[2,512,128]{2,1,0:T(8,128)(2,1)S(1)} %collective-permute-done.5.in_refs_1_) | copy-start | bytes 786436
  32.7 2.7 %copy-start.3 = (bf16[2,512,128]{2,1,0:T(8,128)(2,1)}, bf16[2,512,128]{2,1,0:T(8,128)(2,1)S(1)}, u32[]{:S(2)}) copy-start(bf16[2,512,128]{2,1,0:T(8,128)(2,1)S(1)} %collective-permute-done.6.in_refs_2_) | copy-start | bytes 786436
  33.2 2.2 %copy-start.4 = (bf16[2,512,128]{2,1,0:T(8,128)(2,1)}, bf16[2,512,128]{2,1,0:T(8,128)(2,1)S(1)}, u32[]{:S(2)}) copy-start(bf16[2,512,128]{2,1,0:T(8,128)(2,1)S(1)} %collective-permute-done.7.in_refs_3_) | copy-start | bytes 786436
  33.2 10.6 %collective-permute-start.9 = (bf16[4,528,128]{2,1,0:T(8,128)(2,1)}, bf16[4,528,128]{2,1,0:T(8,128)(2,1)}, u32[]{:S(2)}, u32[]{:S(2)}) collective-permute-start(bf16[4,528,128]{2,1,0:T(8,128)(2,1)} %collective-permute-done.3.mine_refs_1_), channel_id=1, source_target_pairs={{0,8},{8,0},{16,24},{24,16},{32,40},{40,32},{48,56},{56,48},{64,72... | collective-permute-start | bytes 1622024 | tf_op jit(solution)/shard_map/ppermute | solution.py:40
  37.9 28.0 %collective-permute-start.12 = (bf16[128,4096]{1,0:T(8,128)(2,1)}, bf16[128,4096]{1,0:T(8,128)(2,1)S(1)}, u32[]{:S(2)}, u32[]{:S(2)}) collective-permute-start(bf16[128,4096]{1,0:T(8,128)(2,1)} %shard_map.110.own_refs_0_), channel_id=1, source_target_pairs={{0,8},{8,0},{16,24},{24,16},{32,40},{40,32},{48,56},{56,48},{64,72... | collective-permute-start | bytes 3145736 | tf_op jit(solution)/shard_map/ppermute | solution.py:40
  38.6 27.3 %collective-permute-start.11 = (bf16[128,4096]{1,0:T(8,128)(2,1)}, bf16[128,4096]{1,0:T(8,128)(2,1)S(1)}, u32[]{:S(2)}, u32[]{:S(2)}) collective-permute-start(bf16[128,4096]{1,0:T(8,128)(2,1)} %shard_map.110.own_refs_0_), channel_id=1, source_target_pairs={{0,96},{8,104},{16,112},{24,120},{32,0},{40,8},{48,16},{56,24},{64... | collective-permute-start | bytes 3145736 | tf_op jit(solution)/shard_map/ppermute | solution.py:36
  42.3 26.0 %collective-permute-start.10 = (bf16[128,4096]{1,0:T(8,128)(2,1)}, bf16[128,4096]{1,0:T(8,128)(2,1)}, u32[]{:S(2)}, u32[]{:S(2)}) collective-permute-start(bf16[128,4096]{1,0:T(8,128)(2,1)} %shard_map.110.own_refs_0_), channel_id=1, source_target_pairs={{0,32},{8,40},{16,48},{24,56},{32,64},{40,72},{48,80},{56,88},{64,... | collective-permute-start | bytes 3145736 | tf_op jit(solution)/shard_map/ppermute | solution.py:36
  43.8 25.7 %copy-start = (bf16[128,4096]{1,0:T(8,128)(2,1)S(1)}, bf16[128,4096]{1,0:T(8,128)(2,1)}, u32[]{:S(2)}) copy-start(bf16[128,4096]{1,0:T(8,128)(2,1)} %shard_map.110.own_refs_0_) | copy-start | bytes 3145732
  68.3 6.7 %copy-start.1 = (bf16[4,512,128]{2,1,0:T(8,128)(2,1)S(1)}, bf16[4,512,128]{2,1,0:T(8,128)(2,1)}, u32[]{:S(2)}) copy-start(bf16[4,512,128]{2,1,0:T(8,128)(2,1)} %get-tuple-element.53.grad_refs_0_) | copy-start | bytes 1572868
  68.3 3.6 %collective-permute-start.13 = (bf16[8,512,128]{2,1,0:T(8,128)(2,1)}, bf16[8,512,128]{2,1,0:T(8,128)(2,1)S(1)}, u32[]{:S(2)}, u32[]{:S(2)}) collective-permute-start(bf16[8,512,128]{2,1,0:T(8,128)(2,1)} %get-tuple-element.55), channel_id=1, source_target_pairs={{0,8},{8,0},{16,24},{24,16},{32,40},{40,32},{48,56},{56,48},{64,72... | collective-permute-start | bytes 3145736 | tf_op jit(solution)/shard_map/ppermute | solution.py:40
  69.5 4.0 %collective-permute-start.14 = (bf16[128,4096]{1,0:T(8,128)(2,1)}, bf16[128,4096]{1,0:T(8,128)(2,1)S(1)}, u32[]{:S(2)}, u32[]{:S(2)}) collective-permute-start(bf16[128,4096]{1,0:T(8,128)(2,1)} %collective-permute-done.10.own_refs_3_), channel_id=1, source_target_pairs={{0,8},{8,0},{16,24},{24,16},{32,40},{40,32},{48,56},{56,48},{64,72... | collective-permute-start | bytes 3145736 | tf_op jit(solution)/shard_map/ppermute | solution.py:40
  69.5 25.7 %collective-permute-start.19 = (bf16[128,4096]{1,0:T(8,128)(2,1)S(1)}, bf16[128,4096]{1,0:T(8,128)(2,1)S(1)}, u32[]{:S(2)}, u32[]{:S(2)}) collective-permute-start(bf16[128,4096]{1,0:T(8,128)(2,1)S(1)} %copy-done), channel_id=1, source_target_pairs={{0,64},{8,72},{16,80},{24,88},{32,96},{40,104},{48,112},{56,120},{... | collective-permute-start | bytes 3145736 | tf_op jit(solution)/shard_map/ppermute | solution.py:36
  75.1 26.5 %collective-permute-start.16 = (bf16[6,512,128]{2,1,0:T(8,128)(2,1)S(1)}, bf16[6,512,128]{2,1,0:T(8,128)(2,1)S(1)}, u32[]{:S(2)}, u32[]{:S(2)}) collective-permute-start(bf16[6,512,128]{2,1,0:T(8,128)(2,1)S(1)} %get-tuple-element.85), channel_id=1, source_target_pairs={{0,6},{1,7},{2,0},{3,1},{4,2},{5,3},{6,4},{7,5},{8,14},{9,15},{10,... | collective-permute-start | bytes 2359304 | tf_op jit(solution)/shard_map/ppermute | solution.py:28
  77.4 25.3 %collective-permute-start.15 = (bf16[6,512,128]{2,1,0:T(8,128)(2,1)S(1)}, bf16[6,512,128]{2,1,0:T(8,128)(2,1)S(1)}, u32[]{:S(2)}, u32[]{:S(2)}) collective-permute-start(bf16[6,512,128]{2,1,0:T(8,128)(2,1)S(1)} %get-tuple-element.86), channel_id=1, source_target_pairs={{0,2},{1,3},{2,4},{3,5},{4,6},{5,7},{6,0},{7,1},{8,10},{9,11},{10,... | collective-permute-start | bytes 2359304 | tf_op jit(solution)/shard_map/ppermute | solution.py:28
  77.4 14.3 %collective-permute-start.18 = (bf16[4,512,128]{2,1,0:T(8,128)(2,1)S(1)}, bf16[4,512,128]{2,1,0:T(8,128)(2,1)S(1)}, u32[]{:S(2)}, u32[]{:S(2)}) collective-permute-start(bf16[4,512,128]{2,1,0:T(8,128)(2,1)S(1)} %copy-done.1), channel_id=1, source_target_pairs={{0,1},{1,0},{2,3},{3,2},{4,5},{5,4},{6,7},{7,6},{8,9},{9,8},{10,11... | collective-permute-start | bytes 1572872 | tf_op jit(solution)/shard_map/ppermute | solution.py:32
  79.8 21.8 %collective-permute-start.17 = (bf16[2,512,128]{2,1,0:T(8,128)(2,1)S(1)}, bf16[2,512,128]{2,1,0:T(8,128)(2,1)S(1)}, u32[]{:S(2)}, u32[]{:S(2)}) collective-permute-start(bf16[2,512,128]{2,1,0:T(8,128)(2,1)S(1)} %get-tuple-element.82), channel_id=1, source_target_pairs={{0,4},{1,5},{2,6},{3,7},{4,0},{5,1},{6,2},{7,3},{8,12},{9,13},{10,... | collective-permute-start | bytes 786440 | tf_op jit(solution)/shard_map/ppermute | solution.py:28
  91.7 15.8 %collective-permute-start.22 = (bf16[128,4096]{1,0:T(8,128)(2,1)S(1)}, bf16[128,4096]{1,0:T(8,128)(2,1)S(1)}, u32[]{:S(2)}, u32[]{:S(2)}) collective-permute-start(bf16[128,4096]{1,0:T(8,128)(2,1)S(1)} %collective-permute-done.11.own_refs_1_), channel_id=1, source_target_pairs={{0,8},{8,0},{16,24},{24,16},{32,40},{40,32},{48,56},{56,48},{64,72... | collective-permute-start | bytes 3145736 | tf_op jit(solution)/shard_map/ppermute | solution.py:40
  102.6 11.3 %collective-permute-start.21 = (bf16[128,4096]{1,0:T(8,128)(2,1)S(1)}, bf16[128,4096]{1,0:T(8,128)(2,1)S(1)}, u32[]{:S(2)}, u32[]{:S(2)}) collective-permute-start(bf16[128,4096]{1,0:T(8,128)(2,1)S(1)} %collective-permute-done.19.own_refs_2_), channel_id=1, source_target_pairs={{0,8},{8,0},{16,24},{24,16},{32,40},{40,32},{48,56},{56,48},{64,72... | collective-permute-start | bytes 3145736 | tf_op jit(solution)/shard_map/ppermute | solution.py:40
  104.4 9.5 %collective-permute-start.20 = (bf16[2,512,128]{2,1,0:T(8,128)(2,1)S(1)}, bf16[2,512,128]{2,1,0:T(8,128)(2,1)S(1)}, u32[]{:S(2)}, u32[]{:S(2)}) collective-permute-start(bf16[2,512,128]{2,1,0:T(8,128)(2,1)S(1)} %fusion.2), channel_id=1, source_target_pairs={{0,1},{1,0},{2,3},{3,2},{4,5},{5,4},{6,7},{7,6},{8,9},{9,8},{10,11... | collective-permute-start | bytes 786440 | tf_op jit(solution)/shard_map/ppermute | solution.py:32
  107.0 26.1 %collective-permute-start.23 = (bf16[8,512,128]{2,1,0:T(8,128)(2,1)S(1)}, bf16[8,512,128]{2,1,0:T(8,128)(2,1)S(1)}, u32[]{:S(2)}, u32[]{:S(2)}) collective-permute-start(bf16[8,512,128]{2,1,0:T(8,128)(2,1)S(1)} %pad_maximum_fusion.1), channel_id=1, source_target_pairs={{0,4},{1,5},{2,6},{3,7},{4,0},{5,1},{6,2},{7,3},{8,12},{9,13},{10,... | collective-permute-start | bytes 3145736 | tf_op jit(solution)/shard_map/ppermute | solution.py:28
  113.9 31.0 %collective-permute-start.24 = (bf16[8,512,128]{2,1,0:T(8,128)(2,1)S(1)}, bf16[8,512,128]{2,1,0:T(8,128)(2,1)S(1)}, u32[]{:S(2)}, u32[]{:S(2)}) collective-permute-start(bf16[8,512,128]{2,1,0:T(8,128)(2,1)S(1)} %pad_maximum_fusion), channel_id=1, source_target_pairs={{0,1},{1,0},{2,3},{3,2},{4,5},{5,4},{6,7},{7,6},{8,9},{9,8},{10,11... | collective-permute-start | bytes 3145736 | tf_op jit(solution)/shard_map/ppermute | solution.py:32
  116.4 19.9 %collective-permute-start.27 = (bf16[2,512,128]{2,1,0:T(8,128)(2,1)S(1)}, bf16[2,512,128]{2,1,0:T(8,128)(2,1)S(1)}, u32[]{:S(2)}, u32[]{:S(2)}) collective-permute-start(bf16[2,512,128]{2,1,0:T(8,128)(2,1)S(1)} %add_convert_fusion.1.rest_1__0_), channel_id=1, source_target_pairs={{0,6},{1,7},{2,0},{3,1},{4,2},{5,3},{6,4},{7,5},{8,14},{9,15},{10,... | collective-permute-start | bytes 786440 | tf_op jit(solution)/shard_map/ppermute | solution.py:28
  116.7 21.9 %collective-permute-start.26 = (bf16[2,512,128]{2,1,0:T(8,128)(2,1)S(1)}, bf16[2,512,128]{2,1,0:T(8,128)(2,1)S(1)}, u32[]{:S(2)}, u32[]{:S(2)}) collective-permute-start(bf16[2,512,128]{2,1,0:T(8,128)(2,1)S(1)} %add_convert_fusion.1.rest_1__0_), channel_id=1, source_target_pairs={{0,4},{1,5},{2,6},{3,7},{4,0},{5,1},{6,2},{7,3},{8,12},{9,13},{10,... | collective-permute-start | bytes 786440 | tf_op jit(solution)/shard_map/ppermute | solution.py:28
  117.1 27.8 %collective-permute-start.25 = (bf16[2,512,128]{2,1,0:T(8,128)(2,1)S(1)}, bf16[2,512,128]{2,1,0:T(8,128)(2,1)S(1)}, u32[]{:S(2)}, u32[]{:S(2)}) collective-permute-start(bf16[2,512,128]{2,1,0:T(8,128)(2,1)S(1)} %add_convert_fusion.1.rest_1__0_), channel_id=1, source_target_pairs={{0,2},{1,3},{2,4},{3,5},{4,6},{5,7},{6,0},{7,1},{8,10},{9,11},{10,... | collective-permute-start | bytes 786440 | tf_op jit(solution)/shard_map/ppermute | solution.py:28

commit v13 on v12

--- a/solution.py
+++ b/solution.py
@@ -15,7 +15,7 @@
 LOW = -1e30
 LOG2E = 1.4426950408889634
 VMEM_BYTES = 60 * 1024 * 1024
-WEIGHT_VMEM_BYTES = 20 * 1024 * 1024
+WEIGHT_VMEM_BYTES = 16 * 1024 * 1024
 
 
 def contract(left, right, left_dim, right_dim):

time: 156 us -> 156 us (level)
  transfers between devices with their start and end apart: 28 -> 28, of which waited for: 17 -> 17; matrix products, arithmetic and copies ran while one was open for 5% -> 5% of each run, Pallas kernels for 19% -> 20%
where the time goes in v13:
time: 156 us
  waiting for transfers between devices  63.7 us (41%)
  Pallas kernels  41.5 us (27%)
  starting transfers between devices  40.1 us (26%)
  other arithmetic  6.96 us (4%)
  local copies, waits for them, and re-layouts  2.52 us (2%)
    ppermute x13, waiting for transfers between devices, along_y(): lax.ppermute(value, 'ctx', [(i, (i + 2 * step) % 8) for i in range(8)])  34.3 us
    pallas_call x1, Pallas kernels, attention(): pl.pallas_call(functools.partial(attention_kernel, heads), out_shape=(jax...  23.6 us
    ppermute x5, waiting for transfers between devices, swap_x(): return lax.ppermute(value, 'ctx', [(i, i ^ 1) for i in range(8)])  22.5 us
    ppermute x13, starting transfers between devices, along_y(): lax.ppermute(value, 'ctx', [(i, (i + 2 * step) % 8) for i in range(8)])  15.9 us
    pallas_call x2, Pallas kernels, weights(): pl.pallas_call(functools.partial(weight_kernel, last, tuple((start for _,...  15.4 us
    ppermute x5, starting transfers between devices, swap_x(): return lax.ppermute(value, 'ctx', [(i, i ^ 1) for i in range(8)])  11.1 us
    ppermute x7, starting transfers between devices, swap_cores(): return lax.ppermute(value, 'dp', [(i, i ^ 1) for i in range(16)])  9.43 us
    ppermute x7, waiting for transfers between devices, swap_cores(): return lax.ppermute(value, 'dp', [(i, i ^ 1) for i in range(16)])  4 us
  transfers between devices with their start and end apart: 28, of which 17 were waited for; matrix products, arithmetic and copies ran while one was open for 5% of the time, Pallas kernels for 20%

profile of v13, /device:TPU:1, one launch (start us, length us, event | category | flops | bytes accessed | tf_op | source)
XLA Modules:
  0.0 156.0 jit_solution(6043875687082645854)
XLA Ops:
  0.8 1.4 dynamic-slice_bitcast_fusion
  2.3 3.7 %collective-permute-start.4 = (bf16[4,512,128]{2,1,0:T(8,128)(2,1)S(1)}, bf16[4,512,128]{2,1,0:T(8,128)(2,1)S(1)}, u32[]{:S(2)}, u32[]{:S(2)}) collective-permute-start(bf16[4,512,128]{2,1,0:T(8,128)(2,1)S(1)} %pad_maximum_fusion.5), channel_id=1, source_target_pairs={{0,1},{1,0},{2,3},{3,2},{4,5},{5,4},{6,7},{7,6},{8,9},{9,8},{10,11... | collective-permute-start | bytes 1572872 | tf_op jit(solution)/shard_map/ppermute | solution.py:32
  5.9 0.8 slice.48
  6.8 1.0 dynamic-slice_select_fusion
  7.8 3.0 %collective-permute-start.1 = (bf16[528,128]{1,0:T(8,128)(2,1)S(1)}, bf16[528,128]{1,0:T(8,128)(2,1)S(1)}, u32[]{:S(2)}, u32[]{:S(2)}) collective-permute-start(bf16[528,128]{1,0:T(8,128)(2,1)S(1)} %get-tuple-element.92), channel_id=1, source_target_pairs={{0,4},{1,5},{2,6},{3,7},{4,0},{5,1},{6,2},{7,3},{8,12},{9,13},{10,... | collective-permute-start | bytes 405512 | tf_op jit(solution)/shard_map/ppermute | solution.py:28
  10.8 0.4 collective-permute-start
  11.2 2.3 %collective-permute-start.2 = (bf16[528,128]{1,0:T(8,128)(2,1)S(1)}, bf16[528,128]{1,0:T(8,128)(2,1)S(1)}, u32[]{:S(2)}, u32[]{:S(2)}) collective-permute-start(bf16[528,128]{1,0:T(8,128)(2,1)S(1)} %get-tuple-element.92), channel_id=1, source_target_pairs={{0,6},{1,7},{2,0},{3,1},{4,2},{5,3},{6,4},{7,5},{8,14},{9,15},{10,... | collective-permute-start | bytes 405512 | tf_op jit(solution)/shard_map/ppermute | solution.py:28
  13.6 3.7 %collective-permute-done = bf16[528,128]{1,0:T(8,128)(2,1)S(1)} collective-permute-done((bf16[528,128]{1,0:T(8,128)(2,1)S(1)}, bf16[528,128]{1,0:T(8,128)(2,1)S(1)}, u32[]{:S(2)}, u32[]{:S(2)}) %collective-permute-start) | collective-permute-done | bytes 135200 | tf_op jit(solution)/shard_map/ppermute | solution.py:28
  17.2 0.9 pad_maximum_fusion.4.mine_refs_0_
  18.3 2.0 %collective-permute-start.5 = (bf16[2,512,128]{2,1,0:T(8,128)(2,1)S(1)}, bf16[2,512,128]{2,1,0:T(8,128)(2,1)S(1)}, u32[]{:S(2)}, u32[]{:S(2)}) collective-permute-start(bf16[2,512,128]{2,1,0:T(8,128)(2,1)S(1)} %pad_maximum_fusion.7), channel_id=1, source_target_pairs={{0,2},{1,3},{2,4},{3,5},{4,6},{5,7},{6,0},{7,1},{8,10},{9,11},{10,... | collective-permute-start | bytes 786440 | tf_op jit(solution)/shard_map/ppermute | solution.py:28
  20.3 2.3 %collective-permute-start.6 = (bf16[2,512,128]{2,1,0:T(8,128)(2,1)S(1)}, bf16[2,512,128]{2,1,0:T(8,128)(2,1)S(1)}, u32[]{:S(2)}, u32[]{:S(2)}) collective-permute-start(bf16[2,512,128]{2,1,0:T(8,128)(2,1)S(1)} %pad_maximum_fusion.8), channel_id=1, source_target_pairs={{0,4},{1,5},{2,6},{3,7},{4,0},{5,1},{6,2},{7,3},{8,12},{9,13},{10,... | collective-permute-start | bytes 786440 | tf_op jit(solution)/shard_map/ppermute | solution.py:28
  23.0 2.4 %collective-permute-start.8 = (bf16[4,528,128]{2,1,0:T(8,128)(2,1)}, bf16[4,528,128]{2,1,0:T(8,128)(2,1)}, u32[]{:S(2)}, u32[]{:S(2)}) collective-permute-start(bf16[4,528,128]{2,1,0:T(8,128)(2,1)} %pad_maximum_fusion.4.mine_refs_0_), channel_id=1, source_target_pairs={{0,8},{8,0},{16,24},{24,16},{32,40},{40,32},{48,56},{56,48},{64,72... | collective-permute-start | bytes 1622024 | tf_op jit(solution)/shard_map/ppermute | solution.py:40
  25.3 0.7 fusion.3
  26.1 0.7 pad_maximum_fusion.6.in_refs_0_
  26.8 5.4 %collective-permute-done.3.mine_refs_1_ = bf16[4,528,128]{2,1,0:T(8,128)(2,1)} collective-permute-done((bf16[4,528,128]{2,1,0:T(8,128)(2,1)}, bf16[4,528,128]{2,1,0:T(8,128)(2,1)}, u32[]{:S(2)}, u32[]{:S(2)}) %collective-permute-start.3) | collective-permute-done | bytes 540704 | tf_op jit(solution)/shard_map/ppermute | solution.py:32
  32.2 0.5 collective-permute-done.6.in_refs_2_
  32.7 0.5 collective-permute-done.7.in_refs_3_
  33.2 2.2 %collective-permute-start.9 = (bf16[4,528,128]{2,1,0:T(8,128)(2,1)}, bf16[4,528,128]{2,1,0:T(8,128)(2,1)}, u32[]{:S(2)}, u32[]{:S(2)}) collective-permute-start(bf16[4,528,128]{2,1,0:T(8,128)(2,1)} %collective-permute-done.3.mine_refs_1_), channel_id=1, source_target_pairs={{0,8},{8,0},{16,24},{24,16},{32,40},{40,32},{48,56},{56,48},{64,72... | collective-permute-start | bytes 1622024 | tf_op jit(solution)/shard_map/ppermute | solution.py:40
  35.4 2.5 %shard_map.110.own_refs_0_ = bf16[128,4096]{1,0:T(8,128)(2,1)} custom-call(bf16[2,512,128]{2,1,0:T(8,128)(2,1)} %pad_maximum_fusion.6.in_refs_0_, bf16[2,512,128]{2,1,0:T(8,128)(2,1)} %copy-done.2, bf16[2,512,128]{2,1,0:T(8,128)(2,1)} %copy-done.3, bf16[2,512,128]{2,1,0:T(8,128)(2,1)} %copy-done.4), custom_call_target="tpu_custom_call" | custom-call | bytes 2097152 | tf_op jit(solution)/shard_map/pallas_call | solution.py:227
  37.9 0.7 collective-permute-start.12
  38.6 3.8 %collective-permute-start.11 = (bf16[128,4096]{1,0:T(8,128)(2,1)}, bf16[128,4096]{1,0:T(8,128)(2,1)S(1)}, u32[]{:S(2)}, u32[]{:S(2)}) collective-permute-start(bf16[128,4096]{1,0:T(8,128)(2,1)} %shard_map.110.own_refs_0_), channel_id=1, source_target_pairs={{0,96},{8,104},{16,112},{24,120},{32,0},{40,8},{48,16},{56,24},{64... | collective-permute-start | bytes 3145736 | tf_op jit(solution)/shard_map/ppermute | solution.py:36
  42.3 0.7 convert_reduce_fusion
  43.2 0.6 pad_add_fusion.1.info_ref
  43.8 23.6 %shard_map.109 = (bf16[512,512]{1,0:T(8,128)(2,1)}, bf16[4,512,128]{2,1,0:T(8,128)(2,1)}, bf16[8,512,128]{2,1,0:T(8,128)(2,1)}, bf16[8,512,128]{2,1,0:T(8,128)(2,1)}) custom-call(s32[17]{0:T(128)} %pad_add_fusion.1.info_ref, bf16[512,512]{1,0:T(8,128)(2,1)} %q_ref.1, bf16[512,512]{1,0:T(8,128)(2,1)} %g_ref.1, ...), custom_call_target="tpu_custom_call" | custom-call | flops 10737418240 | bytes 8388608 | tf_op jit(solution)/shard_map/pallas_call | solution.py:187
  67.4 1.0 collective-permute-done.10.own_refs_3_
  68.3 1.1 collective-permute-start.13
  69.5 2.5 %collective-permute-done.13 = bf16[8,512,128]{2,1,0:T(8,128)(2,1)S(1)} collective-permute-done((bf16[8,512,128]{2,1,0:T(8,128)(2,1)}, bf16[8,512,128]{2,1,0:T(8,128)(2,1)S(1)}, u32[]{:S(2)}, u32[]{:S(2)}) %collective-permute-start.13) | collective-permute-done | bytes 1048608 | tf_op jit(solution)/shard_map/ppermute | solution.py:40
  71.9 1.5 collective-permute-done.14.other_refs_3_
  73.4 1.5 add_convert_fusion
  75.1 2.2 %collective-permute-start.16 = (bf16[6,512,128]{2,1,0:T(8,128)(2,1)S(1)}, bf16[6,512,128]{2,1,0:T(8,128)(2,1)S(1)}, u32[]{:S(2)}, u32[]{:S(2)}) collective-permute-start(bf16[6,512,128]{2,1,0:T(8,128)(2,1)S(1)} %get-tuple-element.85), channel_id=1, source_target_pairs={{0,6},{1,7},{2,0},{3,1},{4,2},{5,3},{6,4},{7,5},{8,14},{9,15},{10,... | collective-permute-start | bytes 2359304 | tf_op jit(solution)/shard_map/ppermute | solution.py:28
  77.4 2.4 %collective-permute-start.18 = (bf16[4,512,128]{2,1,0:T(8,128)(2,1)S(1)}, bf16[4,512,128]{2,1,0:T(8,128)(2,1)S(1)}, u32[]{:S(2)}, u32[]{:S(2)}) collective-permute-start(bf16[4,512,128]{2,1,0:T(8,128)(2,1)S(1)} %copy-done.1), channel_id=1, source_target_pairs={{0,1},{1,0},{2,3},{3,2},{4,5},{5,4},{6,7},{7,6},{8,9},{9,8},{10,11... | collective-permute-start | bytes 1572872 | tf_op jit(solution)/shard_map/ppermute | solution.py:32
  79.8 1.3 collective-permute-start.17
  81.0 10.7 %collective-permute-done.18.grad_refs_3_ = bf16[4,512,128]{2,1,0:T(8,128)(2,1)S(1)} collective-permute-done((bf16[4,512,128]{2,1,0:T(8,128)(2,1)S(1)}, bf16[4,512,128]{2,1,0:T(8,128)(2,1)S(1)}, u32[]{:S(2)}, u32[]{:S(2)}) %collective-permute-start.18) | collective-permute-done | bytes 524320 | tf_op jit(solution)/shard_map/ppermute | solution.py:32
  91.7 1.5 collective-permute-start.22
  93.2 1.9 %collective-permute-done.19.own_refs_2_ = bf16[128,4096]{1,0:T(8,128)(2,1)S(1)} collective-permute-done((bf16[128,4096]{1,0:T(8,128)(2,1)S(1)}, bf16[128,4096]{1,0:T(8,128)(2,1)S(1)}, u32[]{:S(2)}, u32[]{:S(2)}) %collective-permute-start.19) | collective-permute-done | bytes 1048608 | tf_op jit(solution)/shard_map/ppermute | solution.py:36
  95.2 6.4 %collective-permute-done.17 = bf16[2,512,128]{2,1,0:T(8,128)(2,1)S(1)} collective-permute-done((bf16[2,512,128]{2,1,0:T(8,128)(2,1)S(1)}, bf16[2,512,128]{2,1,0:T(8,128)(2,1)S(1)}, u32[]{:S(2)}, u32[]{:S(2)}) %collective-permute-start.17) | collective-permute-done | bytes 262176 | tf_op jit(solution)/shard_map/ppermute | solution.py:28
  101.6 1.0 collective-permute-done.15.grad_refs_1_
  102.6 1.5 collective-permute-start.21
  104.4 2.5 %collective-permute-start.20 = (bf16[2,512,128]{2,1,0:T(8,128)(2,1)S(1)}, bf16[2,512,128]{2,1,0:T(8,128)(2,1)S(1)}, u32[]{:S(2)}, u32[]{:S(2)}) collective-permute-start(bf16[2,512,128]{2,1,0:T(8,128)(2,1)S(1)} %fusion.2), channel_id=1, source_target_pairs={{0,1},{1,0},{2,3},{3,2},{4,5},{5,4},{6,7},{7,6},{8,9},{9,8},{10,11... | collective-permute-start | bytes 786440 | tf_op jit(solution)/shard_map/ppermute | solution.py:32
  107.5 6.5 %collective-permute-done.20 = bf16[2,512,128]{2,1,0:T(8,128)(2,1)S(1)} collective-permute-done((bf16[2,512,128]{2,1,0:T(8,128)(2,1)S(1)}, bf16[2,512,128]{2,1,0:T(8,128)(2,1)S(1)}, u32[]{:S(2)}, u32[]{:S(2)}) %collective-permute-start.20) | collective-permute-done | bytes 262176 | tf_op jit(solution)/shard_map/ppermute | solution.py:32
  113.9 2.4 %collective-permute-start.24 = (bf16[8,512,128]{2,1,0:T(8,128)(2,1)S(1)}, bf16[8,512,128]{2,1,0:T(8,128)(2,1)S(1)}, u32[]{:S(2)}, u32[]{:S(2)}) collective-permute-start(bf16[8,512,128]{2,1,0:T(8,128)(2,1)S(1)} %pad_maximum_fusion), channel_id=1, source_target_pairs={{0,1},{1,0},{2,3},{3,2},{4,5},{5,4},{6,7},{7,6},{8,9},{9,8},{10,11... | collective-permute-start | bytes 3145736 | tf_op jit(solution)/shard_map/ppermute | solution.py:32
  117.1 1.1 collective-permute-start.25
  118.2 4.5 %shard_map.111.rest_0_ = f32[1024,512]{1,0:T(8,128)S(1)} custom-call(s32[2]{0:T(128)S(1)} %pad_add_fusion.place_ref, bf16[128,4096]{1,0:T(8,128)(2,1)S(1)} %copy-done, bf16[128,4096]{1,0:T(8,128)(2,1)S(1)} %collective-permute-done.11.own_refs_1_, bf16[128,4096]{1,0:T(8,128)(2,1)S(1)} %collective-permute-done.19.own_refs_2_, ...), custom_call_target="tpu_custom_call" | custom-call | flops 2147483648 | bytes 10485760 | tf_op jit(solution)/shard_map/pallas_call | solution.py:382
  122.7 10.3 %collective-permute-done.23.grad_refs_0_.grad_refs_2_ = bf16[8,512,128]{2,1,0:T(8,128)(2,1)S(1)} collective-permute-done((bf16[8,512,128]{2,1,0:T(8,128)(2,1)S(1)}, bf16[8,512,128]{2,1,0:T(8,128)(2,1)S(1)}, u32[]{:S(2)}, u32[]{:S(2)}) %collective-permute-start.23) | collective-permute-done | bytes 1048608 | tf_op jit(solution)/shard_map/ppermute | solution.py:28
  133.1 3.2 %collective-permute-done.27.rest_1__3_ = bf16[2,512,128]{2,1,0:T(8,128)(2,1)S(1)} collective-permute-done((bf16[2,512,128]{2,1,0:T(8,128)(2,1)S(1)}, bf16[2,512,128]{2,1,0:T(8,128)(2,1)S(1)}, u32[]{:S(2)}, u32[]{:S(2)}) %collective-permute-start.27) | collective-permute-done | bytes 262176 | tf_op jit(solution)/shard_map/ppermute | solution.py:28
  136.3 2.4 %collective-permute-done.26.rest_1__2_ = bf16[2,512,128]{2,1,0:T(8,128)(2,1)S(1)} collective-permute-done((bf16[2,512,128]{2,1,0:T(8,128)(2,1)S(1)}, bf16[2,512,128]{2,1,0:T(8,128)(2,1)S(1)}, u32[]{:S(2)}, u32[]{:S(2)}) %collective-permute-start.26) | collective-permute-done | bytes 262176 | tf_op jit(solution)/shard_map/ppermute | solution.py:28
  138.7 6.2 %collective-permute-done.25.rest_1__1_ = bf16[2,512,128]{2,1,0:T(8,128)(2,1)S(1)} collective-permute-done((bf16[2,512,128]{2,1,0:T(8,128)(2,1)S(1)}, bf16[2,512,128]{2,1,0:T(8,128)(2,1)S(1)}, u32[]{:S(2)}, u32[]{:S(2)}) %collective-permute-start.25) | collective-permute-done | bytes 262176 | tf_op jit(solution)/shard_map/ppermute | solution.py:28
  144.9 10.9 %shard_map.112 = (f32[1024,512]{1,0:T(8,128)}, f32[64,1024]{1,0:T(8,128)}, f32[64,1024]{1,0:T(8,128)}, bf16[64,512]{1,0:T(8,128)(2,1)}, bf16[64,512]{1,0:T(8,128)(2,1)}) custom-call(s32[2]{0:T(128)S(1)} %pad_add_fusion.place_ref, bf16[128,4096]{1,0:T(8,128)(2,1)S(1)} %copy-done, bf16[128,4096]{1,0:T(8,128)(2,1)S(1)} %collective-permute-done.11.own_refs_1_, ...), custom_call_target="tpu_custom_call" | custom-call | flops 2147483648 | bytes 10485760 | tf_op jit(solution)/shard_map/pallas_call | solution.py:382
  (52 shorter events, 2.7 us)
Async XLA Ops:
  2.3 15.9 %collective-permute-start.4 = (bf16[4,512,128]{2,1,0:T(8,128)(2,1)S(1)}, bf16[4,512,128]{2,1,0:T(8,128)(2,1)S(1)}, u32[]{:S(2)}, u32[]{:S(2)}) collective-permute-start(bf16[4,512,128]{2,1,0:T(8,128)(2,1)S(1)} %pad_maximum_fusion.5), channel_id=1, source_target_pairs={{0,1},{1,0},{2,3},{3,2},{4,5},{5,4},{6,7},{7,6},{8,9},{9,8},{10,11... | collective-permute-start | bytes 1572872 | tf_op jit(solution)/shard_map/ppermute | solution.py:32
  7.8 5.7 %collective-permute-start.1 = (bf16[528,128]{1,0:T(8,128)(2,1)S(1)}, bf16[528,128]{1,0:T(8,128)(2,1)S(1)}, u32[]{:S(2)}, u32[]{:S(2)}) collective-permute-start(bf16[528,128]{1,0:T(8,128)(2,1)S(1)} %get-tuple-element.92), channel_id=1, source_target_pairs={{0,4},{1,5},{2,6},{3,7},{4,0},{5,1},{6,2},{7,3},{8,12},{9,13},{10,... | collective-permute-start | bytes 405512 | tf_op jit(solution)/shard_map/ppermute | solution.py:28
  10.8 6.4 %collective-permute-start = (bf16[528,128]{1,0:T(8,128)(2,1)S(1)}, bf16[528,128]{1,0:T(8,128)(2,1)S(1)}, u32[]{:S(2)}, u32[]{:S(2)}) collective-permute-start(bf16[528,128]{1,0:T(8,128)(2,1)S(1)} %get-tuple-element.92), channel_id=1, source_target_pairs={{0,2},{1,3},{2,4},{3,5},{4,6},{5,7},{6,0},{7,1},{8,10},{9,11},{10,... | collective-permute-start | bytes 405512 | tf_op jit(solution)/shard_map/ppermute | solution.py:28
  11.2 6.0 %collective-permute-start.2 = (bf16[528,128]{1,0:T(8,128)(2,1)S(1)}, bf16[528,128]{1,0:T(8,128)(2,1)S(1)}, u32[]{:S(2)}, u32[]{:S(2)}) collective-permute-start(bf16[528,128]{1,0:T(8,128)(2,1)S(1)} %get-tuple-element.92), channel_id=1, source_target_pairs={{0,6},{1,7},{2,0},{3,1},{4,2},{5,3},{6,4},{7,5},{8,14},{9,15},{10,... | collective-permute-start | bytes 405512 | tf_op jit(solution)/shard_map/ppermute | solution.py:28
  18.1 14.1 %collective-permute-start.3 = (bf16[4,528,128]{2,1,0:T(8,128)(2,1)}, bf16[4,528,128]{2,1,0:T(8,128)(2,1)}, u32[]{:S(2)}, u32[]{:S(2)}) collective-permute-start(bf16[4,528,128]{2,1,0:T(8,128)(2,1)} %pad_maximum_fusion.4.mine_refs_0_), channel_id=1, source_target_pairs={{0,1},{1,0},{2,3},{3,2},{4,5},{5,4},{6,7},{7,6},{8,9},{9,8},{10,11... | collective-permute-start | bytes 1622024 | tf_op jit(solution)/shard_map/ppermute | solution.py:32
  18.3 13.9 %collective-permute-start.5 = (bf16[2,512,128]{2,1,0:T(8,128)(2,1)S(1)}, bf16[2,512,128]{2,1,0:T(8,128)(2,1)S(1)}, u32[]{:S(2)}, u32[]{:S(2)}) collective-permute-start(bf16[2,512,128]{2,1,0:T(8,128)(2,1)S(1)} %pad_maximum_fusion.7), channel_id=1, source_target_pairs={{0,2},{1,3},{2,4},{3,5},{4,6},{5,7},{6,0},{7,1},{8,10},{9,11},{10,... | collective-permute-start | bytes 786440 | tf_op jit(solution)/shard_map/ppermute | solution.py:28
  20.3 12.4 %collective-permute-start.6 = (bf16[2,512,128]{2,1,0:T(8,128)(2,1)S(1)}, bf16[2,512,128]{2,1,0:T(8,128)(2,1)S(1)}, u32[]{:S(2)}, u32[]{:S(2)}) collective-permute-start(bf16[2,512,128]{2,1,0:T(8,128)(2,1)S(1)} %pad_maximum_fusion.8), channel_id=1, source_target_pairs={{0,4},{1,5},{2,6},{3,7},{4,0},{5,1},{6,2},{7,3},{8,12},{9,13},{10,... | collective-permute-start | bytes 786440 | tf_op jit(solution)/shard_map/ppermute | solution.py:28
  22.6 10.6 %collective-permute-start.7 = (bf16[2,512,128]{2,1,0:T(8,128)(2,1)S(1)}, bf16[2,512,128]{2,1,0:T(8,128)(2,1)S(1)}, u32[]{:S(2)}, u32[]{:S(2)}) collective-permute-start(bf16[2,512,128]{2,1,0:T(8,128)(2,1)S(1)} %pad_maximum_fusion.9), channel_id=1, source_target_pairs={{0,6},{1,7},{2,0},{3,1},{4,2},{5,3},{6,4},{7,5},{8,14},{9,15},{10,... | collective-permute-start | bytes 786440 | tf_op jit(solution)/shard_map/ppermute | solution.py:28
  23.0 20.8 %collective-permute-start.8 = (bf16[4,528,128]{2,1,0:T(8,128)(2,1)}, bf16[4,528,128]{2,1,0:T(8,128)(2,1)}, u32[]{:S(2)}, u32[]{:S(2)}) collective-permute-start(bf16[4,528,128]{2,1,0:T(8,128)(2,1)} %pad_maximum_fusion.4.mine_refs_0_), channel_id=1, source_target_pairs={{0,8},{8,0},{16,24},{24,16},{32,40},{40,32},{48,56},{56,48},{64,72... | collective-permute-start | bytes 1622024 | tf_op jit(solution)/shard_map/ppermute | solution.py:40
  32.2 3.2 %copy-start.2 = (bf16[2,512,128]{2,1,0:T(8,128)(2,1)}, bf16[2,512,128]{2,1,0:T(8,128)(2,1)S(1)}, u32[]{:S(2)}) copy-start(bf16[2,512,128]{2,1,0:T(8,128)(2,1)S(1)} %collective-permute-done.5.in_refs_1_) | copy-start | bytes 786436
  32.7 2.7 %copy-start.3 = (bf16[2,512,128]{2,1,0:T(8,128)(2,1)}, bf16[2,512,128]{2,1,0:T(8,128)(2,1)S(1)}, u32[]{:S(2)}) copy-start(bf16[2,512,128]{2,1,0:T(8,128)(2,1)S(1)} %collective-permute-done.6.in_refs_2_) | copy-start | bytes 786436
  33.2 2.2 %copy-start.4 = (bf16[2,512,128]{2,1,0:T(8,128)(2,1)}, bf16[2,512,128]{2,1,0:T(8,128)(2,1)S(1)}, u32[]{:S(2)}) copy-start(bf16[2,512,128]{2,1,0:T(8,128)(2,1)S(1)} %collective-permute-done.7.in_refs_3_) | copy-start | bytes 786436
  33.2 10.6 %collective-permute-start.9 = (bf16[4,528,128]{2,1,0:T(8,128)(2,1)}, bf16[4,528,128]{2,1,0:T(8,128)(2,1)}, u32[]{:S(2)}, u32[]{:S(2)}) collective-permute-start(bf16[4,528,128]{2,1,0:T(8,128)(2,1)} %collective-permute-done.3.mine_refs_1_), channel_id=1, source_target_pairs={{0,8},{8,0},{16,24},{24,16},{32,40},{40,32},{48,56},{56,48},{64,72... | collective-permute-start | bytes 1622024 | tf_op jit(solution)/shard_map/ppermute | solution.py:40
  37.9 29.5 %collective-permute-start.12 = (bf16[128,4096]{1,0:T(8,128)(2,1)}, bf16[128,4096]{1,0:T(8,128)(2,1)S(1)}, u32[]{:S(2)}, u32[]{:S(2)}) collective-permute-start(bf16[128,4096]{1,0:T(8,128)(2,1)} %shard_map.110.own_refs_0_), channel_id=1, source_target_pairs={{0,8},{8,0},{16,24},{24,16},{32,40},{40,32},{48,56},{56,48},{64,72... | collective-permute-start | bytes 3145736 | tf_op jit(solution)/shard_map/ppermute | solution.py:40
  38.6 28.8 %collective-permute-start.11 = (bf16[128,4096]{1,0:T(8,128)(2,1)}, bf16[128,4096]{1,0:T(8,128)(2,1)S(1)}, u32[]{:S(2)}, u32[]{:S(2)}) collective-permute-start(bf16[128,4096]{1,0:T(8,128)(2,1)} %shard_map.110.own_refs_0_), channel_id=1, source_target_pairs={{0,96},{8,104},{16,112},{24,120},{32,0},{40,8},{48,16},{56,24},{64... | collective-permute-start | bytes 3145736 | tf_op jit(solution)/shard_map/ppermute | solution.py:36
  42.3 26.0 %collective-permute-start.10 = (bf16[128,4096]{1,0:T(8,128)(2,1)}, bf16[128,4096]{1,0:T(8,128)(2,1)}, u32[]{:S(2)}, u32[]{:S(2)}) collective-permute-start(bf16[128,4096]{1,0:T(8,128)(2,1)} %shard_map.110.own_refs_0_), channel_id=1, source_target_pairs={{0,32},{8,40},{16,48},{24,56},{32,64},{40,72},{48,80},{56,88},{64,... | collective-permute-start | bytes 3145736 | tf_op jit(solution)/shard_map/ppermute | solution.py:36
  43.8 25.7 %copy-start = (bf16[128,4096]{1,0:T(8,128)(2,1)S(1)}, bf16[128,4096]{1,0:T(8,128)(2,1)}, u32[]{:S(2)}) copy-start(bf16[128,4096]{1,0:T(8,128)(2,1)} %shard_map.110.own_refs_0_) | copy-start | bytes 3145732
  68.3 6.7 %copy-start.1 = (bf16[4,512,128]{2,1,0:T(8,128)(2,1)S(1)}, bf16[4,512,128]{2,1,0:T(8,128)(2,1)}, u32[]{:S(2)}) copy-start(bf16[4,512,128]{2,1,0:T(8,128)(2,1)} %get-tuple-element.53.grad_refs_0_) | copy-start | bytes 1572868
  68.3 3.6 %collective-permute-start.13 = (bf16[8,512,128]{2,1,0:T(8,128)(2,1)}, bf16[8,512,128]{2,1,0:T(8,128)(2,1)S(1)}, u32[]{:S(2)}, u32[]{:S(2)}) collective-permute-start(bf16[8,512,128]{2,1,0:T(8,128)(2,1)} %get-tuple-element.55), channel_id=1, source_target_pairs={{0,8},{8,0},{16,24},{24,16},{32,40},{40,32},{48,56},{56,48},{64,72... | collective-permute-start | bytes 3145736 | tf_op jit(solution)/shard_map/ppermute | solution.py:40
  69.5 4.0 %collective-permute-start.14 = (bf16[128,4096]{1,0:T(8,128)(2,1)}, bf16[128,4096]{1,0:T(8,128)(2,1)S(1)}, u32[]{:S(2)}, u32[]{:S(2)}) collective-permute-start(bf16[128,4096]{1,0:T(8,128)(2,1)} %collective-permute-done.10.own_refs_3_), channel_id=1, source_target_pairs={{0,8},{8,0},{16,24},{24,16},{32,40},{40,32},{48,56},{56,48},{64,72... | collective-permute-start | bytes 3145736 | tf_op jit(solution)/shard_map/ppermute | solution.py:40
  69.5 25.7 %collective-permute-start.19 = (bf16[128,4096]{1,0:T(8,128)(2,1)S(1)}, bf16[128,4096]{1,0:T(8,128)(2,1)S(1)}, u32[]{:S(2)}, u32[]{:S(2)}) collective-permute-start(bf16[128,4096]{1,0:T(8,128)(2,1)S(1)} %copy-done), channel_id=1, source_target_pairs={{0,64},{8,72},{16,80},{24,88},{32,96},{40,104},{48,112},{56,120},{... | collective-permute-start | bytes 3145736 | tf_op jit(solution)/shard_map/ppermute | solution.py:36
  75.1 26.5 %collective-permute-start.16 = (bf16[6,512,128]{2,1,0:T(8,128)(2,1)S(1)}, bf16[6,512,128]{2,1,0:T(8,128)(2,1)S(1)}, u32[]{:S(2)}, u32[]{:S(2)}) collective-permute-start(bf16[6,512,128]{2,1,0:T(8,128)(2,1)S(1)} %get-tuple-element.85), channel_id=1, source_target_pairs={{0,6},{1,7},{2,0},{3,1},{4,2},{5,3},{6,4},{7,5},{8,14},{9,15},{10,... | collective-permute-start | bytes 2359304 | tf_op jit(solution)/shard_map/ppermute | solution.py:28
  77.4 25.3 %collective-permute-start.15 = (bf16[6,512,128]{2,1,0:T(8,128)(2,1)S(1)}, bf16[6,512,128]{2,1,0:T(8,128)(2,1)S(1)}, u32[]{:S(2)}, u32[]{:S(2)}) collective-permute-start(bf16[6,512,128]{2,1,0:T(8,128)(2,1)S(1)} %get-tuple-element.86), channel_id=1, source_target_pairs={{0,2},{1,3},{2,4},{3,5},{4,6},{5,7},{6,0},{7,1},{8,10},{9,11},{10,... | collective-permute-start | bytes 2359304 | tf_op jit(solution)/shard_map/ppermute | solution.py:28
  77.4 14.3 %collective-permute-start.18 = (bf16[4,512,128]{2,1,0:T(8,128)(2,1)S(1)}, bf16[4,512,128]{2,1,0:T(8,128)(2,1)S(1)}, u32[]{:S(2)}, u32[]{:S(2)}) collective-permute-start(bf16[4,512,128]{2,1,0:T(8,128)(2,1)S(1)} %copy-done.1), channel_id=1, source_target_pairs={{0,1},{1,0},{2,3},{3,2},{4,5},{5,4},{6,7},{7,6},{8,9},{9,8},{10,11... | collective-permute-start | bytes 1572872 | tf_op jit(solution)/shard_map/ppermute | solution.py:32
  79.8 21.8 %collective-permute-start.17 = (bf16[2,512,128]{2,1,0:T(8,128)(2,1)S(1)}, bf16[2,512,128]{2,1,0:T(8,128)(2,1)S(1)}, u32[]{:S(2)}, u32[]{:S(2)}) collective-permute-start(bf16[2,512,128]{2,1,0:T(8,128)(2,1)S(1)} %get-tuple-element.82), channel_id=1, source_target_pairs={{0,4},{1,5},{2,6},{3,7},{4,0},{5,1},{6,2},{7,3},{8,12},{9,13},{10,... | collective-permute-start | bytes 786440 | tf_op jit(solution)/shard_map/ppermute | solution.py:28
  91.7 15.8 %collective-permute-start.22 = (bf16[128,4096]{1,0:T(8,128)(2,1)S(1)}, bf16[128,4096]{1,0:T(8,128)(2,1)S(1)}, u32[]{:S(2)}, u32[]{:S(2)}) collective-permute-start(bf16[128,4096]{1,0:T(8,128)(2,1)S(1)} %collective-permute-done.11.own_refs_1_), channel_id=1, source_target_pairs={{0,8},{8,0},{16,24},{24,16},{32,40},{40,32},{48,56},{56,48},{64,72... | collective-permute-start | bytes 3145736 | tf_op jit(solution)/shard_map/ppermute | solution.py:40
  102.6 11.3 %collective-permute-start.21 = (bf16[128,4096]{1,0:T(8,128)(2,1)S(1)}, bf16[128,4096]{1,0:T(8,128)(2,1)S(1)}, u32[]{:S(2)}, u32[]{:S(2)}) collective-permute-start(bf16[128,4096]{1,0:T(8,128)(2,1)S(1)} %collective-permute-done.19.own_refs_2_), channel_id=1, source_target_pairs={{0,8},{8,0},{16,24},{24,16},{32,40},{40,32},{48,56},{56,48},{64,72... | collective-permute-start | bytes 3145736 | tf_op jit(solution)/shard_map/ppermute | solution.py:40
  104.4 9.5 %collective-permute-start.20 = (bf16[2,512,128]{2,1,0:T(8,128)(2,1)S(1)}, bf16[2,512,128]{2,1,0:T(8,128)(2,1)S(1)}, u32[]{:S(2)}, u32[]{:S(2)}) collective-permute-start(bf16[2,512,128]{2,1,0:T(8,128)(2,1)S(1)} %fusion.2), channel_id=1, source_target_pairs={{0,1},{1,0},{2,3},{3,2},{4,5},{5,4},{6,7},{7,6},{8,9},{9,8},{10,11... | collective-permute-start | bytes 786440 | tf_op jit(solution)/shard_map/ppermute | solution.py:32
  107.0 26.1 %collective-permute-start.23 = (bf16[8,512,128]{2,1,0:T(8,128)(2,1)S(1)}, bf16[8,512,128]{2,1,0:T(8,128)(2,1)S(1)}, u32[]{:S(2)}, u32[]{:S(2)}) collective-permute-start(bf16[8,512,128]{2,1,0:T(8,128)(2,1)S(1)} %pad_maximum_fusion.1), channel_id=1, source_target_pairs={{0,4},{1,5},{2,6},{3,7},{4,0},{5,1},{6,2},{7,3},{8,12},{9,13},{10,... | collective-permute-start | bytes 3145736 | tf_op jit(solution)/shard_map/ppermute | solution.py:28
  113.9 31.0 %collective-permute-start.24 = (bf16[8,512,128]{2,1,0:T(8,128)(2,1)S(1)}, bf16[8,512,128]{2,1,0:T(8,128)(2,1)S(1)}, u32[]{:S(2)}, u32[]{:S(2)}) collective-permute-start(bf16[8,512,128]{2,1,0:T(8,128)(2,1)S(1)} %pad_maximum_fusion), channel_id=1, source_target_pairs={{0,1},{1,0},{2,3},{3,2},{4,5},{5,4},{6,7},{7,6},{8,9},{9,8},{10,11... | collective-permute-start | bytes 3145736 | tf_op jit(solution)/shard_map/ppermute | solution.py:32
  116.4 19.9 %collective-permute-start.27 = (bf16[2,512,128]{2,1,0:T(8,128)(2,1)S(1)}, bf16[2,512,128]{2,1,0:T(8,128)(2,1)S(1)}, u32[]{:S(2)}, u32[]{:S(2)}) collective-permute-start(bf16[2,512,128]{2,1,0:T(8,128)(2,1)S(1)} %add_convert_fusion.1.rest_1__0_), channel_id=1, source_target_pairs={{0,6},{1,7},{2,0},{3,1},{4,2},{5,3},{6,4},{7,5},{8,14},{9,15},{10,... | collective-permute-start | bytes 786440 | tf_op jit(solution)/shard_map/ppermute | solution.py:28
  116.7 21.9 %collective-permute-start.26 = (bf16[2,512,128]{2,1,0:T(8,128)(2,1)S(1)}, bf16[2,512,128]{2,1,0:T(8,128)(2,1)S(1)}, u32[]{:S(2)}, u32[]{:S(2)}) collective-permute-start(bf16[2,512,128]{2,1,0:T(8,128)(2,1)S(1)} %add_convert_fusion.1.rest_1__0_), channel_id=1, source_target_pairs={{0,4},{1,5},{2,6},{3,7},{4,0},{5,1},{6,2},{7,3},{8,12},{9,13},{10,... | collective-permute-start | bytes 786440 | tf_op jit(solution)/shard_map/ppermute | solution.py:28
  117.1 27.8 %collective-permute-start.25 = (bf16[2,512,128]{2,1,0:T(8,128)(2,1)S(1)}, bf16[2,512,128]{2,1,0:T(8,128)(2,1)S(1)}, u32[]{:S(2)}, u32[]{:S(2)}) collective-permute-start(bf16[2,512,128]{2,1,0:T(8,128)(2,1)S(1)} %add_convert_fusion.1.rest_1__0_), channel_id=1, source_target_pairs={{0,2},{1,3},{2,4},{3,5},{4,6},{5,7},{6,0},{7,1},{8,10},{9,11},{10,... | collective-permute-start | bytes 786440 | tf_op jit(solution)/shard_map/ppermute | solution.py:28
